TPU v7x, 32 devices: a whole 2x2x4 slice. The times are simulated.
32 devices in a mesh: groups: 2 (over y), seq: 4 (over z), head: 2 (over x), rep: 2 (over core).
Axes of the slice: x: 2, y: 2, z: 4, core: 2. Of those that a mesh axis runs over, the one named last changes fastest.
Arguments:
- prefix_x: bfloat16 [1024, 8192], P(('groups', 'seq'), ('head', 'rep')), parts along dimension 0, may hold values from -6 to 6
- prefix_b: bfloat16 [1024, 8, 256], P(('groups', 'seq'), ('head', 'rep')), parts along dimension 0, may hold values from -0.09375 to 0.09375
- prefix_c: bfloat16 [1024, 8, 256], P(('groups', 'seq'), ('head', 'rep')), parts along dimension 0, may hold values from -0.375 to 0.375
- prefix_decay: float32 [1024, 128], P(('groups', 'seq'), ('head', 'rep')), parts along dimension 0, may hold values from 0 to 1.5, as said below
- bypass_weight: float32 [128], replicated, may hold values from 0.1 to 1.9
- prefix_key_rows: bfloat16 [1024, 4, 128], P(('groups', 'seq'), 'head'), parts along dimension 0, may hold values from -8 to 8
- prefix_values: bfloat16 [1024, 4, 128], P(('groups', 'seq'), 'head'), parts along dimension 0, may hold values from -6 to 6
- cand_x: bfloat16 [16, 32, 8192], P(('groups', 'seq', 'rep'), None, 'head'), parts along dimension 0, may hold values from -6 to 6
- cand_b: bfloat16 [16, 32, 8, 256], P(('groups', 'seq', 'rep'), None, 'head'), parts along dimension 0, may hold values from -0.09375 to 0.09375
- cand_c: bfloat16 [16, 32, 8, 256], P(('groups', 'seq', 'rep'), None, 'head'), parts along dimension 0, may hold values from -0.375 to 0.375
- cand_decay: float32 [16, 32, 128], P(('groups', 'seq', 'rep'), None, 'head'), parts along dimension 0, may hold values from 0 to 1.5, as said below
- cand_queries: bfloat16 [16, 32, 32, 128], P(('groups', 'seq', 'rep'), None, 'head'), parts along dimension 0, may hold values from -8 to 8
- cand_keys: bfloat16 [16, 32, 4, 128], P(('groups', 'seq', 'rep'), None, 'head'), parts along dimension 0, may hold values from -16 to 16
- cand_values: bfloat16 [16, 32, 4, 128], P(('groups', 'seq', 'rep'), None, 'head'), parts along dimension 0, may hold values from -6 to 6
- cand_length: int32 [16], P(('groups', 'seq', 'rep')), parts along dimension 0, may hold values from 16 to 32
Outputs:
- prefix_out: bfloat16 [1024, 8192], P(('groups', 'seq'), ('head', 'rep')), parts along dimension 0
- cand_ssm: bfloat16 [16, 32, 8192], P(('groups', 'seq', 'rep'), None, 'head'), parts along dimension 0
- cand_attn: bfloat16 [16, 32, 32, 128], P(('groups', 'seq', 'rep'), None, 'head'), parts along dimension 0
There are 2 independent parts, one for each index of `groups`. A program takes and returns all parts, laid end to end along the dimension named above; an argument that names none is the same for every part. Nothing has to cross between parts.
Inputs may be any that keep to these rules, and one draw needn't show every extreme that they name: `prefix_decay`: positive. `cand_decay`: positive.
All inputs are finite; a program needn't handle non-finite values.
Results may differ from a plain program's by a relative error of at most 0.008.
Values may be sent and summed in bfloat16 or wider, within the bound.
No kernel may reach another device: no remote copies, remote signals or barrier semaphores. Data moves between devices by JAX's collectives and lax.ppermute only.
A program may use at most 128 MiB of HBM per device.

v0:
```python
import math

import jax
import jax.numpy as jnp
from jax import lax
from jax.sharding import PartitionSpec as P

EPSILON = 1e-06
FLOOR = -1e30
HIGH = lax.Precision.HIGHEST


def entering(part, axis, combine, identity, reverse):
    count = lax.axis_size(axis)
    place = lax.axis_index(axis)
    ahead = count - 1 - place if reverse else place
    gathered = jax.tree.map(lambda a: lax.all_gather(a, axis), part)
    state = jax.tree.map(lambda a, e: jnp.zeros_like(a) + jnp.asarray(e, a.dtype), part, identity)

    def one(hop, state):
        source = count - 1 - hop if reverse else hop
        return combine(
            state, jax.tree.map(lambda a: lax.dynamic_index_in_dim(a, source, 0, False), gathered)
        )

    return lax.fori_loop(0, ahead, one, state)


def summarize(x, bmat, decay):
    length, groups, state = bmat.shape
    heads = decay.shape[1]
    per_group = heads // groups
    width = x.shape[1] // heads
    cum = jnp.cumsum(decay, axis=0)
    total = jnp.exp(-cum[-1])
    weights = jnp.exp(cum[-1][None, :] - cum)
    inputs = x.reshape(length, heads, width)
    weighted = (inputs.astype(jnp.float32) * weights[:, :, None]).astype(jnp.bfloat16)
    weighted = weighted.reshape(length, groups, per_group, width)
    local = jnp.einsum("sgn,sgkp->gknp", bmat, weighted, preferred_element_type=jnp.float32)
    return (cum, total, local.reshape(heads, state, width))


def emit(x, bmat, cmat, cum, skip, start):
    length, groups, state = bmat.shape
    heads = cum.shape[1]
    per_group = heads // groups
    width = x.shape[1] // heads
    inputs = x.reshape(length, heads, width)
    gram = jnp.einsum("tgn,sgn->gts", cmat, bmat, preferred_element_type=jnp.float32)
    span = math.gcd(per_group, 4)
    count = heads // span
    causal = lax.broadcasted_iota(jnp.int32, (length, length), 0) >= lax.broadcasted_iota(
        jnp.int32, (length, length), 1
    )
    cum_sets = cum.T.reshape(count, span, length)
    input_sets = inputs.reshape(length, count, span, width).transpose(1, 0, 2, 3)

    def one_set(piece):
        index, cum_set, input_set = piece
        gram_set = lax.dynamic_index_in_dim(gram, index * span // per_group, 0, keepdims=False)
        gap = cum_set[:, :, None] - cum_set[:, None, :]
        state_mixing = jnp.where(causal, jnp.exp(-jnp.where(causal, gap, 0.0)), 0.0) * gram_set
        return jnp.einsum(
            "hts,shp->thp",
            state_mixing.astype(jnp.bfloat16),
            input_set,
            preferred_element_type=jnp.float32,
        )

    intra = lax.map(one_set, (jnp.arange(count, dtype=jnp.int32), cum_sets, input_sets))
    intra = intra.transpose(1, 0, 2, 3).reshape(length, heads, width)
    start_set = start.reshape(groups, per_group, state, width)
    carried = jnp.einsum("tgn,gknp->tgkp", cmat.astype(jnp.float32), start_set, precision=HIGH)
    carried = carried.reshape(length, heads, width)
    result = (
        intra
        + jnp.exp(-cum)[:, :, None] * carried
        + skip[None, :, None] * inputs.astype(jnp.float32)
    )
    return result.reshape(length, heads * width).astype(jnp.bfloat16)


def chain_step(earlier, later):
    return (earlier[0] * later[0], later[0][:, None, None] * earlier[1] + later[1])


def elementwise_product(earlier, later):
    return earlier * later


def blend(carry, scores, values):
    top, mass, acc = carry
    new_top = jnp.maximum(top, scores.max(-1))
    fade = jnp.exp(top - new_top)
    weights = jnp.exp(scores - new_top[..., None])
    mass = mass * fade + weights.sum(-1)
    acc = acc * fade[..., None] + jnp.einsum(
        "ctkqs,skd->ctkqd", weights.astype(jnp.bfloat16), values, preferred_element_type=jnp.float32
    )
    return (new_top, mass, acc)


def join(first, second):
    top = jnp.maximum(first[0], second[0])
    one = jnp.exp(first[0] - top)
    two = jnp.exp(second[0] - top)
    return (
        top,
        first[1] * one + second[1] * two,
        first[2] * one[..., None] + second[2] * two[..., None],
    )


def key_folder(query_set, scale, carry, piece):
    keys, values = piece
    rows = keys.shape[0]
    step = math.gcd(rows, 1024)

    def one_block(inner, index):
        key_block = lax.dynamic_slice_in_dim(keys, index * step, step, 0)
        value_block = lax.dynamic_slice_in_dim(values, index * step, step, 0)
        scores = (
            jnp.einsum("ctkqd,skd->ctkqs", query_set, key_block, preferred_element_type=jnp.float32)
            * scale
        )
        return (blend(inner, scores, value_block), None)

    carry, unused = lax.scan(one_block, carry, jnp.arange(rows // step, dtype=jnp.int32))
    return carry


def empty_softmax(count, steps, kv_local, per_kv, dim):
    shape = (count, steps, kv_local, per_kv)
    return (
        jnp.full(shape, FLOOR, jnp.float32),
        jnp.zeros(shape, jnp.float32),
        jnp.zeros(shape + (dim,), jnp.float32),
    )


def on_device(
    prefix_x,
    prefix_b,
    prefix_c,
    prefix_decay,
    bypass_weight,
    prefix_key_rows,
    prefix_values,
    cand_x,
    cand_b,
    cand_c,
    cand_decay,
    cand_queries,
    cand_keys,
    cand_values,
    cand_length,
):
    local_heads = prefix_decay.shape[1]
    spread = lax.axis_size("rep")
    offset = (lax.axis_index("head") * spread + lax.axis_index("rep")) * local_heads
    skip_local = lax.dynamic_slice_in_dim(bypass_weight, offset, local_heads)
    cum, total, local = summarize(prefix_x, prefix_b, prefix_decay)
    identity = (jnp.ones_like(total), jnp.zeros_like(local))
    carried_in = entering((total, local), "seq", chain_step, identity, False)[1]
    prefix_out = emit(prefix_x, prefix_b, prefix_c, cum, skip_local, carried_in)
    beyond = entering(total, "seq", elementwise_product, jnp.ones_like(total), True)
    final = lax.psum(beyond[:, None, None] * local, "seq")
    heads_final = lax.all_gather(final, "rep", axis=0, tiled=True)
    cand_heads = cand_decay.shape[2]
    cand_skip = lax.dynamic_slice_in_dim(
        bypass_weight, lax.axis_index("head") * cand_heads, cand_heads
    )
    steps = cand_x.shape[1]
    valid = lax.broadcasted_iota(jnp.int32, (steps,), 0) < cand_length[0]
    cand_cum = jnp.cumsum(cand_decay[0], axis=0)
    cand_out = emit(cand_x[0], cand_b[0], cand_c[0], cand_cum, cand_skip, heads_final)
    cand_ssm = jnp.where(valid[:, None], cand_out, jnp.zeros((), jnp.bfloat16))[None]
    kv_local = prefix_key_rows.shape[1]
    dim = prefix_key_rows.shape[2]
    per_kv = cand_queries.shape[2] // kv_local
    scale = dim ** (-0.5)
    query = cand_queries[0].reshape(steps, kv_local, per_kv, dim)
    init = empty_softmax(1, steps, kv_local, per_kv, dim)
    part = key_folder(
        query[None],
        scale,
        init,
        (
            lax.all_gather(prefix_key_rows, "seq", axis=0, tiled=True),
            lax.all_gather(prefix_values, "seq", axis=0, tiled=True),
        ),
    )
    part = (part[0][0], part[1][0], part[2][0])
    own_scores = (
        jnp.einsum("tkqd,skd->tkqs", query, cand_keys[0], preferred_element_type=jnp.float32)
        * scale
    )
    visible = lax.broadcasted_iota(jnp.int32, (steps, 1, 1, steps), 0) >= lax.broadcasted_iota(
        jnp.int32, (steps, 1, 1, steps), 3
    )
    own_scores = jnp.where(visible, own_scores, FLOOR)
    own_top = own_scores.max(-1)
    own_weights = jnp.exp(own_scores - own_top[..., None])
    own_acc = jnp.einsum(
        "tkqs,skd->tkqd",
        own_weights.astype(jnp.bfloat16),
        cand_values[0],
        preferred_element_type=jnp.float32,
    )
    top, mass, acc = join(part, (own_top, own_weights.sum(-1), own_acc))
    mixed = acc / mass[..., None]
    mixed = mixed * lax.rsqrt(jnp.mean(mixed * mixed, axis=-1, keepdims=True) + EPSILON)
    mixed = mixed.reshape(steps, kv_local * per_kv, dim)
    cand_attn = jnp.where(valid[:, None, None], mixed, 0.0).astype(jnp.bfloat16)[None]
    return (prefix_out, cand_ssm, cand_attn)


def solution(mesh):
    placed = (
        P(("groups", "seq"), ("head", "rep")),
        P(("groups", "seq"), ("head", "rep"), None),
        P(("groups", "seq"), ("head", "rep"), None),
        P(("groups", "seq"), ("head", "rep")),
        P(),
        P(("groups", "seq"), "head", None),
        P(("groups", "seq"), "head", None),
        P(("groups", "seq", "rep"), None, "head"),
        P(("groups", "seq", "rep"), None, "head", None),
        P(("groups", "seq", "rep"), None, "head", None),
        P(("groups", "seq", "rep"), None, "head"),
        P(("groups", "seq", "rep"), None, "head", None),
        P(("groups", "seq", "rep"), None, "head", None),
        P(("groups", "seq", "rep"), None, "head", None),
        P(("groups", "seq", "rep")),
    )
    return jax.shard_map(
        on_device,
        mesh=mesh,
        in_specs=placed,
        out_specs=(
            P(("groups", "seq"), ("head", "rep")),
            P(("groups", "seq", "rep"), None, "head"),
            P(("groups", "seq", "rep"), None, "head", None),
        ),
        check_vma=False,
    )
```

profile of v0, /device:TPU:27, one launch (start us, length us, event | category | flops | bytes accessed | tf_op | source)
XLA Modules:
  0.0 333.7 jit_solution(1568227480460070948)
XLA Ops:
  7.2 0.8 copy.82
  8.4 5.7 %all-gather = f32[4,1,32]{2,1,0:T(1,128)} all-gather(f32[1,1,32]{2,1,0:T(1,128)S(1)} %get-tuple-element.463), channel_id=1, replica_groups=mesh['groups'=2,'seq'=4,'head'=2,'rep'=2] {'seq'}, dimensions={0}, use_global_device_ids=true | all-gather | bytes 640 | tf_op jit(solution)/shard_map/all_gather | solution.py:17
  14.1 1.3 copy.81
  16.0 1.8 bitcast_multiply_fusion.1
  17.9 90.4 %all-reduce.2.cloned.1.call-done = f32[32,256,64]{1,2,0:T(8,128)} async-done(((f32[32,256,64]{1,2,0:T(8,128)}), f32[32,256,64]{1,2,0:T(8,128)}) %all-reduce.2.cloned.1.call-update) | async-done | bytes 2097168 | tf_op jit(solution)/shard_map/psum | solution.py:168
  109.9 35.0 %while.61 = (s32[]{:T(128)}, f32[16,32,4,64]{3,1,2,0:T(8,128)}, bf16[16,32,4,64]{3,2,0,1:T(4,128)(2,1)S(1)}, f32[16,4,32]{2,1,0:T(4,128)S(1)}, s32[16]{0:T(128)S...) while((s32[]{:T(128)}, f32[16,32,4,64]{3,1,2,0:T(8,128)}, ...), condition=%wide.region_7.8_spmd.clone.clone, body=%wide.region_6.7_spmd.clone.clone.sunk | while | flops 549909 | bytes 166237 | solution.py:71
  111.3 0.8 fusion.74
  113.4 0.8 fusion.74
  115.6 0.8 fusion.74
  117.8 0.8 fusion.74
  120.0 0.8 fusion.74
  122.2 0.8 fusion.74
  124.4 0.8 fusion.74
  126.6 0.8 fusion.74
  128.8 0.8 fusion.74
  131.0 0.8 fusion.74
  133.1 0.8 fusion.74
  135.3 0.8 fusion.74
  137.5 0.8 fusion.74
  139.7 0.8 fusion.74
  141.9 0.8 fusion.74
  144.1 0.8 fusion.74
  148.0 0.9 copy.100
  149.0 1.5 copy.103
  150.4 1.3 fusion.64
  151.8 0.8 copy.108
  152.6 16.9 %all_gather.21 = bf16[512,2,128]{2,0,1:T(8,128)(2,1)S(1)} all-gather(bf16[128,2,128]{2,0,1:T(8,128)(2,1)S(1)} %copy.100), channel_id=1, replica_groups=mesh['groups'=2,'seq'=4,'head'=2,'rep'=2] {'seq'}, dimensions={0}, use_global_device_ids=true | all-gather | bytes 327680 | tf_op jit(solution)/shard_map/all_gather | solution.py:190
  169.9 1.0 fusion.33
  170.9 0.7 copy.111
  171.6 0.7 copy.110
  173.0 0.7 copy.102
  175.1 0.8 reshape.257
  175.9 18.5 %all_gather.22 = bf16[512,2,128]{2,0,1:T(8,128)(2,1)S(1)} all-gather(bf16[128,2,128]{2,0,1:T(8,128)(2,1)} %copy.103), channel_id=1, replica_groups=mesh['groups'=2,'seq'=4,'head'=2,'rep'=2] {'seq'}, dimensions={0}, use_global_device_ids=true | all-gather | bytes 327680 | tf_op jit(solution)/shard_map/all_gather | solution.py:191
  194.5 1.5 fusion.29
  196.0 1.2 multiply_reduce_fusion
  197.4 0.8 fusion.42
  198.3 23.3 %while.60 = (s32[]{:T(128)}, f32[8,128,4,64]{1,3,2,0:T(8,128)}, bf16[8,128,4,64]{1,3,2,0:T(8,128)(2,1)S(1)}, f32[8,4,128]{2,1,0:T(4,128)}, s32[8]{0:T(128)S(1)},...) while((s32[]{:T(128)}, f32[8,128,4,64]{1,3,2,0:T(8,128)}, ...), condition=%wide.region_2.3_spmd.clone.clone, body=%wide.region_1.2_spmd.clone.clone.sunk | while | flops 8798229 | bytes 435549 | solution.py:71
  200.3 0.9 fusion.73
  203.2 0.9 fusion.73
  206.1 0.9 fusion.73
  209.0 0.9 fusion.73
  211.9 0.9 fusion.73
  214.1 0.7 dynamic-slice_bitcast_fusion.12
  214.8 1.0 fusion.73
  217.7 0.9 fusion.73
  220.7 0.9 fusion.73
  221.6 5.2 %convolution_bitcast_fusion.2 = f32[32,4,16,64]{3,0,2,1:T(8,128)S(1)} fusion(f32[4,16,256,64]{2,3,1,0:T(8,128)} %bitcast.178, bf16[32,4,256,1]{2,1,0,3:T(4,128)(2,1)S(1)} %bitcast.186), kind=kOutput, calls=%fused_computation.36 | convolution fusion | flops 402653184 | bytes 4784128 | tf_op jit(solution)/shard_map/tgn,gknp->tgkp/dot_general | solution.py:74
  227.8 1.6 fusion.39
  229.4 53.1 %all-gather.4.cloned.1.call-done = f32[4,32,256,64]{2,3,1,0:T(8,128)} async-done(((f32[1,32,256,64]{2,3,1,0:T(8,128)}), f32[4,32,256,64]{2,3,1,0:T(8,128)}) %all-gather.4.cloned.1.call-update) | async-done | bytes 8388624 | tf_op jit(solution)/shard_map/all_gather | solution.py:17
  282.5 2.4 broadcast_in_dim.130
  285.0 35.0 %while.58 = (s32[]{:T(128)}, f32[32,256,64]{2,1,0:T(8,128)}, s32[]{:T(128)}, f32[4,32]{1,0:T(4,128)}, f32[4,32,256,64]{2,3,1,0:T(8,128)}, /*index=5*/s32[]{:T(128)}, s32[]{:T(128)}, s32[]{:T(128)}) while((s32[]{:T(128)}, f32[32,256,64]{2,1,0:T(8,128)}, s32[]{:T(128)}, f32[4,32]{1,0:T(4,128)}, f32[4,32,256,64]{2,3,1,0:T(8,128)}, ...), condition=%wide.region_4.5_spmd, body=%wide.region_3.4_spmd.sunk | while | flops 1048581 | bytes 14680583 | solution.py:26
  285.0 0.7 dynamic-slice_bitcast_fusion.10
  285.7 1.8 constant_dynamic-slice_fusion.4
  287.5 2.7 copy.171
  290.2 6.5 %bitcast_add_fusion.2 = f32[32,256,64]{2,1,0:T(8,128)} fusion(f32[1,32,256,64]{3,2,1,0:T(8,128)} %copy.171, f32[32,256,64]{2,1,0:T(8,128)} %get-tuple-element.612, f32[32]{0:T(128)S(1)} %dynamic-slice_bitcast_fusion.10), kind=kLoop, calls=%fused_computation.2.clone.1 | loop fusion | flops 1048576 | bytes 6291584 | tf_op jit(solution)/shard_map/while/body/add | solution.py:85
  296.7 0.7 dynamic-slice_bitcast_fusion.10
  297.4 1.8 constant_dynamic-slice_fusion.4
  299.1 2.7 copy.171
  301.8 6.5 %bitcast_add_fusion.2 = f32[32,256,64]{2,1,0:T(8,128)} fusion(f32[1,32,256,64]{3,2,1,0:T(8,128)} %copy.171, f32[32,256,64]{2,1,0:T(8,128)} %get-tuple-element.612, f32[32]{0:T(128)S(1)} %dynamic-slice_bitcast_fusion.10), kind=kLoop, calls=%fused_computation.2.clone.1 | loop fusion | flops 1048576 | bytes 6291584 | tf_op jit(solution)/shard_map/while/body/add | solution.py:85
  309.0 1.8 constant_dynamic-slice_fusion.4
  310.8 2.7 copy.171
  313.5 6.5 %bitcast_add_fusion.2 = f32[32,256,64]{2,1,0:T(8,128)} fusion(f32[1,32,256,64]{3,2,1,0:T(8,128)} %copy.171, f32[32,256,64]{2,1,0:T(8,128)} %get-tuple-element.612, f32[32]{0:T(128)S(1)} %dynamic-slice_bitcast_fusion.10), kind=kLoop, calls=%fused_computation.2.clone.1 | loop fusion | flops 1048576 | bytes 6291584 | tf_op jit(solution)/shard_map/while/body/add | solution.py:85
  320.0 5.7 %fusion.45 = f32[2,16,64,128]{3,2,1,0:T(8,128)S(1)} fusion(f32[2,16,256,64]{3,2,1,0:T(8,128)} %bitcast.173, bf16[128,2,256,1]{2,1,0,3:T(2,128)(2,1)S(1)} %bitcast.184), kind=kOutput, calls=%fused_computation.72 | convolution fusion | flops 805306368 | bytes 3276800 | tf_op jit(solution)/shard_map/tgn,gknp->tgkp/dot_general | solution.py:74
  326.1 1.0 copy.113
  (190 shorter events, 29.5 us)
Async XLA Ops:
  7.2 8.4 %copy-start = (bf16[128,2,256]{2,1,0:T(2,128)(2,1)S(1)}, bf16[128,2,256]{2,1,0:T(2,128)(2,1)}, u32[]{:S(2)}) copy-start(bf16[128,2,256]{2,1,0:T(2,128)(2,1)} %param.24) | copy-start | bytes 393220
  7.2 101.1 %all-reduce.2.cloned.1.call-start = ((), (), s32[]{:S(2)}) async-start(), calls=%async_computation.1 | async-start | bytes 4194304 | tf_op jit(solution)/shard_map/psum | solution.py:168
  16.0 92.3 %copy-start.1 = (f32[2,16,64,256]{3,2,1,0:T(8,128)}, f32[2,16,64,256]{3,2,1,0:T(8,128)S(1)}, u32[]{:S(2)}) copy-start(f32[2,16,64,256]{3,2,1,0:T(8,128)S(1)} %fusion.36) | copy-start | bytes 6291460
  17.8 91.3 %copy-start.12 = (f32[1,32,64]{2,1,0:T(8,128)S(1)}, f32[1,32,64]{2,1,0:T(8,128)}, u32[]{:S(2)}) copy-start(f32[1,32,64]{2,1,0:T(8,128)} %param.33) | copy-start | bytes 24580
  17.8 91.4 %copy-start.3 = (bf16[1,32,4096]{2,1,0:T(8,128)(2,1)S(1)}, bf16[1,32,4096]{2,1,0:T(8,128)(2,1)}, u32[]{:S(2)}) copy-start(bf16[1,32,4096]{2,1,0:T(8,128)(2,1)} %param.30) | copy-start | bytes 786436
  17.8 92.0 %copy-start.8 = (bf16[1,32,4,256]{3,2,1,0:T(4,128)(2,1)S(1)}, bf16[1,32,4,256]{3,2,1,0:T(4,128)(2,1)}, u32[]{:S(2)}) copy-start(bf16[1,32,4,256]{3,2,1,0:T(4,128)(2,1)} %param.32) | copy-start | bytes 196612
  17.8 92.0 %copy-start.10 = (bf16[1,32,4,256]{3,2,1,0:T(4,128)(2,1)S(1)}, bf16[1,32,4,256]{3,2,1,0:T(4,128)(2,1)}, u32[]{:S(2)}) copy-start(bf16[1,32,4,256]{3,2,1,0:T(4,128)(2,1)} %param.31) | copy-start | bytes 196612
  17.8 127.8 %copy-start.14 = (f32[128]{0:T(128)S(1)}, f32[128]{0:T(128)}, u32[]{:S(2)}) copy-start(f32[128]{0:T(128)} %param.27) | copy-start | bytes 1540
  17.8 203.8 %all-gather.6.cloned.1.call-start = ((), (), s32[]{:S(2)}) async-start(), calls=%async_computation.2 | async-start | bytes 6291456 | tf_op jit(solution)/shard_map/all_gather | solution.py:169
  108.3 174.2 %all-gather.4.cloned.1.call-start = ((), (), s32[]{:S(2)}) async-start(), calls=%async_computation | async-start | bytes 10485760 | tf_op jit(solution)/shard_map/all_gather | solution.py:17
  108.3 61.2 %copy-start.5 = (bf16[1,32,16,128]{3,2,1,0:T(8,128)(2,1)S(1)}, bf16[1,32,16,128]{3,2,1,0:T(8,128)(2,1)}, u32[]{:S(2)}) copy-start(bf16[1,32,16,128]{3,2,1,0:T(8,128)(2,1)} %param.34) | copy-start | bytes 393220
  147.9 26.5 %copy-start.4 = (f32[16,32,4,64]{3,1,2,0:T(8,128)S(1)}, f32[16,32,4,64]{3,1,2,0:T(8,128)}, u32[]{:S(2)}) copy-start(f32[16,32,4,64]{3,1,2,0:T(8,128)} %get-tuple-element.312) | copy-start | bytes 1572868
  175.1 22.1 %copy-start.6 = (bf16[128,2,256]{2,1,0:T(2,128)(2,1)S(1)}, bf16[128,2,256]{2,1,0:T(2,128)(2,1)}, u32[]{:S(2)}) copy-start(bf16[128,2,256]{2,1,0:T(2,128)(2,1)} %param.25) | copy-start | bytes 393220
  175.9 45.7 %copy-start.9 = (bf16[1,32,4,256]{3,2,1,0:T(4,128)(2,1)S(1)}, bf16[1,32,4,256]{3,2,1,0:T(4,128)(2,1)}, u32[]{:S(2)}) copy-start(bf16[1,32,4,256]{3,2,1,0:T(4,128)(2,1)} %param.32) | copy-start | bytes 196612
  194.5 27.2 %copy-start.13 = (pred[32]{0:T(512)(128)(4,1)}, pred[32]{0:T(512)(128)(4,1)S(1)}, u32[]{:S(2)}) copy-start(pred[32]{0:T(512)(128)(4,1)S(1)} %iota_compare_fusion.3) | copy-start | bytes 100
  285.0 35.0 %copy-start.7 = (bf16[128,2,256]{2,1,0:T(2,128)(2,1)S(1)}, bf16[128,2,256]{2,1,0:T(2,128)(2,1)}, u32[]{:S(2)}) copy-start(bf16[128,2,256]{2,1,0:T(2,128)(2,1)} %param.25) | copy-start | bytes 393220
  320.0 5.7 %copy-start.2 = (f32[8,128,4,64]{1,3,2,0:T(8,128)S(1)}, f32[8,128,4,64]{1,3,2,0:T(8,128)}, u32[]{:S(2)}) copy-start(f32[8,128,4,64]{1,3,2,0:T(8,128)} %get-tuple-element.310) | copy-start | bytes 3145732
  320.0 5.7 %copy-start.11 = (f32[2048]{0:T(1024)S(1)}, f32[2048]{0:T(1024)}, u32[]{:S(2)}) copy-start(f32[2048]{0:T(1024)} %mul.257) | copy-start | bytes 24580
Sparse Core Ops, SparseCore 0:
  17.9 90.2 all-reduce.1
  109.9 15.0 all-gather.5
  126.6 155.8 all-gather.3
where the time goes:
time: 335 us; the launch traced here: 334 us
  waiting for transfers between devices  144 us (43%)
  local copies, waits for them, and re-layouts  53.7 us (16%)
  blocking collectives  41.2 us (12%)
  matrix products  37 us (11%)
  other arithmetic  25.8 us (8%)
  loops' own time  16.9 us (5%)
  between operations  14.7 us (4%)
    psum x1, waiting for transfers between devices, on_device(): final = lax.psum(beyond[:, None, None] * local, 'seq')  90.4 us
    all_gather x1, waiting for transfers between devices, entering(): gathered = jax.tree.map(lambda a: lax.all_gather(a, axis), part)  53.1 us
    dot_general x24, matrix products, one_set(): jnp.einsum('hts,shp->thp', state_mixing.astype(jnp.bfloat16), input_set,...  21 us
    add x3, other arithmetic, chain_step(): later[0][:, None, None] * earlier[1] + later[1]  19.5 us
    all_gather x1, blocking collectives, on_device(): lax.all_gather(prefix_values, 'seq', axis=0, tiled=True)  18.5 us
    all_gather x1, blocking collectives, on_device(): lax.all_gather(prefix_key_rows, 'seq', axis=0, tiled=True)  16.9 us
    another operation x2, loops' own time, emit(): lax.map(one_set, (jnp.arange(count, dtype=jnp.int32), cum_sets, input_sets))  16.9 us
    dynamic_slice x40, local copies, waits for them, and re-layouts, emit(): lax.map(one_set, (jnp.arange(count, dtype=jnp.int32), cum_sets, input_sets))  14.4 us
  transfers between devices with their start and end apart: 3, of which 2 were waited for; matrix products, arithmetic and copies ran while one was open for 20% of the time, Pallas kernels for 0%

commit v1 on v0

v1 whole, which is shorter than its diff:
```python
import functools

import jax
import jax.numpy as jnp
from jax import lax
from jax.experimental import pallas as pl
from jax.experimental.pallas import tpu as pltpu
from jax.sharding import PartitionSpec as P

EPSILON = 1e-06
NEG = -1e30
CHUNKS = 4
F32 = jnp.float32
BF16 = jnp.bfloat16


def mm(a, b):
    return lax.dot_general(a, b, (((1,), (0,)), ((), ())), preferred_element_type=F32)


def mm_nt(a, b):
    return lax.dot_general(a, b, (((1,), (1,)), ((), ())), preferred_element_type=F32)


def mm_tn(a, b):
    return lax.dot_general(a, b, (((0,), (0,)), ((), ())), preferred_element_type=F32)


def exact_nt(a, b):
    return lax.dot_general(
        a, b, (((1,), (1,)), ((), ())), preferred_element_type=F32, precision=lax.Precision.HIGHEST
    )


def exact(a, b):
    return lax.dot_general(
        a, b, (((1,), (0,)), ((), ())), preferred_element_type=F32, precision=lax.Precision.HIGHEST
    )


def iota(shape, dim):
    return lax.broadcasted_iota(jnp.int32, shape, dim)


def split3(a):
    hi = a.astype(BF16)
    rest = a - hi.astype(F32)
    mid = rest.astype(BF16)
    return hi, mid, (rest - mid.astype(F32)).astype(BF16)


def spread(a, width, first=0, count=None):
    rows, cols = a.shape
    count = cols if count is None else count
    parts = jnp.concatenate(split3(a), axis=1)
    shape = (3 * cols, count * width)
    source = iota(shape, 0)
    source = jnp.where(source >= 2 * cols, source - 2 * cols, jnp.where(source >= cols, source - cols, source))
    unit = (source == first + iota(shape, 1) // width).astype(F32).astype(BF16)
    return mm(parts, unit)


def group_of(array, g):
    return array.astype(F32)[:, g, :].astype(BF16)


def pack_kernel(c_ref, k_ref, v_ref, out_ref):
    rep = lax.axis_index("rep")
    steps, groups, state = c_ref.shape[1:]
    c = c_ref[0].astype(F32)
    for g in range(groups):
        out_ref[:steps, g * state : (g + 1) * state] = c[:, g, :].astype(BF16)
    k = k_ref[...].astype(F32)
    v = v_ref[...].astype(F32)
    tokens, heads, dim = k.shape
    kv = jnp.where(rep == 0, k, v)
    parts = groups * state // (heads * dim)
    rows = tokens // parts
    for i in range(parts):
        for j in range(heads):
            at = (i * heads + j) * dim
            out_ref[steps : steps + rows, at : at + dim] = kv[i * rows : (i + 1) * rows, j, :].astype(BF16)


def local_kernel(x_ref, b_ref, decay_t_ref, b2_ref, cum_ref, total_ref, *outs):
    local_refs, send_refs = outs[:CHUNKS], outs[CHUNKS:]
    tokens, groups, state = b_ref.shape
    heads = decay_t_ref.shape[0]
    width = x_ref.shape[1] // heads
    lower = (iota((tokens, tokens), 0) >= iota((tokens, tokens), 1)).astype(F32)
    cum = exact_nt(lower, decay_t_ref[...])
    cum_ref[...] = cum
    last = cum[tokens - 1 : tokens, :]
    total = jnp.exp(-last)
    total_ref[...] = spread(jnp.broadcast_to(total, (8, heads)), width)
    weights = spread(jnp.exp(last - cum), width)
    b = b_ref[...].astype(F32)
    for g in range(groups):
        b2_ref[:, g * state : (g + 1) * state] = b[:, g, :].astype(BF16)
    cols = x_ref.shape[1] // CHUNKS
    for q in range(CHUNKS):
        g = q * groups // CHUNKS
        at = slice(q * cols, (q + 1) * cols)
        weighted = (x_ref[:, at].astype(F32) * weights[:, at]).astype(BF16)
        local = mm_tn(b2_ref[:, g * state : (g + 1) * state], weighted)
        local_refs[q][...] = local
        send_refs[q][...] = local.astype(BF16)


def intra_kernel(x_ref, b2_ref, c_ref, cum_ref, skip_ref, c2_ref, base_ref):
    tokens, groups, state = c_ref.shape
    heads = cum_ref.shape[1]
    width = x_ref.shape[1] // heads
    per_group = heads // groups
    first = (lax.axis_index("head") * lax.axis_size("rep") + lax.axis_index("rep")) * heads
    c = c_ref[...].astype(F32)
    for g in range(groups):
        c2_ref[:, g * state : (g + 1) * state] = c[:, g, :].astype(BF16)
    skip = spread(jnp.broadcast_to(skip_ref[...], (8, skip_ref.shape[1])), width, first, heads)[:1]
    cum = cum_ref[...]
    cum_t = cum.T
    shape = (tokens, tokens)
    hidden = jnp.where(iota(shape, 0) >= iota(shape, 1), 0.0, NEG)
    pair = 2 * width
    lane = iota((tokens, pair), 1)
    for g in range(groups):
        here = slice(g * state, (g + 1) * state)
        gram = mm_nt(c2_ref[:, here], b2_ref[:, here])
        for h in range(g * per_group, (g + 1) * per_group, 2):
            mixing = []
            for i in (h, h + 1):
                gap = cum_t[i : i + 1, :] - jnp.broadcast_to(cum[:, i : i + 1], shape)
                mixing.append((jnp.exp(gap + hidden) * gram).astype(BF16))
            at = slice(h * width, (h + 2) * width)
            x = x_ref[:, at]
            zero = jnp.zeros_like(x)
            inputs = jnp.concatenate(
                [jnp.where(lane < width, x, zero), jnp.where(lane < width, zero, x)], axis=0
            )
            base_ref[:, at] = mm(jnp.concatenate(mixing, axis=1), inputs) + skip[:, at] * x.astype(F32)


def cand_kernel(x_ref, b_ref, c_ref, decay_ref, skip_ref, base_ref, fade_ref):
    steps, groups, state = b_ref.shape[1:]
    heads = decay_ref.shape[2]
    width = x_ref.shape[2] // heads
    per_group = heads // groups
    first = lax.axis_index("head") * heads
    skip = spread(jnp.broadcast_to(skip_ref[...], (8, skip_ref.shape[1])), width, first, heads)[:1]
    lower = (iota((steps, steps), 0) >= iota((steps, steps), 1)).astype(F32)
    cum = exact(lower, decay_ref[0])
    fade_ref[...] = spread(jnp.exp(-cum), width)
    wide = (steps, heads * steps)
    cum_t = spread(cum, steps)
    place = iota(wide, 1) % steps
    row = iota(wide, 0)
    cum_s = jnp.sum(jnp.where(row == place, cum_t, 0.0), axis=0, keepdims=True)
    fall = jnp.exp(jnp.where(row >= place, cum_s - cum_t, NEG))
    b = b_ref[0].astype(F32)
    c = c_ref[0].astype(F32)
    quad = 128 // steps
    shape = (quad * steps, quad * width)
    mine = iota(shape, 0) // steps == iota(shape, 1) // width
    for g in range(groups):
        b_g = b[:, g, :].astype(BF16)
        gram = mm_nt(c[:, g, :].astype(BF16), jnp.concatenate([b_g] * quad, axis=0))
        for h in range(g * per_group, (g + 1) * per_group, quad):
            mixing = (fall[:, h * steps : (h + quad) * steps] * gram).astype(BF16)
            at = slice(h * width, (h + quad) * width)
            x = x_ref[0, :, at]
            tall = jnp.concatenate([x] * quad, axis=0)
            inputs = jnp.where(mine, tall, jnp.zeros_like(tall))
            base_ref[:, at] = mm(mixing, inputs) + skip[:, at] * x.astype(F32)


def attend_kernel(length_ref, q_ref, own_k_ref, own_v_ref, *refs):
    packets, out_ref = refs[:-1], refs[-1]
    count = len(packets) // 2
    rep = lax.axis_index("rep")
    steps, heads, dim = q_ref.shape[1:]
    kv_heads = own_k_ref.shape[2]
    per_kv = heads // kv_heads
    rows = steps * per_kv
    keys, values = [], []
    for d in range(count):
        mine, other = packets[d][steps:, :], packets[count + d][steps:, :]
        keys.append(jnp.where(rep == 0, mine, other))
        values.append(jnp.where(rep == 0, other, mine))
    parts = packets[0].shape[1] // (kv_heads * dim)
    q = q_ref[0].astype(F32)
    own_k = own_k_ref[0].astype(F32)
    own_v = own_v_ref[0].astype(F32)
    scale = dim ** (-0.5)
    step_of = iota((rows, steps), 0) // per_kv
    visible = step_of >= iota((rows, steps), 1)
    live = iota((rows, dim), 0) // per_kv < length_ref[0]
    mixed_of = []
    for j in range(kv_heads):
        query = q[:, j * per_kv : (j + 1) * per_kv, :].reshape(rows, dim).astype(BF16)

        def gather(arrays):
            return jnp.concatenate(
                [a[:, (i * kv_heads + j) * dim : (i * kv_heads + j + 1) * dim] for a in arrays for i in range(parts)],
                axis=0,
            )

        far = mm_nt(query, gather(keys)) * scale
        near = jnp.where(visible, mm_nt(query, own_k[:, j, :].astype(BF16)) * scale, NEG)
        top = jnp.maximum(jnp.max(far, axis=1, keepdims=True), jnp.max(near, axis=1, keepdims=True))
        far = jnp.exp(far - top)
        near = jnp.exp(near - top)
        mass = jnp.sum(far, axis=1, keepdims=True) + jnp.sum(near, axis=1, keepdims=True)
        mixed = mm(far.astype(BF16), gather(values)) + mm(near.astype(BF16), own_v[:, j, :].astype(BF16))
        mixed = mixed / mass
        mixed = mixed * lax.rsqrt(jnp.mean(mixed * mixed, axis=1, keepdims=True) + EPSILON)
        mixed = jnp.where(live, mixed, 0.0)
        mixed_of.append(mixed.reshape(steps, per_kv, dim))
    out_ref[0] = (jnp.concatenate(mixed_of, axis=1) if kv_heads > 1 else mixed_of[0]).astype(BF16)


def both_candidates(mine_ref, other_ref, groups, state):
    rep = lax.axis_index("rep")
    steps = mine_ref.shape[0] // 2
    mine, other = mine_ref[:steps, :], other_ref[:steps, :]
    zero, one = jnp.where(rep == 0, mine, other), jnp.where(rep == 0, other, mine)
    half = groups * state
    pick = [jnp.where(rep == 0, a[:, :half], a[:, half : 2 * half]) for a in (zero, one)]
    return jnp.concatenate(pick, axis=0)


def share_kernel(total_ref, *refs, groups):
    count = (len(refs) - CHUNKS) // 3
    send_refs = refs[:CHUNKS]
    mine_refs, other_refs = refs[CHUNKS : CHUNKS + count], refs[CHUNKS + count : CHUNKS + 2 * count]
    out_refs = refs[CHUNKS + 2 * count :]
    state, cols = send_refs[0].shape
    projections = [both_candidates(m, o, groups, state) for m, o in zip(mine_refs, other_refs)]
    rows = projections[0].shape[0]
    for q in range(CHUNKS):
        g = q * groups // CHUNKS
        at = slice(q * cols, (q + 1) * cols)
        stacked = jnp.concatenate([p[:, g * state : (g + 1) * state] for p in projections], axis=0)
        result = mm(stacked, send_refs[q][...])
        out_refs[0][:, at] = result[:rows]
        for d in range(1, count):
            out_refs[d][:rows, at] = result[d * rows : (d + 1) * rows].astype(BF16)
    hi, mid, lo = [a.astype(F32) for a in split3(total_ref[...])]
    line = iota(hi.shape, 0)
    tail = jnp.where(line == 0, hi, jnp.where(line == 1, mid, jnp.where(line == 2, lo, 0.0)))
    tail = jnp.concatenate([tail, jnp.zeros_like(tail)], axis=0).astype(BF16)
    for d in range(1, count):
        out_refs[d][rows:, :] = tail


def carry_kernel(cum_ref, base_ref, c2_ref, total_ref, mine_ref, other_ref, own_ref, *refs, groups, hops):
    size = lax.axis_size("seq")
    place = lax.axis_index("seq")
    rep = lax.axis_index("rep")
    received, refs = refs[: CHUNKS * hops], refs[CHUNKS * hops :]
    shares, (out_ref, keep_ref, give_ref) = refs[:-3], refs[-3:]
    state, cols = received[0].shape
    heads = cum_ref.shape[1]
    width = base_ref.shape[1] // heads
    fade = spread(jnp.exp(-cum_ref[...]), width)
    projections = both_candidates(mine_ref, other_ref, groups, state)
    rows = projections.shape[0]
    tokens = c2_ref.shape[0]
    for q in range(CHUNKS):
        g = q * groups // CHUNKS
        at = slice(q * cols, (q + 1) * cols)
        here = slice(g * state, (g + 1) * state)
        start = received[q][...]
        for i in range(1, hops):
            start = start + received[i * CHUNKS + q][...]
        carried = mm(jnp.concatenate([c2_ref[:, here], projections[:, here]], axis=0), start)
        out_ref[:, at] = (base_ref[:, at] + fade[:, at] * carried[:tokens]).astype(BF16)
        acc = total_ref[:1, at] * carried[tokens:] + own_ref[:, at]
        for d in range(1, size):
            share = shares[d - 1]
            tail = share[rows:, at].astype(F32)
            total = tail[0:1] + tail[1:2] + tail[2:3]
            total = jnp.where(place + d < size, total, 1.0)
            acc = acc * total + share[:rows, at].astype(F32)
        half = rows // 2
        keep_ref[:, at] = jnp.where(rep == 0, acc[:half], acc[half:])
        give_ref[:, at] = jnp.where(rep == 0, acc[half:], acc[:half]).astype(BF16)


def close_kernel(length_ref, base_ref, fade_ref, keep_ref, got_ref, out_ref):
    rep = lax.axis_index("rep")
    keep, got = keep_ref[...], got_ref[...].astype(F32)
    cols = keep.shape[1]
    live = iota(keep.shape, 0) < length_ref[0]
    for i in range(2):
        at = slice(i * cols, (i + 1) * cols)
        carried = jnp.where(rep == i, keep, got)
        result = base_ref[:, at] + fade_ref[:, at] * carried
        out_ref[0, :, at] = jnp.where(live, result, 0.0).astype(BF16)


def call(kernel, name, outs, *args, flops=1e8, scalars=0):
    shapes = [jax.ShapeDtypeStruct(shape, dtype) for shape, dtype in outs]
    moved = sum(a.size * a.dtype.itemsize for a in args) + sum(s.size * s.dtype.itemsize for s in shapes)
    vmem = pl.BlockSpec(memory_space=pltpu.VMEM)
    smem = pl.BlockSpec(memory_space=pltpu.SMEM)
    return pl.pallas_call(
        kernel,
        out_shape=shapes,
        in_specs=[smem] * scalars + [vmem] * (len(args) - scalars),
        out_specs=[vmem] * len(shapes),
        compiler_params=pltpu.CompilerParams(vmem_limit_bytes=32 * 2**20),
        cost_estimate=pl.CostEstimate(flops=int(flops), bytes_accessed=int(moved), transcendentals=0),
        name=name,
    )(*args)


def on_device(
    prefix_x,
    prefix_b,
    prefix_c,
    prefix_decay,
    bypass_weight,
    prefix_key_rows,
    prefix_values,
    cand_x,
    cand_b,
    cand_c,
    cand_decay,
    cand_queries,
    cand_keys,
    cand_values,
    cand_length,
):
    size = lax.axis_size("seq")
    hops = size - 1
    tokens, groups, state = prefix_b.shape
    heads = prefix_decay.shape[1]
    wide = prefix_x.shape[1]
    steps = cand_x.shape[1]
    cand_wide = cand_x.shape[2]
    cand_groups = cand_b.shape[2]
    cols = wide // CHUNKS
    swap = [(0, 1), (1, 0)]
    skip = bypass_weight.reshape(1, -1)

    (packet,) = call(
        pack_kernel, "pack", [((2 * steps, cand_groups * state), BF16)], cand_c, prefix_key_rows, prefix_values
    )
    mine = [packet] + [
        lax.ppermute(packet, "seq", [(i, (i + d) % size) for i in range(size)]) for d in range(1, size)
    ]
    b2, cum, total, *parts = call(
        local_kernel,
        "local_state",
        [((tokens, groups * state), BF16), ((tokens, heads), F32), ((8, wide), F32)]
        + [((state, cols), F32)] * CHUNKS
        + [((state, cols), BF16)] * CHUNKS,
        prefix_x,
        prefix_b,
        prefix_decay.T,
    )
    local, send = parts[:CHUNKS], parts[CHUNKS:]
    received = []
    sent = send
    for hop in range(hops):
        got = [lax.ppermute(a, "seq", [(hop, hop + 1)]) for a in sent]
        received += got
        sent = [
            (total[:1, q * cols : (q + 1) * cols] * got[q].astype(F32) + local[q]).astype(BF16)
            for q in range(CHUNKS)
        ]
    other = [lax.ppermute(p, "rep", swap) for p in mine]
    own, *shares = call(
        functools.partial(share_kernel, groups=groups),
        "shares",
        [((2 * steps, wide), F32)] + [((2 * steps + 16, wide), BF16)] * hops,
        total,
        *send,
        *mine,
        *other,
    )
    back = [
        lax.ppermute(shares[d - 1], "seq", [(i, i - d) for i in range(d, size)]) for d in range(1, size)
    ]
    c2, base = call(
        intra_kernel,
        "intra",
        [((tokens, groups * state), BF16), ((tokens, wide), F32)],
        prefix_x,
        b2,
        prefix_c,
        cum,
        skip,
    )
    cand_base, cand_fade = call(
        cand_kernel,
        "candidates",
        [((steps, cand_wide), F32), ((steps, cand_wide), F32)],
        cand_x,
        cand_b,
        cand_c,
        cand_decay,
        skip,
    )
    (cand_attn,) = call(
        attend_kernel,
        "attend",
        [(cand_queries.shape, BF16)],
        cand_length,
        cand_queries,
        cand_keys,
        cand_values,
        *mine,
        *other,
        scalars=1,
    )
    prefix_out, keep, give = call(
        functools.partial(carry_kernel, groups=groups, hops=hops),
        "carried",
        [((tokens, wide), BF16), ((steps, wide), F32), ((steps, wide), BF16)],
        cum,
        base,
        c2,
        total,
        mine[0],
        other[0],
        own,
        *received,
        *back,
    )
    (cand_ssm,) = call(
        close_kernel,
        "close",
        [((1, steps, cand_wide), BF16)],
        cand_length,
        cand_base,
        cand_fade,
        keep,
        lax.ppermute(give, "rep", swap),
        scalars=1,
    )
    return (prefix_out, cand_ssm, cand_attn)


def solution(mesh):
    placed = (
        P(("groups", "seq"), ("head", "rep")),
        P(("groups", "seq"), ("head", "rep"), None),
        P(("groups", "seq"), ("head", "rep"), None),
        P(("groups", "seq"), ("head", "rep")),
        P(),
        P(("groups", "seq"), "head", None),
        P(("groups", "seq"), "head", None),
        P(("groups", "seq", "rep"), None, "head"),
        P(("groups", "seq", "rep"), None, "head", None),
        P(("groups", "seq", "rep"), None, "head", None),
        P(("groups", "seq", "rep"), None, "head"),
        P(("groups", "seq", "rep"), None, "head", None),
        P(("groups", "seq", "rep"), None, "head", None),
        P(("groups", "seq", "rep"), None, "head", None),
        P(("groups", "seq", "rep")),
    )
    return jax.shard_map(
        on_device,
        mesh=mesh,
        in_specs=placed,
        out_specs=(
            P(("groups", "seq"), ("head", "rep")),
            P(("groups", "seq", "rep"), None, "head"),
            P(("groups", "seq", "rep"), None, "head", None),
        ),
        check_vma=False,
    )
```

time: 335 us -> 83.5 us (0.25)
  the two profiles are of different devices: /device:TPU:27 before, /device:TPU:25 now
where the time goes in v1:
time: 83.5 us; the launch traced here: 83 us
  waiting for transfers between devices  40.8 us (49%)
  starting transfers between devices  26.4 us (32%)
  Pallas kernels  9.15 us (11%)
  local copies, waits for them, and re-layouts  4.28 us (5%)
  between operations  1.75 us (2%)
    ppermute x12, waiting for transfers between devices, on_device(): got = [lax.ppermute(a, 'seq', [(hop, hop + 1)]) for a in sent]  31.5 us
    ppermute x12, starting transfers between devices, on_device(): got = [lax.ppermute(a, 'seq', [(hop, hop + 1)]) for a in sent]  10.7 us
    pallas_call x8, Pallas kernels, call(): pl.pallas_call(kernel, out_shape=shapes, in_specs=[smem] * scalars + [vme...  9.15 us
    ppermute x3, starting transfers between devices, on_device(): lax.ppermute(shares[d - 1], 'seq', [(i, i - d) for i in range(d, size)])  8.55 us
    ppermute x3, waiting for transfers between devices, on_device(): lax.ppermute(packet, 'seq', [(i, (i + d) % size) for i in range(size)])  6.08 us
    unnamed x32, local copies, waits for them, and re-layouts  4.27 us
    ppermute x4, starting transfers between devices, on_device(): other = [lax.ppermute(p, 'rep', swap) for p in mine]  3.57 us
    ppermute x3, waiting for transfers between devices, on_device(): lax.ppermute(shares[d - 1], 'seq', [(i, i - d) for i in range(d, size)])  2.69 us
  transfers between devices with their start and end apart: 23, of which 7 were waited for; matrix products, arithmetic and copies ran while one was open for 1% of the time, Pallas kernels for 8%

profile of v1, /device:TPU:25, one launch (start us, length us, event | category | flops | bytes accessed | tf_op | source)
XLA Modules:
  0.0 83.0 jit_solution(6929611659456993503)
XLA Ops:
  0.6 0.0 copy-start.6
  0.7 0.9 %copy-done.6 = bf16[1,32,4,256]{3,2,1,0:T(4,128)(2,1)S(1)} copy-done((bf16[1,32,4,256]{3,2,1,0:T(4,128)(2,1)S(1)}, bf16[1,32,4,256]{3,2,1,0:T(4,128)(2,1)}, u32[]{:S(2)}) %copy-start.6) | copy-done | bytes 65560
  1.5 0.8 %copy-done.14 = bf16[128,2,128]{2,1,0:T(2,128)(2,1)S(1)} copy-done((bf16[128,2,128]{2,1,0:T(2,128)(2,1)S(1)}, bf16[128,2,128]{2,1,0:T(2,128)(2,1)}, u32[]{:S(2)}) %copy-start.14) | copy-done | bytes 65560
  2.4 0.8 %copy-done.15 = bf16[128,2,128]{2,1,0:T(2,128)(2,1)S(1)} copy-done((bf16[128,2,128]{2,1,0:T(2,128)(2,1)S(1)}, bf16[128,2,128]{2,1,0:T(2,128)(2,1)}, u32[]{:S(2)}) %copy-start.15) | copy-done | bytes 65560
  3.2 0.3 pack.1.refs_4_.mine_ref.refs_0_
  3.5 0.1 collective-permute-start.1
  3.6 1.3 %collective-permute-start.2 = (bf16[64,1024]{1,0:T(8,128)(2,1)S(1)}, bf16[64,1024]{1,0:T(8,128)(2,1)S(1)}, u32[]{:S(2)}, u32[]{:S(2)}) collective-permute-start(bf16[64,1024]{1,0:T(8,128)(2,1)S(1)} %pack.1.refs_4_.mine_ref.refs_0_), channel_id=1, source_target_pairs={{0,8},{4,12},{8,0},{12,4},{1,9},{5,13},{9,1},{13,5},{2,10},{6,14},... | collective-permute-start | bytes 393224 | tf_op jit(solution)/shard_map/ppermute | solution.py:350
  4.9 0.2 collective-permute-start.3
  5.1 1.5 %collective-permute-start = (bf16[64,1024]{1,0:T(8,128)(2,1)S(1)}, bf16[64,1024]{1,0:T(8,128)(2,1)S(1)}, u32[]{:S(2)}, u32[]{:S(2)}) collective-permute-start(bf16[64,1024]{1,0:T(8,128)(2,1)S(1)} %pack.1.refs_4_.mine_ref.refs_0_), channel_id=1, source_target_pairs={{0,1},{1,0},{2,3},{3,2},{4,5},{5,4},{6,7},{7,6},{8,9},{9,8},{10,11... | collective-permute-start | bytes 393224 | tf_op jit(solution)/shard_map/ppermute | solution.py:372
  6.6 1.0 %copy-done = bf16[128,2048]{1,0:T(8,128)(2,1)S(1)} copy-done((bf16[128,2048]{1,0:T(8,128)(2,1)S(1)}, bf16[128,2048]{1,0:T(8,128)(2,1)}, u32[]{:S(2)}) %copy-start) | copy-done | bytes 524312
  7.7 1.1 %local_state.1 = (bf16[128,512]{1,0:T(8,128)(2,1)S(1)}, f32[128,32]{1,0:T(8,128)S(1)}, f32[8,2048]{1,0:T(8,128)S(1)}, f32[256,512]{1,0:T(8,128)S(1)}, f32[256,51...) custom-call(bf16[128,2048]{1,0:T(8,128)(2,1)S(1)} %copy-done, ...), custom_call_target="tpu_custom_call" | custom-call | flops 100000000 | bytes 4030464 | tf_op jit(solution)/shard_map/local_state/pallas_call | solution.py:306
  8.8 0.7 collective-permute-start.10
  9.5 0.0 collective-permute-done.1.refs_5_.refs_1_
  9.5 0.7 collective-permute-start.9
  10.2 6.1 %collective-permute-done.2.refs_6_.refs_2_ = bf16[64,1024]{1,0:T(8,128)(2,1)S(1)} collective-permute-done((bf16[64,1024]{1,0:T(8,128)(2,1)S(1)}, bf16[64,1024]{1,0:T(8,128)(2,1)S(1)}, u32[]{:S(2)}, u32[]{:S(2)}) %collective-permute-start.2) | collective-permute-done | bytes 131104 | tf_op jit(solution)/shard_map/ppermute | solution.py:350
  16.3 1.5 %collective-permute-start.4 = (bf16[64,1024]{1,0:T(8,128)(2,1)S(1)}, bf16[64,1024]{1,0:T(8,128)(2,1)S(1)}, u32[]{:S(2)}, u32[]{:S(2)}) collective-permute-start(bf16[64,1024]{1,0:T(8,128)(2,1)S(1)} %collective-permute-done.1.refs_5_.refs_1_), channel_id=1, source_target_pairs={{0,1},{1,0},{2,3},{3,2},{4,5},{5,4},{6,7},{7,6},{8,9},{9,8},{10,11... | collective-permute-start | bytes 393224 | tf_op jit(solution)/shard_map/ppermute | solution.py:372
  17.8 0.0 collective-permute-done.3.refs_7_.refs_3_
  17.8 0.0 collective-permute-start.5
  17.8 0.0 collective-permute-done.refs_8_.other_ref.refs_4_
  17.8 0.5 collective-permute-start.6
  18.3 0.5 collective-permute-done.4.refs_9_.refs_5_
  18.8 0.7 collective-permute-start.8
  19.5 0.0 collective-permute-done.5.refs_10_.refs_6_
  19.5 0.7 collective-permute-start.7
  20.2 0.0 collective-permute-done.6.refs_11_.refs_7_
  20.2 0.4 shares.1
  20.6 1.3 %collective-permute-start.19 = (bf16[80,2048]{1,0:T(8,128)(2,1)S(1)}, bf16[80,2048]{1,0:T(8,128)(2,1)S(1)}, u32[]{:S(2)}, u32[]{:S(2)}) collective-permute-start(bf16[80,2048]{1,0:T(8,128)(2,1)S(1)} %get-tuple-element.39), channel_id=1, source_target_pairs={{4,0},{8,4},{12,8},{5,1},{9,5},{13,9},{6,2},{10,6},{14,10},{7,3},{... | collective-permute-start | bytes 983048 | tf_op jit(solution)/shard_map/ppermute | solution.py:383
  21.9 0.0 collective-permute-done.10.refs_3_
  21.9 5.9 %collective-permute-start.20 = (bf16[80,2048]{1,0:T(8,128)(2,1)S(1)}, bf16[80,2048]{1,0:T(8,128)(2,1)S(1)}, u32[]{:S(2)}, u32[]{:S(2)}) collective-permute-start(bf16[80,2048]{1,0:T(8,128)(2,1)S(1)} %get-tuple-element.40), channel_id=1, source_target_pairs={{8,0},{12,4},{9,1},{13,5},{10,2},{14,6},{11,3},{15,7},{24,16},{28,... | collective-permute-start | bytes 983048 | tf_op jit(solution)/shard_map/ppermute | solution.py:383
  27.9 0.1 add_convert_fusion.4
  28.0 1.3 %collective-permute-start.21 = (bf16[80,2048]{1,0:T(8,128)(2,1)S(1)}, bf16[80,2048]{1,0:T(8,128)(2,1)S(1)}, u32[]{:S(2)}, u32[]{:S(2)}) collective-permute-start(bf16[80,2048]{1,0:T(8,128)(2,1)S(1)} %get-tuple-element.41), channel_id=1, source_target_pairs={{12,0},{13,1},{14,2},{15,3},{28,16},{29,17},{30,18},{31,19}} | collective-permute-start | bytes 983048 | tf_op jit(solution)/shard_map/ppermute | solution.py:383
  29.3 0.1 add_convert_fusion.5
  29.4 0.7 collective-permute-start.14
  30.1 0.1 add_convert_fusion.6
  30.2 0.7 collective-permute-start.13
  30.9 0.1 add_convert_fusion.7
  31.0 0.7 collective-permute-start.12
  31.6 0.1 add_convert_fusion
  31.7 0.7 collective-permute-start.11
  32.4 0.1 add_convert_fusion.1
  32.5 1.3 %collective-permute-start.18 = (bf16[256,512]{1,0:T(8,128)(2,1)S(1)}, bf16[256,512]{1,0:T(8,128)(2,1)S(1)}, u32[]{:S(2)}, u32[]{:S(2)}) collective-permute-start(bf16[256,512]{1,0:T(8,128)(2,1)S(1)} %add_convert_fusion), channel_id=1, source_target_pairs={{8,12},{9,13},{10,14},{11,15},{24,28},{25,29},{26,30},{27,31}} | collective-permute-start | bytes 786440 | tf_op jit(solution)/shard_map/ppermute | solution.py:366
  33.8 0.1 add_convert_fusion.2
  33.9 0.0 copy-start.1
  33.9 0.0 copy-start.5
  33.9 1.4 %collective-permute-start.17 = (bf16[256,512]{1,0:T(8,128)(2,1)S(1)}, bf16[256,512]{1,0:T(8,128)(2,1)S(1)}, u32[]{:S(2)}, u32[]{:S(2)}) collective-permute-start(bf16[256,512]{1,0:T(8,128)(2,1)S(1)} %add_convert_fusion.1), channel_id=1, source_target_pairs={{8,12},{9,13},{10,14},{11,15},{24,28},{25,29},{26,30},{27,31}} | collective-permute-start | bytes 786440 | tf_op jit(solution)/shard_map/ppermute | solution.py:366
  35.4 0.1 add_convert_fusion.3
  35.5 1.3 %collective-permute-start.16 = (bf16[256,512]{1,0:T(8,128)(2,1)S(1)}, bf16[256,512]{1,0:T(8,128)(2,1)S(1)}, u32[]{:S(2)}, u32[]{:S(2)}) collective-permute-start(bf16[256,512]{1,0:T(8,128)(2,1)S(1)} %add_convert_fusion.2), channel_id=1, source_target_pairs={{8,12},{9,13},{10,14},{11,15},{24,28},{25,29},{26,30},{27,31}} | collective-permute-start | bytes 786440 | tf_op jit(solution)/shard_map/ppermute | solution.py:366
  36.8 1.3 %collective-permute-start.15 = (bf16[256,512]{1,0:T(8,128)(2,1)S(1)}, bf16[256,512]{1,0:T(8,128)(2,1)S(1)}, u32[]{:S(2)}, u32[]{:S(2)}) collective-permute-start(bf16[256,512]{1,0:T(8,128)(2,1)S(1)} %add_convert_fusion.3), channel_id=1, source_target_pairs={{8,12},{9,13},{10,14},{11,15},{24,28},{25,29},{26,30},{27,31}} | collective-permute-start | bytes 786440 | tf_op jit(solution)/shard_map/ppermute | solution.py:366
  38.1 0.0 copy-start.13
  38.1 0.6 copy-done.13
  38.7 1.3 %intra.1 = (bf16[128,512]{1,0:T(8,128)(2,1)S(1)}, f32[128,2048]{1,0:T(8,128)S(1)}) custom-call(bf16[128,2048]{1,0:T(8,128)(2,1)S(1)} %copy-done.1, bf16[128,512]{1,0:T(8,128)(2,1)S(1)} %get-tuple-element.26.b2_ref, bf16[128,2,256]{2,1,0:T(2,128)(2,1)S(1)} %copy-done.5, f32[128,32]{1,0:T(8,128)S(1)} %get-tuple-element.25.cum_ref, f32[1,128]{1,0:T(1,128)S(1)} %bitcast.7), custom_call_target="tpu_custom_call" | custom-call | flops 100000000 | bytes 1982976 | tf_op jit(solution)/shard_map/intra/pallas_call | solution.py:306
  40.1 2.7 %collective-permute-done.21.refs_14_ = bf16[80,2048]{1,0:T(8,128)(2,1)S(1)} collective-permute-done((bf16[80,2048]{1,0:T(8,128)(2,1)S(1)}, bf16[80,2048]{1,0:T(8,128)(2,1)S(1)}, u32[]{:S(2)}, u32[]{:S(2)}) %collective-permute-start.21) | collective-permute-done | bytes 327712 | tf_op jit(solution)/shard_map/ppermute | solution.py:383
  42.7 13.7 %collective-permute-done.18.refs_11_ = bf16[256,512]{1,0:T(8,128)(2,1)S(1)} collective-permute-done((bf16[256,512]{1,0:T(8,128)(2,1)S(1)}, bf16[256,512]{1,0:T(8,128)(2,1)S(1)}, u32[]{:S(2)}, u32[]{:S(2)}) %collective-permute-start.18) | collective-permute-done | bytes 262176 | tf_op jit(solution)/shard_map/ppermute | solution.py:366
  56.4 6.6 %collective-permute-done.17.refs_10_ = bf16[256,512]{1,0:T(8,128)(2,1)S(1)} collective-permute-done((bf16[256,512]{1,0:T(8,128)(2,1)S(1)}, bf16[256,512]{1,0:T(8,128)(2,1)S(1)}, u32[]{:S(2)}, u32[]{:S(2)}) %collective-permute-start.17) | collective-permute-done | bytes 262176 | tf_op jit(solution)/shard_map/ppermute | solution.py:366
  63.0 5.6 %collective-permute-done.16.refs_9_ = bf16[256,512]{1,0:T(8,128)(2,1)S(1)} collective-permute-done((bf16[256,512]{1,0:T(8,128)(2,1)S(1)}, bf16[256,512]{1,0:T(8,128)(2,1)S(1)}, u32[]{:S(2)}, u32[]{:S(2)}) %collective-permute-start.16) | collective-permute-done | bytes 262176 | tf_op jit(solution)/shard_map/ppermute | solution.py:366
  68.6 5.6 %collective-permute-done.15.refs_8_ = bf16[256,512]{1,0:T(8,128)(2,1)S(1)} collective-permute-done((bf16[256,512]{1,0:T(8,128)(2,1)S(1)}, bf16[256,512]{1,0:T(8,128)(2,1)S(1)}, u32[]{:S(2)}, u32[]{:S(2)}) %collective-permute-start.15) | collective-permute-done | bytes 262176 | tf_op jit(solution)/shard_map/ppermute | solution.py:366
  74.3 1.5 %carried.1 = (bf16[128,2048]{1,0:T(8,128)(2,1)}, f32[32,2048]{1,0:T(8,128)S(1)}, bf16[32,2048]{1,0:T(8,128)(2,1)S(1)}) custom-call(f32[128,32]{1,0:T(8,128)S(1)} %get-tuple-element.25.cum_ref, f32[128,2048]{1,0:T(8,128)S(1)} %get-tuple-element.27.base_ref, bf16[128,512]{1,0:T(8,128)(2,1)S(1)} %get-tuple-element.28.c2_ref, ...), custom_call_target="tpu_custom_call" | custom-call | flops 100000000 | bytes 7094272 | tf_op jit(solution)/shard_map/carried/pallas_call | solution.py:306
  75.8 2.0 %collective-permute-start.22 = (bf16[32,2048]{1,0:T(8,128)(2,1)S(1)}, bf16[32,2048]{1,0:T(8,128)(2,1)S(1)}, u32[]{:S(2)}, u32[]{:S(2)}) collective-permute-start(bf16[32,2048]{1,0:T(8,128)(2,1)S(1)} %get-tuple-element.46), channel_id=1, source_target_pairs={{0,1},{1,0},{2,3},{3,2},{4,5},{5,4},{6,7},{7,6},{8,9},{9,8},{10,11... | collective-permute-start | bytes 393224 | tf_op jit(solution)/shard_map/ppermute | solution.py:439
  78.5 0.0 copy-start.3
  78.5 0.0 copy-start.9
  78.5 0.0 copy-start.10
  78.5 1.8 %candidates.1 = (f32[32,4096]{1,0:T(8,128)S(1)}, f32[32,4096]{1,0:T(8,128)S(1)}) custom-call(bf16[1,32,4096]{2,1,0:T(8,128)(2,1)S(1)} %copy-done.2, bf16[1,32,4,256]{3,2,1,0:T(4,128)(2,1)S(1)} %copy-done.8, bf16[1,32,4,256]{3,2,1,0:T(4,128)(2,1)S(1)} %copy-done.7, f32[1,32,64]{2,1,0:T(8,128)S(1)} %copy-done.11, f32[1,128]{1,0:T(1,128)S(1)} %bitcast.8), custom_call_target="tpu_custom_call" | custom-call | flops 100000000 | bytes 1450496 | tf_op jit(solution)/shard_map/candidates/pallas_call | solution.py:306
  80.3 1.8 %attend.1 = bf16[1,32,16,128]{3,2,1,0:T(8,128)(2,1)} custom-call(s32[1]{0:T(128)S(6)} %copy.18.length_ref, bf16[1,32,16,128]{3,2,1,0:T(8,128)(2,1)S(1)} %copy-done.3, bf16[1,32,2,128]{3,2,1,0:T(2,128)(2,1)S(1)} %copy-done.9, bf16[1,32,2,128]{3,2,1,0:T(2,128)(2,1)S(1)} %copy-done.10, bf16[64,1024]{1,0:T(8,128)(2,1)S(1)} %pack.1.refs_4_.mine_ref.refs_0_, ...), custom_call_target="tpu_custom_call" | custom-call | flops 100000000 | bytes 1343492 | tf_op jit(solution)/shard_map/attend/pallas_call | solution.py:306
  82.1 0.8 close.1
  (31 shorter events, 0.1 us)
Async XLA Ops:
  0.6 6.0 %copy-start.4 = (bf16[128,2,256]{2,1,0:T(2,128)(2,1)S(1)}, bf16[128,2,256]{2,1,0:T(2,128)(2,1)}, u32[]{:S(2)}) copy-start(bf16[128,2,256]{2,1,0:T(2,128)(2,1)} %b_ref.2) | copy-start | bytes 393220
  0.6 0.9 %copy-start.6 = (bf16[1,32,4,256]{3,2,1,0:T(4,128)(2,1)S(1)}, bf16[1,32,4,256]{3,2,1,0:T(4,128)(2,1)}, u32[]{:S(2)}) copy-start(bf16[1,32,4,256]{3,2,1,0:T(4,128)(2,1)} %c_ref.5) | copy-start | bytes 196612
  1.5 0.8 %copy-start.14 = (bf16[128,2,128]{2,1,0:T(2,128)(2,1)S(1)}, bf16[128,2,128]{2,1,0:T(2,128)(2,1)}, u32[]{:S(2)}) copy-start(bf16[128,2,128]{2,1,0:T(2,128)(2,1)} %k_ref.1) | copy-start | bytes 196612
  2.4 0.8 %copy-start.15 = (bf16[128,2,128]{2,1,0:T(2,128)(2,1)S(1)}, bf16[128,2,128]{2,1,0:T(2,128)(2,1)}, u32[]{:S(2)}) copy-start(bf16[128,2,128]{2,1,0:T(2,128)(2,1)} %v_ref.1) | copy-start | bytes 196612
  3.2 3.4 %copy-start.12 = (f32[128,32]{0,1:T(8,128)S(1)}, f32[128,32]{0,1:T(8,128)}, u32[]{:S(2)}) copy-start(f32[128,32]{0,1:T(8,128)} %param.18) | copy-start | bytes 49156
  3.5 6.0 %collective-permute-start.1 = (bf16[64,1024]{1,0:T(8,128)(2,1)S(1)}, bf16[64,1024]{1,0:T(8,128)(2,1)S(1)}, u32[]{:S(2)}, u32[]{:S(2)}) collective-permute-start(bf16[64,1024]{1,0:T(8,128)(2,1)S(1)} %pack.1.refs_4_.mine_ref.refs_0_), channel_id=1, source_target_pairs={{0,4},{4,8},{8,12},{12,0},{1,5},{5,9},{9,13},{13,1},{2,6},{6,10},{... | collective-permute-start | bytes 393224 | tf_op jit(solution)/shard_map/ppermute | solution.py:350
  3.6 12.7 %collective-permute-start.2 = (bf16[64,1024]{1,0:T(8,128)(2,1)S(1)}, bf16[64,1024]{1,0:T(8,128)(2,1)S(1)}, u32[]{:S(2)}, u32[]{:S(2)}) collective-permute-start(bf16[64,1024]{1,0:T(8,128)(2,1)S(1)} %pack.1.refs_4_.mine_ref.refs_0_), channel_id=1, source_target_pairs={{0,8},{4,12},{8,0},{12,4},{1,9},{5,13},{9,1},{13,5},{2,10},{6,14},... | collective-permute-start | bytes 393224 | tf_op jit(solution)/shard_map/ppermute | solution.py:350
  4.9 12.9 %collective-permute-start.3 = (bf16[64,1024]{1,0:T(8,128)(2,1)S(1)}, bf16[64,1024]{1,0:T(8,128)(2,1)S(1)}, u32[]{:S(2)}, u32[]{:S(2)}) collective-permute-start(bf16[64,1024]{1,0:T(8,128)(2,1)S(1)} %pack.1.refs_4_.mine_ref.refs_0_), channel_id=1, source_target_pairs={{0,12},{4,0},{8,4},{12,8},{1,13},{5,1},{9,5},{13,9},{2,14},{6,2},{... | collective-permute-start | bytes 393224 | tf_op jit(solution)/shard_map/ppermute | solution.py:350
  5.1 12.7 %collective-permute-start = (bf16[64,1024]{1,0:T(8,128)(2,1)S(1)}, bf16[64,1024]{1,0:T(8,128)(2,1)S(1)}, u32[]{:S(2)}, u32[]{:S(2)}) collective-permute-start(bf16[64,1024]{1,0:T(8,128)(2,1)S(1)} %pack.1.refs_4_.mine_ref.refs_0_), channel_id=1, source_target_pairs={{0,1},{1,0},{2,3},{3,2},{4,5},{5,4},{6,7},{7,6},{8,9},{9,8},{10,11... | collective-permute-start | bytes 393224 | tf_op jit(solution)/shard_map/ppermute | solution.py:372
  6.6 1.0 %copy-start = (bf16[128,2048]{1,0:T(8,128)(2,1)S(1)}, bf16[128,2048]{1,0:T(8,128)(2,1)}, u32[]{:S(2)}) copy-start(bf16[128,2048]{1,0:T(8,128)(2,1)} %x_ref.4) | copy-start | bytes 1572868
  8.8 13.1 %collective-permute-start.10 = (bf16[256,512]{1,0:T(8,128)(2,1)S(1)}, bf16[256,512]{1,0:T(8,128)(2,1)S(1)}, u32[]{:S(2)}, u32[]{:S(2)}) collective-permute-start(bf16[256,512]{1,0:T(8,128)(2,1)S(1)} %get-tuple-element.33.refs_3_), channel_id=1, source_target_pairs={{0,4},{1,5},{2,6},{3,7},{16,20},{17,21},{18,22},{19,23}} | collective-permute-start | bytes 786440 | tf_op jit(solution)/shard_map/ppermute | solution.py:366
  9.5 18.5 %collective-permute-start.9 = (bf16[256,512]{1,0:T(8,128)(2,1)S(1)}, bf16[256,512]{1,0:T(8,128)(2,1)S(1)}, u32[]{:S(2)}, u32[]{:S(2)}) collective-permute-start(bf16[256,512]{1,0:T(8,128)(2,1)S(1)} %get-tuple-element.32.refs_2_), channel_id=1, source_target_pairs={{0,4},{1,5},{2,6},{3,7},{16,20},{17,21},{18,22},{19,23}} | collective-permute-start | bytes 786440 | tf_op jit(solution)/shard_map/ppermute | solution.py:366
  16.3 2.5 %collective-permute-start.4 = (bf16[64,1024]{1,0:T(8,128)(2,1)S(1)}, bf16[64,1024]{1,0:T(8,128)(2,1)S(1)}, u32[]{:S(2)}, u32[]{:S(2)}) collective-permute-start(bf16[64,1024]{1,0:T(8,128)(2,1)S(1)} %collective-permute-done.1.refs_5_.refs_1_), channel_id=1, source_target_pairs={{0,1},{1,0},{2,3},{3,2},{4,5},{5,4},{6,7},{7,6},{8,9},{9,8},{10,11... | collective-permute-start | bytes 393224 | tf_op jit(solution)/shard_map/ppermute | solution.py:372
  17.8 1.7 %collective-permute-start.5 = (bf16[64,1024]{1,0:T(8,128)(2,1)S(1)}, bf16[64,1024]{1,0:T(8,128)(2,1)S(1)}, u32[]{:S(2)}, u32[]{:S(2)}) collective-permute-start(bf16[64,1024]{1,0:T(8,128)(2,1)S(1)} %collective-permute-done.2.refs_6_.refs_2_), channel_id=1, source_target_pairs={{0,1},{1,0},{2,3},{3,2},{4,5},{5,4},{6,7},{7,6},{8,9},{9,8},{10,11... | collective-permute-start | bytes 393224 | tf_op jit(solution)/shard_map/ppermute | solution.py:372
  17.8 2.3 %collective-permute-start.6 = (bf16[64,1024]{1,0:T(8,128)(2,1)S(1)}, bf16[64,1024]{1,0:T(8,128)(2,1)S(1)}, u32[]{:S(2)}, u32[]{:S(2)}) collective-permute-start(bf16[64,1024]{1,0:T(8,128)(2,1)S(1)} %collective-permute-done.3.refs_7_.refs_3_), channel_id=1, source_target_pairs={{0,1},{1,0},{2,3},{3,2},{4,5},{5,4},{6,7},{7,6},{8,9},{9,8},{10,11... | collective-permute-start | bytes 393224 | tf_op jit(solution)/shard_map/ppermute | solution.py:372
  18.8 10.6 %collective-permute-start.8 = (bf16[256,512]{1,0:T(8,128)(2,1)S(1)}, bf16[256,512]{1,0:T(8,128)(2,1)S(1)}, u32[]{:S(2)}, u32[]{:S(2)}) collective-permute-start(bf16[256,512]{1,0:T(8,128)(2,1)S(1)} %get-tuple-element.31.refs_1_), channel_id=1, source_target_pairs={{0,4},{1,5},{2,6},{3,7},{16,20},{17,21},{18,22},{19,23}} | collective-permute-start | bytes 786440 | tf_op jit(solution)/shard_map/ppermute | solution.py:366
  19.5 10.7 %collective-permute-start.7 = (bf16[256,512]{1,0:T(8,128)(2,1)S(1)}, bf16[256,512]{1,0:T(8,128)(2,1)S(1)}, u32[]{:S(2)}, u32[]{:S(2)}) collective-permute-start(bf16[256,512]{1,0:T(8,128)(2,1)S(1)} %get-tuple-element.30.refs_0_), channel_id=1, source_target_pairs={{0,4},{1,5},{2,6},{3,7},{16,20},{17,21},{18,22},{19,23}} | collective-permute-start | bytes 786440 | tf_op jit(solution)/shard_map/ppermute | solution.py:366
  20.6 14.8 %collective-permute-start.19 = (bf16[80,2048]{1,0:T(8,128)(2,1)S(1)}, bf16[80,2048]{1,0:T(8,128)(2,1)S(1)}, u32[]{:S(2)}, u32[]{:S(2)}) collective-permute-start(bf16[80,2048]{1,0:T(8,128)(2,1)S(1)} %get-tuple-element.39), channel_id=1, source_target_pairs={{4,0},{8,4},{12,8},{5,1},{9,5},{13,9},{6,2},{10,6},{14,10},{7,3},{... | collective-permute-start | bytes 983048 | tf_op jit(solution)/shard_map/ppermute | solution.py:383
  21.9 14.8 %collective-permute-start.20 = (bf16[80,2048]{1,0:T(8,128)(2,1)S(1)}, bf16[80,2048]{1,0:T(8,128)(2,1)S(1)}, u32[]{:S(2)}, u32[]{:S(2)}) collective-permute-start(bf16[80,2048]{1,0:T(8,128)(2,1)S(1)} %get-tuple-element.40), channel_id=1, source_target_pairs={{8,0},{12,4},{9,1},{13,5},{10,2},{14,6},{11,3},{15,7},{24,16},{28,... | collective-permute-start | bytes 983048 | tf_op jit(solution)/shard_map/ppermute | solution.py:383
  28.0 14.8 %collective-permute-start.21 = (bf16[80,2048]{1,0:T(8,128)(2,1)S(1)}, bf16[80,2048]{1,0:T(8,128)(2,1)S(1)}, u32[]{:S(2)}, u32[]{:S(2)}) collective-permute-start(bf16[80,2048]{1,0:T(8,128)(2,1)S(1)} %get-tuple-element.41), channel_id=1, source_target_pairs={{12,0},{13,1},{14,2},{15,3},{28,16},{29,17},{30,18},{31,19}} | collective-permute-start | bytes 983048 | tf_op jit(solution)/shard_map/ppermute | solution.py:383
  29.4 1.6 %collective-permute-start.14 = (bf16[256,512]{1,0:T(8,128)(2,1)S(1)}, bf16[256,512]{1,0:T(8,128)(2,1)S(1)}, u32[]{:S(2)}, u32[]{:S(2)}) collective-permute-start(bf16[256,512]{1,0:T(8,128)(2,1)S(1)} %add_convert_fusion.4), channel_id=1, source_target_pairs={{4,8},{5,9},{6,10},{7,11},{20,24},{21,25},{22,26},{23,27}} | collective-permute-start | bytes 786440 | tf_op jit(solution)/shard_map/ppermute | solution.py:366
  30.2 1.6 %collective-permute-start.13 = (bf16[256,512]{1,0:T(8,128)(2,1)S(1)}, bf16[256,512]{1,0:T(8,128)(2,1)S(1)}, u32[]{:S(2)}, u32[]{:S(2)}) collective-permute-start(bf16[256,512]{1,0:T(8,128)(2,1)S(1)} %add_convert_fusion.5), channel_id=1, source_target_pairs={{4,8},{5,9},{6,10},{7,11},{20,24},{21,25},{22,26},{23,27}} | collective-permute-start | bytes 786440 | tf_op jit(solution)/shard_map/ppermute | solution.py:366
  31.0 1.6 %collective-permute-start.12 = (bf16[256,512]{1,0:T(8,128)(2,1)S(1)}, bf16[256,512]{1,0:T(8,128)(2,1)S(1)}, u32[]{:S(2)}, u32[]{:S(2)}) collective-permute-start(bf16[256,512]{1,0:T(8,128)(2,1)S(1)} %add_convert_fusion.6), channel_id=1, source_target_pairs={{4,8},{5,9},{6,10},{7,11},{20,24},{21,25},{22,26},{23,27}} | collective-permute-start | bytes 786440 | tf_op jit(solution)/shard_map/ppermute | solution.py:366
  31.7 2.2 %collective-permute-start.11 = (bf16[256,512]{1,0:T(8,128)(2,1)S(1)}, bf16[256,512]{1,0:T(8,128)(2,1)S(1)}, u32[]{:S(2)}, u32[]{:S(2)}) collective-permute-start(bf16[256,512]{1,0:T(8,128)(2,1)S(1)} %add_convert_fusion.7), channel_id=1, source_target_pairs={{4,8},{5,9},{6,10},{7,11},{20,24},{21,25},{22,26},{23,27}} | collective-permute-start | bytes 786440 | tf_op jit(solution)/shard_map/ppermute | solution.py:366
  32.5 23.9 %collective-permute-start.18 = (bf16[256,512]{1,0:T(8,128)(2,1)S(1)}, bf16[256,512]{1,0:T(8,128)(2,1)S(1)}, u32[]{:S(2)}, u32[]{:S(2)}) collective-permute-start(bf16[256,512]{1,0:T(8,128)(2,1)S(1)} %add_convert_fusion), channel_id=1, source_target_pairs={{8,12},{9,13},{10,14},{11,15},{24,28},{25,29},{26,30},{27,31}} | collective-permute-start | bytes 786440 | tf_op jit(solution)/shard_map/ppermute | solution.py:366
  33.9 4.2 %copy-start.1 = (bf16[128,2048]{1,0:T(8,128)(2,1)S(1)}, bf16[128,2048]{1,0:T(8,128)(2,1)}, u32[]{:S(2)}) copy-start(bf16[128,2048]{1,0:T(8,128)(2,1)} %x_ref.4) | copy-start | bytes 1572868
  33.9 4.2 %copy-start.5 = (bf16[128,2,256]{2,1,0:T(2,128)(2,1)S(1)}, bf16[128,2,256]{2,1,0:T(2,128)(2,1)}, u32[]{:S(2)}) copy-start(bf16[128,2,256]{2,1,0:T(2,128)(2,1)} %c_ref.3) | copy-start | bytes 393220
  33.9 29.1 %collective-permute-start.17 = (bf16[256,512]{1,0:T(8,128)(2,1)S(1)}, bf16[256,512]{1,0:T(8,128)(2,1)S(1)}, u32[]{:S(2)}, u32[]{:S(2)}) collective-permute-start(bf16[256,512]{1,0:T(8,128)(2,1)S(1)} %add_convert_fusion.1), channel_id=1, source_target_pairs={{8,12},{9,13},{10,14},{11,15},{24,28},{25,29},{26,30},{27,31}} | collective-permute-start | bytes 786440 | tf_op jit(solution)/shard_map/ppermute | solution.py:366
  35.5 33.2 %collective-permute-start.16 = (bf16[256,512]{1,0:T(8,128)(2,1)S(1)}, bf16[256,512]{1,0:T(8,128)(2,1)S(1)}, u32[]{:S(2)}, u32[]{:S(2)}) collective-permute-start(bf16[256,512]{1,0:T(8,128)(2,1)S(1)} %add_convert_fusion.2), channel_id=1, source_target_pairs={{8,12},{9,13},{10,14},{11,15},{24,28},{25,29},{26,30},{27,31}} | collective-permute-start | bytes 786440 | tf_op jit(solution)/shard_map/ppermute | solution.py:366
  36.8 37.5 %collective-permute-start.15 = (bf16[256,512]{1,0:T(8,128)(2,1)S(1)}, bf16[256,512]{1,0:T(8,128)(2,1)S(1)}, u32[]{:S(2)}, u32[]{:S(2)}) collective-permute-start(bf16[256,512]{1,0:T(8,128)(2,1)S(1)} %add_convert_fusion.3), channel_id=1, source_target_pairs={{8,12},{9,13},{10,14},{11,15},{24,28},{25,29},{26,30},{27,31}} | collective-permute-start | bytes 786440 | tf_op jit(solution)/shard_map/ppermute | solution.py:366
  38.1 0.7 copy-start.13
  74.2 4.2 %copy-start.2 = (bf16[1,32,4096]{2,1,0:T(8,128)(2,1)S(1)}, bf16[1,32,4096]{2,1,0:T(8,128)(2,1)}, u32[]{:S(2)}) copy-start(bf16[1,32,4096]{2,1,0:T(8,128)(2,1)} %x_ref.5) | copy-start | bytes 786436
  74.2 4.2 %copy-start.7 = (bf16[1,32,4,256]{3,2,1,0:T(4,128)(2,1)S(1)}, bf16[1,32,4,256]{3,2,1,0:T(4,128)(2,1)}, u32[]{:S(2)}) copy-start(bf16[1,32,4,256]{3,2,1,0:T(4,128)(2,1)} %c_ref.5) | copy-start | bytes 196612
  74.2 4.2 %copy-start.8 = (bf16[1,32,4,256]{3,2,1,0:T(4,128)(2,1)S(1)}, bf16[1,32,4,256]{3,2,1,0:T(4,128)(2,1)}, u32[]{:S(2)}) copy-start(bf16[1,32,4,256]{3,2,1,0:T(4,128)(2,1)} %b_ref.3) | copy-start | bytes 196612
  74.2 4.2 %copy-start.11 = (f32[1,32,64]{2,1,0:T(8,128)S(1)}, f32[1,32,64]{2,1,0:T(8,128)}, u32[]{:S(2)}) copy-start(f32[1,32,64]{2,1,0:T(8,128)} %decay_ref.1) | copy-start | bytes 24580
  75.8 6.3 %collective-permute-start.22 = (bf16[32,2048]{1,0:T(8,128)(2,1)S(1)}, bf16[32,2048]{1,0:T(8,128)(2,1)S(1)}, u32[]{:S(2)}, u32[]{:S(2)}) collective-permute-start(bf16[32,2048]{1,0:T(8,128)(2,1)S(1)} %get-tuple-element.46), channel_id=1, source_target_pairs={{0,1},{1,0},{2,3},{3,2},{4,5},{5,4},{6,7},{7,6},{8,9},{9,8},{10,11... | collective-permute-start | bytes 393224 | tf_op jit(solution)/shard_map/ppermute | solution.py:439
  78.5 1.8 %copy-start.3 = (bf16[1,32,16,128]{3,2,1,0:T(8,128)(2,1)S(1)}, bf16[1,32,16,128]{3,2,1,0:T(8,128)(2,1)}, u32[]{:S(2)}) copy-start(bf16[1,32,16,128]{3,2,1,0:T(8,128)(2,1)} %q_ref.1) | copy-start | bytes 393220
  78.5 1.8 %copy-start.9 = (bf16[1,32,2,128]{3,2,1,0:T(2,128)(2,1)S(1)}, bf16[1,32,2,128]{3,2,1,0:T(2,128)(2,1)}, u32[]{:S(2)}) copy-start(bf16[1,32,2,128]{3,2,1,0:T(2,128)(2,1)} %own_k_ref.1) | copy-start | bytes 49156
  78.5 1.8 %copy-start.10 = (bf16[1,32,2,128]{3,2,1,0:T(2,128)(2,1)S(1)}, bf16[1,32,2,128]{3,2,1,0:T(2,128)(2,1)}, u32[]{:S(2)}) copy-start(bf16[1,32,2,128]{3,2,1,0:T(2,128)(2,1)} %own_v_ref.1) | copy-start | bytes 49156

commit v2 on v1

v2 whole, which is shorter than its diff:
```python
import functools

import jax
import jax.numpy as jnp
from jax import lax
from jax.experimental import pallas as pl
from jax.experimental.pallas import tpu as pltpu
from jax.sharding import PartitionSpec as P

EPSILON = 1e-06
NEG = -1e30
CHUNKS = 4
F32 = jnp.float32
BF16 = jnp.bfloat16


def mm(a, b):
    return lax.dot_general(a, b, (((1,), (0,)), ((), ())), preferred_element_type=F32)


def mm_nt(a, b):
    return lax.dot_general(a, b, (((1,), (1,)), ((), ())), preferred_element_type=F32)


def mm_tn(a, b):
    return lax.dot_general(a, b, (((0,), (0,)), ((), ())), preferred_element_type=F32)


def exact_nt(a, b):
    return lax.dot_general(
        a, b, (((1,), (1,)), ((), ())), preferred_element_type=F32, precision=lax.Precision.HIGHEST
    )


def exact(a, b):
    return lax.dot_general(
        a, b, (((1,), (0,)), ((), ())), preferred_element_type=F32, precision=lax.Precision.HIGHEST
    )


def iota(shape, dim):
    return lax.broadcasted_iota(jnp.int32, shape, dim)


def split3(a):
    hi = a.astype(BF16)
    rest = a - hi.astype(F32)
    mid = rest.astype(BF16)
    return hi, mid, (rest - mid.astype(F32)).astype(BF16)


def spread(a, width, first=0, count=None):
    rows, cols = a.shape
    count = cols if count is None else count
    parts = jnp.concatenate(split3(a), axis=1)
    shape = (3 * cols, count * width)
    source = iota(shape, 0)
    source = jnp.where(source >= 2 * cols, source - 2 * cols, jnp.where(source >= cols, source - cols, source))
    unit = (source == first + iota(shape, 1) // width).astype(F32).astype(BF16)
    return mm(parts, unit)


def group_of(array, g):
    return array.astype(F32)[:, g, :].astype(BF16)


def payload_plan(groups):
    of = [q * groups // CHUNKS for q in range(CHUNKS)]
    plan, seen = [], set()
    for chunks in ([0], [1], list(range(2, CHUNKS))):
        fresh = [g for g in sorted({of[q] for q in chunks}) if g not in seen]
        seen |= set(fresh)
        plan.append((chunks, fresh))
    return plan


def totals_to_lines(total):
    hi, mid, lo = [a.astype(F32) for a in split3(jnp.broadcast_to(total, (16, total.shape[1])))]
    line = iota(hi.shape, 0)
    return jnp.where(line == 0, hi, jnp.where(line == 1, mid, jnp.where(line == 2, lo, 0.0))).astype(BF16)


def lines_to_totals(lines):
    lines = lines.astype(F32)
    return lines[0:1] + lines[1:2] + lines[2:3]


def as_row(total, width):
    return spread(jnp.broadcast_to(total, (8, total.shape[1])), width)


def local_kernel(x_ref, b_ref, decay_t_ref, b2_ref, cum_ref, total_ref, *outs):
    local_refs, load_refs = outs[:CHUNKS], outs[CHUNKS:]
    tokens, groups, state = b_ref.shape
    heads = decay_t_ref.shape[0]
    width = x_ref.shape[1] // heads
    lower = (iota((tokens, tokens), 0) >= iota((tokens, tokens), 1)).astype(F32)
    cum = exact_nt(lower, decay_t_ref[...])
    cum_ref[...] = cum
    last = cum[tokens - 1 : tokens, :]
    weights = spread(jnp.exp(last - cum), width)
    b = b_ref[...].astype(F32)
    for g in range(groups):
        b2_ref[:, g * state : (g + 1) * state] = b[:, g, :].astype(BF16)
    cols = x_ref.shape[1] // CHUNKS
    for (chunks, fresh), load in zip(payload_plan(groups), load_refs):
        for i, q in enumerate(chunks):
            g = q * groups // CHUNKS
            at = slice(q * cols, (q + 1) * cols)
            weighted = (x_ref[:, at].astype(F32) * weights[:, at]).astype(BF16)
            load[:tokens, i * cols : (i + 1) * cols] = weighted
            local_refs[q][...] = mm_tn(b2_ref[:, g * state : (g + 1) * state], weighted)
        for i, g in enumerate(fresh):
            at = len(chunks) * cols + i * state
            load[:tokens, at : at + state] = b2_ref[:, g * state : (g + 1) * state]
    load = load_refs[0]
    load[tokens:, :] = jnp.zeros((16, load.shape[1]), BF16)
    total = jnp.exp(-last)
    total_ref[...] = jnp.broadcast_to(total, (8, heads))
    load[tokens:, :heads] = totals_to_lines(total)


def pack_kernel(k_ref, v_ref, out_ref):
    rep = lax.axis_index("rep")
    tokens, heads, dim = k_ref.shape
    kv = jnp.where(rep == 0, k_ref[...].astype(F32), v_ref[...].astype(F32))
    rows, wide = out_ref.shape
    for i in range(wide // (heads * dim)):
        for j in range(heads):
            at = (i * heads + j) * dim
            out_ref[:, at : at + dim] = kv[i * rows : (i + 1) * rows, j, :].astype(BF16)


def collect_kernel(*refs):
    out_ref = refs[-1]
    at = 0
    for ref in refs[:-1]:
        out_ref[at : at + ref.shape[0], :] = ref[...]
        at += ref.shape[0]


def half_of(place, level):
    odd = lax.rem(place, 2)
    return jnp.where(lax.rem(lax.div(place, 2**level), 2) == 0, 1 - odd, odd)


def merge_kernel(*refs, level, last, chunks, cols, groups, heads, tokens, carry):
    refs = list(refs)

    def take(count):
        taken = refs[:count]
        del refs[:count]
        return taken

    place = lax.axis_index("seq")
    right = lax.rem(lax.div(place, 2**level), 2) == 1
    width = cols * CHUNKS // heads
    first = 0 in chunks
    outs = []
    others = []
    if level == 0:
        for q in chunks:
            w_ref, b_ref = take(2)
            at_w, at_b = carry[q]
            others.append(mm_tn(b_ref[:tokens, at_b], w_ref[:tokens, at_w]))
    else:
        half = half_of(place, level)
        for q in chunks:
            near_ref, far_ref = take(2)
            rows = near_ref.shape[0] - 16 if q == 0 else near_ref.shape[0]
            near, far = near_ref[:rows, :], far_ref[:rows, :]
            pieces = [jnp.where(half == 0, near, far), jnp.where(half == 0, far, near)]
            others.append(jnp.concatenate(pieces, axis=1).astype(F32))
    if first:
        mine_ref, lines_ref = take(2)
        mine = mine_ref[:1, :]
        theirs = lines_to_totals(lines_ref[lines_ref.shape[0] - 16 :, :heads])
        later = as_row(jnp.where(right, mine, theirs), width)
        pair = mine * theirs
        if level == 0:
            before = jnp.ones_like(mine)
        else:
            before = take(1)[0][:1, :]
        before_row = as_row(before, width)
        before = jnp.where(right, before * theirs, before)
        outs += [later, before_row, jnp.broadcast_to(pair, (8, heads)), jnp.broadcast_to(before, (8, heads))]
    else:
        later_ref, before_ref = take(2)
        later, before_row = later_ref[...], before_ref[...]
    for q, other in zip(chunks, others, strict=True):
        at = slice(q * cols, (q + 1) * cols)
        own = take(1)[0][...]
        earlier, following = jnp.where(right, other, own), jnp.where(right, own, other)
        joined = later[:1, at] * earlier + following
        if level == 0:
            start = jnp.where(right, other, 0.0)
        else:
            start = take(1)[0][...]
            start = jnp.where(right, before_row[:1, at] * other + start, start)
        if not last:
            send = jnp.where(half_of(place, level + 1) == 0, joined[:, : cols // 2], joined[:, cols // 2 :]).astype(BF16)
            if q == 0:
                tail = jnp.zeros((16, cols // 2 - heads), BF16)
                lines = jnp.concatenate([totals_to_lines(pair), tail], axis=1)
                send = jnp.concatenate([send, lines], axis=0)
            outs += [joined, start, send]
        else:
            c2_ref, mine_c_ref, base_ref, cum_ref = take(4)
            state = own.shape[0]
            g = q * groups // CHUNKS
            here = slice(g * state, (g + 1) * state)
            fade = spread(jnp.exp(-cum_ref[...]), width, q * heads // CHUNKS, heads // CHUNKS)
            carried = mm(c2_ref[:, here], start.astype(BF16))
            outs.append((base_ref[:, at] + fade * carried).astype(BF16))
            outs.append(mm(mine_c_ref[:, here], joined.astype(BF16)))
    if last and CHUNKS - 1 in chunks:
        parts = take(2 * (CHUNKS - 1))
        out_parts = [ref[...] for ref in parts[: CHUNKS - 1]] + [outs[-2]]
        raws = [ref[...] for ref in parts[CHUNKS - 1 :]] + [outs[-1]]
        rep = lax.axis_index("rep")
        out_ref, keep_ref, give_ref = refs
        rows = keep_ref.shape[0]
        for q in range(CHUNKS):
            at = slice(q * cols, (q + 1) * cols)
            out_ref[:, at] = out_parts[q]
            keep_ref[:, at] = jnp.where(rep == 0, raws[q][:rows], raws[q][rows:])
            give_ref[:, at] = jnp.where(rep == 0, raws[q][rows:], raws[q][:rows]).astype(BF16)
    else:
        for ref, value in zip(refs, outs, strict=True):
            ref[...] = value


def projections_kernel(mine_ref, other_ref, out_ref):
    rep = lax.axis_index("rep")
    steps, all_groups, state = mine_ref.shape[1:]
    groups = all_groups // 2
    mine, other = mine_ref[0].astype(F32), other_ref[0].astype(F32)
    zero, one = jnp.where(rep == 0, mine, other), jnp.where(rep == 0, other, mine)
    for i, c in enumerate((zero, one)):
        for g in range(groups):
            part = jnp.where(rep == 0, c[:, g, :], c[:, groups + g, :])
            out_ref[i * steps : (i + 1) * steps, g * state : (g + 1) * state] = part.astype(BF16)


def intra_kernel(x_ref, b2_ref, c_ref, cum_ref, skip_ref, c2_ref, base_ref):
    tokens, groups, state = c_ref.shape
    heads = cum_ref.shape[1]
    width = x_ref.shape[1] // heads
    per_group = heads // groups
    first = (lax.axis_index("head") * lax.axis_size("rep") + lax.axis_index("rep")) * heads
    c = c_ref[...].astype(F32)
    for g in range(groups):
        c2_ref[:, g * state : (g + 1) * state] = c[:, g, :].astype(BF16)
    skip = spread(jnp.broadcast_to(skip_ref[...], (8, skip_ref.shape[1])), width, first, heads)[:1]
    cum = cum_ref[...]
    cum_t = cum.T
    shape = (tokens, tokens)
    hidden = jnp.where(iota(shape, 0) >= iota(shape, 1), 0.0, NEG)
    pair = 2 * width
    lane = iota((tokens, pair), 1)
    for g in range(groups):
        here = slice(g * state, (g + 1) * state)
        gram = mm_nt(c2_ref[:, here], b2_ref[:, here])
        for h in range(g * per_group, (g + 1) * per_group, 2):
            mixing = []
            for i in (h, h + 1):
                gap = cum_t[i : i + 1, :] - jnp.broadcast_to(cum[:, i : i + 1], shape)
                mixing.append((jnp.exp(gap + hidden) * gram).astype(BF16))
            at = slice(h * width, (h + 2) * width)
            x = x_ref[:, at]
            zero = jnp.zeros_like(x)
            inputs = jnp.concatenate(
                [jnp.where(lane < width, x, zero), jnp.where(lane < width, zero, x)], axis=0
            )
            base_ref[:, at] = mm(jnp.concatenate(mixing, axis=1), inputs) + skip[:, at] * x.astype(F32)


def cand_kernel(x_ref, b_ref, c_ref, decay_ref, skip_ref, base_ref, fade_ref):
    steps, groups, state = b_ref.shape[1:]
    heads = decay_ref.shape[2]
    width = x_ref.shape[2] // heads
    per_group = heads // groups
    first = lax.axis_index("head") * heads
    skip = spread(jnp.broadcast_to(skip_ref[...], (8, skip_ref.shape[1])), width, first, heads)[:1]
    lower = (iota((steps, steps), 0) >= iota((steps, steps), 1)).astype(F32)
    cum = exact(lower, decay_ref[0])
    fade_ref[...] = spread(jnp.exp(-cum), width)
    wide = (steps, heads * steps)
    cum_t = spread(cum, steps)
    place = iota(wide, 1) % steps
    row = iota(wide, 0)
    cum_s = jnp.sum(jnp.where(row == place, cum_t, 0.0), axis=0, keepdims=True)
    fall = jnp.exp(jnp.where(row >= place, cum_s - cum_t, NEG))
    b = b_ref[0].astype(F32)
    c = c_ref[0].astype(F32)
    quad = 128 // steps
    shape = (quad * steps, quad * width)
    mine = iota(shape, 0) // steps == iota(shape, 1) // width
    for g in range(groups):
        b_g = b[:, g, :].astype(BF16)
        gram = mm_nt(c[:, g, :].astype(BF16), jnp.concatenate([b_g] * quad, axis=0))
        for h in range(g * per_group, (g + 1) * per_group, quad):
            mixing = (fall[:, h * steps : (h + quad) * steps] * gram).astype(BF16)
            at = slice(h * width, (h + quad) * width)
            x = x_ref[0, :, at]
            tall = jnp.concatenate([x] * quad, axis=0)
            inputs = jnp.where(mine, tall, jnp.zeros_like(tall))
            base_ref[:, at] = mm(mixing, inputs) + skip[:, at] * x.astype(F32)


def attend_kernel(length_ref, q_ref, own_k_ref, own_v_ref, k_ref, v_ref, mine_ref, other_ref, *refs):
    out_ref = refs[-1]
    rep = lax.axis_index("rep")
    steps, heads, dim = q_ref.shape[1:]
    kv_heads = own_k_ref.shape[2]
    per_kv = heads // kv_heads
    rows = steps * per_kv
    mine, other = mine_ref[...], other_ref[...]
    keys, values = jnp.where(rep == 0, mine, other), jnp.where(rep == 0, other, mine)
    parts = mine.shape[1] // (kv_heads * dim)
    q = q_ref[0].astype(F32)
    own_k = own_k_ref[0].astype(F32)
    own_v = own_v_ref[0].astype(F32)
    block_k = k_ref[...].astype(F32)
    block_v = v_ref[...].astype(F32)
    scale = dim ** (-0.5)
    step_of = iota((rows, steps), 0) // per_kv
    visible = step_of >= iota((rows, steps), 1)
    live = iota((rows, dim), 0) // per_kv < length_ref[0]
    mixed_of = []
    for j in range(kv_heads):
        query = q[:, j * per_kv : (j + 1) * per_kv, :].reshape(rows, dim).astype(BF16)

        def gather(far, block):
            pieces = [far[:, (i * kv_heads + j) * dim : (i * kv_heads + j + 1) * dim] for i in range(parts)]
            return jnp.concatenate([*pieces, block[:, j, :].astype(BF16)], axis=0)

        far = mm_nt(query, gather(keys, block_k)) * scale
        near = jnp.where(visible, mm_nt(query, own_k[:, j, :].astype(BF16)) * scale, NEG)
        top = jnp.maximum(jnp.max(far, axis=1, keepdims=True), jnp.max(near, axis=1, keepdims=True))
        far = jnp.exp(far - top)
        near = jnp.exp(near - top)
        mass = jnp.sum(far, axis=1, keepdims=True) + jnp.sum(near, axis=1, keepdims=True)
        mixed = mm(far.astype(BF16), gather(values, block_v)) + mm(near.astype(BF16), own_v[:, j, :].astype(BF16))
        mixed = mixed / mass
        mixed = mixed * lax.rsqrt(jnp.mean(mixed * mixed, axis=1, keepdims=True) + EPSILON)
        mixed = jnp.where(live, mixed, 0.0)
        mixed_of.append(mixed.reshape(steps, per_kv, dim))
    out_ref[0] = (jnp.concatenate(mixed_of, axis=1) if kv_heads > 1 else mixed_of[0]).astype(BF16)


def close_kernel(length_ref, base_ref, fade_ref, keep_ref, got_ref, out_ref):
    rep = lax.axis_index("rep")
    keep, got = keep_ref[...], got_ref[...].astype(F32)
    cols = keep.shape[1]
    live = iota(keep.shape, 0) < length_ref[0]
    for i in range(2):
        at = slice(i * cols, (i + 1) * cols)
        carried = jnp.where(rep == i, keep, got)
        result = base_ref[:, at] + fade_ref[:, at] * carried
        out_ref[0, :, at] = jnp.where(live, result, 0.0).astype(BF16)


def call(kernel, name, outs, *args, scalars=0, after=()):
    shapes = [jax.ShapeDtypeStruct(shape, dtype) for shape, dtype in outs]
    moved = sum(a.size * a.dtype.itemsize for a in args) + sum(s.size * s.dtype.itemsize for s in shapes)
    vmem = pl.BlockSpec(memory_space=pltpu.VMEM)
    smem = pl.BlockSpec(memory_space=pltpu.SMEM)
    count, rest = len(args), len(args) + len(after)

    def body(*refs):
        kernel(*refs[:count], *refs[rest:])

    return pl.pallas_call(
        body,
        out_shape=shapes,
        in_specs=[smem] * scalars + [vmem] * (count - scalars) + [pl.BlockSpec(memory_space=pl.ANY)] * len(after),
        out_specs=[vmem] * len(shapes),
        compiler_params=pltpu.CompilerParams(vmem_limit_bytes=32 * 2**20),
        cost_estimate=pl.CostEstimate(flops=10**8, bytes_accessed=int(moved), transcendentals=0),
        name=name,
    )(*args, *after)


def on_device(
    prefix_x,
    prefix_b,
    prefix_c,
    prefix_decay,
    bypass_weight,
    prefix_key_rows,
    prefix_values,
    cand_x,
    cand_b,
    cand_c,
    cand_decay,
    cand_queries,
    cand_keys,
    cand_values,
    cand_length,
):
    size = lax.axis_size("seq")
    levels = size.bit_length() - 1
    assert size == 2**levels and lax.axis_size("rep") == 2
    tokens, groups, state = prefix_b.shape
    heads = prefix_decay.shape[1]
    wide = prefix_x.shape[1]
    steps = cand_x.shape[1]
    cand_wide = cand_x.shape[2]
    cols = wide // CHUNKS
    skip = bypass_weight.reshape(1, -1)
    plan = payload_plan(groups)

    def to_core(array):
        return lax.ppermute(array, "rep", [(0, 1), (1, 0)])

    def to_neighbour(array):
        return lax.ppermute(array, "seq", [(i, i ^ 1) for i in range(size)])

    def to_mirror(array, level):
        return lax.ppermute(array, "seq", [(i, i ^ (2 ** (level + 1) - 1)) for i in range(size)])

    other_c = to_core(cand_c)
    b2, cum, total, *parts = call(
        local_kernel,
        "local_state",
        [((tokens, groups * state), BF16), ((tokens, heads), F32), ((8, heads), F32)]
        + [((state, cols), F32)] * CHUNKS
        + [
            ((tokens + (16 if p == 0 else 0), len(chunks) * cols + len(fresh) * state), BF16)
            for p, (chunks, fresh) in enumerate(plan)
        ],
        prefix_x,
        prefix_b,
        prefix_decay.T,
    )
    local, loads = parts[:CHUNKS], parts[CHUNKS:]
    got = [to_neighbour(a) for a in loads]
    kv_rows = prefix_key_rows.size // (groups * state)
    (kv,) = call(
        pack_kernel, "pack", [((kv_rows, groups * state), BF16)], prefix_key_rows, prefix_values, after=(loads[0],)
    )
    halves = [kv, to_neighbour(kv)]
    for level in range(1, levels):
        mirrored = to_mirror(halves[0], level)
        halves = [halves[0], halves[1], mirrored, to_neighbour(mirrored)]
        if level < levels - 1:
            halves = [jnp.concatenate([halves[0], halves[2]]), jnp.concatenate([halves[1], halves[3]])]
    c2, base = call(
        intra_kernel,
        "intra",
        [((tokens, groups * state), BF16), ((tokens, wide), F32)],
        prefix_x,
        b2,
        prefix_c,
        cum,
        skip,
        after=(kv,),
    )
    (both_c,) = call(
        projections_kernel, "projections", [((2 * steps, groups * state), BF16)], cand_c, other_c, after=(base,)
    )
    where = {}
    spot = {}
    for p, (chunks, fresh) in enumerate(plan):
        for i, g in enumerate(fresh):
            at = len(chunks) * cols + i * state
            where[g] = (p, slice(at, at + state))
        for i, q in enumerate(chunks):
            spot[q] = (p, slice(i * cols, (i + 1) * cols))
    mark = both_c
    own, start = dict(enumerate(local)), {}
    before = None
    near, far = {}, {}
    cand_base = cand_attn = None
    out_parts, raws = [], []

    def attend(mark):
        (mine,) = call(
            collect_kernel,
            "collect",
            [((kv_rows * (size - 1), groups * state), BF16)],
            *halves[1:],
            after=(mark,),
        )
        return call(
            attend_kernel,
            "attend",
            [(cand_queries.shape, BF16)],
            cand_length,
            cand_queries,
            cand_keys,
            cand_values,
            prefix_key_rows,
            prefix_values,
            mine,
            to_core(mine),
            scalars=1,
        )[0]

    for level in range(levels):
        last = level == levels - 1
        rows = None
        for batch in [chunks for chunks, _ in plan] if level == 0 else [[q] for q in range(CHUNKS)]:
            args, outs = [], []
            if level == 0:
                for q in batch:
                    args += [got[spot[q][0]], got[where[q * groups // CHUNKS][0]]]
                lines = got[0]
            else:
                for q in batch:
                    args += [near[q], far[q]]
                lines = near.get(0)
            if 0 in batch:
                args += [total, lines] + ([] if level == 0 else [before])
                outs += [((8, wide), F32)] * 2 + [((8, heads), F32)] * 2
            else:
                args += rows
            for q in batch:
                args += [own[q]] + ([] if level == 0 else [start[q]])
                if last:
                    args += [c2, both_c, base, cum]
                    outs += [((tokens, cols), BF16), ((2 * steps, cols), F32)]
                else:
                    outs += [((state, cols), F32)] * 2
                    outs += [((state + (16 if q == 0 else 0), cols // 2), BF16)]
            if last and batch == [CHUNKS - 1]:
                args += out_parts + raws
                outs = [((tokens, wide), BF16), ((steps, wide), F32), ((steps, wide), BF16)]
            results = list(
                call(
                    functools.partial(
                        merge_kernel,
                        level=level,
                        last=last,
                        chunks=batch,
                        cols=cols,
                        groups=groups,
                        heads=heads,
                        tokens=tokens,
                        carry={q: (spot[q][1], where[q * groups // CHUNKS][1]) for q in batch},
                    ),
                    "merge",
                    outs,
                    *args,
                    after=(mark,),
                )
            )
            mark = results[0]
            if last and batch == [CHUNKS - 1]:
                prefix_out, keep, give = results
                continue
            if 0 in batch:
                rows, results = results[:2], results[2:]
                total, before = results[:2]
                results = results[2:]
            for q in batch:
                if last:
                    out_parts.append(results.pop(0))
                    raws.append(results.pop(0))
                else:
                    own[q], start[q], sent = results[:3]
                    results = results[3:]
                    near[q] = to_mirror(sent, level + 1)
                    far[q] = to_neighbour(near[q])
            if level == 0 and 0 in batch:
                cand_base, cand_fade = call(
                    cand_kernel,
                    "candidates",
                    [((steps, cand_wide), F32), ((steps, cand_wide), F32)],
                    cand_x,
                    cand_b,
                    cand_c,
                    cand_decay,
                    skip,
                    after=(mark,),
                )
                mark = cand_base
        if level == 0:
            cand_attn = attend(mark)
            mark = cand_attn
    (cand_ssm,) = call(
        close_kernel,
        "close",
        [((1, steps, cand_wide), BF16)],
        cand_length,
        cand_base,
        cand_fade,
        keep,
        to_core(give),
        scalars=1,
    )
    return (prefix_out, cand_ssm, cand_attn)


def solution(mesh):
    placed = (
        P(("groups", "seq"), ("head", "rep")),
        P(("groups", "seq"), ("head", "rep"), None),
        P(("groups", "seq"), ("head", "rep"), None),
        P(("groups", "seq"), ("head", "rep")),
        P(),
        P(("groups", "seq"), "head", None),
        P(("groups", "seq"), "head", None),
        P(("groups", "seq", "rep"), None, "head"),
        P(("groups", "seq", "rep"), None, "head", None),
        P(("groups", "seq", "rep"), None, "head", None),
        P(("groups", "seq", "rep"), None, "head"),
        P(("groups", "seq", "rep"), None, "head", None),
        P(("groups", "seq", "rep"), None, "head", None),
        P(("groups", "seq", "rep"), None, "head", None),
        P(("groups", "seq", "rep")),
    )
    return jax.shard_map(
        on_device,
        mesh=mesh,
        in_specs=placed,
        out_specs=(
            P(("groups", "seq"), ("head", "rep")),
            P(("groups", "seq", "rep"), None, "head"),
            P(("groups", "seq", "rep"), None, "head", None),
        ),
        check_vma=False,
    )
```

time: 83.5 us -> 62 us (0.74)
  the two profiles are of different devices: /device:TPU:25 before, /device:TPU:0 now
where the time goes in v2:
time: 62 us; the launch traced here: 61.7 us
  starting transfers between devices  30.9 us (50%)
  waiting for transfers between devices  12.7 us (20%)
  Pallas kernels  11.5 us (19%)
  local copies, waits for them, and re-layouts  5.1 us (8%)
  between operations  1.49 us (2%)
    ppermute x9, starting transfers between devices, to_neighbour(): return lax.ppermute(array, 'seq', [(i, i ^ 1) for i in range(size)])  20.5 us
    pallas_call x15, Pallas kernels, call(): pl.pallas_call(body, out_shape=shapes, in_specs=[smem] * scalars + [vmem]...  11.5 us
    ppermute x5, waiting for transfers between devices, to_mirror(): lax.ppermute(array, 'seq', [(i, i ^ 2 ** (level + 1) - 1) for i in range(...  11.3 us
    ppermute x5, starting transfers between devices, to_mirror(): lax.ppermute(array, 'seq', [(i, i ^ 2 ** (level + 1) - 1) for i in range(...  10.4 us
    unnamed x34, local copies, waits for them, and re-layouts  5.1 us
    ppermute x3, waiting for transfers between devices, to_core(): return lax.ppermute(array, 'rep', [(0, 1), (1, 0)])  1.35 us
  transfers between devices with their start and end apart: 17, of which 2 were waited for; matrix products, arithmetic and copies ran while one was open for 0% of the time, Pallas kernels for 13%

profile of v2, /device:TPU:0, one launch (start us, length us, event | category | flops | bytes accessed | tf_op | source)
XLA Modules:
  0.0 61.7 jit_solution(14379740327282340074)
XLA Ops:
  0.6 0.0 copy-start
  0.6 1.0 %copy-done = bf16[128,2048]{1,0:T(8,128)(2,1)S(1)} copy-done((bf16[128,2048]{1,0:T(8,128)(2,1)S(1)}, bf16[128,2048]{1,0:T(8,128)(2,1)}, u32[]{:S(2)}) %copy-start) | copy-done | bytes 524312
  1.7 0.9 %copy-done.9 = bf16[128,2,256]{2,1,0:T(2,128)(2,1)S(1)} copy-done((bf16[128,2,256]{2,1,0:T(2,128)(2,1)S(1)}, bf16[128,2,256]{2,1,0:T(2,128)(2,1)}, u32[]{:S(2)}) %copy-start.9) | copy-done | bytes 131096
  2.6 0.7 %copy-done.15 = f32[128,32]{0,1:T(8,128)S(1)} copy-done((f32[128,32]{0,1:T(8,128)S(1)}, f32[128,32]{0,1:T(8,128)}, u32[]{:S(2)}) %copy-start.15) | copy-done | bytes 16408
  3.3 1.2 %local_state.1 = (bf16[128,512]{1,0:T(8,128)(2,1)S(1)}, f32[128,32]{1,0:T(8,128)S(1)}, f32[8,32]{1,0:T(8,128)S(1)}, f32[256,512]{1,0:T(8,128)S(1)}, f32[256,512]...) custom-call(bf16[128,2048]{1,0:T(8,128)(2,1)S(1)} %copy-done, ...), custom_call_target="tpu_custom_call" | custom-call | flops 100000000 | bytes 3597312 | tf_op jit(solution)/shard_map/local_state/pallas_call | solution.py:374
  4.5 3.1 %collective-permute-start = (bf16[128,1280]{1,0:T(8,128)(2,1)S(1)}, bf16[128,1280]{1,0:T(8,128)(2,1)S(1)}, u32[]{:S(2)}, u32[]{:S(2)}) collective-permute-start(bf16[128,1280]{1,0:T(8,128)(2,1)S(1)} %get-tuple-element.44), channel_id=1, source_target_pairs={{0,4},{4,0},{8,12},{12,8},{1,5},{5,1},{9,13},{13,9},{2,6},{6,2},{1... | collective-permute-start | bytes 983048 | tf_op jit(solution)/shard_map/ppermute | solution.py:418
  7.6 0.1 collective-permute-start.1
  7.7 1.9 %collective-permute-start.3 = (bf16[128,512]{1,0:T(8,128)(2,1)S(1)}, bf16[128,512]{1,0:T(8,128)(2,1)S(1)}, u32[]{:S(2)}, u32[]{:S(2)}) collective-permute-start(bf16[128,512]{1,0:T(8,128)(2,1)S(1)} %get-tuple-element.55), channel_id=1, source_target_pairs={{0,4},{4,0},{8,12},{12,8},{1,5},{5,1},{9,13},{13,9},{2,6},{6,2},{1... | collective-permute-start | bytes 393224 | tf_op jit(solution)/shard_map/ppermute | solution.py:418
  9.6 0.0 copy-done.4
  9.6 0.0 collective-permute-start.2
  9.6 0.0 copy-done.5
  9.6 0.0 copy-start.6
  9.6 0.8 %copy-done.6 = bf16[128,2,128]{2,1,0:T(2,128)(2,1)S(1)} copy-done((bf16[128,2,128]{2,1,0:T(2,128)(2,1)S(1)}, bf16[128,2,128]{2,1,0:T(2,128)(2,1)}, u32[]{:S(2)}) %copy-start.6) | copy-done | bytes 65560
  10.5 0.2 pack.1.refs_5_
  10.6 2.5 %collective-permute-start.9 = (bf16[64,512]{1,0:T(8,128)(2,1)S(1)}, bf16[64,512]{1,0:T(8,128)(2,1)S(1)}, u32[]{:S(2)}, u32[]{:S(2)}) collective-permute-start(bf16[64,512]{1,0:T(8,128)(2,1)S(1)} %pack.1.refs_5_), channel_id=1, source_target_pairs={{0,12},{4,8},{8,4},{12,0},{1,13},{5,9},{9,5},{13,1},{2,14},{6,10},... | collective-permute-start | bytes 196616 | tf_op jit(solution)/shard_map/ppermute | solution.py:421
  13.2 0.0 collective-permute-done.2.refs_1_
  13.2 0.7 %collective-permute-start.8 = (bf16[64,512]{1,0:T(8,128)(2,1)S(1)}, bf16[64,512]{1,0:T(8,128)(2,1)S(1)}, u32[]{:S(2)}, u32[]{:S(2)}) collective-permute-start(bf16[64,512]{1,0:T(8,128)(2,1)S(1)} %pack.1.refs_5_), channel_id=1, source_target_pairs={{0,4},{4,0},{8,12},{12,8},{1,5},{5,1},{9,13},{13,9},{2,6},{6,2},{1... | collective-permute-start | bytes 196616 | tf_op jit(solution)/shard_map/ppermute | solution.py:418
  13.9 0.0 copy-done.1
  13.9 0.6 %copy-done.16 = f32[128]{0:T(128)S(1)} copy-done((f32[128]{0:T(128)S(1)}, f32[128]{0:T(128)}, u32[]{:S(2)}) %copy-start.16) | copy-done | bytes 536
  14.5 1.4 %intra.1 = (bf16[128,512]{1,0:T(8,128)(2,1)S(1)}, f32[128,2048]{1,0:T(8,128)S(1)}) custom-call(bf16[128,2048]{1,0:T(8,128)(2,1)S(1)} %copy-done.1, bf16[128,512]{1,0:T(8,128)(2,1)S(1)} %get-tuple-element.48.refs_1_, bf16[128,2,256]{2,1,0:T(2,128)(2,1)S(1)} %copy-done.8, f32[128,32]{1,0:T(8,128)S(1)} %get-tuple-element.49.refs_3_.refs_10_.refs_9_, ...), custom_call_target="tpu_custom_call" | custom-call | flops 100000000 | bytes 1982976 | tf_op jit(solution)/shard_map/intra/pallas_call | solution.py:374
  15.9 11.3 %collective-permute-done.9.refs_1_ = bf16[64,512]{1,0:T(8,128)(2,1)S(1)} collective-permute-done((bf16[64,512]{1,0:T(8,128)(2,1)S(1)}, bf16[64,512]{1,0:T(8,128)(2,1)S(1)}, u32[]{:S(2)}, u32[]{:S(2)}) %collective-permute-start.9) | collective-permute-done | bytes 65568 | tf_op jit(solution)/shard_map/ppermute | solution.py:421
  27.1 0.0 collective-permute-start.10
  27.1 0.2 projections.1.refs_5_.refs_8_.refs_7_
  27.4 0.0 collective-permute-done.1.refs_0_.refs_1_.refs_3_
  27.4 0.0 copy-start.3
  27.4 0.0 copy-start.11
  27.4 0.0 copy-start.12
  27.4 0.4 merge.7
  27.9 1.5 %collective-permute-start.6 = (bf16[272,256]{1,0:T(8,128)(2,1)S(1)}, bf16[272,256]{1,0:T(8,128)(2,1)S(1)}, u32[]{:S(2)}, u32[]{:S(2)}) collective-permute-start(bf16[272,256]{1,0:T(8,128)(2,1)S(1)} %get-tuple-element.60), channel_id=1, source_target_pairs={{0,12},{4,8},{8,4},{12,0},{1,13},{5,9},{9,5},{13,1},{2,14},{6,10},... | collective-permute-start | bytes 417800 | tf_op jit(solution)/shard_map/ppermute | solution.py:421
  29.4 0.0 copy-done.12
  29.4 1.8 %candidates.1 = (f32[32,4096]{1,0:T(8,128)S(1)}, f32[32,4096]{1,0:T(8,128)S(1)}) custom-call(bf16[1,32,4096]{2,1,0:T(8,128)(2,1)S(1)} %copy-done.3, bf16[1,32,4,256]{3,2,1,0:T(4,128)(2,1)S(1)} %copy-done.11, bf16[1,32,4,256]{3,2,1,0:T(4,128)(2,1)S(1)} %copy-done.4, f32[1,32,64]{2,1,0:T(8,128)S(1)} %copy-done.12, f32[1,128]{1,0:T(1,128)S(1)} %bitcast.4, ...), custom_call_target="tpu_custom_call" | custom-call | flops 100000000 | bytes 1450496 | tf_op jit(solution)/shard_map/candidates/pallas_call | solution.py:374
  31.2 0.0 collective-permute-done.3.refs_0_
  31.2 0.3 merge.8
  31.5 2.4 %collective-permute-start.12 = (bf16[256,256]{1,0:T(8,128)(2,1)S(1)}, bf16[256,256]{1,0:T(8,128)(2,1)S(1)}, u32[]{:S(2)}, u32[]{:S(2)}) collective-permute-start(bf16[256,256]{1,0:T(8,128)(2,1)S(1)} %get-tuple-element.72), channel_id=1, source_target_pairs={{0,12},{4,8},{8,4},{12,0},{1,13},{5,9},{9,5},{13,1},{2,14},{6,10},... | collective-permute-start | bytes 393224 | tf_op jit(solution)/shard_map/ppermute | solution.py:421
  33.9 0.0 collective-permute-done.refs_0_.refs_1_.refs_2_.refs_3_
  33.9 0.4 merge.9
  34.3 1.5 %collective-permute-start.14 = (bf16[256,256]{1,0:T(8,128)(2,1)S(1)}, bf16[256,256]{1,0:T(8,128)(2,1)S(1)}, u32[]{:S(2)}, u32[]{:S(2)}) collective-permute-start(bf16[256,256]{1,0:T(8,128)(2,1)S(1)} %get-tuple-element.75), channel_id=1, source_target_pairs={{0,12},{4,8},{8,4},{12,0},{1,13},{5,9},{9,5},{13,1},{2,14},{6,10},... | collective-permute-start | bytes 393224 | tf_op jit(solution)/shard_map/ppermute | solution.py:421
  35.8 0.0 collective-permute-done.8.refs_0_
  35.8 2.4 %collective-permute-start.4 = (bf16[256,256]{1,0:T(8,128)(2,1)S(1)}, bf16[256,256]{1,0:T(8,128)(2,1)S(1)}, u32[]{:S(2)}, u32[]{:S(2)}) collective-permute-start(bf16[256,256]{1,0:T(8,128)(2,1)S(1)} %get-tuple-element.59), channel_id=1, source_target_pairs={{0,12},{4,8},{8,4},{12,0},{1,13},{5,9},{9,5},{13,1},{2,14},{6,10},... | collective-permute-start | bytes 393224 | tf_op jit(solution)/shard_map/ppermute | solution.py:421
  38.2 0.0 collective-permute-done.10.refs_2_
  38.2 0.0 copy-start.14
  38.2 0.1 collective-permute-start.11
  38.3 0.0 collective-permute-done.6.refs_0_.refs_3_
  38.3 8.1 %collective-permute-start.7 = (bf16[272,256]{1,0:T(8,128)(2,1)S(1)}, bf16[272,256]{1,0:T(8,128)(2,1)S(1)}, u32[]{:S(2)}, u32[]{:S(2)}) collective-permute-start(bf16[272,256]{1,0:T(8,128)(2,1)S(1)} %collective-permute-done.6.refs_0_.refs_3_), channel_id=1, source_target_pairs={{0,4},{4,0},{8,12},{12,8},{1,5},{5,1},{9,13},{13,9},{2,6},{6,2},{1... | collective-permute-start | bytes 417800 | tf_op jit(solution)/shard_map/ppermute | solution.py:418
  46.5 0.0 collective-permute-done.12.refs_0_
  46.5 2.8 %collective-permute-start.13 = (bf16[256,256]{1,0:T(8,128)(2,1)S(1)}, bf16[256,256]{1,0:T(8,128)(2,1)S(1)}, u32[]{:S(2)}, u32[]{:S(2)}) collective-permute-start(bf16[256,256]{1,0:T(8,128)(2,1)S(1)} %collective-permute-done.12.refs_0_), channel_id=1, source_target_pairs={{0,4},{4,0},{8,12},{12,8},{1,5},{5,1},{9,13},{13,9},{2,6},{6,2},{1... | collective-permute-start | bytes 393224 | tf_op jit(solution)/shard_map/ppermute | solution.py:418
  49.3 0.0 collective-permute-done.14.refs_0_
  49.3 2.4 %collective-permute-start.15 = (bf16[256,256]{1,0:T(8,128)(2,1)S(1)}, bf16[256,256]{1,0:T(8,128)(2,1)S(1)}, u32[]{:S(2)}, u32[]{:S(2)}) collective-permute-start(bf16[256,256]{1,0:T(8,128)(2,1)S(1)} %collective-permute-done.14.refs_0_), channel_id=1, source_target_pairs={{0,4},{4,0},{8,12},{12,8},{1,5},{5,1},{9,13},{13,9},{2,6},{6,2},{1... | collective-permute-start | bytes 393224 | tf_op jit(solution)/shard_map/ppermute | solution.py:418
  51.6 0.0 collective-permute-done.4.refs_0_
  51.6 1.4 %collective-permute-start.5 = (bf16[256,256]{1,0:T(8,128)(2,1)S(1)}, bf16[256,256]{1,0:T(8,128)(2,1)S(1)}, u32[]{:S(2)}, u32[]{:S(2)}) collective-permute-start(bf16[256,256]{1,0:T(8,128)(2,1)S(1)} %collective-permute-done.4.refs_0_), channel_id=1, source_target_pairs={{0,4},{4,0},{8,12},{12,8},{1,5},{5,1},{9,13},{13,9},{2,6},{6,2},{1... | collective-permute-start | bytes 393224 | tf_op jit(solution)/shard_map/ppermute | solution.py:418
  53.7 0.0 collective-permute-done.11.refs_7_
  53.7 1.9 %attend.1.refs_11_ = bf16[1,32,16,128]{3,2,1,0:T(8,128)(2,1)} custom-call(s32[1]{0:T(128)S(6)} %copy.18.refs_0_, bf16[1,32,16,128]{3,2,1,0:T(8,128)(2,1)S(1)} %copy-done.10, bf16[1,32,2,128]{3,2,1,0:T(2,128)(2,1)S(1)} %copy-done.13, bf16[1,32,2,128]{3,2,1,0:T(2,128)(2,1)S(1)} %copy-done.14, bf16[128,2,128]{2,1,0:T(2,128)(2,1)S(1)} %copy-done.5, ...), custom_call_target="tpu_custom_call" | custom-call | flops 100000000 | bytes 819204 | tf_op jit(solution)/shard_map/attend/pallas_call | solution.py:374
  55.7 0.0 collective-permute-done.7.refs_1_
  55.7 0.9 %copy-done.2 = bf16[1,32,16,128]{3,2,1,0:T(8,128)(2,1)S(1)} copy-done((bf16[1,32,16,128]{3,2,1,0:T(8,128)(2,1)S(1)}, bf16[1,32,16,128]{3,2,1,0:T(8,128)(2,1)}, u32[]{:S(2)}) %copy-start.2) | copy-done | bytes 131096
  56.6 1.0 %merge.10 = (f32[8,2048]{1,0:T(8,128)S(1)}, f32[8,2048]{1,0:T(8,128)S(1)}, f32[8,32]{1,0:T(8,128)}, f32[8,32]{1,0:T(8,128)}, bf16[128,512]{1,0:T(8,128)(2,1)S(1)}, /*index=5*/f32[64,512]{1,0:T(8,128)S(1)}) custom-call(bf16[272,256]{1,0:T(8,128)(2,1)S(1)} %collective-permute-done.6.refs_0_.refs_3_, bf16[272,256]{1,0:T(8,128)(2,1)S(1)} %collective-permute-done.7.refs_1_, ...), custom_call_target="tpu_custom_call" | custom-call | flops 100000000 | bytes 3125248 | tf_op jit(solution)/shard_map/merge/pallas_call | solution.py:374
  57.6 0.0 collective-permute-done.13.refs_1_
  57.6 0.4 merge.11
  58.0 0.0 collective-permute-done.15.refs_1_
  58.0 0.4 merge.12
  58.3 0.0 collective-permute-done.5.refs_1_
  58.3 1.2 %merge.13 = (bf16[128,2048]{1,0:T(8,128)(2,1)}, f32[32,2048]{1,0:T(8,128)S(1)}, bf16[32,2048]{1,0:T(8,128)(2,1)S(1)}) custom-call(bf16[256,256]{1,0:T(8,128)(2,1)S(1)} %collective-permute-done.4.refs_0_, bf16[256,256]{1,0:T(8,128)(2,1)S(1)} %collective-permute-done.5.refs_1_, f32[8,2048]{1,0:T(8,128)S(1)} %get-tuple-element.67.refs_2_.refs_10_, ...), custom_call_target="tpu_custom_call" | custom-call | flops 100000000 | bytes 4407296 | tf_op jit(solution)/shard_map/merge/pallas_call | solution.py:374
  59.5 0.0 collective-permute-start.16
  59.5 1.3 %collective-permute-done.16.refs_4_ = bf16[32,2048]{1,0:T(8,128)(2,1)S(1)} collective-permute-done((bf16[32,2048]{1,0:T(8,128)(2,1)S(1)}, bf16[32,2048]{1,0:T(8,128)(2,1)S(1)}, u32[]{:S(2)}, u32[]{:S(2)}) %collective-permute-start.16) | collective-permute-done | bytes 131104 | tf_op jit(solution)/shard_map/ppermute | solution.py:415
  60.9 0.8 %close.1 = bf16[1,32,4096]{2,1,0:T(8,128)(2,1)} custom-call(s32[1]{0:T(128)S(6)} %copy.18.refs_0_, f32[32,4096]{1,0:T(8,128)S(1)} %get-tuple-element.57.refs_5_.refs_1_, f32[32,4096]{1,0:T(8,128)S(1)} %get-tuple-element.82.refs_2_, f32[32,2048]{1,0:T(8,128)S(1)} %get-tuple-element.83.refs_3_, bf16[32,2048]{1,0:T(8,128)(2,1)S(1)} %collective-permute-done.16.refs_4_), custom_call_target="tpu_custom_call" | custom-call | flops 100000000 | bytes 1703940 | tf_op jit(solution)/shard_map/close/pallas_call | solution.py:374
  (19 shorter events, 0.0 us)
Async XLA Ops:
  0.6 1.0 %copy-start = (bf16[128,2048]{1,0:T(8,128)(2,1)S(1)}, bf16[128,2048]{1,0:T(8,128)(2,1)}, u32[]{:S(2)}) copy-start(bf16[128,2048]{1,0:T(8,128)(2,1)} %refs_0_.9) | copy-start | bytes 1572868
  1.7 0.9 %copy-start.9 = (bf16[128,2,256]{2,1,0:T(2,128)(2,1)S(1)}, bf16[128,2,256]{2,1,0:T(2,128)(2,1)}, u32[]{:S(2)}) copy-start(bf16[128,2,256]{2,1,0:T(2,128)(2,1)} %refs_1_.4) | copy-start | bytes 393220
  2.6 0.7 %copy-start.15 = (f32[128,32]{0,1:T(8,128)S(1)}, f32[128,32]{0,1:T(8,128)}, u32[]{:S(2)}) copy-start(f32[128,32]{0,1:T(8,128)} %param.18) | copy-start | bytes 49156
  3.3 6.3 %copy-start.4 = (bf16[1,32,4,256]{3,2,1,0:T(4,128)(2,1)S(1)}, bf16[1,32,4,256]{3,2,1,0:T(4,128)(2,1)}, u32[]{:S(2)}) copy-start(bf16[1,32,4,256]{3,2,1,0:T(4,128)(2,1)} %refs_2_.4) | copy-start | bytes 196612
  3.3 6.3 %copy-start.5 = (bf16[128,2,128]{2,1,0:T(2,128)(2,1)S(1)}, bf16[128,2,128]{2,1,0:T(2,128)(2,1)}, u32[]{:S(2)}) copy-start(bf16[128,2,128]{2,1,0:T(2,128)(2,1)} %refs_4_.1) | copy-start | bytes 196612
  3.3 10.6 %copy-start.1 = (bf16[128,2048]{1,0:T(8,128)(2,1)S(1)}, bf16[128,2048]{1,0:T(8,128)(2,1)}, u32[]{:S(2)}) copy-start(bf16[128,2048]{1,0:T(8,128)(2,1)} %refs_0_.9) | copy-start | bytes 1572868
  4.5 29.4 %collective-permute-start = (bf16[128,1280]{1,0:T(8,128)(2,1)S(1)}, bf16[128,1280]{1,0:T(8,128)(2,1)S(1)}, u32[]{:S(2)}, u32[]{:S(2)}) collective-permute-start(bf16[128,1280]{1,0:T(8,128)(2,1)S(1)} %get-tuple-element.44), channel_id=1, source_target_pairs={{0,4},{4,0},{8,12},{12,8},{1,5},{5,1},{9,13},{13,9},{2,6},{6,2},{1... | collective-permute-start | bytes 983048 | tf_op jit(solution)/shard_map/ppermute | solution.py:418
  7.6 19.8 %collective-permute-start.1 = (bf16[144,768]{1,0:T(8,128)(2,1)S(1)}, bf16[144,768]{1,0:T(8,128)(2,1)S(1)}, u32[]{:S(2)}, u32[]{:S(2)}) collective-permute-start(bf16[144,768]{1,0:T(8,128)(2,1)S(1)} %get-tuple-element.45.refs_2_), channel_id=1, source_target_pairs={{0,4},{4,0},{8,12},{12,8},{1,5},{5,1},{9,13},{13,9},{2,6},{6,2},{1... | collective-permute-start | bytes 663560 | tf_op jit(solution)/shard_map/ppermute | solution.py:418
  7.7 23.5 %collective-permute-start.3 = (bf16[128,512]{1,0:T(8,128)(2,1)S(1)}, bf16[128,512]{1,0:T(8,128)(2,1)S(1)}, u32[]{:S(2)}, u32[]{:S(2)}) collective-permute-start(bf16[128,512]{1,0:T(8,128)(2,1)S(1)} %get-tuple-element.55), channel_id=1, source_target_pairs={{0,4},{4,0},{8,12},{12,8},{1,5},{5,1},{9,13},{13,9},{2,6},{6,2},{1... | collective-permute-start | bytes 393224 | tf_op jit(solution)/shard_map/ppermute | solution.py:418
  9.6 3.6 %collective-permute-start.2 = (bf16[1,32,4,256]{3,2,1,0:T(4,128)(2,1)S(1)}, bf16[1,32,4,256]{3,2,1,0:T(4,128)(2,1)S(1)}, u32[]{:S(2)}, u32[]{:S(2)}) collective-permute-start(bf16[1,32,4,256]{3,2,1,0:T(4,128)(2,1)S(1)} %copy-done.4), channel_id=1, source_target_pairs={{0,1},{1,0},{2,3},{3,2},{4,5},{5,4},{6,7},{7,6},{8,9},{9,8},{10,11... | collective-permute-start | bytes 196616 | tf_op jit(solution)/shard_map/ppermute | solution.py:415
  9.6 0.8 %copy-start.6 = (bf16[128,2,128]{2,1,0:T(2,128)(2,1)S(1)}, bf16[128,2,128]{2,1,0:T(2,128)(2,1)}, u32[]{:S(2)}) copy-start(bf16[128,2,128]{2,1,0:T(2,128)(2,1)} %refs_5_.1) | copy-start | bytes 196612
  10.5 3.4 %copy-start.8 = (bf16[128,2,256]{2,1,0:T(2,128)(2,1)S(1)}, bf16[128,2,256]{2,1,0:T(2,128)(2,1)}, u32[]{:S(2)}) copy-start(bf16[128,2,256]{2,1,0:T(2,128)(2,1)} %refs_2_.3) | copy-start | bytes 393220
  10.6 16.5 %collective-permute-start.9 = (bf16[64,512]{1,0:T(8,128)(2,1)S(1)}, bf16[64,512]{1,0:T(8,128)(2,1)S(1)}, u32[]{:S(2)}, u32[]{:S(2)}) collective-permute-start(bf16[64,512]{1,0:T(8,128)(2,1)S(1)} %pack.1.refs_5_), channel_id=1, source_target_pairs={{0,12},{4,8},{8,4},{12,0},{1,13},{5,9},{9,5},{13,1},{2,14},{6,10},... | collective-permute-start | bytes 196616 | tf_op jit(solution)/shard_map/ppermute | solution.py:421
  13.2 22.7 %collective-permute-start.8 = (bf16[64,512]{1,0:T(8,128)(2,1)S(1)}, bf16[64,512]{1,0:T(8,128)(2,1)S(1)}, u32[]{:S(2)}, u32[]{:S(2)}) collective-permute-start(bf16[64,512]{1,0:T(8,128)(2,1)S(1)} %pack.1.refs_5_), channel_id=1, source_target_pairs={{0,4},{4,0},{8,12},{12,8},{1,5},{5,1},{9,13},{13,9},{2,6},{6,2},{1... | collective-permute-start | bytes 196616 | tf_op jit(solution)/shard_map/ppermute | solution.py:418
  13.9 0.7 %copy-start.16 = (f32[128]{0:T(128)S(1)}, f32[128]{0:T(128)}, u32[]{:S(2)}) copy-start(f32[128]{0:T(128)} %param.19) | copy-start | bytes 1540
  27.1 11.1 %collective-permute-start.10 = (bf16[64,512]{1,0:T(8,128)(2,1)S(1)}, bf16[64,512]{1,0:T(8,128)(2,1)S(1)}, u32[]{:S(2)}, u32[]{:S(2)}) collective-permute-start(bf16[64,512]{1,0:T(8,128)(2,1)S(1)} %collective-permute-done.9.refs_1_), channel_id=1, source_target_pairs={{0,4},{4,0},{8,12},{12,8},{1,5},{5,1},{9,13},{13,9},{2,6},{6,2},{1... | collective-permute-start | bytes 196616 | tf_op jit(solution)/shard_map/ppermute | solution.py:418
  27.4 2.0 %copy-start.3 = (bf16[1,32,4096]{2,1,0:T(8,128)(2,1)S(1)}, bf16[1,32,4096]{2,1,0:T(8,128)(2,1)}, u32[]{:S(2)}) copy-start(bf16[1,32,4096]{2,1,0:T(8,128)(2,1)} %refs_0_.11) | copy-start | bytes 786436
  27.4 2.0 %copy-start.11 = (bf16[1,32,4,256]{3,2,1,0:T(4,128)(2,1)S(1)}, bf16[1,32,4,256]{3,2,1,0:T(4,128)(2,1)}, u32[]{:S(2)}) copy-start(bf16[1,32,4,256]{3,2,1,0:T(4,128)(2,1)} %refs_1_.6) | copy-start | bytes 196612
  27.4 2.0 %copy-start.12 = (f32[1,32,64]{2,1,0:T(8,128)S(1)}, f32[1,32,64]{2,1,0:T(8,128)}, u32[]{:S(2)}) copy-start(f32[1,32,64]{2,1,0:T(8,128)} %refs_3_.2) | copy-start | bytes 24580
  27.9 10.5 %collective-permute-start.6 = (bf16[272,256]{1,0:T(8,128)(2,1)S(1)}, bf16[272,256]{1,0:T(8,128)(2,1)S(1)}, u32[]{:S(2)}, u32[]{:S(2)}) collective-permute-start(bf16[272,256]{1,0:T(8,128)(2,1)S(1)} %get-tuple-element.60), channel_id=1, source_target_pairs={{0,12},{4,8},{8,4},{12,0},{1,13},{5,9},{9,5},{13,1},{2,14},{6,10},... | collective-permute-start | bytes 417800 | tf_op jit(solution)/shard_map/ppermute | solution.py:421
  31.5 15.0 %collective-permute-start.12 = (bf16[256,256]{1,0:T(8,128)(2,1)S(1)}, bf16[256,256]{1,0:T(8,128)(2,1)S(1)}, u32[]{:S(2)}, u32[]{:S(2)}) collective-permute-start(bf16[256,256]{1,0:T(8,128)(2,1)S(1)} %get-tuple-element.72), channel_id=1, source_target_pairs={{0,12},{4,8},{8,4},{12,0},{1,13},{5,9},{9,5},{13,1},{2,14},{6,10},... | collective-permute-start | bytes 393224 | tf_op jit(solution)/shard_map/ppermute | solution.py:421
  34.3 15.0 %collective-permute-start.14 = (bf16[256,256]{1,0:T(8,128)(2,1)S(1)}, bf16[256,256]{1,0:T(8,128)(2,1)S(1)}, u32[]{:S(2)}, u32[]{:S(2)}) collective-permute-start(bf16[256,256]{1,0:T(8,128)(2,1)S(1)} %get-tuple-element.75), channel_id=1, source_target_pairs={{0,12},{4,8},{8,4},{12,0},{1,13},{5,9},{9,5},{13,1},{2,14},{6,10},... | collective-permute-start | bytes 393224 | tf_op jit(solution)/shard_map/ppermute | solution.py:421
  35.8 15.8 %collective-permute-start.4 = (bf16[256,256]{1,0:T(8,128)(2,1)S(1)}, bf16[256,256]{1,0:T(8,128)(2,1)S(1)}, u32[]{:S(2)}, u32[]{:S(2)}) collective-permute-start(bf16[256,256]{1,0:T(8,128)(2,1)S(1)} %get-tuple-element.59), channel_id=1, source_target_pairs={{0,12},{4,8},{8,4},{12,0},{1,13},{5,9},{9,5},{13,1},{2,14},{6,10},... | collective-permute-start | bytes 393224 | tf_op jit(solution)/shard_map/ppermute | solution.py:421
  38.2 15.5 %copy-start.7 = (bf16[128,2,128]{2,1,0:T(2,128)(2,1)S(1)}, bf16[128,2,128]{2,1,0:T(2,128)(2,1)}, u32[]{:S(2)}) copy-start(bf16[128,2,128]{2,1,0:T(2,128)(2,1)} %refs_5_.1) | copy-start | bytes 196612
  38.2 15.5 %copy-start.10 = (bf16[1,32,16,128]{3,2,1,0:T(8,128)(2,1)S(1)}, bf16[1,32,16,128]{3,2,1,0:T(8,128)(2,1)}, u32[]{:S(2)}) copy-start(bf16[1,32,16,128]{3,2,1,0:T(8,128)(2,1)} %refs_1_.7) | copy-start | bytes 393220
  38.2 15.5 %copy-start.13 = (bf16[1,32,2,128]{3,2,1,0:T(2,128)(2,1)S(1)}, bf16[1,32,2,128]{3,2,1,0:T(2,128)(2,1)}, u32[]{:S(2)}) copy-start(bf16[1,32,2,128]{3,2,1,0:T(2,128)(2,1)} %refs_2_.5) | copy-start | bytes 49156
  38.2 15.5 %copy-start.14 = (bf16[1,32,2,128]{3,2,1,0:T(2,128)(2,1)S(1)}, bf16[1,32,2,128]{3,2,1,0:T(2,128)(2,1)}, u32[]{:S(2)}) copy-start(bf16[1,32,2,128]{3,2,1,0:T(2,128)(2,1)} %refs_3_.3) | copy-start | bytes 49156
  38.2 15.5 %collective-permute-start.11 = (bf16[192,512]{1,0:T(8,128)(2,1)S(1)}, bf16[192,512]{1,0:T(8,128)(2,1)S(1)}, u32[]{:S(2)}, u32[]{:S(2)}) collective-permute-start(bf16[192,512]{1,0:T(8,128)(2,1)S(1)} %collect.1.refs_6_), channel_id=1, source_target_pairs={{0,1},{1,0},{2,3},{3,2},{4,5},{5,4},{6,7},{7,6},{8,9},{9,8},{10,11... | collective-permute-start | bytes 589832 | tf_op jit(solution)/shard_map/ppermute | solution.py:415
  38.3 17.3 %collective-permute-start.7 = (bf16[272,256]{1,0:T(8,128)(2,1)S(1)}, bf16[272,256]{1,0:T(8,128)(2,1)S(1)}, u32[]{:S(2)}, u32[]{:S(2)}) collective-permute-start(bf16[272,256]{1,0:T(8,128)(2,1)S(1)} %collective-permute-done.6.refs_0_.refs_3_), channel_id=1, source_target_pairs={{0,4},{4,0},{8,12},{12,8},{1,5},{5,1},{9,13},{13,9},{2,6},{6,2},{1... | collective-permute-start | bytes 417800 | tf_op jit(solution)/shard_map/ppermute | solution.py:418
  46.5 11.1 %collective-permute-start.13 = (bf16[256,256]{1,0:T(8,128)(2,1)S(1)}, bf16[256,256]{1,0:T(8,128)(2,1)S(1)}, u32[]{:S(2)}, u32[]{:S(2)}) collective-permute-start(bf16[256,256]{1,0:T(8,128)(2,1)S(1)} %collective-permute-done.12.refs_0_), channel_id=1, source_target_pairs={{0,4},{4,0},{8,12},{12,8},{1,5},{5,1},{9,13},{13,9},{2,6},{6,2},{1... | collective-permute-start | bytes 393224 | tf_op jit(solution)/shard_map/ppermute | solution.py:418
  49.3 8.7 %collective-permute-start.15 = (bf16[256,256]{1,0:T(8,128)(2,1)S(1)}, bf16[256,256]{1,0:T(8,128)(2,1)S(1)}, u32[]{:S(2)}, u32[]{:S(2)}) collective-permute-start(bf16[256,256]{1,0:T(8,128)(2,1)S(1)} %collective-permute-done.14.refs_0_), channel_id=1, source_target_pairs={{0,4},{4,0},{8,12},{12,8},{1,5},{5,1},{9,13},{13,9},{2,6},{6,2},{1... | collective-permute-start | bytes 393224 | tf_op jit(solution)/shard_map/ppermute | solution.py:418
  51.6 6.7 %collective-permute-start.5 = (bf16[256,256]{1,0:T(8,128)(2,1)S(1)}, bf16[256,256]{1,0:T(8,128)(2,1)S(1)}, u32[]{:S(2)}, u32[]{:S(2)}) collective-permute-start(bf16[256,256]{1,0:T(8,128)(2,1)S(1)} %collective-permute-done.4.refs_0_), channel_id=1, source_target_pairs={{0,4},{4,0},{8,12},{12,8},{1,5},{5,1},{9,13},{13,9},{2,6},{6,2},{1... | collective-permute-start | bytes 393224 | tf_op jit(solution)/shard_map/ppermute | solution.py:418
  55.7 0.9 %copy-start.2 = (bf16[1,32,16,128]{3,2,1,0:T(8,128)(2,1)S(1)}, bf16[1,32,16,128]{3,2,1,0:T(8,128)(2,1)}, u32[]{:S(2)}) copy-start(bf16[1,32,16,128]{3,2,1,0:T(8,128)(2,1)} %attend.1.refs_11_) | copy-start | bytes 393220
  59.5 1.3 %collective-permute-start.16 = (bf16[32,2048]{1,0:T(8,128)(2,1)S(1)}, bf16[32,2048]{1,0:T(8,128)(2,1)S(1)}, u32[]{:S(2)}, u32[]{:S(2)}) collective-permute-start(bf16[32,2048]{1,0:T(8,128)(2,1)S(1)} %get-tuple-element.84), channel_id=1, source_target_pairs={{0,1},{1,0},{2,3},{3,2},{4,5},{5,4},{6,7},{7,6},{8,9},{9,8},{10,11... | collective-permute-start | bytes 393224 | tf_op jit(solution)/shard_map/ppermute | solution.py:415

commit v3 on v2

--- a/solution.py
+++ b/solution.py
@@ -10,6 +10,8 @@
 EPSILON = 1e-06
 NEG = -1e30
 CHUNKS = 4
+SECOND_COST = 1.0
+FIRST_COST = 2.0
 F32 = jnp.float32
 BF16 = jnp.bfloat16
 
@@ -66,12 +68,7 @@
 
 def payload_plan(groups):
     of = [q * groups // CHUNKS for q in range(CHUNKS)]
-    plan, seen = [], set()
-    for chunks in ([0], [1], list(range(2, CHUNKS))):
-        fresh = [g for g in sorted({of[q] for q in chunks}) if g not in seen]
-        seen |= set(fresh)
-        plan.append((chunks, fresh))
-    return plan
+    return [([g] if g not in of[:q] else []) for q, g in enumerate(of)]
 
 
 def totals_to_lines(total):
@@ -89,54 +86,82 @@
     return spread(jnp.broadcast_to(total, (8, total.shape[1])), width)
 
 
-def local_kernel(x_ref, b_ref, decay_t_ref, b2_ref, cum_ref, total_ref, *outs):
-    local_refs, load_refs = outs[:CHUNKS], outs[CHUNKS:]
+def pack(k_ref, v_ref):
+    rep = lax.axis_index("rep")
+    kv = jnp.where(rep == 0, k_ref[...].astype(F32), v_ref[...].astype(F32))
+    return jnp.concatenate([kv[:, j, :] for j in range(kv.shape[1])], axis=1).astype(BF16)
+
+
+def head_kernel(x_any, b_any, decay_t_any, cum_ref, total_ref, load_ref, x_ref, b_ref, decay_t_ref, sems):
     tokens, groups, state = b_ref.shape
     heads = decay_t_ref.shape[0]
-    width = x_ref.shape[1] // heads
+    cols = x_ref.shape[1]
+    width = cols * CHUNKS // heads
+    copies = [
+        pltpu.make_async_copy(source, target, sems.at[i])
+        for i, (source, target) in enumerate(
+            ((decay_t_any, decay_t_ref), (x_any.at[:, pl.ds(0, cols)], x_ref), (b_any, b_ref))
+        )
+    ]
+    for copy in copies:
+        copy.start()
+    copies[0].wait()
     lower = (iota((tokens, tokens), 0) >= iota((tokens, tokens), 1)).astype(F32)
     cum = exact_nt(lower, decay_t_ref[...])
     cum_ref[...] = cum
     last = cum[tokens - 1 : tokens, :]
-    weights = spread(jnp.exp(last - cum), width)
+    total = jnp.exp(-last)
+    total_ref[...] = jnp.broadcast_to(total, (8, heads))
+    load_ref[tokens:, :] = jnp.zeros((16, load_ref.shape[1]), BF16)
+    load_ref[tokens:, :heads] = totals_to_lines(total)
+    weights = spread(jnp.exp(last - cum), width, 0, heads // CHUNKS)
+    copies[1].wait()
+    load_ref[:tokens, :cols] = (x_ref[...].astype(F32) * weights).astype(BF16)
+    copies[2].wait()
+    load_ref[:tokens, cols:] = b_ref[...].astype(F32)[:, 0, :].astype(BF16)
+
+
+def local_kernel(x_ref, b_ref, cum_ref, first_ref, k_ref, v_ref, b2_ref, kv_ref, *outs):
+    local_refs, load_refs = outs[:CHUNKS], outs[CHUNKS:]
+    tokens, groups, state = b_ref.shape
+    heads = cum_ref.shape[1]
+    width = x_ref.shape[1] // heads
+    cols = x_ref.shape[1] // CHUNKS
+    cum = cum_ref[...]
+    weights = spread(jnp.exp(cum[tokens - 1 : tokens, :] - cum), width)
     b = b_ref[...].astype(F32)
     for g in range(groups):
         b2_ref[:, g * state : (g + 1) * state] = b[:, g, :].astype(BF16)
-    cols = x_ref.shape[1] // CHUNKS
-    for (chunks, fresh), load in zip(payload_plan(groups), load_refs):
-        for i, q in enumerate(chunks):
-            g = q * groups // CHUNKS
-            at = slice(q * cols, (q + 1) * cols)
+    kv = pack(k_ref, v_ref)
+    kv_ref[...] = kv
+    for q, fresh in enumerate(payload_plan(groups)):
+        g = q * groups // CHUNKS
+        at = slice(q * cols, (q + 1) * cols)
+        if q == 0:
+            weighted = first_ref[:tokens, :cols]
+        else:
             weighted = (x_ref[:, at].astype(F32) * weights[:, at]).astype(BF16)
-            load[:tokens, i * cols : (i + 1) * cols] = weighted
-            local_refs[q][...] = mm_tn(b2_ref[:, g * state : (g + 1) * state], weighted)
-        for i, g in enumerate(fresh):
-            at = len(chunks) * cols + i * state
-            load[:tokens, at : at + state] = b2_ref[:, g * state : (g + 1) * state]
-    load = load_refs[0]
-    load[tokens:, :] = jnp.zeros((16, load.shape[1]), BF16)
-    total = jnp.exp(-last)
-    total_ref[...] = jnp.broadcast_to(total, (8, heads))
-    load[tokens:, :heads] = totals_to_lines(total)
-
-
-def pack_kernel(k_ref, v_ref, out_ref):
-    rep = lax.axis_index("rep")
-    tokens, heads, dim = k_ref.shape
-    kv = jnp.where(rep == 0, k_ref[...].astype(F32), v_ref[...].astype(F32))
-    rows, wide = out_ref.shape
-    for i in range(wide // (heads * dim)):
-        for j in range(heads):
-            at = (i * heads + j) * dim
-            out_ref[:, at : at + dim] = kv[i * rows : (i + 1) * rows, j, :].astype(BF16)
-
-
-def collect_kernel(*refs):
-    out_ref = refs[-1]
+            load = load_refs[q - 1]
+            load[:, :cols] = weighted
+            if fresh:
+                load[:, cols : cols + state] = b2_ref[:, g * state : (g + 1) * state]
+            if q == 1:
+                load[:, load.shape[1] - kv.shape[1] :] = kv
+        local_refs[q][...] = mm_tn(b2_ref[:, g * state : (g + 1) * state], weighted)
+
+
+def collect_kernel(*refs, inner):
+    refs, out_ref = list(refs[:-1]), refs[-1]
+    place = lax.axis_index("seq")
+    pieces = [ref[...] for ref in refs]
+    if inner:
+        second = pieces.pop()
+        pieces[-1] = jnp.where((place == 1) | (place == 2), pieces[-1], second)
+        pieces[0] = pieces[0][pieces[0].shape[0] // 2 :]
     at = 0
-    for ref in refs[:-1]:
-        out_ref[at : at + ref.shape[0], :] = ref[...]
-        at += ref.shape[0]
+    for piece in pieces:
+        out_ref[at : at + piece.shape[0], :] = piece
+        at += piece.shape[0]
 
 
 def half_of(place, level):
@@ -144,7 +169,7 @@
     return jnp.where(lax.rem(lax.div(place, 2**level), 2) == 0, 1 - odd, odd)
 
 
-def merge_kernel(*refs, level, last, chunks, cols, groups, heads, tokens, carry):
+def merge_kernel(*refs, level, last, chunks, cols, groups, heads, tokens, state):
     refs = list(refs)
 
     def take(count):
@@ -161,8 +186,7 @@
     if level == 0:
         for q in chunks:
             w_ref, b_ref = take(2)
-            at_w, at_b = carry[q]
-            others.append(mm_tn(b_ref[:tokens, at_b], w_ref[:tokens, at_w]))
+            others.append(mm_tn(b_ref[:tokens, cols : cols + state], w_ref[:tokens, :cols]))
     else:
         half = half_of(place, level)
         for q in chunks:
@@ -205,14 +229,13 @@
                 send = jnp.concatenate([send, lines], axis=0)
             outs += [joined, start, send]
         else:
-            c2_ref, mine_c_ref, base_ref, cum_ref = take(4)
-            state = own.shape[0]
+            cc_ref, base_ref, cum_ref = take(3)
             g = q * groups // CHUNKS
             here = slice(g * state, (g + 1) * state)
             fade = spread(jnp.exp(-cum_ref[...]), width, q * heads // CHUNKS, heads // CHUNKS)
-            carried = mm(c2_ref[:, here], start.astype(BF16))
+            carried = mm(cc_ref[:tokens, here], start.astype(BF16))
             outs.append((base_ref[:, at] + fade * carried).astype(BF16))
-            outs.append(mm(mine_c_ref[:, here], joined.astype(BF16)))
+            outs.append(mm(cc_ref[tokens:, here], joined.astype(BF16)))
     if last and CHUNKS - 1 in chunks:
         parts = take(2 * (CHUNKS - 1))
         out_parts = [ref[...] for ref in parts[: CHUNKS - 1]] + [outs[-2]]
@@ -230,27 +253,134 @@
             ref[...] = value
 
 
-def projections_kernel(mine_ref, other_ref, out_ref):
+def projections_kernel(c_ref, mine_ref, other_ref, out_ref):
     rep = lax.axis_index("rep")
-    steps, all_groups, state = mine_ref.shape[1:]
-    groups = all_groups // 2
+    tokens, groups, state = c_ref.shape
+    steps = mine_ref.shape[1]
     mine, other = mine_ref[0].astype(F32), other_ref[0].astype(F32)
     zero, one = jnp.where(rep == 0, mine, other), jnp.where(rep == 0, other, mine)
-    for i, c in enumerate((zero, one)):
-        for g in range(groups):
+    prefix = c_ref[...].astype(F32)
+    for g in range(groups):
+        at = slice(g * state, (g + 1) * state)
+        out_ref[:tokens, at] = prefix[:, g, :].astype(BF16)
+        for i, c in enumerate((zero, one)):
             part = jnp.where(rep == 0, c[:, g, :], c[:, groups + g, :])
-            out_ref[i * steps : (i + 1) * steps, g * state : (g + 1) * state] = part.astype(BF16)
-
-
-def intra_kernel(x_ref, b2_ref, c_ref, cum_ref, skip_ref, c2_ref, base_ref):
-    tokens, groups, state = c_ref.shape
-    heads = cum_ref.shape[1]
+            out_ref[tokens + i * steps : tokens + (i + 1) * steps, at] = part.astype(BF16)
+
+
+def first_kernel(*refs, q, cols, groups, heads, tokens, state):
+    refs = list(refs)
+    w_ref, b_ref, local_ref = refs[:3]
+    left = lax.axis_index("seq") < 2
+    width = cols * CHUNKS // heads
+    other = mm_tn(b_ref[:tokens, cols : cols + state], w_ref[:tokens, :cols])
+    if q == 0:
+        mine_ref, own_row_ref, near_row_ref, near_ref, other_ref, send_ref = refs[3:]
+        mine = mine_ref[:1, :]
+        near = lines_to_totals(w_ref[tokens:, :heads])
+        own_row, near_row = as_row(mine, width), as_row(near, width)
+        own_row_ref[...] = own_row
+        near_row_ref[...] = near_row
+        near_ref[...] = jnp.broadcast_to(near, (8, heads))
+        send_ref[state:, :] = jnp.zeros((16, cols), BF16)
+        send_ref[state:, :heads] = totals_to_lines(mine * near)
+    else:
+        own_row_ref, near_row_ref = refs[3:5]
+        refs = refs[5:]
+        if q == 1:
+            kv_ref, pair_ref = refs[0], refs.pop()
+            refs = refs[1:]
+            pair_ref[:tokens, :] = kv_ref[...]
+            pair_ref[tokens:, :] = w_ref[:, w_ref.shape[1] - kv_ref.shape[1] :]
+        other_ref, send_ref = refs
+        own_row, near_row = own_row_ref[...], near_row_ref[...]
+    at = slice(q * cols, (q + 1) * cols)
+    local = local_ref[...]
+    after = own_row[:1, at] * other + local
+    beyond = other + near_row[:1, at] * local
+    send_ref[:state, :] = jnp.where(left, after, beyond).astype(BF16)
+    other_ref[...] = other
+
+
+def second_kernel(*refs, q, cols, groups, heads, tokens, state):
+    refs = list(refs)
+    got_ref, other_ref, local_ref, own_row_ref, cc_ref, near_cc_ref = refs[:6]
+    place = lax.axis_index("seq")
+    left, inner = place < 2, (place == 1) | (place == 2)
+    width = cols * CHUNKS // heads
+    at = slice(q * cols, (q + 1) * cols)
+    g = q * groups // CHUNKS
+    here = slice(g * state, (g + 1) * state)
+    rows = cc_ref.shape[0]
+    if q == 0:
+        mine_ref, near_ref, later_row_ref, carried_ref, cand_ref, send_ref = refs[6:]
+        later = jnp.where(left, lines_to_totals(got_ref[state:, :heads]), near_ref[:1, :])
+        later_row = as_row(later, width)
+        later_row_ref[...] = later_row
+        send_ref[rows:, :] = jnp.zeros((16, cols), BF16)
+        send_ref[rows:, :heads] = totals_to_lines(later * mine_ref[:1, :])
+    else:
+        later_row_ref, carried_ref, cand_ref, send_ref = refs[6:]
+        later_row = later_row_ref[...]
+    got, other, local = got_ref[:state, :].astype(F32), other_ref[...], local_ref[...]
+    start, beyond = jnp.where(left, other, got), jnp.where(left, got, other)
+    start = jnp.where(inner, start, 0.0)
+    after = own_row_ref[:1, at] * start + local
+    lasting = later_row[:1, at]
+    state_out = jnp.where(left, beyond + lasting * local, after)
+    send_ref[:rows, :] = mm(near_cc_ref[:, here], state_out.astype(BF16)).astype(BF16)
+    final = jnp.where(inner, lasting * after + beyond, local)
+    carried_ref[...] = mm(cc_ref[:tokens, here], start.astype(BF16))
+    cand_ref[...] = mm(cc_ref[tokens:, here], final.astype(BF16))
+
+
+def third_kernel(*refs, q, cols, heads, tokens):
+    refs = list(refs)
+    got_ref, carried_ref, cand_ref, base_ref, cum_ref, own_row_ref = refs[:6]
+    place = lax.axis_index("seq")
+    width = cols * CHUNKS // heads
+    at = slice(q * cols, (q + 1) * cols)
+    rows = cand_ref.shape[0]
+    refs = refs[6:]
+    if q == 0:
+        later_row_ref = refs[0]
+        later_row = as_row(lines_to_totals(got_ref[tokens + rows :, :heads]), width)
+        later_row_ref[...] = later_row
+    else:
+        later_row = refs[0][...]
+    refs = refs[1:]
+    fade = spread(jnp.exp(-cum_ref[...]), width, q * heads // CHUNKS, heads // CHUNKS)
+    got = got_ref[: tokens + rows, :].astype(F32)
+    carried = jnp.where(place == 3, got[:tokens], carried_ref[...])
+    cand = cand_ref[...]
+    cand = jnp.where(
+        place == 3,
+        own_row_ref[:1, at] * got[tokens:] + cand,
+        jnp.where(place == 0, later_row[:1, at] * cand + got[tokens:], cand),
+    )
+    out = (base_ref[:, at] + fade * carried).astype(BF16)
+    if q < CHUNKS - 1:
+        out_ref, raw_ref = refs
+        out_ref[...] = out
+        raw_ref[...] = cand
+        return
+    outs, raws, (out_ref, keep_ref, give_ref) = refs[: CHUNKS - 1], refs[CHUNKS - 1 : 2 * CHUNKS - 2], refs[-3:]
+    rep = lax.axis_index("rep")
+    half = rows // 2
+    for i in range(CHUNKS):
+        at = slice(i * cols, (i + 1) * cols)
+        out_ref[:, at] = out if i == q else outs[i][...]
+        raw = cand if i == q else raws[i][...]
+        keep_ref[:, at] = jnp.where(rep == 0, raw[:half], raw[half:])
+        give_ref[:, at] = jnp.where(rep == 0, raw[half:], raw[:half]).astype(BF16)
+
+
+def intra_kernel(x_ref, b2_ref, c2_ref, cum_ref, skip_ref, base_ref, *, groups):
+    tokens, heads = cum_ref.shape
     width = x_ref.shape[1] // heads
+    state = c2_ref.shape[1] // groups
     per_group = heads // groups
     first = (lax.axis_index("head") * lax.axis_size("rep") + lax.axis_index("rep")) * heads
-    c = c_ref[...].astype(F32)
-    for g in range(groups):
-        c2_ref[:, g * state : (g + 1) * state] = c[:, g, :].astype(BF16)
     skip = spread(jnp.broadcast_to(skip_ref[...], (8, skip_ref.shape[1])), width, first, heads)[:1]
     cum = cum_ref[...]
     cum_t = cum.T
@@ -260,7 +390,7 @@
     lane = iota((tokens, pair), 1)
     for g in range(groups):
         here = slice(g * state, (g + 1) * state)
-        gram = mm_nt(c2_ref[:, here], b2_ref[:, here])
+        gram = mm_nt(c2_ref[:tokens, here], b2_ref[:, here])
         for h in range(g * per_group, (g + 1) * per_group, 2):
             mixing = []
             for i in (h, h + 1):
@@ -317,7 +447,6 @@
     rows = steps * per_kv
     mine, other = mine_ref[...], other_ref[...]
     keys, values = jnp.where(rep == 0, mine, other), jnp.where(rep == 0, other, mine)
-    parts = mine.shape[1] // (kv_heads * dim)
     q = q_ref[0].astype(F32)
     own_k = own_k_ref[0].astype(F32)
     own_v = own_v_ref[0].astype(F32)
@@ -332,8 +461,7 @@
         query = q[:, j * per_kv : (j + 1) * per_kv, :].reshape(rows, dim).astype(BF16)
 
         def gather(far, block):
-            pieces = [far[:, (i * kv_heads + j) * dim : (i * kv_heads + j + 1) * dim] for i in range(parts)]
-            return jnp.concatenate([*pieces, block[:, j, :].astype(BF16)], axis=0)
+            return jnp.concatenate([far[:, j * dim : (j + 1) * dim], block[:, j, :].astype(BF16)], axis=0)
 
         far = mm_nt(query, gather(keys, block_k)) * scale
         near = jnp.where(visible, mm_nt(query, own_k[:, j, :].astype(BF16)) * scale, NEG)
@@ -361,12 +489,14 @@
         out_ref[0, :, at] = jnp.where(live, result, 0.0).astype(BF16)
 
 
-def call(kernel, name, outs, *args, scalars=0, after=()):
+def call(kernel, name, outs, *args, scalars=0, after=(), cost=0.0, scratch=(), limit=32):
     shapes = [jax.ShapeDtypeStruct(shape, dtype) for shape, dtype in outs]
-    moved = sum(a.size * a.dtype.itemsize for a in args) + sum(s.size * s.dtype.itemsize for s in shapes)
     vmem = pl.BlockSpec(memory_space=pltpu.VMEM)
     smem = pl.BlockSpec(memory_space=pltpu.SMEM)
     count, rest = len(args), len(args) + len(after)
+    out_spec = vmem
+    if scratch:
+        vmem = pl.BlockSpec(memory_space=pl.ANY)
 
     def body(*refs):
         kernel(*refs[:count], *refs[rest:])
@@ -375,9 +505,10 @@
         body,
         out_shape=shapes,
         in_specs=[smem] * scalars + [vmem] * (count - scalars) + [pl.BlockSpec(memory_space=pl.ANY)] * len(after),
-        out_specs=[vmem] * len(shapes),
-        compiler_params=pltpu.CompilerParams(vmem_limit_bytes=32 * 2**20),
-        cost_estimate=pl.CostEstimate(flops=10**8, bytes_accessed=int(moved), transcendentals=0),
+        out_specs=[out_spec] * len(shapes),
+        scratch_shapes=list(scratch),
+        compiler_params=pltpu.CompilerParams(vmem_limit_bytes=limit * 2**20),
+        cost_estimate=pl.CostEstimate(flops=int(cost * 10**9), bytes_accessed=0, transcendentals=0),
         name=name,
     )(*args, *after)
 
@@ -420,165 +551,278 @@
     def to_mirror(array, level):
         return lax.ppermute(array, "seq", [(i, i ^ (2 ** (level + 1) - 1)) for i in range(size)])
 
+    def between_inner(array):
+        far = {1: 2, 2: 1}
+        pairs = [(2 * i + r, 2 * far[i] + r if i in far else 2 * i + 1 - r) for i in range(size) for r in range(2)]
+        return lax.ppermute(array, ("seq", "rep"), pairs)
+
     other_c = to_core(cand_c)
-    b2, cum, total, *parts = call(
+    kv_shape = (tokens, prefix_key_rows.shape[1] * prefix_key_rows.shape[2])
+    cum, total, load = call(
+        head_kernel,
+        "head",
+        [((tokens, heads), F32), ((8, heads), F32), ((tokens + 16, cols + state), BF16)],
+        prefix_x,
+        prefix_b,
+        prefix_decay.T,
+        scratch=[
+            pltpu.VMEM((tokens, cols), BF16),
+            pltpu.VMEM(prefix_b.shape, BF16),
+            pltpu.VMEM((heads, tokens), F32),
+            pltpu.SemaphoreType.DMA((3,)),
+        ],
+        limit=60,
+    )
+    b2, kv, *parts = call(
         local_kernel,
         "local_state",
-        [((tokens, groups * state), BF16), ((tokens, heads), F32), ((8, heads), F32)]
+        [((tokens, groups * state), BF16), (kv_shape, BF16)]
         + [((state, cols), F32)] * CHUNKS
         + [
-            ((tokens + (16 if p == 0 else 0), len(chunks) * cols + len(fresh) * state), BF16)
-            for p, (chunks, fresh) in enumerate(plan)
+            ((tokens, cols + len(fresh) * state + (kv_shape[1] if q == 1 else 0)), BF16)
+            for q, fresh in enumerate(plan)
+            if q
         ],
         prefix_x,
         prefix_b,
-        prefix_decay.T,
+        cum,
+        load,
+        prefix_key_rows,
+        prefix_values,
     )
-    local, loads = parts[:CHUNKS], parts[CHUNKS:]
+    local, loads = parts[:CHUNKS], [load] + parts[CHUNKS:]
     got = [to_neighbour(a) for a in loads]
-    kv_rows = prefix_key_rows.size // (groups * state)
-    (kv,) = call(
-        pack_kernel, "pack", [((kv_rows, groups * state), BF16)], prefix_key_rows, prefix_values, after=(loads[0],)
-    )
-    halves = [kv, to_neighbour(kv)]
-    for level in range(1, levels):
-        mirrored = to_mirror(halves[0], level)
-        halves = [halves[0], halves[1], mirrored, to_neighbour(mirrored)]
-        if level < levels - 1:
-            halves = [jnp.concatenate([halves[0], halves[2]]), jnp.concatenate([halves[1], halves[3]])]
-    c2, base = call(
-        intra_kernel,
-        "intra",
-        [((tokens, groups * state), BF16), ((tokens, wide), F32)],
-        prefix_x,
-        b2,
+    first_of = {g: q for q, fresh in enumerate(plan) for g in fresh}
+    (cc,) = call(
+        projections_kernel,
+        "projections",
+        [((tokens + 2 * steps, groups * state), BF16)],
         prefix_c,
-        cum,
-        skip,
+        cand_c,
+        other_c,
         after=(kv,),
     )
-    (both_c,) = call(
-        projections_kernel, "projections", [((2 * steps, groups * state), BF16)], cand_c, other_c, after=(base,)
-    )
-    where = {}
-    spot = {}
-    for p, (chunks, fresh) in enumerate(plan):
-        for i, g in enumerate(fresh):
-            at = len(chunks) * cols + i * state
-            where[g] = (p, slice(at, at + state))
-        for i, q in enumerate(chunks):
-            spot[q] = (p, slice(i * cols, (i + 1) * cols))
-    mark = both_c
-    own, start = dict(enumerate(local)), {}
-    before = None
-    near, far = {}, {}
-    cand_base = cand_attn = None
-    out_parts, raws = [], []
-
-    def attend(mark):
-        (mine,) = call(
-            collect_kernel,
-            "collect",
-            [((kv_rows * (size - 1), groups * state), BF16)],
-            *halves[1:],
+
+    def intra(mark):
+        return call(
+            functools.partial(intra_kernel, groups=groups),
+            "intra",
+            [((tokens, wide), F32)],
+            prefix_x,
+            b2,
+            cc,
+            cum,
+            skip,
+            after=(mark,),
+        )[0]
+
+    def candidates(mark):
+        return call(
+            cand_kernel,
+            "candidates",
+            [((steps, cand_wide), F32), ((steps, cand_wide), F32)],
+            cand_x,
+            cand_b,
+            cand_c,
+            cand_decay,
+            skip,
             after=(mark,),
         )
-        return call(
-            attend_kernel,
-            "attend",
-            [(cand_queries.shape, BF16)],
-            cand_length,
-            cand_queries,
-            cand_keys,
-            cand_values,
-            prefix_key_rows,
-            prefix_values,
-            mine,
-            to_core(mine),
-            scalars=1,
-        )[0]
-
-    for level in range(levels):
-        last = level == levels - 1
-        rows = None
-        for batch in [chunks for chunks, _ in plan] if level == 0 else [[q] for q in range(CHUNKS)]:
-            args, outs = [], []
-            if level == 0:
-                for q in batch:
-                    args += [got[spot[q][0]], got[where[q * groups // CHUNKS][0]]]
-                lines = got[0]
-            else:
-                for q in batch:
-                    args += [near[q], far[q]]
-                lines = near.get(0)
-            if 0 in batch:
-                args += [total, lines] + ([] if level == 0 else [before])
-                outs += [((8, wide), F32)] * 2 + [((8, heads), F32)] * 2
-            else:
-                args += rows
-            for q in batch:
+
+    def attend(mark, pieces, inner):
+        (mine,) = call(
+            functools.partial(collect_kernel, inner=inner),
+            "collect",
+            [((tokens * (size - 1), kv_shape[1]), BF16)],
+            *pieces,
+            after=(mark,),
+        )
+        theirs = to_core(mine)
+
+        def finish(mark):
+            return call(
+                attend_kernel,
+                "attend",
+                [(cand_queries.shape, BF16)],
+                cand_length,
+                cand_queries,
+                cand_keys,
+                cand_values,
+                prefix_key_rows,
+                prefix_values,
+                mine,
+                theirs,
+                scalars=1,
+                after=(mark,),
+            )[0]
+
+        return mine, finish
+
+    shared = dict(cols=cols, heads=heads, tokens=tokens)
+    if size == 4:
+        near_cc = to_neighbour(cc)
+        other, middle, carried, cands, outer, outs, raws = {}, {}, {}, {}, {}, [], []
+        rows = {}
+
+        def first(q, mark):
+            extra = [((8, wide), F32), ((8, wide), F32), ((8, heads), F32)] if q == 0 else []
+            results = call(
+                functools.partial(first_kernel, q=q, groups=groups, state=state, **shared),
+                "first",
+                extra
+                + [((state, cols), F32), ((state + (16 if q == 0 else 0), cols), BF16)]
+                + ([((2 * tokens, kv_shape[1]), BF16)] if q == 1 else []),
+                got[q],
+                got[first_of[q * groups // CHUNKS]],
+                local[q],
+                *([total] if q == 0 else [rows["own"], rows["near"]]),
+                *([kv] if q == 1 else []),
+                after=(mark,),
+                cost=FIRST_COST if q == 1 else 0.0,
+            )
+            if q == 0:
+                rows["own"], rows["near"], rows["near_total"], *results = results
+            other[q] = results[0]
+            middle[q] = between_inner(results[1])
+            if q == 1:
+                rows["kv"] = results[2]
+            return results[0]
+
+        def second(q, mark):
+            results = call(
+                functools.partial(second_kernel, q=q, groups=groups, state=state, **shared),
+                "second",
+                ([((8, wide), F32)] if q == 0 else [])
+                + [
+                    ((tokens, cols), F32),
+                    ((2 * steps, cols), F32),
+                    ((tokens + 2 * steps + (16 if q == 0 else 0), cols), BF16),
+                ],
+                middle[q],
+                other[q],
+                local[q],
+                rows["own"],
+                cc,
+                near_cc,
+                *([total, rows["near_total"]] if q == 0 else [rows["later"]]),
+                after=(mark,),
+                cost=SECOND_COST,
+            )
+            if q == 0:
+                rows["later"], *results = results
+            carried[q], cands[q] = results[:2]
+            outer[q] = to_neighbour(results[2])
+            return results[0]
+
+        def third(q, mark):
+            final = q == CHUNKS - 1
+            results = call(
+                functools.partial(third_kernel, q=q, **shared),
+                "third",
+                [((tokens, wide), BF16), ((steps, wide), F32), ((steps, wide), BF16)]
+                if final
+                else ([((8, wide), F32)] if q == 0 else []) + [((tokens, cols), BF16), ((2 * steps, cols), F32)],
+                outer[q],
+                carried[q],
+                cands[q],
+                base,
+                cum,
+                rows["own"],
+                *([] if q == 0 else [rows["outer"]]),
+                *(outs + raws if final else []),
+                after=(mark,),
+                cost=0.3,
+            )
+            if final:
+                return results
+            if q == 0:
+                rows["outer"], *results = results
+            outs.append(results[0])
+            raws.append(results[1])
+            return results[0]
+
+        mark = first(0, cc)
+        mark = first(1, mark)
+        far_kv = between_inner(rows["kv"])
+        outer_kv = to_neighbour(far_kv)
+        mark = base = intra(mark)
+        mark = first(2, mark)
+        cand_base, cand_fade = candidates(mark)
+        mark = second(0, cand_base)
+        mark = first(3, mark)
+        mark = second(1, mark)
+        mark = third(0, mark)
+        mark, finish_attend = attend(mark, [rows["kv"], far_kv, outer_kv], True)
+        mark = second(2, mark)
+        mark = cand_attn = finish_attend(mark)
+        mark = third(1, mark)
+        mark = second(3, mark)
+        mark = third(2, mark)
+        results = third(3, mark)
+        prefix_out, keep, give = results
+    else:
+        halves = [kv, got[1][:, -kv_shape[1] :]]
+        for level in range(1, levels):
+            mirrored = to_mirror(halves[0], level)
+            halves = [halves[0], halves[1], mirrored, to_neighbour(mirrored)]
+            if level < levels - 1:
+                halves = [jnp.concatenate([halves[0], halves[2]]), jnp.concatenate([halves[1], halves[3]])]
+        mark = base = intra(cc)
+        own, start = dict(enumerate(local)), {}
+        before = None
+        near, far = {}, {}
+        outs, raws = [], []
+        for level in range(levels):
+            last = level == levels - 1
+            rows = None
+            for q in range(CHUNKS):
+                final = last and q == CHUNKS - 1
+                if level == 0:
+                    args, lines = [got[q], got[first_of[q * groups // CHUNKS]]], got[0]
+                else:
+                    args, lines = [near[q], far[q]], near[0]
+                shapes = []
+                if q == 0:
+                    args += [total, lines] + ([] if level == 0 else [before])
+                    shapes += [((8, wide), F32)] * 2 + [((8, heads), F32)] * 2
+                else:
+                    args += rows
                 args += [own[q]] + ([] if level == 0 else [start[q]])
-                if last:
-                    args += [c2, both_c, base, cum]
-                    outs += [((tokens, cols), BF16), ((2 * steps, cols), F32)]
+                if final:
+                    args += [cc, base, cum] + outs + raws
+                    shapes = [((tokens, wide), BF16), ((steps, wide), F32), ((steps, wide), BF16)]
+                elif last:
+                    args += [cc, base, cum]
+                    shapes += [((tokens, cols), BF16), ((2 * steps, cols), F32)]
                 else:
-                    outs += [((state, cols), F32)] * 2
-                    outs += [((state + (16 if q == 0 else 0), cols // 2), BF16)]
-            if last and batch == [CHUNKS - 1]:
-                args += out_parts + raws
-                outs = [((tokens, wide), BF16), ((steps, wide), F32), ((steps, wide), BF16)]
-            results = list(
-                call(
+                    shapes += [((state, cols), F32)] * 2 + [((state + (16 if q == 0 else 0), cols // 2), BF16)]
+                results = call(
                     functools.partial(
-                        merge_kernel,
-                        level=level,
-                        last=last,
-                        chunks=batch,
-                        cols=cols,
-                        groups=groups,
-                        heads=heads,
-                        tokens=tokens,
-                        carry={q: (spot[q][1], where[q * groups // CHUNKS][1]) for q in batch},
+                        merge_kernel, level=level, last=last, chunks=[q], groups=groups, state=state, **shared
                     ),
                     "merge",
-                    outs,
+                    shapes,
                     *args,
                     after=(mark,),
                 )
-            )
-            mark = results[0]
-            if last and batch == [CHUNKS - 1]:
-                prefix_out, keep, give = results
-                continue
-            if 0 in batch:
-                rows, results = results[:2], results[2:]
-                total, before = results[:2]
-                results = results[2:]
-            for q in batch:
+                mark = results[0]
+                if final:
+                    prefix_out, keep, give = results
+                    continue
+                if q == 0:
+                    rows, (total, before) = list(results[:2]), results[2:4]
                 if last:
-                    out_parts.append(results.pop(0))
-                    raws.append(results.pop(0))
+                    outs.append(results[-2])
+                    raws.append(results[-1])
                 else:
-                    own[q], start[q], sent = results[:3]
-                    results = results[3:]
-                    near[q] = to_mirror(sent, level + 1)
+                    own[q], start[q] = results[-3], results[-2]
+                    near[q] = to_mirror(results[-1], level + 1)
                     far[q] = to_neighbour(near[q])
-            if level == 0 and 0 in batch:
-                cand_base, cand_fade = call(
-                    cand_kernel,
-                    "candidates",
-                    [((steps, cand_wide), F32), ((steps, cand_wide), F32)],
-                    cand_x,
-                    cand_b,
-                    cand_c,
-                    cand_decay,
-                    skip,
-                    after=(mark,),
-                )
-                mark = cand_base
-        if level == 0:
-            cand_attn = attend(mark)
-            mark = cand_attn
+            if level == 0:
+                cand_base, cand_fade = candidates(mark)
+                pieces = ([halves[0][tokens:]] if levels > 2 else []) + halves[1:]
+                mark, finish_attend = attend(cand_base, pieces, False)
+                mark = cand_attn = finish_attend(mark)
     (cand_ssm,) = call(
         close_kernel,
         "close",

time: 62 us -> 55.8 us (0.90)
  starting transfers between devices: 30.9 us -> 20.3 us
  Pallas kernels: 11.5 us -> 14.3 us
  waiting for transfers between devices: 12.7 us -> 13.5 us
  local copies, waits for them, and re-layouts: 5.1 us -> 5.84 us
    ppermute x5, waiting for transfers between devices: 11.3 us -> 0.01 us  [between_inner(): return lax.ppermute(array, ('seq', 'rep'), pairs)]
    ppermute x9 -> x10, waiting for transfers between devices: 0.02 us -> 10.9 us  [to_neighbour(): return lax.ppermute(array, 'seq', [(i, i ^ 1) for i in range(size)])]
    ppermute x5, starting transfers between devices: 10.4 us -> 0.44 us  [between_inner(): return lax.ppermute(array, ('seq', 'rep'), pairs)]
    pallas_call x15 -> x20, Pallas kernels: 11.5 us -> 14.3 us  [call(): pl.pallas_call(body, out_shape=shapes, in_specs=[smem] * scalars + [vmem]...]
    ppermute x3, waiting for transfers between devices: 1.35 us -> 2.59 us  [to_core(): return lax.ppermute(array, 'rep', [(0, 1), (1, 0)])]
    ppermute x9 -> x10, starting transfers between devices: 20.5 us -> 19.7 us  [to_neighbour(): return lax.ppermute(array, 'seq', [(i, i ^ 1) for i in range(size)])]
    unnamed x34 -> x40, local copies, waits for them, and re-layouts: 5.1 us -> 5.84 us
  transfers between devices with their start and end apart: 17 -> 18, of which waited for: 2 -> 9; matrix products, arithmetic and copies ran while one was open for 0% -> 0% of each run, Pallas kernels for 13% -> 18%
where the time goes in v3:
time: 55.8 us; the launch traced here: 55.5 us
  starting transfers between devices  20.3 us (36%)
  Pallas kernels  14.3 us (26%)
  waiting for transfers between devices  13.5 us (24%)
  local copies, waits for them, and re-layouts  5.84 us (10%)
  between operations  1.59 us (3%)
    ppermute x10, starting transfers between devices, to_neighbour(): return lax.ppermute(array, 'seq', [(i, i ^ 1) for i in range(size)])  19.7 us
    pallas_call x20, Pallas kernels, call(): pl.pallas_call(body, out_shape=shapes, in_specs=[smem] * scalars + [vmem]...  14.3 us
    ppermute x10, waiting for transfers between devices, to_neighbour(): return lax.ppermute(array, 'seq', [(i, i ^ 1) for i in range(size)])  10.9 us
    unnamed x40, local copies, waits for them, and re-layouts  5.84 us
    ppermute x3, waiting for transfers between devices, to_core(): return lax.ppermute(array, 'rep', [(0, 1), (1, 0)])  2.59 us
  transfers between devices with their start and end apart: 18, of which 9 were waited for; matrix products, arithmetic and copies ran while one was open for 0% of the time, Pallas kernels for 18%

profile of v3, /device:TPU:0, one launch (start us, length us, event | category | flops | bytes accessed | tf_op | source)
XLA Modules:
  0.0 55.5 jit_solution(13512868895684245298)
XLA Ops:
  0.7 2.2 %head.1 = (f32[128,32]{1,0:T(8,128)}, f32[8,32]{1,0:T(8,128)}, bf16[144,768]{1,0:T(8,128)(2,1)}) custom-call(bf16[128,2048]{1,0:T(8,128)(2,1)} %refs_0_.10, bf16[128,2,256]{2,1,0:T(2,128)(2,1)} %refs_1_.6, f32[32,128]{1,0:T(8,128)} %bitcast.4), custom_call_target="tpu_custom_call" | custom-call | tf_op jit(solution)/shard_map/head/pallas_call | solution.py:504
  2.8 3.1 %collective-permute-start.2 = (bf16[144,768]{1,0:T(8,128)(2,1)}, bf16[144,768]{1,0:T(8,128)(2,1)S(1)}, u32[]{:S(2)}, u32[]{:S(2)}) collective-permute-start(bf16[144,768]{1,0:T(8,128)(2,1)} %get-tuple-element.53.refs_3_), channel_id=1, source_target_pairs={{0,4},{4,0},{8,12},{12,8},{1,5},{5,1},{9,13},{13,9},{2,6},{6,2},{1... | collective-permute-start | bytes 663560 | tf_op jit(solution)/shard_map/ppermute | solution.py:549
  5.9 0.8 %copy-done.1 = f32[128,32]{1,0:T(8,128)S(1)} copy-done((f32[128,32]{1,0:T(8,128)S(1)}, f32[128,32]{1,0:T(8,128)}, u32[]{:S(2)}) %copy-start.1) | copy-done | bytes 16408
  6.8 0.8 %copy-done.7 = bf16[128,2,128]{2,1,0:T(2,128)(2,1)S(1)} copy-done((bf16[128,2,128]{2,1,0:T(2,128)(2,1)S(1)}, bf16[128,2,128]{2,1,0:T(2,128)(2,1)}, u32[]{:S(2)}) %copy-start.7) | copy-done | bytes 65560
  7.6 0.8 %copy-done.9 = bf16[128,2,128]{2,1,0:T(2,128)(2,1)S(1)} copy-done((bf16[128,2,128]{2,1,0:T(2,128)(2,1)S(1)}, bf16[128,2,128]{2,1,0:T(2,128)(2,1)}, u32[]{:S(2)}) %copy-start.9) | copy-done | bytes 65560
  8.5 0.9 %copy-done.11 = bf16[144,768]{1,0:T(8,128)(2,1)S(1)} copy-done((bf16[144,768]{1,0:T(8,128)(2,1)S(1)}, bf16[144,768]{1,0:T(8,128)(2,1)}, u32[]{:S(2)}) %copy-start.11) | copy-done | bytes 221208
  9.4 1.1 %local_state.1 = (bf16[128,512]{1,0:T(8,128)(2,1)S(1)}, bf16[128,256]{1,0:T(8,128)(2,1)S(1)}, f32[256,512]{1,0:T(8,128)S(1)}, f32[256,512]{1,0:T(8,128)S(1)}, f3...) custom-call(bf16[128,2048]{1,0:T(8,128)(2,1)S(1)} %copy-done, ...), custom_call_target="tpu_custom_call" | custom-call | tf_op jit(solution)/shard_map/local_state/pallas_call | solution.py:504
  10.5 0.1 collective-permute-start.6
  10.6 0.1 collective-permute-start.3
  10.6 1.2 %collective-permute-done.3.refs_2_ = bf16[1,32,4,256]{3,2,1,0:T(4,128)(2,1)S(1)} collective-permute-done((bf16[1,32,4,256]{3,2,1,0:T(4,128)(2,1)S(1)}, bf16[1,32,4,256]{3,2,1,0:T(4,128)(2,1)S(1)}, u32[]{:S(2)}, u32[]{:S(2)}) %collective-permute-start.3) | collective-permute-done | bytes 65568 | tf_op jit(solution)/shard_map/ppermute | solution.py:546
  11.9 0.6 projections.1.refs_4_.refs_2_
  12.4 0.0 collective-permute-done.2.refs_0_.refs_1_
  12.4 0.1 copy-done.18
  12.6 0.5 first.4
  13.0 0.2 collective-permute-start.4
  13.3 3.4 %collective-permute-start.1 = (bf16[128,768]{1,0:T(8,128)(2,1)S(1)}, bf16[128,768]{1,0:T(8,128)(2,1)S(1)}, u32[]{:S(2)}, u32[]{:S(2)}) collective-permute-start(bf16[128,768]{1,0:T(8,128)(2,1)S(1)} %get-tuple-element.55), channel_id=1, source_target_pairs={{0,4},{4,0},{8,12},{12,8},{1,5},{5,1},{9,13},{13,9},{2,6},{6,2},{1... | collective-permute-start | bytes 589832 | tf_op jit(solution)/shard_map/ppermute | solution.py:549
  16.6 0.0 collective-permute-start.5
  16.6 0.3 collective-permute-done.6.refs_0_
  16.9 0.3 first.5
  17.2 0.1 collective-permute-start.8
  17.3 3.6 %collective-permute-start = (bf16[128,512]{1,0:T(8,128)(2,1)S(1)}, bf16[128,512]{1,0:T(8,128)(2,1)S(1)}, u32[]{:S(2)}, u32[]{:S(2)}) collective-permute-start(bf16[128,512]{1,0:T(8,128)(2,1)S(1)} %get-tuple-element.54), channel_id=1, source_target_pairs={{0,4},{4,0},{8,12},{12,8},{1,5},{5,1},{9,13},{13,9},{2,6},{6,2},{1... | collective-permute-start | bytes 393224 | tf_op jit(solution)/shard_map/ppermute | solution.py:549
  20.8 0.7 %copy-done.19 = f32[128]{0:T(128)S(1)} copy-done((f32[128]{0:T(128)S(1)}, f32[128]{0:T(128)}, u32[]{:S(2)}) %copy-start.19) | copy-done | bytes 536
  21.5 1.0 %intra.1.refs_5_.refs_3_ = f32[128,2048]{1,0:T(8,128)S(1)} custom-call(bf16[128,2048]{1,0:T(8,128)(2,1)S(1)} %copy-done, bf16[128,512]{1,0:T(8,128)(2,1)S(1)} %get-tuple-element.66.refs_1_, bf16[192,512]{1,0:T(8,128)(2,1)S(1)} %projections.1.refs_4_.refs_2_, f32[128,32]{1,0:T(8,128)S(1)} %copy-done.2, f32[1,128]{1,0:T(1,128)S(1)} %bitcast.2, ...), custom_call_target="tpu_custom_call" | custom-call | tf_op jit(solution)/shard_map/intra/pallas_call | solution.py:504
  22.5 0.0 collective-permute-done.1.refs_0_.refs_1_
  22.5 0.1 collective-permute-start.11
  22.6 0.0 copy-start.5
  22.6 0.0 copy-start.14
  22.6 0.0 copy-start.15
  22.6 0.3 first.6
  22.9 0.6 %copy-done.5 = bf16[1,32,4096]{2,1,0:T(8,128)(2,1)S(1)} copy-done((bf16[1,32,4096]{2,1,0:T(8,128)(2,1)S(1)}, bf16[1,32,4096]{2,1,0:T(8,128)(2,1)}, u32[]{:S(2)}) %copy-start.5) | copy-done | bytes 262168
  23.5 1.8 %candidates.1 = (f32[32,4096]{1,0:T(8,128)S(1)}, f32[32,4096]{1,0:T(8,128)S(1)}) custom-call(bf16[1,32,4096]{2,1,0:T(8,128)(2,1)S(1)} %copy-done.5, bf16[1,32,4,256]{3,2,1,0:T(4,128)(2,1)S(1)} %copy-done.14, bf16[1,32,4,256]{3,2,1,0:T(4,128)(2,1)S(1)} %copy-done.6, f32[1,32,64]{2,1,0:T(8,128)S(1)} %copy-done.15, f32[1,128]{1,0:T(1,128)S(1)} %bitcast.3, ...), custom_call_target="tpu_custom_call" | custom-call | tf_op jit(solution)/shard_map/candidates/pallas_call | solution.py:504
  25.3 1.3 %collective-permute-done.5.refs_5_ = bf16[192,512]{1,0:T(8,128)(2,1)S(1)} collective-permute-done((bf16[192,512]{1,0:T(8,128)(2,1)S(1)}, bf16[192,512]{1,0:T(8,128)(2,1)S(1)}, u32[]{:S(2)}, u32[]{:S(2)}) %collective-permute-start.5) | collective-permute-done | bytes 196640 | tf_op jit(solution)/shard_map/ppermute | solution.py:549
  26.5 0.0 collective-permute-done.4.refs_0_
  26.6 0.6 %second.4 = (f32[8,2048]{1,0:T(8,128)S(1)}, f32[128,512]{1,0:T(8,128)S(1)}, f32[64,512]{1,0:T(8,128)S(1)}, bf16[208,512]{1,0:T(8,128)(2,1)S(1)}) custom-call(bf16[272,512]{1,0:T(8,128)(2,1)S(1)} %collective-permute-done.4.refs_0_, f32[256,512]{1,0:T(8,128)S(1)} %get-tuple-element.63.refs_6_.refs_1_, f32[256,512]{1,0:T(8,128)S(1)} %get-tuple-element.57.refs_2_, ...), custom_call_target="tpu_custom_call" | custom-call | flops 1000000000 | tf_op jit(solution)/shard_map/second/pallas_call | solution.py:504
  27.1 2.1 %collective-permute-start.10 = (bf16[208,512]{1,0:T(8,128)(2,1)S(1)}, bf16[208,512]{1,0:T(8,128)(2,1)S(1)}, u32[]{:S(2)}, u32[]{:S(2)}) collective-permute-start(bf16[208,512]{1,0:T(8,128)(2,1)S(1)} %get-tuple-element.80), channel_id=1, source_target_pairs={{0,4},{4,0},{8,12},{12,8},{1,5},{5,1},{9,13},{13,9},{2,6},{6,2},{1... | collective-permute-start | bytes 638984 | tf_op jit(solution)/shard_map/ppermute | solution.py:549
  29.2 0.0 collective-permute-start.14
  29.3 3.7 %collective-permute-start.12 = (bf16[256,256]{1,0:T(8,128)(2,1)S(1)}, bf16[256,256]{1,0:T(8,128)(2,1)S(1)}, u32[]{:S(2)}, u32[]{:S(2)}) collective-permute-start(bf16[256,256]{1,0:T(8,128)(2,1)S(1)} %collective-permute-done.11.refs_1_), channel_id=1, source_target_pairs={{0,4},{4,0},{8,12},{12,8},{1,5},{5,1},{9,13},{13,9},{2,6},{6,2},{1... | collective-permute-start | bytes 393224 | tf_op jit(solution)/shard_map/ppermute | solution.py:549
  33.0 0.3 first.7
  33.2 0.1 collective-permute-start.7
  33.3 0.4 second.5
  33.8 1.0 %collective-permute-done.10.refs_0_ = bf16[208,512]{1,0:T(8,128)(2,1)S(1)} collective-permute-done((bf16[208,512]{1,0:T(8,128)(2,1)S(1)}, bf16[208,512]{1,0:T(8,128)(2,1)S(1)}, u32[]{:S(2)}, u32[]{:S(2)}) %collective-permute-start.10) | collective-permute-done | bytes 213024 | tf_op jit(solution)/shard_map/ppermute | solution.py:549
  34.8 0.3 third.4
  35.1 1.3 %collective-permute-done.12.refs_2_ = bf16[256,256]{1,0:T(8,128)(2,1)S(1)} collective-permute-done((bf16[256,256]{1,0:T(8,128)(2,1)S(1)}, bf16[256,256]{1,0:T(8,128)(2,1)S(1)}, u32[]{:S(2)}, u32[]{:S(2)}) %collective-permute-start.12) | collective-permute-done | bytes 131104 | tf_op jit(solution)/shard_map/ppermute | solution.py:549
  36.4 0.1 collective-permute-start.13
  36.5 1.6 %collective-permute-start.9 = (bf16[192,512]{1,0:T(8,128)(2,1)S(1)}, bf16[192,512]{1,0:T(8,128)(2,1)S(1)}, u32[]{:S(2)}, u32[]{:S(2)}) collective-permute-start(bf16[192,512]{1,0:T(8,128)(2,1)S(1)} %get-tuple-element.77), channel_id=1, source_target_pairs={{0,4},{4,0},{8,12},{12,8},{1,5},{5,1},{9,13},{13,9},{2,6},{6,2},{1... | collective-permute-start | bytes 589832 | tf_op jit(solution)/shard_map/ppermute | solution.py:549
  38.8 0.0 copy-start.8
  38.8 0.0 copy-start.10
  38.8 0.0 copy-start.13
  38.8 0.0 copy-start.16
  38.8 0.0 copy-start.17
  38.8 0.4 second.6
  39.3 0.6 %collective-permute-start.16 = (bf16[192,512]{1,0:T(8,128)(2,1)S(1)}, bf16[192,512]{1,0:T(8,128)(2,1)S(1)}, u32[]{:S(2)}, u32[]{:S(2)}) collective-permute-start(bf16[192,512]{1,0:T(8,128)(2,1)S(1)} %get-tuple-element.91), channel_id=1, source_target_pairs={{0,4},{4,0},{8,12},{12,8},{1,5},{5,1},{9,13},{13,9},{2,6},{6,2},{1... | collective-permute-start | bytes 589832 | tf_op jit(solution)/shard_map/ppermute | solution.py:549
  39.9 1.9 %attend.1.refs_7_ = bf16[1,32,16,128]{3,2,1,0:T(8,128)(2,1)} custom-call(s32[1]{0:T(128)S(6)} %copy.18.refs_0_, bf16[1,32,16,128]{3,2,1,0:T(8,128)(2,1)S(1)} %copy-done.13, bf16[1,32,2,128]{3,2,1,0:T(2,128)(2,1)S(1)} %copy-done.16, bf16[1,32,2,128]{3,2,1,0:T(2,128)(2,1)S(1)} %copy-done.17, bf16[128,2,128]{2,1,0:T(2,128)(2,1)S(1)} %copy-done.8, ...), custom_call_target="tpu_custom_call" | custom-call | tf_op jit(solution)/shard_map/attend/pallas_call | solution.py:504
  41.8 2.5 %collective-permute-done.9.refs_0_ = bf16[192,512]{1,0:T(8,128)(2,1)S(1)} collective-permute-done((bf16[192,512]{1,0:T(8,128)(2,1)S(1)}, bf16[192,512]{1,0:T(8,128)(2,1)S(1)}, u32[]{:S(2)}, u32[]{:S(2)}) %collective-permute-start.9) | collective-permute-done | bytes 196640 | tf_op jit(solution)/shard_map/ppermute | solution.py:549
  44.3 0.9 %copy-done.4 = bf16[1,32,16,128]{3,2,1,0:T(8,128)(2,1)S(1)} copy-done((bf16[1,32,16,128]{3,2,1,0:T(8,128)(2,1)S(1)}, bf16[1,32,16,128]{3,2,1,0:T(8,128)(2,1)}, u32[]{:S(2)}) %copy-start.4) | copy-done | bytes 131096
  45.2 0.2 third.5
  45.4 0.4 second.7
  45.9 1.6 %collective-permute-start.15 = (bf16[192,512]{1,0:T(8,128)(2,1)S(1)}, bf16[192,512]{1,0:T(8,128)(2,1)S(1)}, u32[]{:S(2)}, u32[]{:S(2)}) collective-permute-start(bf16[192,512]{1,0:T(8,128)(2,1)S(1)} %get-tuple-element.88), channel_id=1, source_target_pairs={{0,4},{4,0},{8,12},{12,8},{1,5},{5,1},{9,13},{13,9},{2,6},{6,2},{1... | collective-permute-start | bytes 589832 | tf_op jit(solution)/shard_map/ppermute | solution.py:549
  47.5 0.8 %collective-permute-done.16.refs_0_ = bf16[192,512]{1,0:T(8,128)(2,1)S(1)} collective-permute-done((bf16[192,512]{1,0:T(8,128)(2,1)S(1)}, bf16[192,512]{1,0:T(8,128)(2,1)S(1)}, u32[]{:S(2)}, u32[]{:S(2)}) %collective-permute-start.16) | collective-permute-done | bytes 196640 | tf_op jit(solution)/shard_map/ppermute | solution.py:549
  48.3 0.2 third.6
  48.5 3.8 %collective-permute-done.15.refs_0_ = bf16[192,512]{1,0:T(8,128)(2,1)S(1)} collective-permute-done((bf16[192,512]{1,0:T(8,128)(2,1)S(1)}, bf16[192,512]{1,0:T(8,128)(2,1)S(1)}, u32[]{:S(2)}, u32[]{:S(2)}) %collective-permute-start.15) | collective-permute-done | bytes 196640 | tf_op jit(solution)/shard_map/ppermute | solution.py:549
  52.3 1.0 %third.7 = (bf16[128,2048]{1,0:T(8,128)(2,1)}, f32[32,2048]{1,0:T(8,128)S(1)}, bf16[32,2048]{1,0:T(8,128)(2,1)S(1)}) custom-call(bf16[192,512]{1,0:T(8,128)(2,1)S(1)} %collective-permute-done.15.refs_0_, f32[128,512]{1,0:T(8,128)S(1)} %get-tuple-element.89.refs_7_.refs_1_, f32[64,512]{1,0:T(8,128)S(1)} %get-tuple-element.90.refs_2_, ...), custom_call_target="tpu_custom_call" | custom-call | flops 300000000 | tf_op jit(solution)/shard_map/third/pallas_call | solution.py:504
  53.3 1.3 %collective-permute-done.17.refs_4_ = bf16[32,2048]{1,0:T(8,128)(2,1)S(1)} collective-permute-done((bf16[32,2048]{1,0:T(8,128)(2,1)S(1)}, bf16[32,2048]{1,0:T(8,128)(2,1)S(1)}, u32[]{:S(2)}, u32[]{:S(2)}) %collective-permute-start.17) | collective-permute-done | bytes 131104 | tf_op jit(solution)/shard_map/ppermute | solution.py:546
  54.7 0.8 %close.1 = bf16[1,32,4096]{2,1,0:T(8,128)(2,1)} custom-call(s32[1]{0:T(128)S(6)} %copy.18.refs_0_, f32[32,4096]{1,0:T(8,128)S(1)} %get-tuple-element.71.refs_8_.refs_1_, f32[32,4096]{1,0:T(8,128)S(1)} %get-tuple-element.98.refs_2_, f32[32,2048]{1,0:T(8,128)S(1)} %get-tuple-element.99.refs_3_, bf16[32,2048]{1,0:T(8,128)(2,1)S(1)} %collective-permute-done.17.refs_4_), custom_call_target="tpu_custom_call" | custom-call | tf_op jit(solution)/shard_map/close/pallas_call | solution.py:504
  (32 shorter events, 0.1 us)
Async XLA Ops:
  0.6 5.3 %copy-start = (bf16[128,2048]{1,0:T(8,128)(2,1)S(1)}, bf16[128,2048]{1,0:T(8,128)(2,1)}, u32[]{:S(2)}) copy-start(bf16[128,2048]{1,0:T(8,128)(2,1)} %refs_0_.10) | copy-start | bytes 1572868
  0.6 5.3 %copy-start.3 = (bf16[128,2,256]{2,1,0:T(2,128)(2,1)S(1)}, bf16[128,2,256]{2,1,0:T(2,128)(2,1)}, u32[]{:S(2)}) copy-start(bf16[128,2,256]{2,1,0:T(2,128)(2,1)} %refs_1_.6) | copy-start | bytes 393220
  2.8 9.6 %collective-permute-start.2 = (bf16[144,768]{1,0:T(8,128)(2,1)}, bf16[144,768]{1,0:T(8,128)(2,1)S(1)}, u32[]{:S(2)}, u32[]{:S(2)}) collective-permute-start(bf16[144,768]{1,0:T(8,128)(2,1)} %get-tuple-element.53.refs_3_), channel_id=1, source_target_pairs={{0,4},{4,0},{8,12},{12,8},{1,5},{5,1},{9,13},{13,9},{2,6},{6,2},{1... | collective-permute-start | bytes 663560 | tf_op jit(solution)/shard_map/ppermute | solution.py:549
  5.9 0.8 %copy-start.1 = (f32[128,32]{1,0:T(8,128)S(1)}, f32[128,32]{1,0:T(8,128)}, u32[]{:S(2)}) copy-start(f32[128,32]{1,0:T(8,128)} %get-tuple-element.52.refs_2_.refs_3_.refs_4_) | copy-start | bytes 49156
  6.8 0.8 %copy-start.7 = (bf16[128,2,128]{2,1,0:T(2,128)(2,1)S(1)}, bf16[128,2,128]{2,1,0:T(2,128)(2,1)}, u32[]{:S(2)}) copy-start(bf16[128,2,128]{2,1,0:T(2,128)(2,1)} %refs_4_.3) | copy-start | bytes 196612
  7.6 0.8 %copy-start.9 = (bf16[128,2,128]{2,1,0:T(2,128)(2,1)S(1)}, bf16[128,2,128]{2,1,0:T(2,128)(2,1)}, u32[]{:S(2)}) copy-start(bf16[128,2,128]{2,1,0:T(2,128)(2,1)} %refs_5_.3) | copy-start | bytes 196612
  8.5 0.9 %copy-start.11 = (bf16[144,768]{1,0:T(8,128)(2,1)S(1)}, bf16[144,768]{1,0:T(8,128)(2,1)}, u32[]{:S(2)}) copy-start(bf16[144,768]{1,0:T(8,128)(2,1)} %get-tuple-element.53.refs_3_) | copy-start | bytes 663556
  9.4 1.2 %copy-start.6 = (bf16[1,32,4,256]{3,2,1,0:T(4,128)(2,1)S(1)}, bf16[1,32,4,256]{3,2,1,0:T(4,128)(2,1)}, u32[]{:S(2)}) copy-start(bf16[1,32,4,256]{3,2,1,0:T(4,128)(2,1)} %refs_2_.2) | copy-start | bytes 196612
  9.4 2.5 %copy-start.12 = (bf16[128,2,256]{2,1,0:T(2,128)(2,1)S(1)}, bf16[128,2,256]{2,1,0:T(2,128)(2,1)}, u32[]{:S(2)}) copy-start(bf16[128,2,256]{2,1,0:T(2,128)(2,1)} %refs_0_.9) | copy-start | bytes 393220
  10.5 6.4 %collective-permute-start.6 = (bf16[128,768]{1,0:T(8,128)(2,1)S(1)}, bf16[128,768]{1,0:T(8,128)(2,1)S(1)}, u32[]{:S(2)}, u32[]{:S(2)}) collective-permute-start(bf16[128,768]{1,0:T(8,128)(2,1)S(1)} %get-tuple-element.67), channel_id=1, source_target_pairs={{0,4},{4,0},{8,12},{12,8},{1,5},{5,1},{9,13},{13,9},{2,6},{6,2},{1... | collective-permute-start | bytes 589832 | tf_op jit(solution)/shard_map/ppermute | solution.py:549
  10.6 1.3 %collective-permute-start.3 = (bf16[1,32,4,256]{3,2,1,0:T(4,128)(2,1)S(1)}, bf16[1,32,4,256]{3,2,1,0:T(4,128)(2,1)S(1)}, u32[]{:S(2)}, u32[]{:S(2)}) collective-permute-start(bf16[1,32,4,256]{3,2,1,0:T(4,128)(2,1)S(1)} %copy-done.6), channel_id=1, source_target_pairs={{0,1},{1,0},{2,3},{3,2},{4,5},{5,4},{6,7},{7,6},{8,9},{9,8},{10,11... | collective-permute-start | bytes 196616 | tf_op jit(solution)/shard_map/ppermute | solution.py:546
  11.9 0.7 %copy-start.18 = (f32[8,32]{1,0:T(8,128)S(1)}, f32[8,32]{1,0:T(8,128)}, u32[]{:S(2)}) copy-start(f32[8,32]{1,0:T(8,128)} %get-tuple-element.58.refs_3_.refs_6_) | copy-start | bytes 3076
  13.0 13.5 %collective-permute-start.4 = (bf16[272,512]{1,0:T(8,128)(2,1)S(1)}, bf16[272,512]{1,0:T(8,128)(2,1)S(1)}, u32[]{:S(2)}, u32[]{:S(2)}) collective-permute-start(bf16[272,512]{1,0:T(8,128)(2,1)S(1)} %get-tuple-element.62), channel_id=1, source_target_pairs={{0,1},{1,0},{4,8},{5,9},{8,4},{9,5},{12,13},{13,12},{2,3},{3,2},{6... | collective-permute-start | bytes 835592 | tf_op jit(solution)/shard_map/ppermute | solution.py:557
  13.3 9.2 %collective-permute-start.1 = (bf16[128,768]{1,0:T(8,128)(2,1)S(1)}, bf16[128,768]{1,0:T(8,128)(2,1)S(1)}, u32[]{:S(2)}, u32[]{:S(2)}) collective-permute-start(bf16[128,768]{1,0:T(8,128)(2,1)S(1)} %get-tuple-element.55), channel_id=1, source_target_pairs={{0,4},{4,0},{8,12},{12,8},{1,5},{5,1},{9,13},{13,9},{2,6},{6,2},{1... | collective-permute-start | bytes 589832 | tf_op jit(solution)/shard_map/ppermute | solution.py:549
  16.6 9.9 %collective-permute-start.5 = (bf16[192,512]{1,0:T(8,128)(2,1)S(1)}, bf16[192,512]{1,0:T(8,128)(2,1)S(1)}, u32[]{:S(2)}, u32[]{:S(2)}) collective-permute-start(bf16[192,512]{1,0:T(8,128)(2,1)S(1)} %projections.1.refs_4_.refs_2_), channel_id=1, source_target_pairs={{0,4},{4,0},{8,12},{12,8},{1,5},{5,1},{9,13},{13,9},{2,6},{6,2},{1... | collective-permute-start | bytes 589832 | tf_op jit(solution)/shard_map/ppermute | solution.py:549
  16.9 3.9 %copy-start.2 = (f32[128,32]{1,0:T(8,128)S(1)}, f32[128,32]{1,0:T(8,128)}, u32[]{:S(2)}) copy-start(f32[128,32]{1,0:T(8,128)} %get-tuple-element.52.refs_2_.refs_3_.refs_4_) | copy-start | bytes 49156
  17.2 16.1 %collective-permute-start.8 = (bf16[256,512]{1,0:T(8,128)(2,1)S(1)}, bf16[256,512]{1,0:T(8,128)(2,1)S(1)}, u32[]{:S(2)}, u32[]{:S(2)}) collective-permute-start(bf16[256,512]{1,0:T(8,128)(2,1)S(1)} %get-tuple-element.76), channel_id=1, source_target_pairs={{0,1},{1,0},{4,8},{5,9},{8,4},{9,5},{12,13},{13,12},{2,3},{3,2},{6... | collective-permute-start | bytes 786440 | tf_op jit(solution)/shard_map/ppermute | solution.py:557
  17.3 15.7 %collective-permute-start = (bf16[128,512]{1,0:T(8,128)(2,1)S(1)}, bf16[128,512]{1,0:T(8,128)(2,1)S(1)}, u32[]{:S(2)}, u32[]{:S(2)}) collective-permute-start(bf16[128,512]{1,0:T(8,128)(2,1)S(1)} %get-tuple-element.54), channel_id=1, source_target_pairs={{0,4},{4,0},{8,12},{12,8},{1,5},{5,1},{9,13},{13,9},{2,6},{6,2},{1... | collective-permute-start | bytes 393224 | tf_op jit(solution)/shard_map/ppermute | solution.py:549
  20.8 0.7 %copy-start.19 = (f32[128]{0:T(128)S(1)}, f32[128]{0:T(128)}, u32[]{:S(2)}) copy-start(f32[128]{0:T(128)} %param.19) | copy-start | bytes 1540
  22.5 6.8 %collective-permute-start.11 = (bf16[256,256]{1,0:T(8,128)(2,1)S(1)}, bf16[256,256]{1,0:T(8,128)(2,1)S(1)}, u32[]{:S(2)}, u32[]{:S(2)}) collective-permute-start(bf16[256,256]{1,0:T(8,128)(2,1)S(1)} %get-tuple-element.83.refs_0_), channel_id=1, source_target_pairs={{0,1},{1,0},{4,8},{5,9},{8,4},{9,5},{12,13},{13,12},{2,3},{3,2},{6... | collective-permute-start | bytes 393224 | tf_op jit(solution)/shard_map/ppermute | solution.py:557
  22.6 1.0 %copy-start.5 = (bf16[1,32,4096]{2,1,0:T(8,128)(2,1)S(1)}, bf16[1,32,4096]{2,1,0:T(8,128)(2,1)}, u32[]{:S(2)}) copy-start(bf16[1,32,4096]{2,1,0:T(8,128)(2,1)} %refs_0_.11) | copy-start | bytes 786436
  22.6 0.9 %copy-start.14 = (bf16[1,32,4,256]{3,2,1,0:T(4,128)(2,1)S(1)}, bf16[1,32,4,256]{3,2,1,0:T(4,128)(2,1)}, u32[]{:S(2)}) copy-start(bf16[1,32,4,256]{3,2,1,0:T(4,128)(2,1)} %refs_1_.8) | copy-start | bytes 196612
  22.6 0.9 %copy-start.15 = (f32[1,32,64]{2,1,0:T(8,128)S(1)}, f32[1,32,64]{2,1,0:T(8,128)}, u32[]{:S(2)}) copy-start(f32[1,32,64]{2,1,0:T(8,128)} %refs_3_.2) | copy-start | bytes 24580
  27.1 7.7 %collective-permute-start.10 = (bf16[208,512]{1,0:T(8,128)(2,1)S(1)}, bf16[208,512]{1,0:T(8,128)(2,1)S(1)}, u32[]{:S(2)}, u32[]{:S(2)}) collective-permute-start(bf16[208,512]{1,0:T(8,128)(2,1)S(1)} %get-tuple-element.80), channel_id=1, source_target_pairs={{0,4},{4,0},{8,12},{12,8},{1,5},{5,1},{9,13},{13,9},{2,6},{6,2},{1... | collective-permute-start | bytes 638984 | tf_op jit(solution)/shard_map/ppermute | solution.py:549
  29.2 9.6 %collective-permute-start.14 = (bf16[256,512]{1,0:T(8,128)(2,1)S(1)}, bf16[256,512]{1,0:T(8,128)(2,1)S(1)}, u32[]{:S(2)}, u32[]{:S(2)}) collective-permute-start(bf16[256,512]{1,0:T(8,128)(2,1)S(1)} %get-tuple-element.85), channel_id=1, source_target_pairs={{0,1},{1,0},{4,8},{5,9},{8,4},{9,5},{12,13},{13,12},{2,3},{3,2},{6... | collective-permute-start | bytes 786440 | tf_op jit(solution)/shard_map/ppermute | solution.py:557
  29.3 7.2 %collective-permute-start.12 = (bf16[256,256]{1,0:T(8,128)(2,1)S(1)}, bf16[256,256]{1,0:T(8,128)(2,1)S(1)}, u32[]{:S(2)}, u32[]{:S(2)}) collective-permute-start(bf16[256,256]{1,0:T(8,128)(2,1)S(1)} %collective-permute-done.11.refs_1_), channel_id=1, source_target_pairs={{0,4},{4,0},{8,12},{12,8},{1,5},{5,1},{9,13},{13,9},{2,6},{6,2},{1... | collective-permute-start | bytes 393224 | tf_op jit(solution)/shard_map/ppermute | solution.py:549
  33.2 12.2 %collective-permute-start.7 = (bf16[256,512]{1,0:T(8,128)(2,1)S(1)}, bf16[256,512]{1,0:T(8,128)(2,1)S(1)}, u32[]{:S(2)}, u32[]{:S(2)}) collective-permute-start(bf16[256,512]{1,0:T(8,128)(2,1)S(1)} %get-tuple-element.73), channel_id=1, source_target_pairs={{0,1},{1,0},{4,8},{5,9},{8,4},{9,5},{12,13},{13,12},{2,3},{3,2},{6... | collective-permute-start | bytes 786440 | tf_op jit(solution)/shard_map/ppermute | solution.py:557
  36.4 3.4 %collective-permute-start.13 = (bf16[384,256]{1,0:T(8,128)(2,1)S(1)}, bf16[384,256]{1,0:T(8,128)(2,1)S(1)}, u32[]{:S(2)}, u32[]{:S(2)}) collective-permute-start(bf16[384,256]{1,0:T(8,128)(2,1)S(1)} %collect.1.refs_7_.refs_6_), channel_id=1, source_target_pairs={{0,1},{1,0},{2,3},{3,2},{4,5},{5,4},{6,7},{7,6},{8,9},{9,8},{10,11... | collective-permute-start | bytes 589832 | tf_op jit(solution)/shard_map/ppermute | solution.py:546
  36.5 7.8 %collective-permute-start.9 = (bf16[192,512]{1,0:T(8,128)(2,1)S(1)}, bf16[192,512]{1,0:T(8,128)(2,1)S(1)}, u32[]{:S(2)}, u32[]{:S(2)}) collective-permute-start(bf16[192,512]{1,0:T(8,128)(2,1)S(1)} %get-tuple-element.77), channel_id=1, source_target_pairs={{0,4},{4,0},{8,12},{12,8},{1,5},{5,1},{9,13},{13,9},{2,6},{6,2},{1... | collective-permute-start | bytes 589832 | tf_op jit(solution)/shard_map/ppermute | solution.py:549
  38.8 1.1 %copy-start.8 = (bf16[128,2,128]{2,1,0:T(2,128)(2,1)S(1)}, bf16[128,2,128]{2,1,0:T(2,128)(2,1)}, u32[]{:S(2)}) copy-start(bf16[128,2,128]{2,1,0:T(2,128)(2,1)} %refs_4_.3) | copy-start | bytes 196612
  38.8 1.1 %copy-start.10 = (bf16[128,2,128]{2,1,0:T(2,128)(2,1)S(1)}, bf16[128,2,128]{2,1,0:T(2,128)(2,1)}, u32[]{:S(2)}) copy-start(bf16[128,2,128]{2,1,0:T(2,128)(2,1)} %refs_5_.3) | copy-start | bytes 196612
  38.8 1.1 %copy-start.13 = (bf16[1,32,16,128]{3,2,1,0:T(8,128)(2,1)S(1)}, bf16[1,32,16,128]{3,2,1,0:T(8,128)(2,1)}, u32[]{:S(2)}) copy-start(bf16[1,32,16,128]{3,2,1,0:T(8,128)(2,1)} %refs_1_.9) | copy-start | bytes 393220
  38.8 1.1 %copy-start.16 = (bf16[1,32,2,128]{3,2,1,0:T(2,128)(2,1)S(1)}, bf16[1,32,2,128]{3,2,1,0:T(2,128)(2,1)}, u32[]{:S(2)}) copy-start(bf16[1,32,2,128]{3,2,1,0:T(2,128)(2,1)} %refs_2_.3) | copy-start | bytes 49156
  38.8 1.1 %copy-start.17 = (bf16[1,32,2,128]{3,2,1,0:T(2,128)(2,1)S(1)}, bf16[1,32,2,128]{3,2,1,0:T(2,128)(2,1)}, u32[]{:S(2)}) copy-start(bf16[1,32,2,128]{3,2,1,0:T(2,128)(2,1)} %refs_3_.3) | copy-start | bytes 49156
  39.3 9.0 %collective-permute-start.16 = (bf16[192,512]{1,0:T(8,128)(2,1)S(1)}, bf16[192,512]{1,0:T(8,128)(2,1)S(1)}, u32[]{:S(2)}, u32[]{:S(2)}) collective-permute-start(bf16[192,512]{1,0:T(8,128)(2,1)S(1)} %get-tuple-element.91), channel_id=1, source_target_pairs={{0,4},{4,0},{8,12},{12,8},{1,5},{5,1},{9,13},{13,9},{2,6},{6,2},{1... | collective-permute-start | bytes 589832 | tf_op jit(solution)/shard_map/ppermute | solution.py:549
  44.3 0.9 %copy-start.4 = (bf16[1,32,16,128]{3,2,1,0:T(8,128)(2,1)S(1)}, bf16[1,32,16,128]{3,2,1,0:T(8,128)(2,1)}, u32[]{:S(2)}) copy-start(bf16[1,32,16,128]{3,2,1,0:T(8,128)(2,1)} %attend.1.refs_7_) | copy-start | bytes 393220
  45.9 6.4 %collective-permute-start.15 = (bf16[192,512]{1,0:T(8,128)(2,1)S(1)}, bf16[192,512]{1,0:T(8,128)(2,1)S(1)}, u32[]{:S(2)}, u32[]{:S(2)}) collective-permute-start(bf16[192,512]{1,0:T(8,128)(2,1)S(1)} %get-tuple-element.88), channel_id=1, source_target_pairs={{0,4},{4,0},{8,12},{12,8},{1,5},{5,1},{9,13},{13,9},{2,6},{6,2},{1... | collective-permute-start | bytes 589832 | tf_op jit(solution)/shard_map/ppermute | solution.py:549
  53.3 1.3 %collective-permute-start.17 = (bf16[32,2048]{1,0:T(8,128)(2,1)S(1)}, bf16[32,2048]{1,0:T(8,128)(2,1)S(1)}, u32[]{:S(2)}, u32[]{:S(2)}) collective-permute-start(bf16[32,2048]{1,0:T(8,128)(2,1)S(1)} %get-tuple-element.100), channel_id=1, source_target_pairs={{0,1},{1,0},{2,3},{3,2},{4,5},{5,4},{6,7},{7,6},{8,9},{9,8},{10,11... | collective-permute-start | bytes 393224 | tf_op jit(solution)/shard_map/ppermute | solution.py:546

commit v4 on v3

--- a/solution.py
+++ b/solution.py
@@ -11,7 +11,8 @@
 NEG = -1e30
 CHUNKS = 4
 SECOND_COST = 1.0
-FIRST_COST = 2.0
+FIRST_COST = 0.0
+THIRD_COST = 0.3
 F32 = jnp.float32
 BF16 = jnp.bfloat16
 
@@ -92,19 +93,15 @@
     return jnp.concatenate([kv[:, j, :] for j in range(kv.shape[1])], axis=1).astype(BF16)
 
 
-def head_kernel(x_any, b_any, decay_t_any, cum_ref, total_ref, load_ref, x_ref, b_ref, decay_t_ref, sems):
+def inputs_kernel(x_any, b_any, decay_t_any, k_any, v_any, cum_ref, total_ref, b2_ref, kv_ref, *refs):
+    load_refs, (x_ref, b_ref, decay_t_ref, k_ref, v_ref, sems) = refs[:-6], refs[-6:]
+    pairs = ((decay_t_any, decay_t_ref), (b_any, b_ref), (x_any, x_ref), (k_any, k_ref), (v_any, v_ref))
+    copies = [pltpu.make_async_copy(source, target, sems.at[i]) for i, (source, target) in enumerate(pairs)]
+    for copy in copies:
+        copy.start()
     tokens, groups, state = b_ref.shape
     heads = decay_t_ref.shape[0]
-    cols = x_ref.shape[1]
-    width = cols * CHUNKS // heads
-    copies = [
-        pltpu.make_async_copy(source, target, sems.at[i])
-        for i, (source, target) in enumerate(
-            ((decay_t_any, decay_t_ref), (x_any.at[:, pl.ds(0, cols)], x_ref), (b_any, b_ref))
-        )
-    ]
-    for copy in copies:
-        copy.start()
+    cols = x_ref.shape[1] // CHUNKS
     copies[0].wait()
     lower = (iota((tokens, tokens), 0) >= iota((tokens, tokens), 1)).astype(F32)
     cum = exact_nt(lower, decay_t_ref[...])
@@ -112,42 +109,32 @@
     last = cum[tokens - 1 : tokens, :]
     total = jnp.exp(-last)
     total_ref[...] = jnp.broadcast_to(total, (8, heads))
-    load_ref[tokens:, :] = jnp.zeros((16, load_ref.shape[1]), BF16)
-    load_ref[tokens:, :heads] = totals_to_lines(total)
-    weights = spread(jnp.exp(last - cum), width, 0, heads // CHUNKS)
-    copies[1].wait()
-    load_ref[:tokens, :cols] = (x_ref[...].astype(F32) * weights).astype(BF16)
-    copies[2].wait()
-    load_ref[:tokens, cols:] = b_ref[...].astype(F32)[:, 0, :].astype(BF16)
-
-
-def local_kernel(x_ref, b_ref, cum_ref, first_ref, k_ref, v_ref, b2_ref, kv_ref, *outs):
-    local_refs, load_refs = outs[:CHUNKS], outs[CHUNKS:]
-    tokens, groups, state = b_ref.shape
-    heads = cum_ref.shape[1]
-    width = x_ref.shape[1] // heads
-    cols = x_ref.shape[1] // CHUNKS
-    cum = cum_ref[...]
-    weights = spread(jnp.exp(cum[tokens - 1 : tokens, :] - cum), width)
+    load_refs[0][tokens:, :] = jnp.zeros((16, cols + state), BF16)
+    load_refs[0][tokens:, :heads] = totals_to_lines(total)
+    weights = spread(jnp.exp(last - cum), x_ref.shape[1] // heads)
+    for copy in copies[1:]:
+        copy.wait()
     b = b_ref[...].astype(F32)
     for g in range(groups):
         b2_ref[:, g * state : (g + 1) * state] = b[:, g, :].astype(BF16)
     kv = pack(k_ref, v_ref)
     kv_ref[...] = kv
-    for q, fresh in enumerate(payload_plan(groups)):
-        g = q * groups // CHUNKS
+    for q, (fresh, load) in enumerate(zip(payload_plan(groups), load_refs)):
         at = slice(q * cols, (q + 1) * cols)
-        if q == 0:
-            weighted = first_ref[:tokens, :cols]
-        else:
-            weighted = (x_ref[:, at].astype(F32) * weights[:, at]).astype(BF16)
-            load = load_refs[q - 1]
-            load[:, :cols] = weighted
-            if fresh:
-                load[:, cols : cols + state] = b2_ref[:, g * state : (g + 1) * state]
-            if q == 1:
-                load[:, load.shape[1] - kv.shape[1] :] = kv
-        local_refs[q][...] = mm_tn(b2_ref[:, g * state : (g + 1) * state], weighted)
+        load[:tokens, :cols] = (x_ref[:, at].astype(F32) * weights[:, at]).astype(BF16)
+        if fresh:
+            load[:tokens, cols : cols + state] = b2_ref[:, fresh[0] * state : (fresh[0] + 1) * state]
+        if q == 1:
+            load[:, load.shape[1] - kv.shape[1] :] = kv
+
+
+def own_kernel(*refs, cols, groups, state):
+    load_refs, out_refs = refs[:CHUNKS], refs[CHUNKS:]
+    tokens = load_refs[1].shape[0]
+    first_of = {g: q for q, fresh in enumerate(payload_plan(groups)) for g in fresh}
+    for q in range(CHUNKS):
+        b_ref = load_refs[first_of[q * groups // CHUNKS]]
+        out_refs[q][...] = mm_tn(b_ref[:tokens, cols : cols + state], load_refs[q][:tokens, :cols])
 
 
 def collect_kernel(*refs, inner):
@@ -155,9 +142,12 @@
     place = lax.axis_index("seq")
     pieces = [ref[...] for ref in refs]
     if inner:
-        second = pieces.pop()
-        pieces[-1] = jnp.where((place == 1) | (place == 2), pieces[-1], second)
-        pieces[0] = pieces[0][pieces[0].shape[0] // 2 :]
+        pair, far, outer = pieces
+        rows, wide = far.shape
+        count = outer.shape[1] // wide
+        first = outer.shape[0] - rows // count
+        outer = jnp.concatenate([outer[first:, i * wide : (i + 1) * wide] for i in range(count)], axis=0)
+        pieces = [pair[pair.shape[0] // 2 :], jnp.where((place == 1) | (place == 2), far, outer)]
     at = 0
     for piece in pieces:
         out_ref[at : at + piece.shape[0], :] = piece
@@ -270,12 +260,13 @@
 
 def first_kernel(*refs, q, cols, groups, heads, tokens, state):
     refs = list(refs)
-    w_ref, b_ref, local_ref = refs[:3]
+    w_ref, b_ref, own_w_ref, own_b_ref = refs[:4]
+    refs = refs[4:]
     left = lax.axis_index("seq") < 2
     width = cols * CHUNKS // heads
     other = mm_tn(b_ref[:tokens, cols : cols + state], w_ref[:tokens, :cols])
     if q == 0:
-        mine_ref, own_row_ref, near_row_ref, near_ref, other_ref, send_ref = refs[3:]
+        mine_ref, own_row_ref, near_row_ref, near_ref, send_ref = refs
         mine = mine_ref[:1, :]
         near = lines_to_totals(w_ref[tokens:, :heads])
         own_row, near_row = as_row(mine, width), as_row(near, width)
@@ -285,26 +276,26 @@
         send_ref[state:, :] = jnp.zeros((16, cols), BF16)
         send_ref[state:, :heads] = totals_to_lines(mine * near)
     else:
-        own_row_ref, near_row_ref = refs[3:5]
-        refs = refs[5:]
+        own_row_ref, near_row_ref = refs[:2]
+        refs = refs[2:]
         if q == 1:
             kv_ref, pair_ref = refs[0], refs.pop()
             refs = refs[1:]
             pair_ref[:tokens, :] = kv_ref[...]
             pair_ref[tokens:, :] = w_ref[:, w_ref.shape[1] - kv_ref.shape[1] :]
-        other_ref, send_ref = refs
+        (send_ref,) = refs
         own_row, near_row = own_row_ref[...], near_row_ref[...]
     at = slice(q * cols, (q + 1) * cols)
-    local = local_ref[...]
+    local = mm_tn(own_b_ref[:tokens, cols : cols + state], own_w_ref[:tokens, :cols])
     after = own_row[:1, at] * other + local
     beyond = other + near_row[:1, at] * local
     send_ref[:state, :] = jnp.where(left, after, beyond).astype(BF16)
-    other_ref[...] = other
 
 
 def second_kernel(*refs, q, cols, groups, heads, tokens, state):
     refs = list(refs)
-    got_ref, other_ref, local_ref, own_row_ref, cc_ref, near_cc_ref = refs[:6]
+    got_ref, w_ref, b_ref, own_w_ref, own_b_ref, own_row_ref, cc_ref, near_cc_ref = refs[:8]
+    refs = refs[8:]
     place = lax.axis_index("seq")
     left, inner = place < 2, (place == 1) | (place == 2)
     width = cols * CHUNKS // heads
@@ -313,16 +304,24 @@
     here = slice(g * state, (g + 1) * state)
     rows = cc_ref.shape[0]
     if q == 0:
-        mine_ref, near_ref, later_row_ref, carried_ref, cand_ref, send_ref = refs[6:]
+        mine_ref, near_ref, later_row_ref, carried_ref, cand_ref, send_ref = refs
         later = jnp.where(left, lines_to_totals(got_ref[state:, :heads]), near_ref[:1, :])
         later_row = as_row(later, width)
         later_row_ref[...] = later_row
         send_ref[rows:, :] = jnp.zeros((16, cols), BF16)
         send_ref[rows:, :heads] = totals_to_lines(later * mine_ref[:1, :])
     else:
-        later_row_ref, carried_ref, cand_ref, send_ref = refs[6:]
+        if q == 1:
+            kv_ref = refs.pop(0)
+            held = kv_ref.shape[0] // (cols // kv_ref.shape[1])
+            for i in range(cols // kv_ref.shape[1]):
+                part = slice(i * kv_ref.shape[1], (i + 1) * kv_ref.shape[1])
+                refs[-1][rows:, part] = kv_ref[i * held : (i + 1) * held, :]
+        later_row_ref, carried_ref, cand_ref, send_ref = refs
         later_row = later_row_ref[...]
-    got, other, local = got_ref[:state, :].astype(F32), other_ref[...], local_ref[...]
+    got = got_ref[:state, :].astype(F32)
+    other = mm_tn(b_ref[:tokens, cols : cols + state], w_ref[:tokens, :cols])
+    local = mm_tn(own_b_ref[:tokens, cols : cols + state], own_w_ref[:tokens, :cols])
     start, beyond = jnp.where(left, other, got), jnp.where(left, got, other)
     start = jnp.where(inner, start, 0.0)
     after = own_row_ref[:1, at] * start + local
@@ -489,28 +488,32 @@
         out_ref[0, :, at] = jnp.where(live, result, 0.0).astype(BF16)
 
 
-def call(kernel, name, outs, *args, scalars=0, after=(), cost=0.0, scratch=(), limit=32):
+def call(kernel, name, outs, *args, scalars=0, after=(), cost=0.0, scratch=(), limit=32, gate=()):
     shapes = [jax.ShapeDtypeStruct(shape, dtype) for shape, dtype in outs]
     vmem = pl.BlockSpec(memory_space=pltpu.VMEM)
     smem = pl.BlockSpec(memory_space=pltpu.SMEM)
-    count, rest = len(args), len(args) + len(after)
+    count, rest = len(args), len(args) + len(after) + len(gate)
+    through = rest + len(shapes)
     out_spec = vmem
     if scratch:
         vmem = pl.BlockSpec(memory_space=pl.ANY)
 
     def body(*refs):
-        kernel(*refs[:count], *refs[rest:])
+        kernel(*refs[:count], *refs[rest:through], *refs[through + len(gate) :])
 
     return pl.pallas_call(
         body,
-        out_shape=shapes,
-        in_specs=[smem] * scalars + [vmem] * (count - scalars) + [pl.BlockSpec(memory_space=pl.ANY)] * len(after),
-        out_specs=[out_spec] * len(shapes),
+        out_shape=shapes + [jax.ShapeDtypeStruct(a.shape, a.dtype) for a in gate],
+        in_specs=[smem] * scalars
+        + [vmem] * (count - scalars)
+        + [pl.BlockSpec(memory_space=pl.ANY)] * (len(after) + len(gate)),
+        out_specs=[out_spec] * len(shapes) + [pl.BlockSpec(memory_space=pl.ANY)] * len(gate),
+        input_output_aliases={count + len(after) + i: len(shapes) + i for i in range(len(gate))},
         scratch_shapes=list(scratch),
         compiler_params=pltpu.CompilerParams(vmem_limit_bytes=limit * 2**20),
         cost_estimate=pl.CostEstimate(flops=int(cost * 10**9), bytes_accessed=0, transcendentals=0),
         name=name,
-    )(*args, *after)
+    )(*args, *after, *gate)
 
 
 def on_device(
@@ -556,43 +559,40 @@
         pairs = [(2 * i + r, 2 * far[i] + r if i in far else 2 * i + 1 - r) for i in range(size) for r in range(2)]
         return lax.ppermute(array, ("seq", "rep"), pairs)
 
+    def inward(array):
+        return lax.ppermute(array, "seq", [(0, 1), (3, 2)])
+
     other_c = to_core(cand_c)
     kv_shape = (tokens, prefix_key_rows.shape[1] * prefix_key_rows.shape[2])
-    cum, total, load = call(
-        head_kernel,
-        "head",
-        [((tokens, heads), F32), ((8, heads), F32), ((tokens + 16, cols + state), BF16)],
+    cum, total, b2, kv, *loads = call(
+        inputs_kernel,
+        "inputs",
+        [((tokens, heads), F32), ((8, heads), F32), ((tokens, groups * state), BF16), (kv_shape, BF16)]
+        + [
+            (
+                (
+                    tokens + (16 if q == 0 else 0),
+                    cols + len(fresh) * state + (kv_shape[1] if q == 1 else 0),
+                ),
+                BF16,
+            )
+            for q, fresh in enumerate(plan)
+        ],
         prefix_x,
         prefix_b,
         prefix_decay.T,
+        prefix_key_rows,
+        prefix_values,
         scratch=[
-            pltpu.VMEM((tokens, cols), BF16),
+            pltpu.VMEM(prefix_x.shape, BF16),
             pltpu.VMEM(prefix_b.shape, BF16),
             pltpu.VMEM((heads, tokens), F32),
-            pltpu.SemaphoreType.DMA((3,)),
+            pltpu.VMEM(prefix_key_rows.shape, BF16),
+            pltpu.VMEM(prefix_values.shape, BF16),
+            pltpu.SemaphoreType.DMA((5,)),
         ],
         limit=60,
     )
-    b2, kv, *parts = call(
-        local_kernel,
-        "local_state",
-        [((tokens, groups * state), BF16), (kv_shape, BF16)]
-        + [((state, cols), F32)] * CHUNKS
-        + [
-            ((tokens, cols + len(fresh) * state + (kv_shape[1] if q == 1 else 0)), BF16)
-            for q, fresh in enumerate(plan)
-            if q
-        ],
-        prefix_x,
-        prefix_b,
-        cum,
-        load,
-        prefix_key_rows,
-        prefix_values,
-    )
-    local, loads = parts[:CHUNKS], [load] + parts[CHUNKS:]
-    got = [to_neighbour(a) for a in loads]
-    first_of = {g: q for q, fresh in enumerate(plan) for g in fresh}
     (cc,) = call(
         projections_kernel,
         "projections",
@@ -600,10 +600,10 @@
         prefix_c,
         cand_c,
         other_c,
-        after=(kv,),
+        after=(cum,),
     )
-
-    def intra(mark):
+    first_of = {g: q for q, fresh in enumerate(plan) for g in fresh}
+    def intra(mark, cc):
         return call(
             functools.partial(intra_kernel, groups=groups),
             "intra",
@@ -614,7 +614,8 @@
             cum,
             skip,
             after=(mark,),
-        )[0]
+            gate=(loads[1],),
+        )
 
     def candidates(mark):
         return call(
@@ -660,9 +661,13 @@
 
     shared = dict(cols=cols, heads=heads, tokens=tokens)
     if size == 4:
-        near_cc = to_neighbour(cc)
-        other, middle, carried, cands, outer, outs, raws = {}, {}, {}, {}, {}, [], []
-        rows = {}
+        mark = cc
+        middle, carried, cands, outer, outs, raws = {}, {}, {}, {}, [], []
+        rows = {"cc": cc}
+
+        def inputs_of(q):
+            p = first_of[q * groups // CHUNKS]
+            return got[q], got[p], loads[q], loads[p]
 
         def first(q, mark):
             extra = [((8, wide), F32), ((8, wide), F32), ((8, heads), F32)] if q == 0 else []
@@ -670,22 +675,26 @@
                 functools.partial(first_kernel, q=q, groups=groups, state=state, **shared),
                 "first",
                 extra
-                + [((state, cols), F32), ((state + (16 if q == 0 else 0), cols), BF16)]
+                + [((state + (16 if q == 0 else 0), cols), BF16)]
                 + ([((2 * tokens, kv_shape[1]), BF16)] if q == 1 else []),
-                got[q],
-                got[first_of[q * groups // CHUNKS]],
-                local[q],
+                *inputs_of(q),
                 *([total] if q == 0 else [rows["own"], rows["near"]]),
                 *([kv] if q == 1 else []),
                 after=(mark,),
                 cost=FIRST_COST if q == 1 else 0.0,
+                gate=[(rows["cc"],), loads[2:], (), ()][q],
             )
             if q == 0:
+                *results, rows["cc"] = results
+                rows["near_cc"] = to_neighbour(rows["cc"])
+            elif q == 1:
+                *results, loads[2], loads[3] = results
+                got.extend((to_neighbour(loads[2]), inward(loads[3])))
+            if q == 0:
                 rows["own"], rows["near"], rows["near_total"], *results = results
-            other[q] = results[0]
-            middle[q] = between_inner(results[1])
+            middle[q] = between_inner(results[0])
             if q == 1:
-                rows["kv"] = results[2]
+                rows["kv"] = results[1]
             return results[0]
 
         def second(q, mark):
@@ -696,14 +705,14 @@
                 + [
                     ((tokens, cols), F32),
                     ((2 * steps, cols), F32),
-                    ((tokens + 2 * steps + (16 if q == 0 else 0), cols), BF16),
+                    ((tokens + 2 * steps + [16, 2 * tokens * kv_shape[1] // cols, 0, 0][q], cols), BF16),
                 ],
                 middle[q],
-                other[q],
-                local[q],
+                *inputs_of(q),
                 rows["own"],
-                cc,
-                near_cc,
+                rows["cc"],
+                rows["near_cc"],
+                *([far_kv] if q == 1 else []),
                 *([total, rows["near_total"]] if q == 0 else [rows["later"]]),
                 after=(mark,),
                 cost=SECOND_COST,
@@ -731,7 +740,7 @@
                 *([] if q == 0 else [rows["outer"]]),
                 *(outs + raws if final else []),
                 after=(mark,),
-                cost=0.3,
+                cost=THIRD_COST,
             )
             if final:
                 return results
@@ -741,34 +750,42 @@
             raws.append(results[1])
             return results[0]
 
-        mark = first(0, cc)
+        base, loads[1] = intra(cc, cc)
+        got = [to_neighbour(a) for a in loads[:2]]
+        mark = first(0, base)
         mark = first(1, mark)
         far_kv = between_inner(rows["kv"])
-        outer_kv = to_neighbour(far_kv)
-        mark = base = intra(mark)
+        mark = second(0, mark)
         mark = first(2, mark)
+        mark = second(1, mark)
+        mark = first(3, mark)
         cand_base, cand_fade = candidates(mark)
-        mark = second(0, cand_base)
-        mark = first(3, mark)
-        mark = second(1, mark)
-        mark = third(0, mark)
-        mark, finish_attend = attend(mark, [rows["kv"], far_kv, outer_kv], True)
+        mark = third(0, cand_base)
         mark = second(2, mark)
+        mark = third(1, mark)
+        mark, finish_attend = attend(mark, [rows["kv"], far_kv, outer[1]], True)
+        mark = second(3, mark)
         mark = cand_attn = finish_attend(mark)
-        mark = third(1, mark)
-        mark = second(3, mark)
         mark = third(2, mark)
         results = third(3, mark)
         prefix_out, keep, give = results
     else:
+        got = [to_neighbour(a) for a in loads]
         halves = [kv, got[1][:, -kv_shape[1] :]]
         for level in range(1, levels):
             mirrored = to_mirror(halves[0], level)
             halves = [halves[0], halves[1], mirrored, to_neighbour(mirrored)]
             if level < levels - 1:
                 halves = [jnp.concatenate([halves[0], halves[2]]), jnp.concatenate([halves[1], halves[3]])]
-        mark = base = intra(cc)
-        own, start = dict(enumerate(local)), {}
+        base, loads[1] = intra(cc, cc)
+        mark = base
+        own = call(
+            functools.partial(own_kernel, cols=cols, groups=groups, state=state),
+            "own",
+            [((state, cols), F32)] * CHUNKS,
+            *loads,
+        )
+        own, start = dict(enumerate(own)), {}
         before = None
         near, far = {}, {}
         outs, raws = [], []

time: 55.8 us -> 53.8 us (0.964)
  waiting for transfers between devices: 13.5 us -> 10.3 us
  local copies, waits for them, and re-layouts: 5.84 us -> 3.02 us
  starting transfers between devices: 20.3 us -> 23 us
  Pallas kernels: 14.3 us -> 15.2 us
    ppermute x10 -> x8, waiting for transfers between devices: 10.9 us -> 7.73 us  [to_neighbour(): return lax.ppermute(array, 'seq', [(i, i ^ 1) for i in range(size)])]
    unnamed x40 -> x44, local copies, waits for them, and re-layouts: 5.84 us -> 3.02 us
    ppermute x0 -> x1, starting transfers between devices: none -> 2.43 us  [inward(): return lax.ppermute(array, 'seq', [(0, 1), (3, 2)])]
    pallas_call x20 -> x19, Pallas kernels: 14.3 us -> 15.2 us  [call(): pl.pallas_call(body, out_shape=shapes + [jax.ShapeDtypeStruct(a.shape, a....]
    ppermute x10 -> x8, starting transfers between devices: 19.7 us -> 20.2 us  [to_neighbour(): return lax.ppermute(array, 'seq', [(i, i ^ 1) for i in range(size)])]
  transfers between devices with their start and end apart: 18 -> 17, of which waited for: 9 -> 7; matrix products, arithmetic and copies ran while one was open for 0% -> 0% of each run, Pallas kernels for 18% -> 20%
where the time goes in v4:
time: 53.8 us; the launch traced here: 53.2 us
  starting transfers between devices  23 us (43%)
  Pallas kernels  15.2 us (28%)
  waiting for transfers between devices  10.3 us (19%)
  local copies, waits for them, and re-layouts  3.02 us (6%)
  between operations  1.67 us (3%)
    ppermute x8, starting transfers between devices, to_neighbour(): return lax.ppermute(array, 'seq', [(i, i ^ 1) for i in range(size)])  20.2 us
    pallas_call x19, Pallas kernels, call(): pl.pallas_call(body, out_shape=shapes + [jax.ShapeDtypeStruct(a.shape, a....  15.2 us
    ppermute x8, waiting for transfers between devices, to_neighbour(): return lax.ppermute(array, 'seq', [(i, i ^ 1) for i in range(size)])  7.73 us
    unnamed x44, local copies, waits for them, and re-layouts  3.02 us
    ppermute x3, waiting for transfers between devices, to_core(): return lax.ppermute(array, 'rep', [(0, 1), (1, 0)])  2.6 us
    ppermute x1, starting transfers between devices, inward(): return lax.ppermute(array, 'seq', [(0, 1), (3, 2)])  2.43 us
  transfers between devices with their start and end apart: 17, of which 7 were waited for; matrix products, arithmetic and copies ran while one was open for 0% of the time, Pallas kernels for 20%

profile of v4, /device:TPU:0, one launch (start us, length us, event | category | flops | bytes accessed | tf_op | source)
XLA Modules:
  0.0 53.2 jit_solution(1249902182209993014)
XLA Ops:
  0.7 3.0 %inputs.1 = (f32[128,32]{1,0:T(8,128)}, f32[8,32]{1,0:T(8,128)}, bf16[128,512]{1,0:T(8,128)(2,1)}, bf16[128,256]{1,0:T(8,128)(2,1)}, bf16[144,768]{1,0:T(8,128)(...) custom-call(bf16[128,2048]{1,0:T(8,128)(2,1)} %refs_0_.8, ...), custom_call_target="tpu_custom_call" | custom-call | tf_op jit(solution)/shard_map/inputs/pallas_call | solution.py:504
  3.6 3.1 %collective-permute-start.2 = (bf16[144,768]{1,0:T(8,128)(2,1)}, bf16[144,768]{1,0:T(8,128)(2,1)S(1)}, u32[]{:S(2)}, u32[]{:S(2)}) collective-permute-start(bf16[144,768]{1,0:T(8,128)(2,1)} %get-tuple-element.51.refs_2_.refs_3_.refs_4_), channel_id=1, source_target_pairs={{0,4},{4,0},{8,12},{12,8},{1,5},{5,1},{9,13},{13,9},{2,6},{6,2},{1... | collective-permute-start | bytes 663560 | tf_op jit(solution)/shard_map/ppermute | solution.py:552
  6.7 0.0 collective-permute-start
  6.7 1.3 %collective-permute-done.refs_2_ = bf16[1,32,4,256]{3,2,1,0:T(4,128)(2,1)S(1)} collective-permute-done((bf16[1,32,4,256]{3,2,1,0:T(4,128)(2,1)S(1)}, bf16[1,32,4,256]{3,2,1,0:T(4,128)(2,1)S(1)}, u32[]{:S(2)}, u32[]{:S(2)}) %collective-permute-start) | collective-permute-done | bytes 65568 | tf_op jit(solution)/shard_map/ppermute | solution.py:549
  8.0 0.8 %copy-done.1 = f32[128,32]{1,0:T(8,128)S(1)} copy-done((f32[128,32]{1,0:T(8,128)S(1)}, f32[128,32]{1,0:T(8,128)}, u32[]{:S(2)}) %copy-start.1) | copy-done | bytes 16408
  8.8 0.6 %projections.1.refs_2_.refs_5_.refs_6_ = bf16[192,512]{1,0:T(8,128)(2,1)S(1)} custom-call(bf16[128,2,256]{2,1,0:T(2,128)(2,1)S(1)} %copy-done.13, bf16[1,32,4,256]{3,2,1,0:T(4,128)(2,1)S(1)} %copy-done.9, bf16[1,32,4,256]{3,2,1,0:T(4,128)(2,1)S(1)} %collective-permute-done.refs_2_, f32[128,32]{1,0:T(8,128)S(1)} %copy-done.1), custom_call_target="tpu_custom_call" | custom-call | tf_op jit(solution)/shard_map/projections/pallas_call | solution.py:504
  9.4 0.0 copy-start.21
  9.4 0.3 copy-done.2
  9.7 0.1 copy-done.5
  9.8 0.1 copy-done.12
  9.9 0.2 copy-done.21
  10.1 1.0 %intra.1 = (f32[128,2048]{1,0:T(8,128)S(1)}, bf16[128,768]{1,0:T(8,128)(2,1)S(1)}) custom-call(bf16[128,2048]{1,0:T(8,128)(2,1)S(1)} %copy-done.3, bf16[128,512]{1,0:T(8,128)(2,1)S(1)} %copy-done.12, bf16[192,512]{1,0:T(8,128)(2,1)S(1)} %projections.1.refs_2_.refs_5_.refs_6_, f32[128,32]{1,0:T(8,128)S(1)} %copy-done.2, ...), custom_call_target="tpu_custom_call", output_to_operand_aliasing={{1}: (6, {})} | custom-call | tf_op jit(solution)/shard_map/intra/pallas_call | solution.py:504
  11.1 0.1 collective-permute-start.1
  11.2 1.1 %collective-permute-done.2.refs_0_.refs_1_.refs_2_ = bf16[144,768]{1,0:T(8,128)(2,1)S(1)} collective-permute-done((bf16[144,768]{1,0:T(8,128)(2,1)}, bf16[144,768]{1,0:T(8,128)(2,1)S(1)}, u32[]{:S(2)}, u32[]{:S(2)}) %collective-permute-start.2) | collective-permute-done | bytes 221216 | tf_op jit(solution)/shard_map/ppermute | solution.py:552
  12.4 0.5 first.4
  12.9 0.1 collective-permute-start.8
  12.9 3.3 %collective-permute-start.6 = (bf16[192,512]{1,0:T(8,128)(2,1)S(1)}, bf16[192,512]{1,0:T(8,128)(2,1)S(1)}, u32[]{:S(2)}, u32[]{:S(2)}) collective-permute-start(bf16[192,512]{1,0:T(8,128)(2,1)S(1)} %get-tuple-element.63.refs_6_), channel_id=1, source_target_pairs={{0,4},{4,0},{8,12},{12,8},{1,5},{5,1},{9,13},{13,9},{2,6},{6,2},{1... | collective-permute-start | bytes 589832 | tf_op jit(solution)/shard_map/ppermute | solution.py:552
  16.2 2.7 %collective-permute-done.1.refs_0_.refs_1_ = bf16[128,768]{1,0:T(8,128)(2,1)S(1)} collective-permute-done((bf16[128,768]{1,0:T(8,128)(2,1)S(1)}, bf16[128,768]{1,0:T(8,128)(2,1)S(1)}, u32[]{:S(2)}, u32[]{:S(2)}) %collective-permute-start.1) | collective-permute-done | bytes 196640 | tf_op jit(solution)/shard_map/ppermute | solution.py:552
  18.9 0.3 first.5
  19.3 0.1 collective-permute-start.5
  19.4 3.1 %collective-permute-start.4 = (bf16[128,768]{1,0:T(8,128)(2,1)S(1)}, bf16[128,768]{1,0:T(8,128)(2,1)S(1)}, u32[]{:S(2)}, u32[]{:S(2)}) collective-permute-start(bf16[128,768]{1,0:T(8,128)(2,1)S(1)} %get-tuple-element.61.refs_2_.refs_3_.refs_4_), channel_id=1, source_target_pairs={{0,4},{4,0},{8,12},{12,8},{1,5},{5,1},{9,13},{13,9},{2,6},{6,2},{1... | collective-permute-start | bytes 589832 | tf_op jit(solution)/shard_map/ppermute | solution.py:552
  22.5 0.0 collective-permute-start.7
  22.5 0.0 collective-permute-done.6.refs_7_
  22.5 2.4 %collective-permute-start.3 = (bf16[128,512]{1,0:T(8,128)(2,1)S(1)}, bf16[128,512]{1,0:T(8,128)(2,1)S(1)}, u32[]{:S(2)}, u32[]{:S(2)}) collective-permute-start(bf16[128,512]{1,0:T(8,128)(2,1)S(1)} %get-tuple-element.60.refs_2_.refs_3_), channel_id=1, source_target_pairs={{0,4},{12,8},{1,5},{13,9},{2,6},{14,10},{3,7},{15,11},{16,20},{28,... | collective-permute-start | bytes 393224 | tf_op jit(solution)/shard_map/ppermute | solution.py:563
  24.9 0.0 collective-permute-done.8.refs_0_
  24.9 0.8 %second.4 = (f32[8,2048]{1,0:T(8,128)S(1)}, f32[128,512]{1,0:T(8,128)S(1)}, f32[64,512]{1,0:T(8,128)S(1)}, bf16[208,512]{1,0:T(8,128)(2,1)S(1)}) custom-call(bf16[272,512]{1,0:T(8,128)(2,1)S(1)} %collective-permute-done.8.refs_0_, bf16[144,768]{1,0:T(8,128)(2,1)S(1)} %collective-permute-done.2.refs_0_.refs_1_.refs_2_, ...), custom_call_target="tpu_custom_call" | custom-call | flops 1000000000 | tf_op jit(solution)/shard_map/second/pallas_call | solution.py:504
  25.7 0.1 collective-permute-start.11
  25.8 0.9 %collective-permute-done.4.refs_0_.refs_1_.refs_2_ = bf16[128,768]{1,0:T(8,128)(2,1)S(1)} collective-permute-done((bf16[128,768]{1,0:T(8,128)(2,1)S(1)}, bf16[128,768]{1,0:T(8,128)(2,1)S(1)}, u32[]{:S(2)}, u32[]{:S(2)}) %collective-permute-start.4) | collective-permute-done | bytes 196640 | tf_op jit(solution)/shard_map/ppermute | solution.py:552
  26.7 0.3 first.6.refs_10_
  27.0 0.1 collective-permute-start.12
  27.1 0.0 collective-permute-done.7.refs_8_.refs_1_
  27.1 0.0 collective-permute-done.5.refs_0_
  27.1 0.7 %second.5 = (f32[128,512]{1,0:T(8,128)S(1)}, f32[64,512]{1,0:T(8,128)S(1)}, bf16[320,512]{1,0:T(8,128)(2,1)S(1)}) custom-call(bf16[256,512]{1,0:T(8,128)(2,1)S(1)} %collective-permute-done.5.refs_0_, bf16[128,768]{1,0:T(8,128)(2,1)S(1)} %collective-permute-done.1.refs_0_.refs_1_, bf16[144,768]{1,0:T(8,128)(2,1)S(1)} %collective-permute-done.2.refs_0_.refs_1_.refs_2_, ...), custom_call_target="tpu_custom_call" | custom-call | flops 1000000000 | tf_op jit(solution)/shard_map/second/pallas_call | solution.py:504
  27.8 4.4 %collective-permute-start.10 = (bf16[320,512]{1,0:T(8,128)(2,1)S(1)}, bf16[320,512]{1,0:T(8,128)(2,1)S(1)}, u32[]{:S(2)}, u32[]{:S(2)}) collective-permute-start(bf16[320,512]{1,0:T(8,128)(2,1)S(1)} %get-tuple-element.69), channel_id=1, source_target_pairs={{0,4},{4,0},{8,12},{12,8},{1,5},{5,1},{9,13},{13,9},{2,6},{6,2},{1... | collective-permute-start | bytes 983048 | tf_op jit(solution)/shard_map/ppermute | solution.py:552
  32.3 0.0 collective-permute-done.3.refs_0_.refs_1_
  32.3 0.3 first.7.refs_5_
  32.6 0.1 collective-permute-start.9
  32.7 0.5 copy-done.8
  33.2 1.8 %candidates.1 = (f32[32,4096]{1,0:T(8,128)S(1)}, f32[32,4096]{1,0:T(8,128)S(1)}) custom-call(bf16[1,32,4096]{2,1,0:T(8,128)(2,1)S(1)} %copy-done.8, bf16[1,32,4,256]{3,2,1,0:T(4,128)(2,1)S(1)} %copy-done.15, bf16[1,32,4,256]{3,2,1,0:T(4,128)(2,1)S(1)} %copy-done.9, f32[1,32,64]{2,1,0:T(8,128)S(1)} %copy-done.19, f32[1,128]{1,0:T(1,128)S(1)} %bitcast.3, ...), custom_call_target="tpu_custom_call" | custom-call | tf_op jit(solution)/shard_map/candidates/pallas_call | solution.py:504
  35.0 0.0 collective-permute-done.11.refs_0_
  35.0 0.3 third.4
  35.3 0.0 collective-permute-done.12.refs_0_
  35.3 0.7 %second.6 = (f32[128,512]{1,0:T(8,128)S(1)}, f32[64,512]{1,0:T(8,128)S(1)}, bf16[192,512]{1,0:T(8,128)(2,1)S(1)}) custom-call(bf16[256,512]{1,0:T(8,128)(2,1)S(1)} %collective-permute-done.12.refs_0_, bf16[128,768]{1,0:T(8,128)(2,1)S(1)} %collective-permute-done.4.refs_0_.refs_1_.refs_2_, ...), custom_call_target="tpu_custom_call" | custom-call | flops 1000000000 | tf_op jit(solution)/shard_map/second/pallas_call | solution.py:504
  36.0 3.4 %collective-permute-start.14 = (bf16[192,512]{1,0:T(8,128)(2,1)S(1)}, bf16[192,512]{1,0:T(8,128)(2,1)S(1)}, u32[]{:S(2)}, u32[]{:S(2)}) collective-permute-start(bf16[192,512]{1,0:T(8,128)(2,1)S(1)} %get-tuple-element.81), channel_id=1, source_target_pairs={{0,4},{4,0},{8,12},{12,8},{1,5},{5,1},{9,13},{13,9},{2,6},{6,2},{1... | collective-permute-start | bytes 589832 | tf_op jit(solution)/shard_map/ppermute | solution.py:552
  39.5 1.3 %collective-permute-done.10.refs_0_.refs_2_ = bf16[320,512]{1,0:T(8,128)(2,1)S(1)} collective-permute-done((bf16[320,512]{1,0:T(8,128)(2,1)S(1)}, bf16[320,512]{1,0:T(8,128)(2,1)S(1)}, u32[]{:S(2)}, u32[]{:S(2)}) %collective-permute-start.10) | collective-permute-done | bytes 327712 | tf_op jit(solution)/shard_map/ppermute | solution.py:552
  40.8 0.2 third.5
  41.1 0.0 copy-start.10
  41.1 0.0 copy-start.11
  41.1 0.0 copy-start.14
  41.1 0.1 collective-permute-start.15
  41.2 0.0 collective-permute-done.9.refs_0_
  41.2 0.0 copy-start.17
  41.2 0.0 copy-start.18
  41.2 0.7 %second.7 = (f32[128,512]{1,0:T(8,128)S(1)}, f32[64,512]{1,0:T(8,128)S(1)}, bf16[192,512]{1,0:T(8,128)(2,1)S(1)}) custom-call(bf16[256,512]{1,0:T(8,128)(2,1)S(1)} %collective-permute-done.9.refs_0_, bf16[128,512]{1,0:T(8,128)(2,1)S(1)} %collective-permute-done.3.refs_0_.refs_1_, bf16[128,768]{1,0:T(8,128)(2,1)S(1)} %collective-permute-done.4.refs_0_.refs_1_.refs_2_, ...), custom_call_target="tpu_custom_call" | custom-call | flops 1000000000 | tf_op jit(solution)/shard_map/second/pallas_call | solution.py:504
  41.9 2.6 %collective-permute-start.13 = (bf16[192,512]{1,0:T(8,128)(2,1)S(1)}, bf16[192,512]{1,0:T(8,128)(2,1)S(1)}, u32[]{:S(2)}, u32[]{:S(2)}) collective-permute-start(bf16[192,512]{1,0:T(8,128)(2,1)S(1)} %get-tuple-element.78), channel_id=1, source_target_pairs={{0,4},{4,0},{8,12},{12,8},{1,5},{5,1},{9,13},{13,9},{2,6},{6,2},{1... | collective-permute-start | bytes 589832 | tf_op jit(solution)/shard_map/ppermute | solution.py:552
  45.1 0.0 collective-permute-done.15.refs_7_
  45.2 1.9 %attend.1.refs_7_ = bf16[1,32,16,128]{3,2,1,0:T(8,128)(2,1)} custom-call(s32[1]{0:T(128)S(6)} %copy.26.refs_0_, bf16[1,32,16,128]{3,2,1,0:T(8,128)(2,1)S(1)} %copy-done.14, bf16[1,32,2,128]{3,2,1,0:T(2,128)(2,1)S(1)} %copy-done.17, bf16[1,32,2,128]{3,2,1,0:T(2,128)(2,1)S(1)} %copy-done.18, bf16[128,2,128]{2,1,0:T(2,128)(2,1)S(1)} %copy-done.10, ...), custom_call_target="tpu_custom_call" | custom-call | tf_op jit(solution)/shard_map/attend/pallas_call | solution.py:504
  47.1 0.0 collective-permute-done.14.refs_0_
  47.1 0.9 %copy-done.7 = bf16[1,32,16,128]{3,2,1,0:T(8,128)(2,1)S(1)} copy-done((bf16[1,32,16,128]{3,2,1,0:T(8,128)(2,1)S(1)}, bf16[1,32,16,128]{3,2,1,0:T(8,128)(2,1)}, u32[]{:S(2)}) %copy-start.7) | copy-done | bytes 131096
  48.0 0.2 third.6
  48.3 1.7 %collective-permute-done.13.refs_0_ = bf16[192,512]{1,0:T(8,128)(2,1)S(1)} collective-permute-done((bf16[192,512]{1,0:T(8,128)(2,1)S(1)}, bf16[192,512]{1,0:T(8,128)(2,1)S(1)}, u32[]{:S(2)}, u32[]{:S(2)}) %collective-permute-start.13) | collective-permute-done | bytes 196640 | tf_op jit(solution)/shard_map/ppermute | solution.py:552
  50.0 1.0 %third.7 = (bf16[128,2048]{1,0:T(8,128)(2,1)}, f32[32,2048]{1,0:T(8,128)S(1)}, bf16[32,2048]{1,0:T(8,128)(2,1)S(1)}) custom-call(bf16[192,512]{1,0:T(8,128)(2,1)S(1)} %collective-permute-done.13.refs_0_, f32[128,512]{1,0:T(8,128)S(1)} %get-tuple-element.79.refs_8_.refs_1_, f32[64,512]{1,0:T(8,128)S(1)} %get-tuple-element.80.refs_2_, ...), custom_call_target="tpu_custom_call" | custom-call | flops 300000000 | tf_op jit(solution)/shard_map/third/pallas_call | solution.py:504
  51.1 1.3 %collective-permute-done.16.refs_4_ = bf16[32,2048]{1,0:T(8,128)(2,1)S(1)} collective-permute-done((bf16[32,2048]{1,0:T(8,128)(2,1)S(1)}, bf16[32,2048]{1,0:T(8,128)(2,1)S(1)}, u32[]{:S(2)}, u32[]{:S(2)}) %collective-permute-start.16) | collective-permute-done | bytes 131104 | tf_op jit(solution)/shard_map/ppermute | solution.py:549
  52.4 0.8 %close.1 = bf16[1,32,4096]{2,1,0:T(8,128)(2,1)} custom-call(s32[1]{0:T(128)S(6)} %copy.26.refs_0_, f32[32,4096]{1,0:T(8,128)S(1)} %get-tuple-element.73.refs_6_.refs_1_, f32[32,4096]{1,0:T(8,128)S(1)} %get-tuple-element.88.refs_2_, f32[32,2048]{1,0:T(8,128)S(1)} %get-tuple-element.89.refs_3_, bf16[32,2048]{1,0:T(8,128)(2,1)S(1)} %collective-permute-done.16.refs_4_), custom_call_target="tpu_custom_call" | custom-call | tf_op jit(solution)/shard_map/close/pallas_call | solution.py:504
  (33 shorter events, 0.1 us)
Async XLA Ops:
  0.6 6.1 %copy-start.9 = (bf16[1,32,4,256]{3,2,1,0:T(4,128)(2,1)S(1)}, bf16[1,32,4,256]{3,2,1,0:T(4,128)(2,1)}, u32[]{:S(2)}) copy-start(bf16[1,32,4,256]{3,2,1,0:T(4,128)(2,1)} %refs_2_.2) | copy-start | bytes 196612
  0.6 7.4 %copy-start.13 = (bf16[128,2,256]{2,1,0:T(2,128)(2,1)S(1)}, bf16[128,2,256]{2,1,0:T(2,128)(2,1)}, u32[]{:S(2)}) copy-start(bf16[128,2,256]{2,1,0:T(2,128)(2,1)} %refs_0_.7) | copy-start | bytes 393220
  0.7 8.8 %copy-start.3 = (bf16[128,2048]{1,0:T(8,128)(2,1)S(1)}, bf16[128,2048]{1,0:T(8,128)(2,1)}, u32[]{:S(2)}) copy-start(bf16[128,2048]{1,0:T(8,128)(2,1)} %refs_0_.8) | copy-start | bytes 1572868
  3.6 8.7 %collective-permute-start.2 = (bf16[144,768]{1,0:T(8,128)(2,1)}, bf16[144,768]{1,0:T(8,128)(2,1)S(1)}, u32[]{:S(2)}, u32[]{:S(2)}) collective-permute-start(bf16[144,768]{1,0:T(8,128)(2,1)} %get-tuple-element.51.refs_2_.refs_3_.refs_4_), channel_id=1, source_target_pairs={{0,4},{4,0},{8,12},{12,8},{1,5},{5,1},{9,13},{13,9},{2,6},{6,2},{1... | collective-permute-start | bytes 663560 | tf_op jit(solution)/shard_map/ppermute | solution.py:552
  6.7 1.3 %collective-permute-start = (bf16[1,32,4,256]{3,2,1,0:T(4,128)(2,1)S(1)}, bf16[1,32,4,256]{3,2,1,0:T(4,128)(2,1)S(1)}, u32[]{:S(2)}, u32[]{:S(2)}) collective-permute-start(bf16[1,32,4,256]{3,2,1,0:T(4,128)(2,1)S(1)} %copy-done.9), channel_id=1, source_target_pairs={{0,1},{1,0},{2,3},{3,2},{4,5},{5,4},{6,7},{7,6},{8,9},{9,8},{10,11... | collective-permute-start | bytes 196616 | tf_op jit(solution)/shard_map/ppermute | solution.py:549
  8.0 0.8 %copy-start.1 = (f32[128,32]{1,0:T(8,128)S(1)}, f32[128,32]{1,0:T(8,128)}, u32[]{:S(2)}) copy-start(f32[128,32]{1,0:T(8,128)} %get-tuple-element.48.refs_3_.refs_4_) | copy-start | bytes 49156
  8.8 0.8 %copy-start.2 = (f32[128,32]{1,0:T(8,128)S(1)}, f32[128,32]{1,0:T(8,128)}, u32[]{:S(2)}) copy-start(f32[128,32]{1,0:T(8,128)} %get-tuple-element.48.refs_3_.refs_4_) | copy-start | bytes 49156
  8.8 1.0 %copy-start.5 = (bf16[128,768]{1,0:T(8,128)(2,1)S(1)}, bf16[128,768]{1,0:T(8,128)(2,1)}, u32[]{:S(2)}) copy-start(bf16[128,768]{1,0:T(8,128)(2,1)} %get-tuple-element.49.refs_6_) | copy-start | bytes 589828
  8.8 1.0 %copy-start.12 = (bf16[128,512]{1,0:T(8,128)(2,1)S(1)}, bf16[128,512]{1,0:T(8,128)(2,1)}, u32[]{:S(2)}) copy-start(bf16[128,512]{1,0:T(8,128)(2,1)} %get-tuple-element.47.refs_1_) | copy-start | bytes 393220
  9.4 0.7 %copy-start.21 = (f32[128]{0:T(128)S(1)}, f32[128]{0:T(128)}, u32[]{:S(2)}) copy-start(f32[128]{0:T(128)} %param.19) | copy-start | bytes 1540
  10.1 2.3 %copy-start.4 = (bf16[144,768]{1,0:T(8,128)(2,1)S(1)}, bf16[144,768]{1,0:T(8,128)(2,1)}, u32[]{:S(2)}) copy-start(bf16[144,768]{1,0:T(8,128)(2,1)} %get-tuple-element.51.refs_2_.refs_3_.refs_4_) | copy-start | bytes 663556
  11.1 1.3 %copy-start.20 = (f32[8,32]{1,0:T(8,128)S(1)}, f32[8,32]{1,0:T(8,128)}, u32[]{:S(2)}) copy-start(f32[8,32]{1,0:T(8,128)} %get-tuple-element.52.refs_4_.refs_8_) | copy-start | bytes 3076
  11.1 7.8 %collective-permute-start.1 = (bf16[128,768]{1,0:T(8,128)(2,1)S(1)}, bf16[128,768]{1,0:T(8,128)(2,1)S(1)}, u32[]{:S(2)}, u32[]{:S(2)}) collective-permute-start(bf16[128,768]{1,0:T(8,128)(2,1)S(1)} %get-tuple-element.50.refs_2_.refs_3_), channel_id=1, source_target_pairs={{0,4},{4,0},{8,12},{12,8},{1,5},{5,1},{9,13},{13,9},{2,6},{6,2},{1... | collective-permute-start | bytes 589832 | tf_op jit(solution)/shard_map/ppermute | solution.py:552
  12.4 6.5 %copy-start = (bf16[128,768]{1,0:T(8,128)(2,1)S(1)}, bf16[128,768]{1,0:T(8,128)(2,1)}, u32[]{:S(2)}) copy-start(bf16[128,768]{1,0:T(8,128)(2,1)} %get-tuple-element.58.refs_8_) | copy-start | bytes 589828
  12.4 6.5 %copy-start.6 = (bf16[128,512]{1,0:T(8,128)(2,1)S(1)}, bf16[128,512]{1,0:T(8,128)(2,1)}, u32[]{:S(2)}) copy-start(bf16[128,512]{1,0:T(8,128)(2,1)} %get-tuple-element.59.refs_9_) | copy-start | bytes 393220
  12.4 6.5 %copy-start.16 = (bf16[128,256]{1,0:T(8,128)(2,1)S(1)}, bf16[128,256]{1,0:T(8,128)(2,1)}, u32[]{:S(2)}) copy-start(bf16[128,256]{1,0:T(8,128)(2,1)} %get-tuple-element.56.refs_6_) | copy-start | bytes 196612
  12.9 12.1 %collective-permute-start.8 = (bf16[272,512]{1,0:T(8,128)(2,1)S(1)}, bf16[272,512]{1,0:T(8,128)(2,1)S(1)}, u32[]{:S(2)}, u32[]{:S(2)}) collective-permute-start(bf16[272,512]{1,0:T(8,128)(2,1)S(1)} %get-tuple-element.57.refs_7_), channel_id=1, source_target_pairs={{0,1},{1,0},{4,8},{5,9},{8,4},{9,5},{12,13},{13,12},{2,3},{3,2},{6... | collective-permute-start | bytes 835592 | tf_op jit(solution)/shard_map/ppermute | solution.py:560
  12.9 9.6 %collective-permute-start.6 = (bf16[192,512]{1,0:T(8,128)(2,1)S(1)}, bf16[192,512]{1,0:T(8,128)(2,1)S(1)}, u32[]{:S(2)}, u32[]{:S(2)}) collective-permute-start(bf16[192,512]{1,0:T(8,128)(2,1)S(1)} %get-tuple-element.63.refs_6_), channel_id=1, source_target_pairs={{0,4},{4,0},{8,12},{12,8},{1,5},{5,1},{9,13},{13,9},{2,6},{6,2},{1... | collective-permute-start | bytes 589832 | tf_op jit(solution)/shard_map/ppermute | solution.py:552
  19.3 7.8 %collective-permute-start.5 = (bf16[256,512]{1,0:T(8,128)(2,1)S(1)}, bf16[256,512]{1,0:T(8,128)(2,1)S(1)}, u32[]{:S(2)}, u32[]{:S(2)}) collective-permute-start(bf16[256,512]{1,0:T(8,128)(2,1)S(1)} %get-tuple-element.62.refs_10_), channel_id=1, source_target_pairs={{0,1},{1,0},{4,8},{5,9},{8,4},{9,5},{12,13},{13,12},{2,3},{3,2},{6... | collective-permute-start | bytes 786440 | tf_op jit(solution)/shard_map/ppermute | solution.py:560
  19.4 7.3 %collective-permute-start.4 = (bf16[128,768]{1,0:T(8,128)(2,1)S(1)}, bf16[128,768]{1,0:T(8,128)(2,1)S(1)}, u32[]{:S(2)}, u32[]{:S(2)}) collective-permute-start(bf16[128,768]{1,0:T(8,128)(2,1)S(1)} %get-tuple-element.61.refs_2_.refs_3_.refs_4_), channel_id=1, source_target_pairs={{0,4},{4,0},{8,12},{12,8},{1,5},{5,1},{9,13},{13,9},{2,6},{6,2},{1... | collective-permute-start | bytes 589832 | tf_op jit(solution)/shard_map/ppermute | solution.py:552
  22.5 4.6 %collective-permute-start.7 = (bf16[256,256]{1,0:T(8,128)(2,1)S(1)}, bf16[256,256]{1,0:T(8,128)(2,1)S(1)}, u32[]{:S(2)}, u32[]{:S(2)}) collective-permute-start(bf16[256,256]{1,0:T(8,128)(2,1)S(1)} %get-tuple-element.64.refs_0_), channel_id=1, source_target_pairs={{0,1},{1,0},{4,8},{5,9},{8,4},{9,5},{12,13},{13,12},{2,3},{3,2},{6... | collective-permute-start | bytes 393224 | tf_op jit(solution)/shard_map/ppermute | solution.py:560
  22.5 9.8 %collective-permute-start.3 = (bf16[128,512]{1,0:T(8,128)(2,1)S(1)}, bf16[128,512]{1,0:T(8,128)(2,1)S(1)}, u32[]{:S(2)}, u32[]{:S(2)}) collective-permute-start(bf16[128,512]{1,0:T(8,128)(2,1)S(1)} %get-tuple-element.60.refs_2_.refs_3_), channel_id=1, source_target_pairs={{0,4},{12,8},{1,5},{13,9},{2,6},{14,10},{3,7},{15,11},{16,20},{28,... | collective-permute-start | bytes 393224 | tf_op jit(solution)/shard_map/ppermute | solution.py:563
  25.7 9.3 %collective-permute-start.11 = (bf16[208,512]{1,0:T(8,128)(2,1)S(1)}, bf16[208,512]{1,0:T(8,128)(2,1)S(1)}, u32[]{:S(2)}, u32[]{:S(2)}) collective-permute-start(bf16[208,512]{1,0:T(8,128)(2,1)S(1)} %get-tuple-element.71), channel_id=1, source_target_pairs={{0,4},{4,0},{8,12},{12,8},{1,5},{5,1},{9,13},{13,9},{2,6},{6,2},{1... | collective-permute-start | bytes 638984 | tf_op jit(solution)/shard_map/ppermute | solution.py:552
  27.0 8.3 %collective-permute-start.12 = (bf16[256,512]{1,0:T(8,128)(2,1)S(1)}, bf16[256,512]{1,0:T(8,128)(2,1)S(1)}, u32[]{:S(2)}, u32[]{:S(2)}) collective-permute-start(bf16[256,512]{1,0:T(8,128)(2,1)S(1)} %first.6.refs_10_), channel_id=1, source_target_pairs={{0,1},{1,0},{4,8},{5,9},{8,4},{9,5},{12,13},{13,12},{2,3},{3,2},{6... | collective-permute-start | bytes 786440 | tf_op jit(solution)/shard_map/ppermute | solution.py:560
  27.8 13.0 %collective-permute-start.10 = (bf16[320,512]{1,0:T(8,128)(2,1)S(1)}, bf16[320,512]{1,0:T(8,128)(2,1)S(1)}, u32[]{:S(2)}, u32[]{:S(2)}) collective-permute-start(bf16[320,512]{1,0:T(8,128)(2,1)S(1)} %get-tuple-element.69), channel_id=1, source_target_pairs={{0,4},{4,0},{8,12},{12,8},{1,5},{5,1},{9,13},{13,9},{2,6},{6,2},{1... | collective-permute-start | bytes 983048 | tf_op jit(solution)/shard_map/ppermute | solution.py:552
  32.3 1.0 %copy-start.8 = (bf16[1,32,4096]{2,1,0:T(8,128)(2,1)S(1)}, bf16[1,32,4096]{2,1,0:T(8,128)(2,1)}, u32[]{:S(2)}) copy-start(bf16[1,32,4096]{2,1,0:T(8,128)(2,1)} %refs_0_.9) | copy-start | bytes 786436
  32.3 1.0 %copy-start.15 = (bf16[1,32,4,256]{3,2,1,0:T(4,128)(2,1)S(1)}, bf16[1,32,4,256]{3,2,1,0:T(4,128)(2,1)}, u32[]{:S(2)}) copy-start(bf16[1,32,4,256]{3,2,1,0:T(4,128)(2,1)} %refs_1_.6) | copy-start | bytes 196612
  32.3 1.0 %copy-start.19 = (f32[1,32,64]{2,1,0:T(8,128)S(1)}, f32[1,32,64]{2,1,0:T(8,128)}, u32[]{:S(2)}) copy-start(f32[1,32,64]{2,1,0:T(8,128)} %refs_3_.4) | copy-start | bytes 24580
  32.6 8.6 %collective-permute-start.9 = (bf16[256,512]{1,0:T(8,128)(2,1)S(1)}, bf16[256,512]{1,0:T(8,128)(2,1)S(1)}, u32[]{:S(2)}, u32[]{:S(2)}) collective-permute-start(bf16[256,512]{1,0:T(8,128)(2,1)S(1)} %first.7.refs_5_), channel_id=1, source_target_pairs={{0,1},{1,0},{4,8},{5,9},{8,4},{9,5},{12,13},{13,12},{2,3},{3,2},{6... | collective-permute-start | bytes 786440 | tf_op jit(solution)/shard_map/ppermute | solution.py:560
  36.0 11.1 %collective-permute-start.14 = (bf16[192,512]{1,0:T(8,128)(2,1)S(1)}, bf16[192,512]{1,0:T(8,128)(2,1)S(1)}, u32[]{:S(2)}, u32[]{:S(2)}) collective-permute-start(bf16[192,512]{1,0:T(8,128)(2,1)S(1)} %get-tuple-element.81), channel_id=1, source_target_pairs={{0,4},{4,0},{8,12},{12,8},{1,5},{5,1},{9,13},{13,9},{2,6},{6,2},{1... | collective-permute-start | bytes 589832 | tf_op jit(solution)/shard_map/ppermute | solution.py:552
  41.1 4.1 %copy-start.10 = (bf16[128,2,128]{2,1,0:T(2,128)(2,1)S(1)}, bf16[128,2,128]{2,1,0:T(2,128)(2,1)}, u32[]{:S(2)}) copy-start(bf16[128,2,128]{2,1,0:T(2,128)(2,1)} %refs_4_.3) | copy-start | bytes 196612
  41.1 4.1 %copy-start.11 = (bf16[128,2,128]{2,1,0:T(2,128)(2,1)S(1)}, bf16[128,2,128]{2,1,0:T(2,128)(2,1)}, u32[]{:S(2)}) copy-start(bf16[128,2,128]{2,1,0:T(2,128)(2,1)} %refs_5_.1) | copy-start | bytes 196612
  41.1 4.1 %copy-start.14 = (bf16[1,32,16,128]{3,2,1,0:T(8,128)(2,1)S(1)}, bf16[1,32,16,128]{3,2,1,0:T(8,128)(2,1)}, u32[]{:S(2)}) copy-start(bf16[1,32,16,128]{3,2,1,0:T(8,128)(2,1)} %refs_1_.7) | copy-start | bytes 393220
  41.1 4.0 %collective-permute-start.15 = (bf16[384,256]{1,0:T(8,128)(2,1)S(1)}, bf16[384,256]{1,0:T(8,128)(2,1)S(1)}, u32[]{:S(2)}, u32[]{:S(2)}) collective-permute-start(bf16[384,256]{1,0:T(8,128)(2,1)S(1)} %collect.1.refs_9_.refs_6_), channel_id=1, source_target_pairs={{0,1},{1,0},{2,3},{3,2},{4,5},{5,4},{6,7},{7,6},{8,9},{9,8},{10,11... | collective-permute-start | bytes 589832 | tf_op jit(solution)/shard_map/ppermute | solution.py:549
  41.2 4.0 %copy-start.17 = (bf16[1,32,2,128]{3,2,1,0:T(2,128)(2,1)S(1)}, bf16[1,32,2,128]{3,2,1,0:T(2,128)(2,1)}, u32[]{:S(2)}) copy-start(bf16[1,32,2,128]{3,2,1,0:T(2,128)(2,1)} %refs_2_.3) | copy-start | bytes 49156
  41.2 4.0 %copy-start.18 = (bf16[1,32,2,128]{3,2,1,0:T(2,128)(2,1)S(1)}, bf16[1,32,2,128]{3,2,1,0:T(2,128)(2,1)}, u32[]{:S(2)}) copy-start(bf16[1,32,2,128]{3,2,1,0:T(2,128)(2,1)} %refs_3_.5) | copy-start | bytes 49156
  41.9 8.1 %collective-permute-start.13 = (bf16[192,512]{1,0:T(8,128)(2,1)S(1)}, bf16[192,512]{1,0:T(8,128)(2,1)S(1)}, u32[]{:S(2)}, u32[]{:S(2)}) collective-permute-start(bf16[192,512]{1,0:T(8,128)(2,1)S(1)} %get-tuple-element.78), channel_id=1, source_target_pairs={{0,4},{4,0},{8,12},{12,8},{1,5},{5,1},{9,13},{13,9},{2,6},{6,2},{1... | collective-permute-start | bytes 589832 | tf_op jit(solution)/shard_map/ppermute | solution.py:552
  47.1 0.9 %copy-start.7 = (bf16[1,32,16,128]{3,2,1,0:T(8,128)(2,1)S(1)}, bf16[1,32,16,128]{3,2,1,0:T(8,128)(2,1)}, u32[]{:S(2)}) copy-start(bf16[1,32,16,128]{3,2,1,0:T(8,128)(2,1)} %attend.1.refs_7_) | copy-start | bytes 393220
  51.1 1.3 %collective-permute-start.16 = (bf16[32,2048]{1,0:T(8,128)(2,1)S(1)}, bf16[32,2048]{1,0:T(8,128)(2,1)S(1)}, u32[]{:S(2)}, u32[]{:S(2)}) collective-permute-start(bf16[32,2048]{1,0:T(8,128)(2,1)S(1)} %get-tuple-element.90), channel_id=1, source_target_pairs={{0,1},{1,0},{2,3},{3,2},{4,5},{5,4},{6,7},{7,6},{8,9},{9,8},{10,11... | collective-permute-start | bytes 393224 | tf_op jit(solution)/shard_map/ppermute | solution.py:549

commit v5 on v4

--- a/solution.py
+++ b/solution.py
@@ -224,7 +224,7 @@
             here = slice(g * state, (g + 1) * state)
             fade = spread(jnp.exp(-cum_ref[...]), width, q * heads // CHUNKS, heads // CHUNKS)
             carried = mm(cc_ref[:tokens, here], start.astype(BF16))
-            outs.append((base_ref[:, at] + fade * carried).astype(BF16))
+            outs.append((base_ref[...] + fade * carried).astype(BF16))
             outs.append(mm(cc_ref[tokens:, here], joined.astype(BF16)))
     if last and CHUNKS - 1 in chunks:
         parts = take(2 * (CHUNKS - 1))
@@ -335,12 +335,12 @@
 
 def third_kernel(*refs, q, cols, heads, tokens):
     refs = list(refs)
-    got_ref, carried_ref, cand_ref, base_ref, cum_ref, own_row_ref = refs[:6]
+    got_ref, cand_ref, own_row_ref = refs[:3]
     place = lax.axis_index("seq")
     width = cols * CHUNKS // heads
     at = slice(q * cols, (q + 1) * cols)
     rows = cand_ref.shape[0]
-    refs = refs[6:]
+    refs = refs[3:]
     if q == 0:
         later_row_ref = refs[0]
         later_row = as_row(lines_to_totals(got_ref[tokens + rows :, :heads]), width)
@@ -348,33 +348,44 @@
     else:
         later_row = refs[0][...]
     refs = refs[1:]
-    fade = spread(jnp.exp(-cum_ref[...]), width, q * heads // CHUNKS, heads // CHUNKS)
-    got = got_ref[: tokens + rows, :].astype(F32)
-    carried = jnp.where(place == 3, got[:tokens], carried_ref[...])
     cand = cand_ref[...]
+    got = got_ref[tokens : tokens + rows, :].astype(F32)
     cand = jnp.where(
         place == 3,
-        own_row_ref[:1, at] * got[tokens:] + cand,
-        jnp.where(place == 0, later_row[:1, at] * cand + got[tokens:], cand),
+        own_row_ref[:1, at] * got + cand,
+        jnp.where(place == 0, later_row[:1, at] * cand + got, cand),
     )
-    out = (base_ref[:, at] + fade * carried).astype(BF16)
     if q < CHUNKS - 1:
-        out_ref, raw_ref = refs
-        out_ref[...] = out
+        (raw_ref,) = refs
         raw_ref[...] = cand
         return
-    outs, raws, (out_ref, keep_ref, give_ref) = refs[: CHUNKS - 1], refs[CHUNKS - 1 : 2 * CHUNKS - 2], refs[-3:]
+    raws, (keep_ref, give_ref) = refs[:-2], refs[-2:]
     rep = lax.axis_index("rep")
     half = rows // 2
     for i in range(CHUNKS):
         at = slice(i * cols, (i + 1) * cols)
-        out_ref[:, at] = out if i == q else outs[i][...]
         raw = cand if i == q else raws[i][...]
         keep_ref[:, at] = jnp.where(rep == 0, raw[:half], raw[half:])
         give_ref[:, at] = jnp.where(rep == 0, raw[half:], raw[:half]).astype(BF16)
 
 
-def intra_kernel(x_ref, b2_ref, c2_ref, cum_ref, skip_ref, base_ref, *, groups):
+def prefix_kernel(*refs, first, cols, tokens):
+    refs, (out_any, buffer, sem) = refs[:-3], refs[-3:]
+    last = lax.axis_index("seq") == 3
+    count = len(refs) // 4
+    if len(refs) % 4:
+        refs[-1][...] = jnp.zeros(refs[-1].shape, F32)
+        refs = refs[:-1]
+    for i in range(count):
+        got_ref, carried_ref, base_ref, fade_ref = refs[i::count]
+        carried = jnp.where(last, got_ref[:tokens, :].astype(F32), carried_ref[...])
+        buffer[:, i * cols : (i + 1) * cols] = (base_ref[...] + fade_ref[...] * carried).astype(BF16)
+    copy = pltpu.make_async_copy(buffer, out_any.at[:, pl.ds(first * cols, count * cols)], sem.at[0])
+    copy.start()
+    copy.wait()
+
+
+def intra_kernel(x_ref, b2_ref, c2_ref, cum_ref, skip_ref, *base_refs, groups):
     tokens, heads = cum_ref.shape
     width = x_ref.shape[1] // heads
     state = c2_ref.shape[1] // groups
@@ -401,10 +412,20 @@
             inputs = jnp.concatenate(
                 [jnp.where(lane < width, x, zero), jnp.where(lane < width, zero, x)], axis=0
             )
-            base_ref[:, at] = mm(jnp.concatenate(mixing, axis=1), inputs) + skip[:, at] * x.astype(F32)
-
-
-def cand_kernel(x_ref, b_ref, c_ref, decay_ref, skip_ref, base_ref, fade_ref):
+            q, start = divmod(h * width, base_refs[0].shape[1])
+            base_refs[q][:, start : start + pair] = (
+                mm(jnp.concatenate(mixing, axis=1), inputs) + skip[:, at] * x.astype(F32)
+            )
+
+
+def cand_kernel(x_ref, b_ref, c_ref, decay_ref, skip_ref, *refs):
+    if len(refs) > 2:
+        cum_ref, *fall_refs = refs[:-2]
+        cols = fall_refs[0].shape[1]
+        fall = spread(jnp.exp(-cum_ref[...]), cols * len(fall_refs) // cum_ref.shape[1])
+        for i, ref in enumerate(fall_refs):
+            ref[...] = fall[:, i * cols : (i + 1) * cols]
+    base_ref, fade_ref = refs[-2:]
     steps, groups, state = b_ref.shape[1:]
     heads = decay_ref.shape[2]
     width = x_ref.shape[2] // heads
@@ -437,8 +458,8 @@
             base_ref[:, at] = mm(mixing, inputs) + skip[:, at] * x.astype(F32)
 
 
-def attend_kernel(length_ref, q_ref, own_k_ref, own_v_ref, k_ref, v_ref, mine_ref, other_ref, *refs):
-    out_ref = refs[-1]
+def attend_kernel(length_ref, q_ref, own_k_ref, own_v_ref, k_ref, v_ref, mine_ref, other_ref, mark_ref, out_any, out_ref, sem):
+    mark_ref[...] = jnp.zeros(mark_ref.shape, F32)
     rep = lax.axis_index("rep")
     steps, heads, dim = q_ref.shape[1:]
     kv_heads = own_k_ref.shape[2]
@@ -474,6 +495,9 @@
         mixed = jnp.where(live, mixed, 0.0)
         mixed_of.append(mixed.reshape(steps, per_kv, dim))
     out_ref[0] = (jnp.concatenate(mixed_of, axis=1) if kv_heads > 1 else mixed_of[0]).astype(BF16)
+    copy = pltpu.make_async_copy(out_ref, out_any, sem.at[0])
+    copy.start()
+    copy.wait()
 
 
 def close_kernel(length_ref, base_ref, fade_ref, keep_ref, got_ref, out_ref):
@@ -488,32 +512,36 @@
         out_ref[0, :, at] = jnp.where(live, result, 0.0).astype(BF16)
 
 
-def call(kernel, name, outs, *args, scalars=0, after=(), cost=0.0, scratch=(), limit=32, gate=()):
+def call(kernel, name, outs, *args, scalars=0, after=(), cost=0.0, scratch=(), limit=32, gate=(), into=(), raw=False):
     shapes = [jax.ShapeDtypeStruct(shape, dtype) for shape, dtype in outs]
     vmem = pl.BlockSpec(memory_space=pltpu.VMEM)
     smem = pl.BlockSpec(memory_space=pltpu.SMEM)
-    count, rest = len(args), len(args) + len(after) + len(gate)
+    anywhere = pl.BlockSpec(memory_space=pl.ANY)
+    given = [a for a in into if hasattr(a, "dtype")]
+    passed = [*gate, *given]
+    count = len(args)
+    rest = count + len(after) + len(passed)
     through = rest + len(shapes)
-    out_spec = vmem
-    if scratch:
-        vmem = pl.BlockSpec(memory_space=pl.ANY)
+    shapes += [jax.ShapeDtypeStruct(a.shape, a.dtype) for a in gate]
+    shapes += [jax.ShapeDtypeStruct(a.shape, a.dtype) if hasattr(a, "dtype") else jax.ShapeDtypeStruct(*a) for a in into]
+    aliases = {count + len(after) + i: len(outs) + i for i in range(len(passed))}
 
     def body(*refs):
         kernel(*refs[:count], *refs[rest:through], *refs[through + len(gate) :])
 
     return pl.pallas_call(
         body,
-        out_shape=shapes + [jax.ShapeDtypeStruct(a.shape, a.dtype) for a in gate],
+        out_shape=shapes,
         in_specs=[smem] * scalars
-        + [vmem] * (count - scalars)
-        + [pl.BlockSpec(memory_space=pl.ANY)] * (len(after) + len(gate)),
-        out_specs=[out_spec] * len(shapes) + [pl.BlockSpec(memory_space=pl.ANY)] * len(gate),
-        input_output_aliases={count + len(after) + i: len(shapes) + i for i in range(len(gate))},
+        + [anywhere if raw else vmem] * (count - scalars)
+        + [anywhere] * (len(after) + len(passed)),
+        out_specs=[vmem] * len(outs) + [anywhere] * (len(gate) + len(into)),
+        input_output_aliases=aliases,
         scratch_shapes=list(scratch),
         compiler_params=pltpu.CompilerParams(vmem_limit_bytes=limit * 2**20),
         cost_estimate=pl.CostEstimate(flops=int(cost * 10**9), bytes_accessed=0, transcendentals=0),
         name=name,
-    )(*args, *after, *gate)
+    )(*args, *after, *passed)
 
 
 def on_device(
@@ -591,6 +619,7 @@
             pltpu.VMEM(prefix_values.shape, BF16),
             pltpu.SemaphoreType.DMA((5,)),
         ],
+        raw=True,
         limit=60,
     )
     (cc,) = call(
@@ -607,7 +636,7 @@
         return call(
             functools.partial(intra_kernel, groups=groups),
             "intra",
-            [((tokens, wide), F32)],
+            [((tokens, cols), F32)] * CHUNKS,
             prefix_x,
             b2,
             cc,
@@ -617,16 +646,17 @@
             gate=(loads[1],),
         )
 
-    def candidates(mark):
+    def candidates(mark, *more):
         return call(
             cand_kernel,
             "candidates",
-            [((steps, cand_wide), F32), ((steps, cand_wide), F32)],
+            [((tokens, cols), F32)] * (CHUNKS * len(more)) + [((steps, cand_wide), F32), ((steps, cand_wide), F32)],
             cand_x,
             cand_b,
             cand_c,
             cand_decay,
             skip,
+            *more,
             after=(mark,),
         )
 
@@ -644,7 +674,7 @@
             return call(
                 attend_kernel,
                 "attend",
-                [(cand_queries.shape, BF16)],
+                [((8, 128), F32)],
                 cand_length,
                 cand_queries,
                 cand_keys,
@@ -655,7 +685,9 @@
                 theirs,
                 scalars=1,
                 after=(mark,),
-            )[0]
+                into=((cand_queries.shape, BF16),),
+                scratch=[pltpu.VMEM(cand_queries.shape, BF16), pltpu.SemaphoreType.DMA((1,))],
+            )
 
         return mine, finish
 
@@ -728,47 +760,56 @@
             results = call(
                 functools.partial(third_kernel, q=q, **shared),
                 "third",
-                [((tokens, wide), BF16), ((steps, wide), F32), ((steps, wide), BF16)]
+                [((steps, wide), F32), ((steps, wide), BF16)]
                 if final
-                else ([((8, wide), F32)] if q == 0 else []) + [((tokens, cols), BF16), ((2 * steps, cols), F32)],
+                else ([((8, wide), F32)] if q == 0 else []) + [((2 * steps, cols), F32)],
                 outer[q],
-                carried[q],
                 cands[q],
-                base,
-                cum,
                 rows["own"],
                 *([] if q == 0 else [rows["outer"]]),
-                *(outs + raws if final else []),
+                *(raws if final else []),
                 after=(mark,),
                 cost=THIRD_COST,
             )
+            if q == 0:
+                rows["outer"], *results = results
             if final:
                 return results
-            if q == 0:
-                rows["outer"], *results = results
-            outs.append(results[0])
-            raws.append(results[1])
+            raws.append(results[0])
             return results[0]
 
-        base, loads[1] = intra(cc, cc)
+        def prefix(start, count, mark, into):
+            span = range(start, start + count)
+            return call(
+                functools.partial(prefix_kernel, first=start, cols=cols, tokens=tokens),
+                "prefix",
+                [((8, 128), F32)] if start == 0 else [],
+                *[each[q] for each in (outer, carried, base, fade) for q in span],
+                after=(mark,),
+                into=(into,),
+                scratch=[pltpu.VMEM((tokens, count * cols), BF16), pltpu.SemaphoreType.DMA((1,))],
+            )
+
+        *base, loads[1] = intra(cc, cc)
         got = [to_neighbour(a) for a in loads[:2]]
-        mark = first(0, base)
+        mark = first(0, base[0])
         mark = first(1, mark)
         far_kv = between_inner(rows["kv"])
         mark = second(0, mark)
         mark = first(2, mark)
         mark = second(1, mark)
         mark = first(3, mark)
-        cand_base, cand_fade = candidates(mark)
+        *fade, cand_base, cand_fade = candidates(mark, cum)
         mark = third(0, cand_base)
         mark = second(2, mark)
         mark = third(1, mark)
         mark, finish_attend = attend(mark, [rows["kv"], far_kv, outer[1]], True)
         mark = second(3, mark)
-        mark = cand_attn = finish_attend(mark)
+        mark, cand_attn = finish_attend(mark)
         mark = third(2, mark)
-        results = third(3, mark)
-        prefix_out, keep, give = results
+        mark, prefix_out = prefix(0, CHUNKS - 1, mark, (prefix_x.shape, BF16))
+        keep, give = third(3, mark)
+        (prefix_out,) = prefix(CHUNKS - 1, 1, keep, prefix_out)
     else:
         got = [to_neighbour(a) for a in loads]
         halves = [kv, got[1][:, -kv_shape[1] :]]
@@ -777,8 +818,8 @@
             halves = [halves[0], halves[1], mirrored, to_neighbour(mirrored)]
             if level < levels - 1:
                 halves = [jnp.concatenate([halves[0], halves[2]]), jnp.concatenate([halves[1], halves[3]])]
-        base, loads[1] = intra(cc, cc)
-        mark = base
+        *base, loads[1] = intra(cc, cc)
+        mark = base[0]
         own = call(
             functools.partial(own_kernel, cols=cols, groups=groups, state=state),
             "own",
@@ -806,10 +847,10 @@
                     args += rows
                 args += [own[q]] + ([] if level == 0 else [start[q]])
                 if final:
-                    args += [cc, base, cum] + outs + raws
+                    args += [cc, base[q], cum] + outs + raws
                     shapes = [((tokens, wide), BF16), ((steps, wide), F32), ((steps, wide), BF16)]
                 elif last:
-                    args += [cc, base, cum]
+                    args += [cc, base[q], cum]
                     shapes += [((tokens, cols), BF16), ((2 * steps, cols), F32)]
                 else:
                     shapes += [((state, cols), F32)] * 2 + [((state + (16 if q == 0 else 0), cols // 2), BF16)]
@@ -839,7 +880,7 @@
                 cand_base, cand_fade = candidates(mark)
                 pieces = ([halves[0][tokens:]] if levels > 2 else []) + halves[1:]
                 mark, finish_attend = attend(cand_base, pieces, False)
-                mark = cand_attn = finish_attend(mark)
+                mark, cand_attn = finish_attend(mark)
     (cand_ssm,) = call(
         close_kernel,
         "close",

time: 53.8 us -> 52.7 us (0.980)
  local copies, waits for them, and re-layouts: 3.02 us -> 2.13 us
  waiting for transfers between devices: 10.3 us -> 9.74 us
    unnamed x44 -> x42, local copies, waits for them, and re-layouts: 3.02 us -> 2.13 us
    ppermute x3, waiting for transfers between devices: 2.6 us -> 1.84 us  [to_core(): return lax.ppermute(array, 'rep', [(0, 1), (1, 0)])]
    pallas_call x19 -> x21, Pallas kernels: 15.2 us -> 15.7 us  [call(): pl.pallas_call(body, out_shape=shapes, in_specs=[smem] * scalars + [anywh...]
  transfers between devices with their start and end apart: 17 -> 17, of which waited for: 7 -> 7; matrix products, arithmetic and copies ran while one was open for 0% -> 0% of each run, Pallas kernels for 20% -> 23%
where the time goes in v5:
time: 52.7 us; the launch traced here: 52.1 us
  starting transfers between devices  22.8 us (43%)
  Pallas kernels  15.7 us (30%)
  waiting for transfers between devices  9.74 us (18%)
  local copies, waits for them, and re-layouts  2.13 us (4%)
  between operations  1.7 us (3%)
    ppermute x8, starting transfers between devices, to_neighbour(): return lax.ppermute(array, 'seq', [(i, i ^ 1) for i in range(size)])  20 us
    pallas_call x21, Pallas kernels, call(): pl.pallas_call(body, out_shape=shapes, in_specs=[smem] * scalars + [anywh...  15.7 us
    ppermute x8, waiting for transfers between devices, to_neighbour(): return lax.ppermute(array, 'seq', [(i, i ^ 1) for i in range(size)])  7.88 us
    ppermute x1, starting transfers between devices, inward(): return lax.ppermute(array, 'seq', [(0, 1), (3, 2)])  2.43 us
    unnamed x42, local copies, waits for them, and re-layouts  2.13 us
    ppermute x3, waiting for transfers between devices, to_core(): return lax.ppermute(array, 'rep', [(0, 1), (1, 0)])  1.84 us
  transfers between devices with their start and end apart: 17, of which 7 were waited for; matrix products, arithmetic and copies ran while one was open for 0% of the time, Pallas kernels for 23%

profile of v5, /device:TPU:0, one launch (start us, length us, event | category | flops | bytes accessed | tf_op | source)
XLA Modules:
  0.0 52.1 jit_solution(3736112602404058052)
XLA Ops:
  0.7 3.0 %inputs.1 = (f32[128,32]{1,0:T(8,128)}, f32[8,32]{1,0:T(8,128)}, bf16[128,512]{1,0:T(8,128)(2,1)}, bf16[128,256]{1,0:T(8,128)(2,1)}, bf16[144,768]{1,0:T(8,128)(...) custom-call(bf16[128,2048]{1,0:T(8,128)(2,1)} %refs_0_.8, ...), custom_call_target="tpu_custom_call" | custom-call | tf_op jit(solution)/shard_map/inputs/pallas_call | solution.py:532
  3.6 3.1 %collective-permute-start.2 = (bf16[144,768]{1,0:T(8,128)(2,1)}, bf16[144,768]{1,0:T(8,128)(2,1)S(1)}, u32[]{:S(2)}, u32[]{:S(2)}) collective-permute-start(bf16[144,768]{1,0:T(8,128)(2,1)} %get-tuple-element.56.refs_2_.refs_3_.refs_4_), channel_id=1, source_target_pairs={{0,4},{4,0},{8,12},{12,8},{1,5},{5,1},{9,13},{13,9},{2,6},{6,2},{1... | collective-permute-start | bytes 663560 | tf_op jit(solution)/shard_map/ppermute | solution.py:580
  6.7 0.0 collective-permute-start
  6.7 1.3 %collective-permute-done.refs_2_ = bf16[1,32,4,256]{3,2,1,0:T(4,128)(2,1)S(1)} collective-permute-done((bf16[1,32,4,256]{3,2,1,0:T(4,128)(2,1)S(1)}, bf16[1,32,4,256]{3,2,1,0:T(4,128)(2,1)S(1)}, u32[]{:S(2)}, u32[]{:S(2)}) %collective-permute-start) | collective-permute-done | bytes 65568 | tf_op jit(solution)/shard_map/ppermute | solution.py:577
  8.0 0.8 %copy-done.4 = f32[128,32]{1,0:T(8,128)S(1)} copy-done((f32[128,32]{1,0:T(8,128)S(1)}, f32[128,32]{1,0:T(8,128)}, u32[]{:S(2)}) %copy-start.4) | copy-done | bytes 16408
  8.8 0.6 %projections.1.refs_2_.refs_5_.refs_6_ = bf16[192,512]{1,0:T(8,128)(2,1)S(1)} custom-call(bf16[128,2,256]{2,1,0:T(2,128)(2,1)S(1)} %copy-done.13, bf16[1,32,4,256]{3,2,1,0:T(4,128)(2,1)S(1)} %copy-done.10, bf16[1,32,4,256]{3,2,1,0:T(4,128)(2,1)S(1)} %collective-permute-done.refs_2_, f32[128,32]{1,0:T(8,128)S(1)} %copy-done.4), custom_call_target="tpu_custom_call" | custom-call | tf_op jit(solution)/shard_map/projections/pallas_call | solution.py:532
  9.4 0.0 copy-start.20
  9.4 0.3 copy-done.3
  9.8 0.1 copy-done.12
  9.8 0.3 copy-done.20
  10.1 1.0 %intra.1 = (f32[128,512]{1,0:T(8,128)S(1)}, f32[128,512]{1,0:T(8,128)S(1)}, f32[128,512]{1,0:T(8,128)S(1)}, f32[128,512]{1,0:T(8,128)S(1)}, bf16[128,768]{1,0:T(8,128)(2,1)S(1)}) custom-call(bf16[128,2048]{1,0:T(8,128)(2,1)S(1)} %copy-done.1, bf16[128,512]{1,0:T(8,128)(2,1)S(1)} %copy-done.12, ...), custom_call_target="tpu_custom_call", output_to_operand_aliasing={{4}: (6, {})} | custom-call | tf_op jit(solution)/shard_map/intra/pallas_call | solution.py:532
  11.1 0.1 collective-permute-start.1
  11.3 1.1 %collective-permute-done.2.refs_0_.refs_1_.refs_2_ = bf16[144,768]{1,0:T(8,128)(2,1)S(1)} collective-permute-done((bf16[144,768]{1,0:T(8,128)(2,1)}, bf16[144,768]{1,0:T(8,128)(2,1)S(1)}, u32[]{:S(2)}, u32[]{:S(2)}) %collective-permute-start.2) | collective-permute-done | bytes 221216 | tf_op jit(solution)/shard_map/ppermute | solution.py:580
  12.4 0.5 first.4
  12.9 0.1 collective-permute-start.8
  12.9 3.3 %collective-permute-start.6 = (bf16[192,512]{1,0:T(8,128)(2,1)S(1)}, bf16[192,512]{1,0:T(8,128)(2,1)S(1)}, u32[]{:S(2)}, u32[]{:S(2)}) collective-permute-start(bf16[192,512]{1,0:T(8,128)(2,1)S(1)} %get-tuple-element.68.refs_6_), channel_id=1, source_target_pairs={{0,4},{4,0},{8,12},{12,8},{1,5},{5,1},{9,13},{13,9},{2,6},{6,2},{1... | collective-permute-start | bytes 589832 | tf_op jit(solution)/shard_map/ppermute | solution.py:580
  16.2 2.7 %collective-permute-done.1.refs_0_.refs_1_ = bf16[128,768]{1,0:T(8,128)(2,1)S(1)} collective-permute-done((bf16[128,768]{1,0:T(8,128)(2,1)S(1)}, bf16[128,768]{1,0:T(8,128)(2,1)S(1)}, u32[]{:S(2)}, u32[]{:S(2)}) %collective-permute-start.1) | collective-permute-done | bytes 196640 | tf_op jit(solution)/shard_map/ppermute | solution.py:580
  18.9 0.4 first.5
  19.3 0.1 collective-permute-start.5
  19.4 3.1 %collective-permute-start.4 = (bf16[128,768]{1,0:T(8,128)(2,1)S(1)}, bf16[128,768]{1,0:T(8,128)(2,1)S(1)}, u32[]{:S(2)}, u32[]{:S(2)}) collective-permute-start(bf16[128,768]{1,0:T(8,128)(2,1)S(1)} %get-tuple-element.66.refs_2_.refs_3_.refs_4_), channel_id=1, source_target_pairs={{0,4},{4,0},{8,12},{12,8},{1,5},{5,1},{9,13},{13,9},{2,6},{6,2},{1... | collective-permute-start | bytes 589832 | tf_op jit(solution)/shard_map/ppermute | solution.py:580
  22.5 0.0 collective-permute-start.7
  22.5 0.0 collective-permute-done.6.refs_7_
  22.5 2.4 %collective-permute-start.3 = (bf16[128,512]{1,0:T(8,128)(2,1)S(1)}, bf16[128,512]{1,0:T(8,128)(2,1)S(1)}, u32[]{:S(2)}, u32[]{:S(2)}) collective-permute-start(bf16[128,512]{1,0:T(8,128)(2,1)S(1)} %get-tuple-element.65.refs_2_.refs_3_), channel_id=1, source_target_pairs={{0,4},{12,8},{1,5},{13,9},{2,6},{14,10},{3,7},{15,11},{16,20},{28,... | collective-permute-start | bytes 393224 | tf_op jit(solution)/shard_map/ppermute | solution.py:591
  24.9 0.0 collective-permute-done.8.refs_0_
  25.0 0.8 %second.4 = (f32[8,2048]{1,0:T(8,128)S(1)}, f32[128,512]{1,0:T(8,128)S(1)}, f32[64,512]{1,0:T(8,128)S(1)}, bf16[208,512]{1,0:T(8,128)(2,1)S(1)}) custom-call(bf16[272,512]{1,0:T(8,128)(2,1)S(1)} %collective-permute-done.8.refs_0_, bf16[144,768]{1,0:T(8,128)(2,1)S(1)} %collective-permute-done.2.refs_0_.refs_1_.refs_2_, ...), custom_call_target="tpu_custom_call" | custom-call | flops 1000000000 | tf_op jit(solution)/shard_map/second/pallas_call | solution.py:532
  25.8 0.1 collective-permute-start.11
  25.8 0.8 %collective-permute-done.4.refs_0_.refs_1_.refs_2_ = bf16[128,768]{1,0:T(8,128)(2,1)S(1)} collective-permute-done((bf16[128,768]{1,0:T(8,128)(2,1)S(1)}, bf16[128,768]{1,0:T(8,128)(2,1)S(1)}, u32[]{:S(2)}, u32[]{:S(2)}) %collective-permute-start.4) | collective-permute-done | bytes 196640 | tf_op jit(solution)/shard_map/ppermute | solution.py:580
  26.7 0.3 first.6.refs_10_
  27.0 0.1 collective-permute-start.12
  27.1 0.0 collective-permute-done.7.refs_8_.refs_1_
  27.1 0.0 collective-permute-done.5.refs_0_
  27.1 0.7 %second.5 = (f32[128,512]{1,0:T(8,128)S(1)}, f32[64,512]{1,0:T(8,128)S(1)}, bf16[320,512]{1,0:T(8,128)(2,1)S(1)}) custom-call(bf16[256,512]{1,0:T(8,128)(2,1)S(1)} %collective-permute-done.5.refs_0_, bf16[128,768]{1,0:T(8,128)(2,1)S(1)} %collective-permute-done.1.refs_0_.refs_1_, bf16[144,768]{1,0:T(8,128)(2,1)S(1)} %collective-permute-done.2.refs_0_.refs_1_.refs_2_, ...), custom_call_target="tpu_custom_call" | custom-call | flops 1000000000 | tf_op jit(solution)/shard_map/second/pallas_call | solution.py:532
  27.9 4.4 %collective-permute-start.10 = (bf16[320,512]{1,0:T(8,128)(2,1)S(1)}, bf16[320,512]{1,0:T(8,128)(2,1)S(1)}, u32[]{:S(2)}, u32[]{:S(2)}) collective-permute-start(bf16[320,512]{1,0:T(8,128)(2,1)S(1)} %get-tuple-element.74), channel_id=1, source_target_pairs={{0,4},{4,0},{8,12},{12,8},{1,5},{5,1},{9,13},{13,9},{2,6},{6,2},{1... | collective-permute-start | bytes 983048 | tf_op jit(solution)/shard_map/ppermute | solution.py:580
  32.3 0.0 collective-permute-done.3.refs_0_.refs_1_
  32.3 0.0 copy-start.18
  32.3 0.3 first.7.refs_6_
  32.7 0.1 collective-permute-start.9
  32.8 0.4 copy-done.5
  33.1 0.1 copy-done.9
  33.3 2.0 %candidates.1 = (f32[128,512]{1,0:T(8,128)S(1)}, f32[128,512]{1,0:T(8,128)S(1)}, f32[128,512]{1,0:T(8,128)S(1)}, f32[128,512]{1,0:T(8,128)S(1)}, f32[32,4096]{1,0:T(8,128)S(1)}, /*index=5*/f32[32,4096]{1,0:T(8,128)S(1)}) custom-call(bf16[1,32,4096]{2,1,0:T(8,128)(2,1)S(1)} %copy-done.9, bf16[1,32,4,256]{3,2,1,0:T(4,128)(2,1)S(1)} %copy-done.14, ...), custom_call_target="tpu_custom_call" | custom-call | tf_op jit(solution)/shard_map/candidates/pallas_call | solution.py:532
  35.3 0.0 collective-permute-done.11.refs_0_
  35.3 0.2 third.4
  35.5 0.0 collective-permute-done.12.refs_0_
  35.6 0.7 %second.6 = (f32[128,512]{1,0:T(8,128)S(1)}, f32[64,512]{1,0:T(8,128)S(1)}, bf16[192,512]{1,0:T(8,128)(2,1)S(1)}) custom-call(bf16[256,512]{1,0:T(8,128)(2,1)S(1)} %collective-permute-done.12.refs_0_, bf16[128,768]{1,0:T(8,128)(2,1)S(1)} %collective-permute-done.4.refs_0_.refs_1_.refs_2_, ...), custom_call_target="tpu_custom_call" | custom-call | flops 1000000000 | tf_op jit(solution)/shard_map/second/pallas_call | solution.py:532
  36.3 3.2 %collective-permute-start.14 = (bf16[192,512]{1,0:T(8,128)(2,1)S(1)}, bf16[192,512]{1,0:T(8,128)(2,1)S(1)}, u32[]{:S(2)}, u32[]{:S(2)}) collective-permute-start(bf16[192,512]{1,0:T(8,128)(2,1)S(1)} %get-tuple-element.87), channel_id=1, source_target_pairs={{0,4},{4,0},{8,12},{12,8},{1,5},{5,1},{9,13},{13,9},{2,6},{6,2},{1... | collective-permute-start | bytes 589832 | tf_op jit(solution)/shard_map/ppermute | solution.py:580
  39.5 1.3 %collective-permute-done.10.refs_0_.refs_2_.refs_1_ = bf16[320,512]{1,0:T(8,128)(2,1)S(1)} collective-permute-done((bf16[320,512]{1,0:T(8,128)(2,1)S(1)}, bf16[320,512]{1,0:T(8,128)(2,1)S(1)}, u32[]{:S(2)}, u32[]{:S(2)}) %collective-permute-start.10) | collective-permute-done | bytes 327712 | tf_op jit(solution)/shard_map/ppermute | solution.py:580
  40.9 0.0 copy-start.7
  40.9 0.0 copy-start.8
  40.9 0.0 copy-start.11
  40.9 0.1 collective-permute-start.15
  41.0 0.0 collective-permute-done.9.refs_0_
  41.0 0.0 copy-start.16
  41.0 0.0 copy-start.17
  41.0 0.7 %second.7 = (f32[128,512]{1,0:T(8,128)S(1)}, f32[64,512]{1,0:T(8,128)S(1)}, bf16[192,512]{1,0:T(8,128)(2,1)S(1)}) custom-call(bf16[256,512]{1,0:T(8,128)(2,1)S(1)} %collective-permute-done.9.refs_0_, bf16[128,512]{1,0:T(8,128)(2,1)S(1)} %collective-permute-done.3.refs_0_.refs_1_, bf16[128,768]{1,0:T(8,128)(2,1)S(1)} %collective-permute-done.4.refs_0_.refs_1_.refs_2_, ...), custom_call_target="tpu_custom_call" | custom-call | flops 1000000000 | tf_op jit(solution)/shard_map/second/pallas_call | solution.py:532
  41.8 2.5 %collective-permute-start.13 = (bf16[192,512]{1,0:T(8,128)(2,1)S(1)}, bf16[192,512]{1,0:T(8,128)(2,1)S(1)}, u32[]{:S(2)}, u32[]{:S(2)}) collective-permute-start(bf16[192,512]{1,0:T(8,128)(2,1)S(1)} %get-tuple-element.82), channel_id=1, source_target_pairs={{0,4},{4,0},{8,12},{12,8},{1,5},{5,1},{9,13},{13,9},{2,6},{6,2},{1... | collective-permute-start | bytes 589832 | tf_op jit(solution)/shard_map/ppermute | solution.py:580
  45.0 0.0 collective-permute-done.15.refs_7_
  45.0 1.9 %attend.1 = (f32[8,128]{1,0:T(8,128)S(1)}, bf16[1,32,16,128]{3,2,1,0:T(8,128)(2,1)}) custom-call(s32[1]{0:T(128)S(6)} %copy.28.refs_0_, bf16[1,32,16,128]{3,2,1,0:T(8,128)(2,1)S(1)} %copy-done.11, bf16[1,32,2,128]{3,2,1,0:T(2,128)(2,1)S(1)} %copy-done.16, bf16[1,32,2,128]{3,2,1,0:T(2,128)(2,1)S(1)} %copy-done.17, bf16[128,2,128]{2,1,0:T(2,128)(2,1)S(1)} %copy-done.7, ...), custom_call_target="tpu_custom_call" | custom-call | tf_op jit(solution)/shard_map/attend/pallas_call | solution.py:532
  47.0 0.9 %prefix.2 = (f32[8,128]{1,0:T(8,128)S(1)}, bf16[128,2048]{1,0:T(8,128)(2,1)}) custom-call(bf16[208,512]{1,0:T(8,128)(2,1)S(1)} %collective-permute-done.11.refs_0_, bf16[320,512]{1,0:T(8,128)(2,1)S(1)} %collective-permute-done.10.refs_0_.refs_2_.refs_1_, bf16[192,512]{1,0:T(8,128)(2,1)S(1)} %collective-permute-done.14.refs_0_.refs_2_, ...), custom_call_target="tpu_custom_call" | custom-call | tf_op jit(solution)/shard_map/prefix/pallas_call | solution.py:532
  47.9 1.9 %collective-permute-done.13.refs_0_ = bf16[192,512]{1,0:T(8,128)(2,1)S(1)} collective-permute-done((bf16[192,512]{1,0:T(8,128)(2,1)S(1)}, bf16[192,512]{1,0:T(8,128)(2,1)S(1)}, u32[]{:S(2)}, u32[]{:S(2)}) %collective-permute-start.13) | collective-permute-done | bytes 196640 | tf_op jit(solution)/shard_map/ppermute | solution.py:580
  49.8 0.1 third.7
  49.9 0.1 collective-permute-start.16
  50.0 0.7 %prefix.3 = bf16[128,2048]{1,0:T(8,128)(2,1)} custom-call(bf16[192,512]{1,0:T(8,128)(2,1)S(1)} %collective-permute-done.13.refs_0_, f32[128,512]{1,0:T(8,128)S(1)} %get-tuple-element.83.refs_8_.refs_1_, f32[128,512]{1,0:T(8,128)S(1)} %get-tuple-element.84.refs_2_, f32[128,512]{1,0:T(8,128)S(1)} %get-tuple-element.85.refs_3_, ...), custom_call_target="tpu_custom_call", output_to_operand_aliasing={{}: (5, {})} | custom-call | tf_op jit(solution)/shard_map/prefix/pallas_call | solution.py:532
  50.7 0.6 %collective-permute-done.16.refs_4_ = bf16[32,2048]{1,0:T(8,128)(2,1)S(1)} collective-permute-done((bf16[32,2048]{1,0:T(8,128)(2,1)S(1)}, bf16[32,2048]{1,0:T(8,128)(2,1)S(1)}, u32[]{:S(2)}, u32[]{:S(2)}) %collective-permute-start.16) | collective-permute-done | bytes 131104 | tf_op jit(solution)/shard_map/ppermute | solution.py:577
  51.3 0.8 %close.1 = bf16[1,32,4096]{2,1,0:T(8,128)(2,1)} custom-call(s32[1]{0:T(128)S(6)} %copy.28.refs_0_, f32[32,4096]{1,0:T(8,128)S(1)} %get-tuple-element.78.refs_3_.refs_1_, f32[32,4096]{1,0:T(8,128)S(1)} %get-tuple-element.98.refs_2_, f32[32,2048]{1,0:T(8,128)S(1)} %get-tuple-element.96.refs_4_.refs_3_, bf16[32,2048]{1,0:T(8,128)(2,1)S(1)} %collective-permute-done.16.refs_4_), custom_call_target="tpu_custom_call" | custom-call | tf_op jit(solution)/shard_map/close/pallas_call | solution.py:532
  (33 shorter events, 0.2 us)
Async XLA Ops:
  0.6 6.1 %copy-start.10 = (bf16[1,32,4,256]{3,2,1,0:T(4,128)(2,1)S(1)}, bf16[1,32,4,256]{3,2,1,0:T(4,128)(2,1)}, u32[]{:S(2)}) copy-start(bf16[1,32,4,256]{3,2,1,0:T(4,128)(2,1)} %refs_2_.2) | copy-start | bytes 196612
  0.6 7.4 %copy-start.13 = (bf16[128,2,256]{2,1,0:T(2,128)(2,1)S(1)}, bf16[128,2,256]{2,1,0:T(2,128)(2,1)}, u32[]{:S(2)}) copy-start(bf16[128,2,256]{2,1,0:T(2,128)(2,1)} %refs_0_.7) | copy-start | bytes 393220
  0.7 8.8 %copy-start.1 = (bf16[128,2048]{1,0:T(8,128)(2,1)S(1)}, bf16[128,2048]{1,0:T(8,128)(2,1)}, u32[]{:S(2)}) copy-start(bf16[128,2048]{1,0:T(8,128)(2,1)} %refs_0_.8) | copy-start | bytes 1572868
  3.6 8.7 %collective-permute-start.2 = (bf16[144,768]{1,0:T(8,128)(2,1)}, bf16[144,768]{1,0:T(8,128)(2,1)S(1)}, u32[]{:S(2)}, u32[]{:S(2)}) collective-permute-start(bf16[144,768]{1,0:T(8,128)(2,1)} %get-tuple-element.56.refs_2_.refs_3_.refs_4_), channel_id=1, source_target_pairs={{0,4},{4,0},{8,12},{12,8},{1,5},{5,1},{9,13},{13,9},{2,6},{6,2},{1... | collective-permute-start | bytes 663560 | tf_op jit(solution)/shard_map/ppermute | solution.py:580
  6.7 1.3 %collective-permute-start = (bf16[1,32,4,256]{3,2,1,0:T(4,128)(2,1)S(1)}, bf16[1,32,4,256]{3,2,1,0:T(4,128)(2,1)S(1)}, u32[]{:S(2)}, u32[]{:S(2)}) collective-permute-start(bf16[1,32,4,256]{3,2,1,0:T(4,128)(2,1)S(1)} %copy-done.10), channel_id=1, source_target_pairs={{0,1},{1,0},{2,3},{3,2},{4,5},{5,4},{6,7},{7,6},{8,9},{9,8},{10,11... | collective-permute-start | bytes 196616 | tf_op jit(solution)/shard_map/ppermute | solution.py:577
  8.0 0.8 %copy-start.4 = (f32[128,32]{1,0:T(8,128)S(1)}, f32[128,32]{1,0:T(8,128)}, u32[]{:S(2)}) copy-start(f32[128,32]{1,0:T(8,128)} %get-tuple-element.53.refs_3_.refs_5_) | copy-start | bytes 49156
  8.8 0.9 %copy-start.3 = (bf16[128,768]{1,0:T(8,128)(2,1)S(1)}, bf16[128,768]{1,0:T(8,128)(2,1)}, u32[]{:S(2)}) copy-start(bf16[128,768]{1,0:T(8,128)(2,1)} %get-tuple-element.54.refs_6_) | copy-start | bytes 589828
  8.8 1.0 %copy-start.12 = (bf16[128,512]{1,0:T(8,128)(2,1)S(1)}, bf16[128,512]{1,0:T(8,128)(2,1)}, u32[]{:S(2)}) copy-start(bf16[128,512]{1,0:T(8,128)(2,1)} %get-tuple-element.52.refs_1_) | copy-start | bytes 393220
  9.4 0.7 %copy-start.20 = (f32[128]{0:T(128)S(1)}, f32[128]{0:T(128)}, u32[]{:S(2)}) copy-start(f32[128]{0:T(128)} %param.19) | copy-start | bytes 1540
  10.1 2.3 %copy-start.2 = (bf16[144,768]{1,0:T(8,128)(2,1)S(1)}, bf16[144,768]{1,0:T(8,128)(2,1)}, u32[]{:S(2)}) copy-start(bf16[144,768]{1,0:T(8,128)(2,1)} %get-tuple-element.56.refs_2_.refs_3_.refs_4_) | copy-start | bytes 663556
  11.1 1.3 %copy-start.19 = (f32[8,32]{1,0:T(8,128)S(1)}, f32[8,32]{1,0:T(8,128)}, u32[]{:S(2)}) copy-start(f32[8,32]{1,0:T(8,128)} %get-tuple-element.57.refs_4_.refs_8_) | copy-start | bytes 3076
  11.1 7.8 %collective-permute-start.1 = (bf16[128,768]{1,0:T(8,128)(2,1)S(1)}, bf16[128,768]{1,0:T(8,128)(2,1)S(1)}, u32[]{:S(2)}, u32[]{:S(2)}) collective-permute-start(bf16[128,768]{1,0:T(8,128)(2,1)S(1)} %get-tuple-element.55.refs_2_.refs_3_), channel_id=1, source_target_pairs={{0,4},{4,0},{8,12},{12,8},{1,5},{5,1},{9,13},{13,9},{2,6},{6,2},{1... | collective-permute-start | bytes 589832 | tf_op jit(solution)/shard_map/ppermute | solution.py:580
  12.4 6.5 %copy-start = (bf16[128,768]{1,0:T(8,128)(2,1)S(1)}, bf16[128,768]{1,0:T(8,128)(2,1)}, u32[]{:S(2)}) copy-start(bf16[128,768]{1,0:T(8,128)(2,1)} %get-tuple-element.63.refs_8_) | copy-start | bytes 589828
  12.4 6.5 %copy-start.6 = (bf16[128,512]{1,0:T(8,128)(2,1)S(1)}, bf16[128,512]{1,0:T(8,128)(2,1)}, u32[]{:S(2)}) copy-start(bf16[128,512]{1,0:T(8,128)(2,1)} %get-tuple-element.64.refs_9_) | copy-start | bytes 393220
  12.4 6.5 %copy-start.15 = (bf16[128,256]{1,0:T(8,128)(2,1)S(1)}, bf16[128,256]{1,0:T(8,128)(2,1)}, u32[]{:S(2)}) copy-start(bf16[128,256]{1,0:T(8,128)(2,1)} %get-tuple-element.61.refs_6_) | copy-start | bytes 196612
  12.9 12.1 %collective-permute-start.8 = (bf16[272,512]{1,0:T(8,128)(2,1)S(1)}, bf16[272,512]{1,0:T(8,128)(2,1)S(1)}, u32[]{:S(2)}, u32[]{:S(2)}) collective-permute-start(bf16[272,512]{1,0:T(8,128)(2,1)S(1)} %get-tuple-element.62.refs_7_), channel_id=1, source_target_pairs={{0,1},{1,0},{4,8},{5,9},{8,4},{9,5},{12,13},{13,12},{2,3},{3,2},{6... | collective-permute-start | bytes 835592 | tf_op jit(solution)/shard_map/ppermute | solution.py:588
  12.9 9.6 %collective-permute-start.6 = (bf16[192,512]{1,0:T(8,128)(2,1)S(1)}, bf16[192,512]{1,0:T(8,128)(2,1)S(1)}, u32[]{:S(2)}, u32[]{:S(2)}) collective-permute-start(bf16[192,512]{1,0:T(8,128)(2,1)S(1)} %get-tuple-element.68.refs_6_), channel_id=1, source_target_pairs={{0,4},{4,0},{8,12},{12,8},{1,5},{5,1},{9,13},{13,9},{2,6},{6,2},{1... | collective-permute-start | bytes 589832 | tf_op jit(solution)/shard_map/ppermute | solution.py:580
  19.3 7.8 %collective-permute-start.5 = (bf16[256,512]{1,0:T(8,128)(2,1)S(1)}, bf16[256,512]{1,0:T(8,128)(2,1)S(1)}, u32[]{:S(2)}, u32[]{:S(2)}) collective-permute-start(bf16[256,512]{1,0:T(8,128)(2,1)S(1)} %get-tuple-element.67.refs_10_), channel_id=1, source_target_pairs={{0,1},{1,0},{4,8},{5,9},{8,4},{9,5},{12,13},{13,12},{2,3},{3,2},{6... | collective-permute-start | bytes 786440 | tf_op jit(solution)/shard_map/ppermute | solution.py:588
  19.4 7.3 %collective-permute-start.4 = (bf16[128,768]{1,0:T(8,128)(2,1)S(1)}, bf16[128,768]{1,0:T(8,128)(2,1)S(1)}, u32[]{:S(2)}, u32[]{:S(2)}) collective-permute-start(bf16[128,768]{1,0:T(8,128)(2,1)S(1)} %get-tuple-element.66.refs_2_.refs_3_.refs_4_), channel_id=1, source_target_pairs={{0,4},{4,0},{8,12},{12,8},{1,5},{5,1},{9,13},{13,9},{2,6},{6,2},{1... | collective-permute-start | bytes 589832 | tf_op jit(solution)/shard_map/ppermute | solution.py:580
  22.5 4.6 %collective-permute-start.7 = (bf16[256,256]{1,0:T(8,128)(2,1)S(1)}, bf16[256,256]{1,0:T(8,128)(2,1)S(1)}, u32[]{:S(2)}, u32[]{:S(2)}) collective-permute-start(bf16[256,256]{1,0:T(8,128)(2,1)S(1)} %get-tuple-element.69.refs_0_), channel_id=1, source_target_pairs={{0,1},{1,0},{4,8},{5,9},{8,4},{9,5},{12,13},{13,12},{2,3},{3,2},{6... | collective-permute-start | bytes 393224 | tf_op jit(solution)/shard_map/ppermute | solution.py:588
  22.5 9.8 %collective-permute-start.3 = (bf16[128,512]{1,0:T(8,128)(2,1)S(1)}, bf16[128,512]{1,0:T(8,128)(2,1)S(1)}, u32[]{:S(2)}, u32[]{:S(2)}) collective-permute-start(bf16[128,512]{1,0:T(8,128)(2,1)S(1)} %get-tuple-element.65.refs_2_.refs_3_), channel_id=1, source_target_pairs={{0,4},{12,8},{1,5},{13,9},{2,6},{14,10},{3,7},{15,11},{16,20},{28,... | collective-permute-start | bytes 393224 | tf_op jit(solution)/shard_map/ppermute | solution.py:591
  25.8 9.5 %collective-permute-start.11 = (bf16[208,512]{1,0:T(8,128)(2,1)S(1)}, bf16[208,512]{1,0:T(8,128)(2,1)S(1)}, u32[]{:S(2)}, u32[]{:S(2)}) collective-permute-start(bf16[208,512]{1,0:T(8,128)(2,1)S(1)} %get-tuple-element.76), channel_id=1, source_target_pairs={{0,4},{4,0},{8,12},{12,8},{1,5},{5,1},{9,13},{13,9},{2,6},{6,2},{1... | collective-permute-start | bytes 638984 | tf_op jit(solution)/shard_map/ppermute | solution.py:580
  27.0 8.5 %collective-permute-start.12 = (bf16[256,512]{1,0:T(8,128)(2,1)S(1)}, bf16[256,512]{1,0:T(8,128)(2,1)S(1)}, u32[]{:S(2)}, u32[]{:S(2)}) collective-permute-start(bf16[256,512]{1,0:T(8,128)(2,1)S(1)} %first.6.refs_10_), channel_id=1, source_target_pairs={{0,1},{1,0},{4,8},{5,9},{8,4},{9,5},{12,13},{13,12},{2,3},{3,2},{6... | collective-permute-start | bytes 786440 | tf_op jit(solution)/shard_map/ppermute | solution.py:588
  27.9 13.0 %collective-permute-start.10 = (bf16[320,512]{1,0:T(8,128)(2,1)S(1)}, bf16[320,512]{1,0:T(8,128)(2,1)S(1)}, u32[]{:S(2)}, u32[]{:S(2)}) collective-permute-start(bf16[320,512]{1,0:T(8,128)(2,1)S(1)} %get-tuple-element.74), channel_id=1, source_target_pairs={{0,4},{4,0},{8,12},{12,8},{1,5},{5,1},{9,13},{13,9},{2,6},{6,2},{1... | collective-permute-start | bytes 983048 | tf_op jit(solution)/shard_map/ppermute | solution.py:580
  32.3 0.8 %copy-start.5 = (f32[128,32]{1,0:T(8,128)S(1)}, f32[128,32]{1,0:T(8,128)}, u32[]{:S(2)}) copy-start(f32[128,32]{1,0:T(8,128)} %get-tuple-element.53.refs_3_.refs_5_) | copy-start | bytes 49156
  32.3 1.0 %copy-start.9 = (bf16[1,32,4096]{2,1,0:T(8,128)(2,1)S(1)}, bf16[1,32,4096]{2,1,0:T(8,128)(2,1)}, u32[]{:S(2)}) copy-start(bf16[1,32,4096]{2,1,0:T(8,128)(2,1)} %refs_0_.9) | copy-start | bytes 786436
  32.3 1.0 %copy-start.14 = (bf16[1,32,4,256]{3,2,1,0:T(4,128)(2,1)S(1)}, bf16[1,32,4,256]{3,2,1,0:T(4,128)(2,1)}, u32[]{:S(2)}) copy-start(bf16[1,32,4,256]{3,2,1,0:T(4,128)(2,1)} %refs_1_.6) | copy-start | bytes 196612
  32.3 1.0 %copy-start.18 = (f32[1,32,64]{2,1,0:T(8,128)S(1)}, f32[1,32,64]{2,1,0:T(8,128)}, u32[]{:S(2)}) copy-start(f32[1,32,64]{2,1,0:T(8,128)} %refs_3_.4) | copy-start | bytes 24580
  32.7 8.3 %collective-permute-start.9 = (bf16[256,512]{1,0:T(8,128)(2,1)S(1)}, bf16[256,512]{1,0:T(8,128)(2,1)S(1)}, u32[]{:S(2)}, u32[]{:S(2)}) collective-permute-start(bf16[256,512]{1,0:T(8,128)(2,1)S(1)} %first.7.refs_6_), channel_id=1, source_target_pairs={{0,1},{1,0},{4,8},{5,9},{8,4},{9,5},{12,13},{13,12},{2,3},{3,2},{6... | collective-permute-start | bytes 786440 | tf_op jit(solution)/shard_map/ppermute | solution.py:588
  36.3 10.7 %collective-permute-start.14 = (bf16[192,512]{1,0:T(8,128)(2,1)S(1)}, bf16[192,512]{1,0:T(8,128)(2,1)S(1)}, u32[]{:S(2)}, u32[]{:S(2)}) collective-permute-start(bf16[192,512]{1,0:T(8,128)(2,1)S(1)} %get-tuple-element.87), channel_id=1, source_target_pairs={{0,4},{4,0},{8,12},{12,8},{1,5},{5,1},{9,13},{13,9},{2,6},{6,2},{1... | collective-permute-start | bytes 589832 | tf_op jit(solution)/shard_map/ppermute | solution.py:580
  40.9 4.1 %copy-start.7 = (bf16[128,2,128]{2,1,0:T(2,128)(2,1)S(1)}, bf16[128,2,128]{2,1,0:T(2,128)(2,1)}, u32[]{:S(2)}) copy-start(bf16[128,2,128]{2,1,0:T(2,128)(2,1)} %refs_4_.3) | copy-start | bytes 196612
  40.9 4.1 %copy-start.8 = (bf16[128,2,128]{2,1,0:T(2,128)(2,1)S(1)}, bf16[128,2,128]{2,1,0:T(2,128)(2,1)}, u32[]{:S(2)}) copy-start(bf16[128,2,128]{2,1,0:T(2,128)(2,1)} %refs_5_.1) | copy-start | bytes 196612
  40.9 4.1 %copy-start.11 = (bf16[1,32,16,128]{3,2,1,0:T(8,128)(2,1)S(1)}, bf16[1,32,16,128]{3,2,1,0:T(8,128)(2,1)}, u32[]{:S(2)}) copy-start(bf16[1,32,16,128]{3,2,1,0:T(8,128)(2,1)} %refs_1_.7) | copy-start | bytes 393220
  40.9 4.0 %collective-permute-start.15 = (bf16[384,256]{1,0:T(8,128)(2,1)S(1)}, bf16[384,256]{1,0:T(8,128)(2,1)S(1)}, u32[]{:S(2)}, u32[]{:S(2)}) collective-permute-start(bf16[384,256]{1,0:T(8,128)(2,1)S(1)} %collect.1.refs_9_.refs_6_), channel_id=1, source_target_pairs={{0,1},{1,0},{2,3},{3,2},{4,5},{5,4},{6,7},{7,6},{8,9},{9,8},{10,11... | collective-permute-start | bytes 589832 | tf_op jit(solution)/shard_map/ppermute | solution.py:577
  41.0 4.0 %copy-start.16 = (bf16[1,32,2,128]{3,2,1,0:T(2,128)(2,1)S(1)}, bf16[1,32,2,128]{3,2,1,0:T(2,128)(2,1)}, u32[]{:S(2)}) copy-start(bf16[1,32,2,128]{3,2,1,0:T(2,128)(2,1)} %refs_2_.3) | copy-start | bytes 49156
  41.0 4.0 %copy-start.17 = (bf16[1,32,2,128]{3,2,1,0:T(2,128)(2,1)S(1)}, bf16[1,32,2,128]{3,2,1,0:T(2,128)(2,1)}, u32[]{:S(2)}) copy-start(bf16[1,32,2,128]{3,2,1,0:T(2,128)(2,1)} %refs_3_.5) | copy-start | bytes 49156
  41.8 8.1 %collective-permute-start.13 = (bf16[192,512]{1,0:T(8,128)(2,1)S(1)}, bf16[192,512]{1,0:T(8,128)(2,1)S(1)}, u32[]{:S(2)}, u32[]{:S(2)}) collective-permute-start(bf16[192,512]{1,0:T(8,128)(2,1)S(1)} %get-tuple-element.82), channel_id=1, source_target_pairs={{0,4},{4,0},{8,12},{12,8},{1,5},{5,1},{9,13},{13,9},{2,6},{6,2},{1... | collective-permute-start | bytes 589832 | tf_op jit(solution)/shard_map/ppermute | solution.py:580
  49.9 1.4 %collective-permute-start.16 = (bf16[32,2048]{1,0:T(8,128)(2,1)S(1)}, bf16[32,2048]{1,0:T(8,128)(2,1)S(1)}, u32[]{:S(2)}, u32[]{:S(2)}) collective-permute-start(bf16[32,2048]{1,0:T(8,128)(2,1)S(1)} %get-tuple-element.99), channel_id=1, source_target_pairs={{0,1},{1,0},{2,3},{3,2},{4,5},{5,4},{6,7},{7,6},{8,9},{9,8},{10,11... | collective-permute-start | bytes 393224 | tf_op jit(solution)/shard_map/ppermute | solution.py:577

commit v6 on v5

--- a/solution.py
+++ b/solution.py
@@ -9,7 +9,9 @@
 
 EPSILON = 1e-06
 NEG = -1e30
+LARGEST = 3.38e38
 CHUNKS = 4
+PARTS = (8, 8, 8, 8)
 SECOND_COST = 1.0
 FIRST_COST = 0.0
 THIRD_COST = 0.3
@@ -46,7 +48,7 @@
 
 
 def split3(a):
-    hi = a.astype(BF16)
+    hi = jnp.clip(a, -LARGEST, LARGEST).astype(BF16)
     rest = a - hi.astype(F32)
     mid = rest.astype(BF16)
     return hi, mid, (rest - mid.astype(F32)).astype(BF16)
@@ -67,9 +69,24 @@
     return array.astype(F32)[:, g, :].astype(BF16)
 
 
-def payload_plan(groups):
-    of = [q * groups // CHUNKS for q in range(CHUNKS)]
-    return [([g] if g not in of[:q] else []) for q, g in enumerate(of)]
+def cut(heads, size):
+    if size == 4 and heads % sum(PARTS) == 0:
+        return tuple(heads // sum(PARTS) * part for part in PARTS)
+    return (heads // CHUNKS,) * CHUNKS
+
+
+def groups_of(groups, counts):
+    of = [sum(counts[:q]) * groups // sum(counts) for q in range(CHUNKS)]
+    return of, {g: of.index(g) for g in of}
+
+
+def columns(q, counts, width):
+    return slice(sum(counts[:q]) * width, sum(counts[: q + 1]) * width)
+
+
+def payload_plan(groups, counts):
+    of, first_of = groups_of(groups, counts)
+    return [[g] if first_of[g] == q else [] for q, g in enumerate(of)]
 
 
 def totals_to_lines(total):
@@ -93,7 +110,7 @@
     return jnp.concatenate([kv[:, j, :] for j in range(kv.shape[1])], axis=1).astype(BF16)
 
 
-def inputs_kernel(x_any, b_any, decay_t_any, k_any, v_any, cum_ref, total_ref, b2_ref, kv_ref, *refs):
+def inputs_kernel(x_any, b_any, decay_t_any, k_any, v_any, cum_ref, total_ref, b2_ref, kv_ref, *refs, counts):
     load_refs, (x_ref, b_ref, decay_t_ref, k_ref, v_ref, sems) = refs[:-6], refs[-6:]
     pairs = ((decay_t_any, decay_t_ref), (b_any, b_ref), (x_any, x_ref), (k_any, k_ref), (v_any, v_ref))
     copies = [pltpu.make_async_copy(source, target, sems.at[i]) for i, (source, target) in enumerate(pairs)]
@@ -101,7 +118,7 @@
         copy.start()
     tokens, groups, state = b_ref.shape
     heads = decay_t_ref.shape[0]
-    cols = x_ref.shape[1] // CHUNKS
+    width = x_ref.shape[1] // heads
     copies[0].wait()
     lower = (iota((tokens, tokens), 0) >= iota((tokens, tokens), 1)).astype(F32)
     cum = exact_nt(lower, decay_t_ref[...])
@@ -109,9 +126,9 @@
     last = cum[tokens - 1 : tokens, :]
     total = jnp.exp(-last)
     total_ref[...] = jnp.broadcast_to(total, (8, heads))
-    load_refs[0][tokens:, :] = jnp.zeros((16, cols + state), BF16)
+    load_refs[0][tokens:, :] = jnp.zeros((16, load_refs[0].shape[1]), BF16)
     load_refs[0][tokens:, :heads] = totals_to_lines(total)
-    weights = spread(jnp.exp(last - cum), x_ref.shape[1] // heads)
+    weights = spread(jnp.exp(last - cum), width)
     for copy in copies[1:]:
         copy.wait()
     b = b_ref[...].astype(F32)
@@ -119,8 +136,9 @@
         b2_ref[:, g * state : (g + 1) * state] = b[:, g, :].astype(BF16)
     kv = pack(k_ref, v_ref)
     kv_ref[...] = kv
-    for q, (fresh, load) in enumerate(zip(payload_plan(groups), load_refs)):
-        at = slice(q * cols, (q + 1) * cols)
+    for q, (fresh, load) in enumerate(zip(payload_plan(groups, counts), load_refs)):
+        at = columns(q, counts, width)
+        cols = counts[q] * width
         load[:tokens, :cols] = (x_ref[:, at].astype(F32) * weights[:, at]).astype(BF16)
         if fresh:
             load[:tokens, cols : cols + state] = b2_ref[:, fresh[0] * state : (fresh[0] + 1) * state]
@@ -128,12 +146,12 @@
             load[:, load.shape[1] - kv.shape[1] :] = kv
 
 
-def own_kernel(*refs, cols, groups, state):
+def own_kernel(*refs, cols, groups, state, counts):
     load_refs, out_refs = refs[:CHUNKS], refs[CHUNKS:]
     tokens = load_refs[1].shape[0]
-    first_of = {g: q for q, fresh in enumerate(payload_plan(groups)) for g in fresh}
+    of, first_of = groups_of(groups, counts)
     for q in range(CHUNKS):
-        b_ref = load_refs[first_of[q * groups // CHUNKS]]
+        b_ref = load_refs[first_of[of[q]]]
         out_refs[q][...] = mm_tn(b_ref[:tokens, cols : cols + state], load_refs[q][:tokens, :cols])
 
 
@@ -258,13 +276,15 @@
             out_ref[tokens + i * steps : tokens + (i + 1) * steps, at] = part.astype(BF16)
 
 
-def first_kernel(*refs, q, cols, groups, heads, tokens, state):
+def first_kernel(*refs, q, counts, width, groups, heads, tokens, state):
     refs = list(refs)
     w_ref, b_ref, own_w_ref, own_b_ref = refs[:4]
     refs = refs[4:]
     left = lax.axis_index("seq") < 2
-    width = cols * CHUNKS // heads
-    other = mm_tn(b_ref[:tokens, cols : cols + state], w_ref[:tokens, :cols])
+    cols = counts[q] * width
+    of, first_of = groups_of(groups, counts)
+    at_b = slice(counts[first_of[of[q]]] * width, counts[first_of[of[q]]] * width + state)
+    other = mm_tn(b_ref[:tokens, at_b], w_ref[:tokens, :cols])
     if q == 0:
         mine_ref, own_row_ref, near_row_ref, near_ref, send_ref = refs
         mine = mine_ref[:1, :]
@@ -285,23 +305,28 @@
             pair_ref[tokens:, :] = w_ref[:, w_ref.shape[1] - kv_ref.shape[1] :]
         (send_ref,) = refs
         own_row, near_row = own_row_ref[...], near_row_ref[...]
-    at = slice(q * cols, (q + 1) * cols)
-    local = mm_tn(own_b_ref[:tokens, cols : cols + state], own_w_ref[:tokens, :cols])
+    at = columns(q, counts, width)
+    local = mm_tn(own_b_ref[:tokens, at_b], own_w_ref[:tokens, :cols])
     after = own_row[:1, at] * other + local
     beyond = other + near_row[:1, at] * local
     send_ref[:state, :] = jnp.where(left, after, beyond).astype(BF16)
 
 
-def second_kernel(*refs, q, cols, groups, heads, tokens, state):
+def second_kernel(*refs, q, counts, width, groups, heads, tokens, state, make):
     refs = list(refs)
     got_ref, w_ref, b_ref, own_w_ref, own_b_ref, own_row_ref, cc_ref, near_cc_ref = refs[:8]
     refs = refs[8:]
+    if make == "send":
+        refs[-1:] = [None, None, refs[-1]]
+    elif make == "keep":
+        refs.append(None)
     place = lax.axis_index("seq")
     left, inner = place < 2, (place == 1) | (place == 2)
-    width = cols * CHUNKS // heads
-    at = slice(q * cols, (q + 1) * cols)
-    g = q * groups // CHUNKS
-    here = slice(g * state, (g + 1) * state)
+    cols = counts[q] * width
+    at = columns(q, counts, width)
+    of, first_of = groups_of(groups, counts)
+    at_b = slice(counts[first_of[of[q]]] * width, counts[first_of[of[q]]] * width + state)
+    here = slice(of[q] * state, (of[q] + 1) * state)
     rows = cc_ref.shape[0]
     if q == 0:
         mine_ref, near_ref, later_row_ref, carried_ref, cand_ref, send_ref = refs
@@ -320,25 +345,27 @@
         later_row_ref, carried_ref, cand_ref, send_ref = refs
         later_row = later_row_ref[...]
     got = got_ref[:state, :].astype(F32)
-    other = mm_tn(b_ref[:tokens, cols : cols + state], w_ref[:tokens, :cols])
-    local = mm_tn(own_b_ref[:tokens, cols : cols + state], own_w_ref[:tokens, :cols])
+    other = mm_tn(b_ref[:tokens, at_b], w_ref[:tokens, :cols])
+    local = mm_tn(own_b_ref[:tokens, at_b], own_w_ref[:tokens, :cols])
     start, beyond = jnp.where(left, other, got), jnp.where(left, got, other)
     start = jnp.where(inner, start, 0.0)
     after = own_row_ref[:1, at] * start + local
     lasting = later_row[:1, at]
-    state_out = jnp.where(left, beyond + lasting * local, after)
-    send_ref[:rows, :] = mm(near_cc_ref[:, here], state_out.astype(BF16)).astype(BF16)
+    if make != "keep":
+        state_out = jnp.where(left, beyond + lasting * local, after)
+        send_ref[:rows, :] = mm(near_cc_ref[:, here], state_out.astype(BF16)).astype(BF16)
+    if make == "send":
+        return
     final = jnp.where(inner, lasting * after + beyond, local)
     carried_ref[...] = mm(cc_ref[:tokens, here], start.astype(BF16))
     cand_ref[...] = mm(cc_ref[tokens:, here], final.astype(BF16))
 
 
-def third_kernel(*refs, q, cols, heads, tokens):
+def third_kernel(*refs, q, counts, width, heads, tokens):
     refs = list(refs)
     got_ref, cand_ref, own_row_ref = refs[:3]
     place = lax.axis_index("seq")
-    width = cols * CHUNKS // heads
-    at = slice(q * cols, (q + 1) * cols)
+    at = columns(q, counts, width)
     rows = cand_ref.shape[0]
     refs = refs[3:]
     if q == 0:
@@ -363,24 +390,26 @@
     rep = lax.axis_index("rep")
     half = rows // 2
     for i in range(CHUNKS):
-        at = slice(i * cols, (i + 1) * cols)
+        at = columns(i, counts, width)
         raw = cand if i == q else raws[i][...]
         keep_ref[:, at] = jnp.where(rep == 0, raw[:half], raw[half:])
         give_ref[:, at] = jnp.where(rep == 0, raw[half:], raw[:half]).astype(BF16)
 
 
-def prefix_kernel(*refs, first, cols, tokens):
+def prefix_kernel(*refs, first, tokens):
     refs, (out_any, buffer, sem) = refs[:-3], refs[-3:]
     last = lax.axis_index("seq") == 3
     count = len(refs) // 4
     if len(refs) % 4:
         refs[-1][...] = jnp.zeros(refs[-1].shape, F32)
         refs = refs[:-1]
+    at = 0
     for i in range(count):
         got_ref, carried_ref, base_ref, fade_ref = refs[i::count]
         carried = jnp.where(last, got_ref[:tokens, :].astype(F32), carried_ref[...])
-        buffer[:, i * cols : (i + 1) * cols] = (base_ref[...] + fade_ref[...] * carried).astype(BF16)
-    copy = pltpu.make_async_copy(buffer, out_any.at[:, pl.ds(first * cols, count * cols)], sem.at[0])
+        buffer[:, at : at + base_ref.shape[1]] = (base_ref[...] + fade_ref[...] * carried).astype(BF16)
+        at += base_ref.shape[1]
+    copy = pltpu.make_async_copy(buffer, out_any.at[:, pl.ds(first, at)], sem.at[0])
     copy.start()
     copy.wait()
 
@@ -412,7 +441,10 @@
             inputs = jnp.concatenate(
                 [jnp.where(lane < width, x, zero), jnp.where(lane < width, zero, x)], axis=0
             )
-            q, start = divmod(h * width, base_refs[0].shape[1])
+            q, start = 0, h * width
+            while start >= base_refs[q].shape[1]:
+                start -= base_refs[q].shape[1]
+                q += 1
             base_refs[q][:, start : start + pair] = (
                 mm(jnp.concatenate(mixing, axis=1), inputs) + skip[:, at] * x.astype(F32)
             )
@@ -421,10 +453,11 @@
 def cand_kernel(x_ref, b_ref, c_ref, decay_ref, skip_ref, *refs):
     if len(refs) > 2:
         cum_ref, *fall_refs = refs[:-2]
-        cols = fall_refs[0].shape[1]
-        fall = spread(jnp.exp(-cum_ref[...]), cols * len(fall_refs) // cum_ref.shape[1])
-        for i, ref in enumerate(fall_refs):
-            ref[...] = fall[:, i * cols : (i + 1) * cols]
+        fall = spread(jnp.exp(-cum_ref[...]), sum(ref.shape[1] for ref in fall_refs) // cum_ref.shape[1])
+        at = 0
+        for ref in fall_refs:
+            ref[...] = fall[:, at : at + ref.shape[1]]
+            at += ref.shape[1]
     base_ref, fade_ref = refs[-2:]
     steps, groups, state = b_ref.shape[1:]
     heads = decay_ref.shape[2]
@@ -571,7 +604,9 @@
     cand_wide = cand_x.shape[2]
     cols = wide // CHUNKS
     skip = bypass_weight.reshape(1, -1)
-    plan = payload_plan(groups)
+    counts = cut(heads, size)
+    width = wide // heads
+    plan = payload_plan(groups, counts)
 
     def to_core(array):
         return lax.ppermute(array, "rep", [(0, 1), (1, 0)])
@@ -593,14 +628,14 @@
     other_c = to_core(cand_c)
     kv_shape = (tokens, prefix_key_rows.shape[1] * prefix_key_rows.shape[2])
     cum, total, b2, kv, *loads = call(
-        inputs_kernel,
+        functools.partial(inputs_kernel, counts=counts),
         "inputs",
         [((tokens, heads), F32), ((8, heads), F32), ((tokens, groups * state), BF16), (kv_shape, BF16)]
         + [
             (
                 (
                     tokens + (16 if q == 0 else 0),
-                    cols + len(fresh) * state + (kv_shape[1] if q == 1 else 0),
+                    counts[q] * width + len(fresh) * state + (kv_shape[1] if q == 1 else 0),
                 ),
                 BF16,
             )
@@ -631,12 +666,12 @@
         other_c,
         after=(cum,),
     )
-    first_of = {g: q for q, fresh in enumerate(plan) for g in fresh}
+    group_of, first_of = groups_of(groups, counts)
     def intra(mark, cc):
         return call(
             functools.partial(intra_kernel, groups=groups),
             "intra",
-            [((tokens, cols), F32)] * CHUNKS,
+            [((tokens, count * width), F32) for count in counts],
             prefix_x,
             b2,
             cc,
@@ -650,7 +685,7 @@
         return call(
             cand_kernel,
             "candidates",
-            [((tokens, cols), F32)] * (CHUNKS * len(more)) + [((steps, cand_wide), F32), ((steps, cand_wide), F32)],
+            [((tokens, count * width), F32) for count in counts if more] + [((steps, cand_wide), F32), ((steps, cand_wide), F32)],
             cand_x,
             cand_b,
             cand_c,
@@ -693,12 +728,14 @@
 
     shared = dict(cols=cols, heads=heads, tokens=tokens)
     if size == 4:
+        shared = dict(counts=counts, width=width, heads=heads, tokens=tokens)
         mark = cc
         middle, carried, cands, outer, outs, raws = {}, {}, {}, {}, [], []
         rows = {"cc": cc}
+        below = (16, 2 * tokens // (counts[1] * width // kv_shape[1]), 0, 0)
 
         def inputs_of(q):
-            p = first_of[q * groups // CHUNKS]
+            p = first_of[group_of[q]]
             return got[q], got[p], loads[q], loads[p]
 
         def first(q, mark):
@@ -707,7 +744,7 @@
                 functools.partial(first_kernel, q=q, groups=groups, state=state, **shared),
                 "first",
                 extra
-                + [((state + (16 if q == 0 else 0), cols), BF16)]
+                + [((state + (16 if q == 0 else 0), counts[q] * width), BF16)]
                 + ([((2 * tokens, kv_shape[1]), BF16)] if q == 1 else []),
                 *inputs_of(q),
                 *([total] if q == 0 else [rows["own"], rows["near"]]),
@@ -729,16 +766,13 @@
                 rows["kv"] = results[1]
             return results[0]
 
-        def second(q, mark):
+        def second(q, mark, make="all"):
             results = call(
-                functools.partial(second_kernel, q=q, groups=groups, state=state, **shared),
+                functools.partial(second_kernel, q=q, groups=groups, state=state, make=make, **shared),
                 "second",
                 ([((8, wide), F32)] if q == 0 else [])
-                + [
-                    ((tokens, cols), F32),
-                    ((2 * steps, cols), F32),
-                    ((tokens + 2 * steps + [16, 2 * tokens * kv_shape[1] // cols, 0, 0][q], cols), BF16),
-                ],
+                + [((tokens, counts[q] * width), F32), ((2 * steps, counts[q] * width), F32)] * (make != "send")
+                + [((tokens + 2 * steps + below[q], counts[q] * width), BF16)] * (make != "keep"),
                 middle[q],
                 *inputs_of(q),
                 rows["own"],
@@ -751,8 +785,10 @@
             )
             if q == 0:
                 rows["later"], *results = results
-            carried[q], cands[q] = results[:2]
-            outer[q] = to_neighbour(results[2])
+            if make != "keep":
+                outer[q] = to_neighbour(results[-1])
+            if make != "send":
+                carried[q], cands[q] = results[:2]
             return results[0]
 
         def third(q, mark):
@@ -762,7 +798,7 @@
                 "third",
                 [((steps, wide), F32), ((steps, wide), BF16)]
                 if final
-                else ([((8, wide), F32)] if q == 0 else []) + [((2 * steps, cols), F32)],
+                else ([((8, wide), F32)] if q == 0 else []) + [((2 * steps, counts[q] * width), F32)],
                 outer[q],
                 cands[q],
                 rows["own"],
@@ -781,13 +817,16 @@
         def prefix(start, count, mark, into):
             span = range(start, start + count)
             return call(
-                functools.partial(prefix_kernel, first=start, cols=cols, tokens=tokens),
+                functools.partial(prefix_kernel, first=sum(counts[:start]) * width, tokens=tokens),
                 "prefix",
                 [((8, 128), F32)] if start == 0 else [],
                 *[each[q] for each in (outer, carried, base, fade) for q in span],
                 after=(mark,),
                 into=(into,),
-                scratch=[pltpu.VMEM((tokens, count * cols), BF16), pltpu.SemaphoreType.DMA((1,))],
+                scratch=[
+                    pltpu.VMEM((tokens, sum(counts[start : start + count]) * width), BF16),
+                    pltpu.SemaphoreType.DMA((1,)),
+                ],
             )
 
         *base, loads[1] = intra(cc, cc)
@@ -804,7 +843,8 @@
         mark = second(2, mark)
         mark = third(1, mark)
         mark, finish_attend = attend(mark, [rows["kv"], far_kv, outer[1]], True)
-        mark = second(3, mark)
+        mark = second(3, mark, "send")
+        mark = second(3, mark, "keep")
         mark, cand_attn = finish_attend(mark)
         mark = third(2, mark)
         mark, prefix_out = prefix(0, CHUNKS - 1, mark, (prefix_x.shape, BF16))
@@ -821,7 +861,7 @@
         *base, loads[1] = intra(cc, cc)
         mark = base[0]
         own = call(
-            functools.partial(own_kernel, cols=cols, groups=groups, state=state),
+            functools.partial(own_kernel, cols=cols, groups=groups, state=state, counts=counts),
             "own",
             [((state, cols), F32)] * CHUNKS,
             *loads,
@@ -836,7 +876,7 @@
             for q in range(CHUNKS):
                 final = last and q == CHUNKS - 1
                 if level == 0:
-                    args, lines = [got[q], got[first_of[q * groups // CHUNKS]]], got[0]
+                    args, lines = [got[q], got[first_of[group_of[q]]]], got[0]
                 else:
                     args, lines = [near[q], far[q]], near[0]
                 shapes = []

time: 52.7 us -> 52.6 us (level)
  waiting for transfers between devices: 9.74 us -> 8.81 us
    ppermute x8, waiting for transfers between devices: 7.88 us -> 6.95 us  [to_neighbour(): return lax.ppermute(array, 'seq', [(i, i ^ 1) for i in range(size)])]
    pallas_call x21 -> x22, Pallas kernels: 15.7 us -> 16.2 us  [call(): pl.pallas_call(body, out_shape=shapes, in_specs=[smem] * scalars + [anywh...]
  transfers between devices with their start and end apart: 17 -> 17, of which waited for: 7 -> 7; matrix products, arithmetic and copies ran while one was open for 0% -> 0% of each run, Pallas kernels for 23% -> 24%
where the time goes in v6:
time: 52.6 us; the launch traced here: 52 us
  starting transfers between devices  22.8 us (43%)
  Pallas kernels  16.2 us (31%)
  waiting for transfers between devices  8.81 us (17%)
  local copies, waits for them, and re-layouts  2.49 us (5%)
  between operations  1.66 us (3%)
    ppermute x8, starting transfers between devices, to_neighbour(): return lax.ppermute(array, 'seq', [(i, i ^ 1) for i in range(size)])  20 us
    pallas_call x22, Pallas kernels, call(): pl.pallas_call(body, out_shape=shapes, in_specs=[smem] * scalars + [anywh...  16.2 us
    ppermute x8, waiting for transfers between devices, to_neighbour(): return lax.ppermute(array, 'seq', [(i, i ^ 1) for i in range(size)])  6.95 us
    unnamed x42, local copies, waits for them, and re-layouts  2.49 us
    ppermute x1, starting transfers between devices, inward(): return lax.ppermute(array, 'seq', [(0, 1), (3, 2)])  2.43 us
    ppermute x3, waiting for transfers between devices, to_core(): return lax.ppermute(array, 'rep', [(0, 1), (1, 0)])  1.84 us
  transfers between devices with their start and end apart: 17, of which 7 were waited for; matrix products, arithmetic and copies ran while one was open for 0% of the time, Pallas kernels for 24%

profile of v6, /device:TPU:0, one launch (start us, length us, event | category | flops | bytes accessed | tf_op | source)
XLA Modules:
  0.0 52.0 jit_solution(1725191243014938160)
XLA Ops:
  0.7 3.0 %inputs.1 = (f32[128,32]{1,0:T(8,128)}, f32[8,32]{1,0:T(8,128)}, bf16[128,512]{1,0:T(8,128)(2,1)}, bf16[128,256]{1,0:T(8,128)(2,1)}, bf16[144,768]{1,0:T(8,128)(...) custom-call(bf16[128,2048]{1,0:T(8,128)(2,1)} %refs_0_.8, ...), custom_call_target="tpu_custom_call" | custom-call | tf_op jit(solution)/shard_map/inputs/pallas_call | solution.py:565
  3.7 3.1 %collective-permute-start.2 = (bf16[144,768]{1,0:T(8,128)(2,1)}, bf16[144,768]{1,0:T(8,128)(2,1)S(1)}, u32[]{:S(2)}, u32[]{:S(2)}) collective-permute-start(bf16[144,768]{1,0:T(8,128)(2,1)} %get-tuple-element.55.refs_2_.refs_3_.refs_4_), channel_id=1, source_target_pairs={{0,4},{4,0},{8,12},{12,8},{1,5},{5,1},{9,13},{13,9},{2,6},{6,2},{1... | collective-permute-start | bytes 663560 | tf_op jit(solution)/shard_map/ppermute | solution.py:615
  6.7 0.0 collective-permute-start
  6.7 1.3 %collective-permute-done.refs_2_ = bf16[1,32,4,256]{3,2,1,0:T(4,128)(2,1)S(1)} collective-permute-done((bf16[1,32,4,256]{3,2,1,0:T(4,128)(2,1)S(1)}, bf16[1,32,4,256]{3,2,1,0:T(4,128)(2,1)S(1)}, u32[]{:S(2)}, u32[]{:S(2)}) %collective-permute-start) | collective-permute-done | bytes 65568 | tf_op jit(solution)/shard_map/ppermute | solution.py:612
  8.0 0.8 %copy-done.4 = f32[128,32]{1,0:T(8,128)S(1)} copy-done((f32[128,32]{1,0:T(8,128)S(1)}, f32[128,32]{1,0:T(8,128)}, u32[]{:S(2)}) %copy-start.4) | copy-done | bytes 16408
  8.8 0.6 %projections.1.refs_2_.refs_5_.refs_6_ = bf16[192,512]{1,0:T(8,128)(2,1)S(1)} custom-call(bf16[128,2,256]{2,1,0:T(2,128)(2,1)S(1)} %copy-done.13, bf16[1,32,4,256]{3,2,1,0:T(4,128)(2,1)S(1)} %copy-done.10, bf16[1,32,4,256]{3,2,1,0:T(4,128)(2,1)S(1)} %collective-permute-done.refs_2_, f32[128,32]{1,0:T(8,128)S(1)} %copy-done.4), custom_call_target="tpu_custom_call" | custom-call | tf_op jit(solution)/shard_map/projections/pallas_call | solution.py:565
  9.4 0.0 copy-start.20
  9.4 0.3 copy-done.3
  9.8 0.1 copy-done.12
  9.8 0.3 copy-done.20
  10.1 1.0 %intra.1 = (f32[128,512]{1,0:T(8,128)S(1)}, f32[128,512]{1,0:T(8,128)S(1)}, f32[128,512]{1,0:T(8,128)S(1)}, f32[128,512]{1,0:T(8,128)S(1)}, bf16[128,768]{1,0:T(8,128)(2,1)S(1)}) custom-call(bf16[128,2048]{1,0:T(8,128)(2,1)S(1)} %copy-done.1, bf16[128,512]{1,0:T(8,128)(2,1)S(1)} %copy-done.12, ...), custom_call_target="tpu_custom_call", output_to_operand_aliasing={{4}: (6, {})} | custom-call | tf_op jit(solution)/shard_map/intra/pallas_call | solution.py:565
  11.1 0.2 collective-permute-start.1
  11.3 1.1 %collective-permute-done.2.refs_0_.refs_1_.refs_2_ = bf16[144,768]{1,0:T(8,128)(2,1)S(1)} collective-permute-done((bf16[144,768]{1,0:T(8,128)(2,1)}, bf16[144,768]{1,0:T(8,128)(2,1)S(1)}, u32[]{:S(2)}, u32[]{:S(2)}) %collective-permute-start.2) | collective-permute-done | bytes 221216 | tf_op jit(solution)/shard_map/ppermute | solution.py:615
  12.4 0.5 first.4
  12.9 0.1 collective-permute-start.8
  12.9 3.3 %collective-permute-start.6 = (bf16[192,512]{1,0:T(8,128)(2,1)S(1)}, bf16[192,512]{1,0:T(8,128)(2,1)S(1)}, u32[]{:S(2)}, u32[]{:S(2)}) collective-permute-start(bf16[192,512]{1,0:T(8,128)(2,1)S(1)} %get-tuple-element.67.refs_6_), channel_id=1, source_target_pairs={{0,4},{4,0},{8,12},{12,8},{1,5},{5,1},{9,13},{13,9},{2,6},{6,2},{1... | collective-permute-start | bytes 589832 | tf_op jit(solution)/shard_map/ppermute | solution.py:615
  16.2 2.7 %collective-permute-done.1.refs_0_.refs_1_ = bf16[128,768]{1,0:T(8,128)(2,1)S(1)} collective-permute-done((bf16[128,768]{1,0:T(8,128)(2,1)S(1)}, bf16[128,768]{1,0:T(8,128)(2,1)S(1)}, u32[]{:S(2)}, u32[]{:S(2)}) %collective-permute-start.1) | collective-permute-done | bytes 196640 | tf_op jit(solution)/shard_map/ppermute | solution.py:615
  18.9 0.4 first.5
  19.3 0.1 collective-permute-start.5
  19.4 3.1 %collective-permute-start.4 = (bf16[128,768]{1,0:T(8,128)(2,1)S(1)}, bf16[128,768]{1,0:T(8,128)(2,1)S(1)}, u32[]{:S(2)}, u32[]{:S(2)}) collective-permute-start(bf16[128,768]{1,0:T(8,128)(2,1)S(1)} %get-tuple-element.65.refs_2_.refs_3_.refs_4_), channel_id=1, source_target_pairs={{0,4},{4,0},{8,12},{12,8},{1,5},{5,1},{9,13},{13,9},{2,6},{6,2},{1... | collective-permute-start | bytes 589832 | tf_op jit(solution)/shard_map/ppermute | solution.py:615
  22.5 0.0 collective-permute-done.6.refs_7_
  22.5 2.4 %collective-permute-start.3 = (bf16[128,512]{1,0:T(8,128)(2,1)S(1)}, bf16[128,512]{1,0:T(8,128)(2,1)S(1)}, u32[]{:S(2)}, u32[]{:S(2)}) collective-permute-start(bf16[128,512]{1,0:T(8,128)(2,1)S(1)} %get-tuple-element.64.refs_2_.refs_3_), channel_id=1, source_target_pairs={{0,4},{12,8},{1,5},{13,9},{2,6},{14,10},{3,7},{15,11},{16,20},{28,... | collective-permute-start | bytes 393224 | tf_op jit(solution)/shard_map/ppermute | solution.py:626
  24.9 0.0 collective-permute-done.8.refs_0_
  25.0 0.8 %second.5 = (f32[8,2048]{1,0:T(8,128)S(1)}, f32[128,512]{1,0:T(8,128)S(1)}, f32[64,512]{1,0:T(8,128)S(1)}, bf16[208,512]{1,0:T(8,128)(2,1)S(1)}) custom-call(bf16[272,512]{1,0:T(8,128)(2,1)S(1)} %collective-permute-done.8.refs_0_, bf16[144,768]{1,0:T(8,128)(2,1)S(1)} %collective-permute-done.2.refs_0_.refs_1_.refs_2_, ...), custom_call_target="tpu_custom_call" | custom-call | flops 1000000000 | tf_op jit(solution)/shard_map/second/pallas_call | solution.py:565
  25.8 0.1 collective-permute-start.11
  25.9 0.8 %collective-permute-done.4.refs_0_.refs_1_.refs_2_ = bf16[128,768]{1,0:T(8,128)(2,1)S(1)} collective-permute-done((bf16[128,768]{1,0:T(8,128)(2,1)S(1)}, bf16[128,768]{1,0:T(8,128)(2,1)S(1)}, u32[]{:S(2)}, u32[]{:S(2)}) %collective-permute-start.4) | collective-permute-done | bytes 196640 | tf_op jit(solution)/shard_map/ppermute | solution.py:615
  26.7 0.3 first.6.refs_10_
  27.0 0.1 collective-permute-start.12
  27.1 0.0 collective-permute-done.7.refs_8_.refs_1_
  27.1 0.0 collective-permute-done.5.refs_0_
  27.1 0.7 %second.6 = (f32[128,512]{1,0:T(8,128)S(1)}, f32[64,512]{1,0:T(8,128)S(1)}, bf16[320,512]{1,0:T(8,128)(2,1)S(1)}) custom-call(bf16[256,512]{1,0:T(8,128)(2,1)S(1)} %collective-permute-done.5.refs_0_, bf16[128,768]{1,0:T(8,128)(2,1)S(1)} %collective-permute-done.1.refs_0_.refs_1_, bf16[144,768]{1,0:T(8,128)(2,1)S(1)} %collective-permute-done.2.refs_0_.refs_1_.refs_2_, ...), custom_call_target="tpu_custom_call" | custom-call | flops 1000000000 | tf_op jit(solution)/shard_map/second/pallas_call | solution.py:565
  27.9 4.5 %collective-permute-start.10 = (bf16[320,512]{1,0:T(8,128)(2,1)S(1)}, bf16[320,512]{1,0:T(8,128)(2,1)S(1)}, u32[]{:S(2)}, u32[]{:S(2)}) collective-permute-start(bf16[320,512]{1,0:T(8,128)(2,1)S(1)} %get-tuple-element.73), channel_id=1, source_target_pairs={{0,4},{4,0},{8,12},{12,8},{1,5},{5,1},{9,13},{13,9},{2,6},{6,2},{1... | collective-permute-start | bytes 983048 | tf_op jit(solution)/shard_map/ppermute | solution.py:615
  32.3 0.0 copy-start.18
  32.3 0.3 first.7.refs_6_
  32.7 0.1 collective-permute-start.9
  32.8 0.4 copy-done.5
  33.2 0.1 copy-done.9
  33.3 2.0 %candidates.1 = (f32[128,512]{1,0:T(8,128)S(1)}, f32[128,512]{1,0:T(8,128)S(1)}, f32[128,512]{1,0:T(8,128)S(1)}, f32[128,512]{1,0:T(8,128)S(1)}, f32[32,4096]{1,0:T(8,128)S(1)}, /*index=5*/f32[32,4096]{1,0:T(8,128)S(1)}) custom-call(bf16[1,32,4096]{2,1,0:T(8,128)(2,1)S(1)} %copy-done.9, bf16[1,32,4,256]{3,2,1,0:T(4,128)(2,1)S(1)} %copy-done.14, ...), custom_call_target="tpu_custom_call" | custom-call | tf_op jit(solution)/shard_map/candidates/pallas_call | solution.py:565
  35.3 0.0 collective-permute-done.11.refs_0_
  35.3 0.2 third.4
  35.6 0.0 collective-permute-done.12.refs_0_
  35.6 0.7 %second.7 = (f32[128,512]{1,0:T(8,128)S(1)}, f32[64,512]{1,0:T(8,128)S(1)}, bf16[192,512]{1,0:T(8,128)(2,1)S(1)}) custom-call(bf16[256,512]{1,0:T(8,128)(2,1)S(1)} %collective-permute-done.12.refs_0_, bf16[128,768]{1,0:T(8,128)(2,1)S(1)} %collective-permute-done.4.refs_0_.refs_1_.refs_2_, ...), custom_call_target="tpu_custom_call" | custom-call | flops 1000000000 | tf_op jit(solution)/shard_map/second/pallas_call | solution.py:565
  36.3 3.2 %collective-permute-start.14 = (bf16[192,512]{1,0:T(8,128)(2,1)S(1)}, bf16[192,512]{1,0:T(8,128)(2,1)S(1)}, u32[]{:S(2)}, u32[]{:S(2)}) collective-permute-start(bf16[192,512]{1,0:T(8,128)(2,1)S(1)} %get-tuple-element.85), channel_id=1, source_target_pairs={{0,4},{4,0},{8,12},{12,8},{1,5},{5,1},{9,13},{13,9},{2,6},{6,2},{1... | collective-permute-start | bytes 589832 | tf_op jit(solution)/shard_map/ppermute | solution.py:615
  39.5 1.3 %collective-permute-done.10.refs_0_.refs_2_.refs_1_ = bf16[320,512]{1,0:T(8,128)(2,1)S(1)} collective-permute-done((bf16[320,512]{1,0:T(8,128)(2,1)S(1)}, bf16[320,512]{1,0:T(8,128)(2,1)S(1)}, u32[]{:S(2)}, u32[]{:S(2)}) %collective-permute-start.10) | collective-permute-done | bytes 327712 | tf_op jit(solution)/shard_map/ppermute | solution.py:615
  40.9 0.1 collective-permute-start.15
  41.0 0.6 %second.8.refs_9_ = bf16[192,512]{1,0:T(8,128)(2,1)S(1)} custom-call(bf16[256,512]{1,0:T(8,128)(2,1)S(1)} %collective-permute-done.9.refs_0_, bf16[128,512]{1,0:T(8,128)(2,1)S(1)} %collective-permute-done.3.refs_0_.refs_1_, bf16[128,768]{1,0:T(8,128)(2,1)S(1)} %collective-permute-done.4.refs_0_.refs_1_.refs_2_, ...), custom_call_target="tpu_custom_call" | custom-call | flops 1000000000 | tf_op jit(solution)/shard_map/second/pallas_call | solution.py:565
  41.6 2.5 %collective-permute-start.13 = (bf16[192,512]{1,0:T(8,128)(2,1)S(1)}, bf16[192,512]{1,0:T(8,128)(2,1)S(1)}, u32[]{:S(2)}, u32[]{:S(2)}) collective-permute-start(bf16[192,512]{1,0:T(8,128)(2,1)S(1)} %second.8.refs_9_), channel_id=1, source_target_pairs={{0,4},{4,0},{8,12},{12,8},{1,5},{5,1},{9,13},{13,9},{2,6},{6,2},{1... | collective-permute-start | bytes 589832 | tf_op jit(solution)/shard_map/ppermute | solution.py:615
  44.8 0.0 copy-start.7
  44.8 0.0 copy-start.8
  44.8 0.0 copy-start.11
  44.8 0.0 copy-start.16
  44.8 0.0 copy-start.17
  44.8 0.5 %second.9 = (f32[128,512]{1,0:T(8,128)S(1)}, f32[64,512]{1,0:T(8,128)S(1)}) custom-call(bf16[256,512]{1,0:T(8,128)(2,1)S(1)} %collective-permute-done.9.refs_0_, bf16[128,512]{1,0:T(8,128)(2,1)S(1)} %collective-permute-done.3.refs_0_.refs_1_, bf16[128,768]{1,0:T(8,128)(2,1)S(1)} %collective-permute-done.4.refs_0_.refs_1_.refs_2_, ...), custom_call_target="tpu_custom_call" | custom-call | flops 1000000000 | tf_op jit(solution)/shard_map/second/pallas_call | solution.py:565
  45.4 0.2 copy-done.7
  45.6 0.0 copy-done.8
  45.6 0.1 copy-done.11
  45.8 1.9 %attend.1 = (f32[8,128]{1,0:T(8,128)S(1)}, bf16[1,32,16,128]{3,2,1,0:T(8,128)(2,1)}) custom-call(s32[1]{0:T(128)S(6)} %copy.28.refs_0_, bf16[1,32,16,128]{3,2,1,0:T(8,128)(2,1)S(1)} %copy-done.11, bf16[1,32,2,128]{3,2,1,0:T(2,128)(2,1)S(1)} %copy-done.16, bf16[1,32,2,128]{3,2,1,0:T(2,128)(2,1)S(1)} %copy-done.17, bf16[128,2,128]{2,1,0:T(2,128)(2,1)S(1)} %copy-done.7, ...), custom_call_target="tpu_custom_call" | custom-call | tf_op jit(solution)/shard_map/attend/pallas_call | solution.py:565
  47.7 0.9 %prefix.2 = (f32[8,128]{1,0:T(8,128)S(1)}, bf16[128,2048]{1,0:T(8,128)(2,1)}) custom-call(bf16[208,512]{1,0:T(8,128)(2,1)S(1)} %collective-permute-done.11.refs_0_, bf16[320,512]{1,0:T(8,128)(2,1)S(1)} %collective-permute-done.10.refs_0_.refs_2_.refs_1_, bf16[192,512]{1,0:T(8,128)(2,1)S(1)} %collective-permute-done.14.refs_0_.refs_2_, ...), custom_call_target="tpu_custom_call" | custom-call | tf_op jit(solution)/shard_map/prefix/pallas_call | solution.py:565
  48.6 1.0 %collective-permute-done.13.refs_0_ = bf16[192,512]{1,0:T(8,128)(2,1)S(1)} collective-permute-done((bf16[192,512]{1,0:T(8,128)(2,1)S(1)}, bf16[192,512]{1,0:T(8,128)(2,1)S(1)}, u32[]{:S(2)}, u32[]{:S(2)}) %collective-permute-start.13) | collective-permute-done | bytes 196640 | tf_op jit(solution)/shard_map/ppermute | solution.py:615
  49.7 0.1 third.7
  49.7 0.1 collective-permute-start.16
  49.8 0.7 %prefix.3 = bf16[128,2048]{1,0:T(8,128)(2,1)} custom-call(bf16[192,512]{1,0:T(8,128)(2,1)S(1)} %collective-permute-done.13.refs_0_, f32[128,512]{1,0:T(8,128)S(1)} %get-tuple-element.81.refs_8_.refs_1_, f32[128,512]{1,0:T(8,128)S(1)} %get-tuple-element.82.refs_2_, f32[128,512]{1,0:T(8,128)S(1)} %get-tuple-element.83.refs_3_, ...), custom_call_target="tpu_custom_call", output_to_operand_aliasing={{}: (5, {})} | custom-call | tf_op jit(solution)/shard_map/prefix/pallas_call | solution.py:565
  50.6 0.6 %collective-permute-done.16.refs_4_ = bf16[32,2048]{1,0:T(8,128)(2,1)S(1)} collective-permute-done((bf16[32,2048]{1,0:T(8,128)(2,1)S(1)}, bf16[32,2048]{1,0:T(8,128)(2,1)S(1)}, u32[]{:S(2)}, u32[]{:S(2)}) %collective-permute-start.16) | collective-permute-done | bytes 131104 | tf_op jit(solution)/shard_map/ppermute | solution.py:612
  51.2 0.8 %close.1 = bf16[1,32,4096]{2,1,0:T(8,128)(2,1)} custom-call(s32[1]{0:T(128)S(6)} %copy.28.refs_0_, f32[32,4096]{1,0:T(8,128)S(1)} %get-tuple-element.77.refs_3_.refs_1_, f32[32,4096]{1,0:T(8,128)S(1)} %get-tuple-element.96.refs_2_, f32[32,2048]{1,0:T(8,128)S(1)} %get-tuple-element.94.refs_4_.refs_3_, bf16[32,2048]{1,0:T(8,128)(2,1)S(1)} %collective-permute-done.16.refs_4_), custom_call_target="tpu_custom_call" | custom-call | tf_op jit(solution)/shard_map/close/pallas_call | solution.py:565
  (34 shorter events, 0.2 us)
Async XLA Ops:
  0.6 6.1 %copy-start.10 = (bf16[1,32,4,256]{3,2,1,0:T(4,128)(2,1)S(1)}, bf16[1,32,4,256]{3,2,1,0:T(4,128)(2,1)}, u32[]{:S(2)}) copy-start(bf16[1,32,4,256]{3,2,1,0:T(4,128)(2,1)} %refs_2_.2) | copy-start | bytes 196612
  0.6 7.4 %copy-start.13 = (bf16[128,2,256]{2,1,0:T(2,128)(2,1)S(1)}, bf16[128,2,256]{2,1,0:T(2,128)(2,1)}, u32[]{:S(2)}) copy-start(bf16[128,2,256]{2,1,0:T(2,128)(2,1)} %refs_0_.7) | copy-start | bytes 393220
  0.7 8.8 %copy-start.1 = (bf16[128,2048]{1,0:T(8,128)(2,1)S(1)}, bf16[128,2048]{1,0:T(8,128)(2,1)}, u32[]{:S(2)}) copy-start(bf16[128,2048]{1,0:T(8,128)(2,1)} %refs_0_.8) | copy-start | bytes 1572868
  3.7 8.7 %collective-permute-start.2 = (bf16[144,768]{1,0:T(8,128)(2,1)}, bf16[144,768]{1,0:T(8,128)(2,1)S(1)}, u32[]{:S(2)}, u32[]{:S(2)}) collective-permute-start(bf16[144,768]{1,0:T(8,128)(2,1)} %get-tuple-element.55.refs_2_.refs_3_.refs_4_), channel_id=1, source_target_pairs={{0,4},{4,0},{8,12},{12,8},{1,5},{5,1},{9,13},{13,9},{2,6},{6,2},{1... | collective-permute-start | bytes 663560 | tf_op jit(solution)/shard_map/ppermute | solution.py:615
  6.7 1.3 %collective-permute-start = (bf16[1,32,4,256]{3,2,1,0:T(4,128)(2,1)S(1)}, bf16[1,32,4,256]{3,2,1,0:T(4,128)(2,1)S(1)}, u32[]{:S(2)}, u32[]{:S(2)}) collective-permute-start(bf16[1,32,4,256]{3,2,1,0:T(4,128)(2,1)S(1)} %copy-done.10), channel_id=1, source_target_pairs={{0,1},{1,0},{2,3},{3,2},{4,5},{5,4},{6,7},{7,6},{8,9},{9,8},{10,11... | collective-permute-start | bytes 196616 | tf_op jit(solution)/shard_map/ppermute | solution.py:612
  8.0 0.8 %copy-start.4 = (f32[128,32]{1,0:T(8,128)S(1)}, f32[128,32]{1,0:T(8,128)}, u32[]{:S(2)}) copy-start(f32[128,32]{1,0:T(8,128)} %get-tuple-element.52.refs_3_.refs_5_) | copy-start | bytes 49156
  8.8 0.9 %copy-start.3 = (bf16[128,768]{1,0:T(8,128)(2,1)S(1)}, bf16[128,768]{1,0:T(8,128)(2,1)}, u32[]{:S(2)}) copy-start(bf16[128,768]{1,0:T(8,128)(2,1)} %get-tuple-element.53.refs_6_) | copy-start | bytes 589828
  8.8 1.0 %copy-start.12 = (bf16[128,512]{1,0:T(8,128)(2,1)S(1)}, bf16[128,512]{1,0:T(8,128)(2,1)}, u32[]{:S(2)}) copy-start(bf16[128,512]{1,0:T(8,128)(2,1)} %get-tuple-element.51.refs_1_) | copy-start | bytes 393220
  9.4 0.7 %copy-start.20 = (f32[128]{0:T(128)S(1)}, f32[128]{0:T(128)}, u32[]{:S(2)}) copy-start(f32[128]{0:T(128)} %param.19) | copy-start | bytes 1540
  10.1 2.3 %copy-start.2 = (bf16[144,768]{1,0:T(8,128)(2,1)S(1)}, bf16[144,768]{1,0:T(8,128)(2,1)}, u32[]{:S(2)}) copy-start(bf16[144,768]{1,0:T(8,128)(2,1)} %get-tuple-element.55.refs_2_.refs_3_.refs_4_) | copy-start | bytes 663556
  11.1 1.3 %copy-start.19 = (f32[8,32]{1,0:T(8,128)S(1)}, f32[8,32]{1,0:T(8,128)}, u32[]{:S(2)}) copy-start(f32[8,32]{1,0:T(8,128)} %get-tuple-element.56.refs_4_.refs_8_) | copy-start | bytes 3076
  11.1 7.8 %collective-permute-start.1 = (bf16[128,768]{1,0:T(8,128)(2,1)S(1)}, bf16[128,768]{1,0:T(8,128)(2,1)S(1)}, u32[]{:S(2)}, u32[]{:S(2)}) collective-permute-start(bf16[128,768]{1,0:T(8,128)(2,1)S(1)} %get-tuple-element.54.refs_2_.refs_3_), channel_id=1, source_target_pairs={{0,4},{4,0},{8,12},{12,8},{1,5},{5,1},{9,13},{13,9},{2,6},{6,2},{1... | collective-permute-start | bytes 589832 | tf_op jit(solution)/shard_map/ppermute | solution.py:615
  12.4 6.5 %copy-start = (bf16[128,768]{1,0:T(8,128)(2,1)S(1)}, bf16[128,768]{1,0:T(8,128)(2,1)}, u32[]{:S(2)}) copy-start(bf16[128,768]{1,0:T(8,128)(2,1)} %get-tuple-element.62.refs_8_) | copy-start | bytes 589828
  12.4 6.5 %copy-start.6 = (bf16[128,512]{1,0:T(8,128)(2,1)S(1)}, bf16[128,512]{1,0:T(8,128)(2,1)}, u32[]{:S(2)}) copy-start(bf16[128,512]{1,0:T(8,128)(2,1)} %get-tuple-element.63.refs_9_) | copy-start | bytes 393220
  12.4 6.5 %copy-start.15 = (bf16[128,256]{1,0:T(8,128)(2,1)S(1)}, bf16[128,256]{1,0:T(8,128)(2,1)}, u32[]{:S(2)}) copy-start(bf16[128,256]{1,0:T(8,128)(2,1)} %get-tuple-element.60.refs_6_) | copy-start | bytes 196612
  12.9 12.1 %collective-permute-start.8 = (bf16[272,512]{1,0:T(8,128)(2,1)S(1)}, bf16[272,512]{1,0:T(8,128)(2,1)S(1)}, u32[]{:S(2)}, u32[]{:S(2)}) collective-permute-start(bf16[272,512]{1,0:T(8,128)(2,1)S(1)} %get-tuple-element.61.refs_7_), channel_id=1, source_target_pairs={{0,1},{1,0},{4,8},{5,9},{8,4},{9,5},{12,13},{13,12},{2,3},{3,2},{6... | collective-permute-start | bytes 835592 | tf_op jit(solution)/shard_map/ppermute | solution.py:623
  12.9 9.6 %collective-permute-start.6 = (bf16[192,512]{1,0:T(8,128)(2,1)S(1)}, bf16[192,512]{1,0:T(8,128)(2,1)S(1)}, u32[]{:S(2)}, u32[]{:S(2)}) collective-permute-start(bf16[192,512]{1,0:T(8,128)(2,1)S(1)} %get-tuple-element.67.refs_6_), channel_id=1, source_target_pairs={{0,4},{4,0},{8,12},{12,8},{1,5},{5,1},{9,13},{13,9},{2,6},{6,2},{1... | collective-permute-start | bytes 589832 | tf_op jit(solution)/shard_map/ppermute | solution.py:615
  19.3 7.8 %collective-permute-start.5 = (bf16[256,512]{1,0:T(8,128)(2,1)S(1)}, bf16[256,512]{1,0:T(8,128)(2,1)S(1)}, u32[]{:S(2)}, u32[]{:S(2)}) collective-permute-start(bf16[256,512]{1,0:T(8,128)(2,1)S(1)} %get-tuple-element.66.refs_10_), channel_id=1, source_target_pairs={{0,1},{1,0},{4,8},{5,9},{8,4},{9,5},{12,13},{13,12},{2,3},{3,2},{6... | collective-permute-start | bytes 786440 | tf_op jit(solution)/shard_map/ppermute | solution.py:623
  19.4 7.3 %collective-permute-start.4 = (bf16[128,768]{1,0:T(8,128)(2,1)S(1)}, bf16[128,768]{1,0:T(8,128)(2,1)S(1)}, u32[]{:S(2)}, u32[]{:S(2)}) collective-permute-start(bf16[128,768]{1,0:T(8,128)(2,1)S(1)} %get-tuple-element.65.refs_2_.refs_3_.refs_4_), channel_id=1, source_target_pairs={{0,4},{4,0},{8,12},{12,8},{1,5},{5,1},{9,13},{13,9},{2,6},{6,2},{1... | collective-permute-start | bytes 589832 | tf_op jit(solution)/shard_map/ppermute | solution.py:615
  22.5 4.6 %collective-permute-start.7 = (bf16[256,256]{1,0:T(8,128)(2,1)S(1)}, bf16[256,256]{1,0:T(8,128)(2,1)S(1)}, u32[]{:S(2)}, u32[]{:S(2)}) collective-permute-start(bf16[256,256]{1,0:T(8,128)(2,1)S(1)} %get-tuple-element.68.refs_0_), channel_id=1, source_target_pairs={{0,1},{1,0},{4,8},{5,9},{8,4},{9,5},{12,13},{13,12},{2,3},{3,2},{6... | collective-permute-start | bytes 393224 | tf_op jit(solution)/shard_map/ppermute | solution.py:623
  22.5 9.8 %collective-permute-start.3 = (bf16[128,512]{1,0:T(8,128)(2,1)S(1)}, bf16[128,512]{1,0:T(8,128)(2,1)S(1)}, u32[]{:S(2)}, u32[]{:S(2)}) collective-permute-start(bf16[128,512]{1,0:T(8,128)(2,1)S(1)} %get-tuple-element.64.refs_2_.refs_3_), channel_id=1, source_target_pairs={{0,4},{12,8},{1,5},{13,9},{2,6},{14,10},{3,7},{15,11},{16,20},{28,... | collective-permute-start | bytes 393224 | tf_op jit(solution)/shard_map/ppermute | solution.py:626
  25.8 9.6 %collective-permute-start.11 = (bf16[208,512]{1,0:T(8,128)(2,1)S(1)}, bf16[208,512]{1,0:T(8,128)(2,1)S(1)}, u32[]{:S(2)}, u32[]{:S(2)}) collective-permute-start(bf16[208,512]{1,0:T(8,128)(2,1)S(1)} %get-tuple-element.75), channel_id=1, source_target_pairs={{0,4},{4,0},{8,12},{12,8},{1,5},{5,1},{9,13},{13,9},{2,6},{6,2},{1... | collective-permute-start | bytes 638984 | tf_op jit(solution)/shard_map/ppermute | solution.py:615
  27.0 8.5 %collective-permute-start.12 = (bf16[256,512]{1,0:T(8,128)(2,1)S(1)}, bf16[256,512]{1,0:T(8,128)(2,1)S(1)}, u32[]{:S(2)}, u32[]{:S(2)}) collective-permute-start(bf16[256,512]{1,0:T(8,128)(2,1)S(1)} %first.6.refs_10_), channel_id=1, source_target_pairs={{0,1},{1,0},{4,8},{5,9},{8,4},{9,5},{12,13},{13,12},{2,3},{3,2},{6... | collective-permute-start | bytes 786440 | tf_op jit(solution)/shard_map/ppermute | solution.py:623
  27.9 13.0 %collective-permute-start.10 = (bf16[320,512]{1,0:T(8,128)(2,1)S(1)}, bf16[320,512]{1,0:T(8,128)(2,1)S(1)}, u32[]{:S(2)}, u32[]{:S(2)}) collective-permute-start(bf16[320,512]{1,0:T(8,128)(2,1)S(1)} %get-tuple-element.73), channel_id=1, source_target_pairs={{0,4},{4,0},{8,12},{12,8},{1,5},{5,1},{9,13},{13,9},{2,6},{6,2},{1... | collective-permute-start | bytes 983048 | tf_op jit(solution)/shard_map/ppermute | solution.py:615
  32.3 0.8 %copy-start.5 = (f32[128,32]{1,0:T(8,128)S(1)}, f32[128,32]{1,0:T(8,128)}, u32[]{:S(2)}) copy-start(f32[128,32]{1,0:T(8,128)} %get-tuple-element.52.refs_3_.refs_5_) | copy-start | bytes 49156
  32.3 1.0 %copy-start.9 = (bf16[1,32,4096]{2,1,0:T(8,128)(2,1)S(1)}, bf16[1,32,4096]{2,1,0:T(8,128)(2,1)}, u32[]{:S(2)}) copy-start(bf16[1,32,4096]{2,1,0:T(8,128)(2,1)} %refs_0_.9) | copy-start | bytes 786436
  32.3 1.0 %copy-start.14 = (bf16[1,32,4,256]{3,2,1,0:T(4,128)(2,1)S(1)}, bf16[1,32,4,256]{3,2,1,0:T(4,128)(2,1)}, u32[]{:S(2)}) copy-start(bf16[1,32,4,256]{3,2,1,0:T(4,128)(2,1)} %refs_1_.6) | copy-start | bytes 196612
  32.3 1.0 %copy-start.18 = (f32[1,32,64]{2,1,0:T(8,128)S(1)}, f32[1,32,64]{2,1,0:T(8,128)}, u32[]{:S(2)}) copy-start(f32[1,32,64]{2,1,0:T(8,128)} %refs_3_.4) | copy-start | bytes 24580
  32.7 8.3 %collective-permute-start.9 = (bf16[256,512]{1,0:T(8,128)(2,1)S(1)}, bf16[256,512]{1,0:T(8,128)(2,1)S(1)}, u32[]{:S(2)}, u32[]{:S(2)}) collective-permute-start(bf16[256,512]{1,0:T(8,128)(2,1)S(1)} %first.7.refs_6_), channel_id=1, source_target_pairs={{0,1},{1,0},{4,8},{5,9},{8,4},{9,5},{12,13},{13,12},{2,3},{3,2},{6... | collective-permute-start | bytes 786440 | tf_op jit(solution)/shard_map/ppermute | solution.py:623
  36.3 11.4 %collective-permute-start.14 = (bf16[192,512]{1,0:T(8,128)(2,1)S(1)}, bf16[192,512]{1,0:T(8,128)(2,1)S(1)}, u32[]{:S(2)}, u32[]{:S(2)}) collective-permute-start(bf16[192,512]{1,0:T(8,128)(2,1)S(1)} %get-tuple-element.85), channel_id=1, source_target_pairs={{0,4},{4,0},{8,12},{12,8},{1,5},{5,1},{9,13},{13,9},{2,6},{6,2},{1... | collective-permute-start | bytes 589832 | tf_op jit(solution)/shard_map/ppermute | solution.py:615
  40.9 4.5 %collective-permute-start.15 = (bf16[384,256]{1,0:T(8,128)(2,1)S(1)}, bf16[384,256]{1,0:T(8,128)(2,1)S(1)}, u32[]{:S(2)}, u32[]{:S(2)}) collective-permute-start(bf16[384,256]{1,0:T(8,128)(2,1)S(1)} %collect.1.refs_9_.refs_6_), channel_id=1, source_target_pairs={{0,1},{1,0},{2,3},{3,2},{4,5},{5,4},{6,7},{7,6},{8,9},{9,8},{10,11... | collective-permute-start | bytes 589832 | tf_op jit(solution)/shard_map/ppermute | solution.py:612
  41.6 8.1 %collective-permute-start.13 = (bf16[192,512]{1,0:T(8,128)(2,1)S(1)}, bf16[192,512]{1,0:T(8,128)(2,1)S(1)}, u32[]{:S(2)}, u32[]{:S(2)}) collective-permute-start(bf16[192,512]{1,0:T(8,128)(2,1)S(1)} %second.8.refs_9_), channel_id=1, source_target_pairs={{0,4},{4,0},{8,12},{12,8},{1,5},{5,1},{9,13},{13,9},{2,6},{6,2},{1... | collective-permute-start | bytes 589832 | tf_op jit(solution)/shard_map/ppermute | solution.py:615
  44.8 0.8 %copy-start.7 = (bf16[128,2,128]{2,1,0:T(2,128)(2,1)S(1)}, bf16[128,2,128]{2,1,0:T(2,128)(2,1)}, u32[]{:S(2)}) copy-start(bf16[128,2,128]{2,1,0:T(2,128)(2,1)} %refs_4_.3) | copy-start | bytes 196612
  44.8 0.9 %copy-start.8 = (bf16[128,2,128]{2,1,0:T(2,128)(2,1)S(1)}, bf16[128,2,128]{2,1,0:T(2,128)(2,1)}, u32[]{:S(2)}) copy-start(bf16[128,2,128]{2,1,0:T(2,128)(2,1)} %refs_5_.1) | copy-start | bytes 196612
  44.8 1.0 %copy-start.11 = (bf16[1,32,16,128]{3,2,1,0:T(8,128)(2,1)S(1)}, bf16[1,32,16,128]{3,2,1,0:T(8,128)(2,1)}, u32[]{:S(2)}) copy-start(bf16[1,32,16,128]{3,2,1,0:T(8,128)(2,1)} %refs_1_.7) | copy-start | bytes 393220
  44.8 0.9 %copy-start.16 = (bf16[1,32,2,128]{3,2,1,0:T(2,128)(2,1)S(1)}, bf16[1,32,2,128]{3,2,1,0:T(2,128)(2,1)}, u32[]{:S(2)}) copy-start(bf16[1,32,2,128]{3,2,1,0:T(2,128)(2,1)} %refs_2_.3) | copy-start | bytes 49156
  44.8 0.9 %copy-start.17 = (bf16[1,32,2,128]{3,2,1,0:T(2,128)(2,1)S(1)}, bf16[1,32,2,128]{3,2,1,0:T(2,128)(2,1)}, u32[]{:S(2)}) copy-start(bf16[1,32,2,128]{3,2,1,0:T(2,128)(2,1)} %refs_3_.5) | copy-start | bytes 49156
  49.7 1.4 %collective-permute-start.16 = (bf16[32,2048]{1,0:T(8,128)(2,1)S(1)}, bf16[32,2048]{1,0:T(8,128)(2,1)S(1)}, u32[]{:S(2)}, u32[]{:S(2)}) collective-permute-start(bf16[32,2048]{1,0:T(8,128)(2,1)S(1)} %get-tuple-element.97), channel_id=1, source_target_pairs={{0,1},{1,0},{2,3},{3,2},{4,5},{5,4},{6,7},{7,6},{8,9},{9,8},{10,11... | collective-permute-start | bytes 393224 | tf_op jit(solution)/shard_map/ppermute | solution.py:612

commit v7 on v6

--- a/solution.py
+++ b/solution.py
@@ -13,7 +13,7 @@
 CHUNKS = 4
 PARTS = (8, 8, 8, 8)
 SECOND_COST = 1.0
-FIRST_COST = 0.0
+FIRST_COST = 1.0
 THIRD_COST = 0.3
 F32 = jnp.float32
 BF16 = jnp.bfloat16

time: 52.6 us -> 52.2 us (level)
  starting transfers between devices: 22.8 us -> 26.2 us
  waiting for transfers between devices: 8.81 us -> 5.45 us
    ppermute x8, waiting for transfers between devices: 6.95 us -> 4.84 us  [to_neighbour(): return lax.ppermute(array, 'seq', [(i, i ^ 1) for i in range(size)])]
    ppermute x8, starting transfers between devices: 20 us -> 21.7 us  [to_neighbour(): return lax.ppermute(array, 'seq', [(i, i ^ 1) for i in range(size)])]
    ppermute x3, waiting for transfers between devices: 1.84 us -> 0.59 us  [to_core(): return lax.ppermute(array, 'rep', [(0, 1), (1, 0)])]
    ppermute x1, starting transfers between devices: 2.43 us -> 3.63 us  [inward(): return lax.ppermute(array, 'seq', [(0, 1), (3, 2)])]
  transfers between devices with their start and end apart: 17 -> 17, of which waited for: 7 -> 4; matrix products, arithmetic and copies ran while one was open for 0% -> 0% of each run, Pallas kernels for 24% -> 29%
where the time goes in v7:
time: 52.2 us; the launch traced here: 52 us
  starting transfers between devices  26.2 us (50%)
  Pallas kernels  16.1 us (31%)
  waiting for transfers between devices  5.45 us (10%)
  local copies, waits for them, and re-layouts  2.48 us (5%)
  between operations  1.65 us (3%)
    ppermute x8, starting transfers between devices, to_neighbour(): return lax.ppermute(array, 'seq', [(i, i ^ 1) for i in range(size)])  21.7 us
    pallas_call x22, Pallas kernels, call(): pl.pallas_call(body, out_shape=shapes, in_specs=[smem] * scalars + [anywh...  16.1 us
    ppermute x8, waiting for transfers between devices, to_neighbour(): return lax.ppermute(array, 'seq', [(i, i ^ 1) for i in range(size)])  4.84 us
    ppermute x1, starting transfers between devices, inward(): return lax.ppermute(array, 'seq', [(0, 1), (3, 2)])  3.63 us
    unnamed x42, local copies, waits for them, and re-layouts  2.48 us
  transfers between devices with their start and end apart: 17, of which 4 were waited for; matrix products, arithmetic and copies ran while one was open for 0% of the time, Pallas kernels for 29%

profile of v7, /device:TPU:0, one launch (start us, length us, event | category | flops | bytes accessed | tf_op | source)
XLA Modules:
  0.0 52.0 jit_solution(17314299297975951453)
XLA Ops:
  0.6 0.5 collective-permute-start
  1.2 3.0 %inputs.1 = (f32[128,32]{1,0:T(8,128)}, f32[8,32]{1,0:T(8,128)}, bf16[128,512]{1,0:T(8,128)(2,1)}, bf16[128,256]{1,0:T(8,128)(2,1)}, bf16[144,768]{1,0:T(8,128)(...) custom-call(bf16[128,2048]{1,0:T(8,128)(2,1)} %refs_0_.8, ...), custom_call_target="tpu_custom_call" | custom-call | tf_op jit(solution)/shard_map/inputs/pallas_call | solution.py:565
  4.1 2.7 %collective-permute-start.2 = (bf16[144,768]{1,0:T(8,128)(2,1)}, bf16[144,768]{1,0:T(8,128)(2,1)S(1)}, u32[]{:S(2)}, u32[]{:S(2)}) collective-permute-start(bf16[144,768]{1,0:T(8,128)(2,1)} %get-tuple-element.55.refs_2_.refs_3_.refs_4_), channel_id=1, source_target_pairs={{0,4},{4,0},{8,12},{12,8},{1,5},{5,1},{9,13},{13,9},{2,6},{6,2},{1... | collective-permute-start | bytes 663560 | tf_op jit(solution)/shard_map/ppermute | solution.py:615
  6.8 0.0 collective-permute-done.refs_2_
  6.8 0.8 %copy-done.3 = f32[128,32]{1,0:T(8,128)S(1)} copy-done((f32[128,32]{1,0:T(8,128)S(1)}, f32[128,32]{1,0:T(8,128)}, u32[]{:S(2)}) %copy-start.3) | copy-done | bytes 16408
  7.7 0.6 %projections.1.refs_2_.refs_5_.refs_6_ = bf16[192,512]{1,0:T(8,128)(2,1)S(1)} custom-call(bf16[128,2,256]{2,1,0:T(2,128)(2,1)S(1)} %copy-done.13, bf16[1,32,4,256]{3,2,1,0:T(4,128)(2,1)S(1)} %copy-done.8, bf16[1,32,4,256]{3,2,1,0:T(4,128)(2,1)S(1)} %collective-permute-done.refs_2_, f32[128,32]{1,0:T(8,128)S(1)} %copy-done.3), custom_call_target="tpu_custom_call" | custom-call | tf_op jit(solution)/shard_map/projections/pallas_call | solution.py:565
  8.2 0.0 copy-start.19
  8.3 0.3 copy-done.9
  8.6 0.1 copy-done.12
  8.7 0.3 copy-done.19
  8.9 1.0 %intra.1 = (f32[128,512]{1,0:T(8,128)S(1)}, f32[128,512]{1,0:T(8,128)S(1)}, f32[128,512]{1,0:T(8,128)S(1)}, f32[128,512]{1,0:T(8,128)S(1)}, bf16[128,768]{1,0:T(8,128)(2,1)S(1)}) custom-call(bf16[128,2048]{1,0:T(8,128)(2,1)S(1)} %copy-done, bf16[128,512]{1,0:T(8,128)(2,1)S(1)} %copy-done.12, ...), custom_call_target="tpu_custom_call", output_to_operand_aliasing={{4}: (6, {})} | custom-call | tf_op jit(solution)/shard_map/intra/pallas_call | solution.py:565
  9.9 0.1 collective-permute-start.1
  10.0 3.3 %collective-permute-done.2.refs_0_.refs_1_.refs_2_ = bf16[144,768]{1,0:T(8,128)(2,1)S(1)} collective-permute-done((bf16[144,768]{1,0:T(8,128)(2,1)}, bf16[144,768]{1,0:T(8,128)(2,1)S(1)}, u32[]{:S(2)}, u32[]{:S(2)}) %collective-permute-start.2) | collective-permute-done | bytes 221216 | tf_op jit(solution)/shard_map/ppermute | solution.py:615
  13.3 0.4 first.4
  13.8 0.1 collective-permute-start.8
  13.9 3.5 %collective-permute-start.6 = (bf16[192,512]{1,0:T(8,128)(2,1)S(1)}, bf16[192,512]{1,0:T(8,128)(2,1)S(1)}, u32[]{:S(2)}, u32[]{:S(2)}) collective-permute-start(bf16[192,512]{1,0:T(8,128)(2,1)S(1)} %get-tuple-element.67.refs_6_), channel_id=1, source_target_pairs={{0,4},{4,0},{8,12},{12,8},{1,5},{5,1},{9,13},{13,9},{2,6},{6,2},{1... | collective-permute-start | bytes 589832 | tf_op jit(solution)/shard_map/ppermute | solution.py:615
  17.4 0.3 first.5
  17.8 0.1 collective-permute-start.5
  17.8 3.4 %collective-permute-start.4 = (bf16[128,768]{1,0:T(8,128)(2,1)S(1)}, bf16[128,768]{1,0:T(8,128)(2,1)S(1)}, u32[]{:S(2)}, u32[]{:S(2)}) collective-permute-start(bf16[128,768]{1,0:T(8,128)(2,1)S(1)} %get-tuple-element.65.refs_2_.refs_3_.refs_4_), channel_id=1, source_target_pairs={{0,4},{4,0},{8,12},{12,8},{1,5},{5,1},{9,13},{13,9},{2,6},{6,2},{1... | collective-permute-start | bytes 589832 | tf_op jit(solution)/shard_map/ppermute | solution.py:615
  21.3 0.0 collective-permute-start.7
  21.3 0.4 collective-permute-done.6.refs_7_
  21.7 3.6 %collective-permute-start.3 = (bf16[128,512]{1,0:T(8,128)(2,1)S(1)}, bf16[128,512]{1,0:T(8,128)(2,1)S(1)}, u32[]{:S(2)}, u32[]{:S(2)}) collective-permute-start(bf16[128,512]{1,0:T(8,128)(2,1)S(1)} %get-tuple-element.64.refs_2_.refs_3_), channel_id=1, source_target_pairs={{0,4},{12,8},{1,5},{13,9},{2,6},{14,10},{3,7},{15,11},{16,20},{28,... | collective-permute-start | bytes 393224 | tf_op jit(solution)/shard_map/ppermute | solution.py:626
  25.3 0.0 collective-permute-done.8.refs_0_
  25.3 0.8 %second.5 = (f32[8,2048]{1,0:T(8,128)S(1)}, f32[128,512]{1,0:T(8,128)S(1)}, f32[64,512]{1,0:T(8,128)S(1)}, bf16[208,512]{1,0:T(8,128)(2,1)S(1)}) custom-call(bf16[272,512]{1,0:T(8,128)(2,1)S(1)} %collective-permute-done.8.refs_0_, bf16[144,768]{1,0:T(8,128)(2,1)S(1)} %collective-permute-done.2.refs_0_.refs_1_.refs_2_, ...), custom_call_target="tpu_custom_call" | custom-call | flops 1000000000 | tf_op jit(solution)/shard_map/second/pallas_call | solution.py:565
  26.1 0.2 collective-permute-start.11
  26.3 0.0 collective-permute-done.4.refs_0_.refs_1_.refs_2_
  26.3 0.3 first.6.refs_10_
  26.6 0.1 collective-permute-start.12
  26.7 0.0 collective-permute-done.7.refs_8_.refs_1_
  26.7 0.7 %second.6 = (f32[128,512]{1,0:T(8,128)S(1)}, f32[64,512]{1,0:T(8,128)S(1)}, bf16[320,512]{1,0:T(8,128)(2,1)S(1)}) custom-call(bf16[256,512]{1,0:T(8,128)(2,1)S(1)} %collective-permute-done.5.refs_0_, bf16[128,768]{1,0:T(8,128)(2,1)S(1)} %collective-permute-done.1.refs_0_.refs_1_, bf16[144,768]{1,0:T(8,128)(2,1)S(1)} %collective-permute-done.2.refs_0_.refs_1_.refs_2_, ...), custom_call_target="tpu_custom_call" | custom-call | flops 1000000000 | tf_op jit(solution)/shard_map/second/pallas_call | solution.py:565
  27.4 7.2 %collective-permute-start.10 = (bf16[320,512]{1,0:T(8,128)(2,1)S(1)}, bf16[320,512]{1,0:T(8,128)(2,1)S(1)}, u32[]{:S(2)}, u32[]{:S(2)}) collective-permute-start(bf16[320,512]{1,0:T(8,128)(2,1)S(1)} %get-tuple-element.73), channel_id=1, source_target_pairs={{0,4},{4,0},{8,12},{12,8},{1,5},{5,1},{9,13},{13,9},{2,6},{6,2},{1... | collective-permute-start | bytes 983048 | tf_op jit(solution)/shard_map/ppermute | solution.py:615
  34.6 0.0 collective-permute-done.3.refs_0_.refs_1_
  34.6 0.0 copy-start.17
  34.6 0.3 first.7.refs_6_
  35.0 0.1 collective-permute-start.9
  35.1 0.4 copy-done.4
  35.4 0.1 copy-done.7
  35.6 2.0 %candidates.1 = (f32[128,512]{1,0:T(8,128)S(1)}, f32[128,512]{1,0:T(8,128)S(1)}, f32[128,512]{1,0:T(8,128)S(1)}, f32[128,512]{1,0:T(8,128)S(1)}, f32[32,4096]{1,0:T(8,128)S(1)}, /*index=5*/f32[32,4096]{1,0:T(8,128)S(1)}) custom-call(bf16[1,32,4096]{2,1,0:T(8,128)(2,1)S(1)} %copy-done.7, bf16[1,32,4,256]{3,2,1,0:T(4,128)(2,1)S(1)} %copy-done.14, ...), custom_call_target="tpu_custom_call" | custom-call | tf_op jit(solution)/shard_map/candidates/pallas_call | solution.py:565
  37.6 0.0 collective-permute-done.11.refs_0_
  37.6 0.2 third.4
  37.9 0.0 collective-permute-done.12.refs_0_
  37.9 0.7 %second.7 = (f32[128,512]{1,0:T(8,128)S(1)}, f32[64,512]{1,0:T(8,128)S(1)}, bf16[192,512]{1,0:T(8,128)(2,1)S(1)}) custom-call(bf16[256,512]{1,0:T(8,128)(2,1)S(1)} %collective-permute-done.12.refs_0_, bf16[128,768]{1,0:T(8,128)(2,1)S(1)} %collective-permute-done.4.refs_0_.refs_1_.refs_2_, ...), custom_call_target="tpu_custom_call" | custom-call | flops 1000000000 | tf_op jit(solution)/shard_map/second/pallas_call | solution.py:565
  38.6 1.6 %collective-permute-start.14 = (bf16[192,512]{1,0:T(8,128)(2,1)S(1)}, bf16[192,512]{1,0:T(8,128)(2,1)S(1)}, u32[]{:S(2)}, u32[]{:S(2)}) collective-permute-start(bf16[192,512]{1,0:T(8,128)(2,1)S(1)} %get-tuple-element.85), channel_id=1, source_target_pairs={{0,4},{4,0},{8,12},{12,8},{1,5},{5,1},{9,13},{13,9},{2,6},{6,2},{1... | collective-permute-start | bytes 589832 | tf_op jit(solution)/shard_map/ppermute | solution.py:615
  40.2 0.0 collective-permute-done.10.refs_0_.refs_2_.refs_1_
  40.3 0.1 collective-permute-start.15
  40.4 0.6 %second.8.refs_9_ = bf16[192,512]{1,0:T(8,128)(2,1)S(1)} custom-call(bf16[256,512]{1,0:T(8,128)(2,1)S(1)} %collective-permute-done.9.refs_0_, bf16[128,512]{1,0:T(8,128)(2,1)S(1)} %collective-permute-done.3.refs_0_.refs_1_, bf16[128,768]{1,0:T(8,128)(2,1)S(1)} %collective-permute-done.4.refs_0_.refs_1_.refs_2_, ...), custom_call_target="tpu_custom_call" | custom-call | flops 1000000000 | tf_op jit(solution)/shard_map/second/pallas_call | solution.py:565
  41.0 3.0 %collective-permute-start.13 = (bf16[192,512]{1,0:T(8,128)(2,1)S(1)}, bf16[192,512]{1,0:T(8,128)(2,1)S(1)}, u32[]{:S(2)}, u32[]{:S(2)}) collective-permute-start(bf16[192,512]{1,0:T(8,128)(2,1)S(1)} %second.8.refs_9_), channel_id=1, source_target_pairs={{0,4},{4,0},{8,12},{12,8},{1,5},{5,1},{9,13},{13,9},{2,6},{6,2},{1... | collective-permute-start | bytes 589832 | tf_op jit(solution)/shard_map/ppermute | solution.py:615
  44.6 0.0 copy-start.5
  44.6 0.0 copy-start.6
  44.6 0.0 copy-start.10
  44.6 0.0 copy-start.15
  44.6 0.0 copy-start.16
  44.6 0.5 %second.9 = (f32[128,512]{1,0:T(8,128)S(1)}, f32[64,512]{1,0:T(8,128)S(1)}) custom-call(bf16[256,512]{1,0:T(8,128)(2,1)S(1)} %collective-permute-done.9.refs_0_, bf16[128,512]{1,0:T(8,128)(2,1)S(1)} %collective-permute-done.3.refs_0_.refs_1_, bf16[128,768]{1,0:T(8,128)(2,1)S(1)} %collective-permute-done.4.refs_0_.refs_1_.refs_2_, ...), custom_call_target="tpu_custom_call" | custom-call | flops 1000000000 | tf_op jit(solution)/shard_map/second/pallas_call | solution.py:565
  45.2 0.2 copy-done.5
  45.4 0.0 copy-done.6
  45.4 0.1 copy-done.10
  45.6 1.9 %attend.1 = (f32[8,128]{1,0:T(8,128)S(1)}, bf16[1,32,16,128]{3,2,1,0:T(8,128)(2,1)}) custom-call(s32[1]{0:T(128)S(6)} %copy.28.refs_0_, bf16[1,32,16,128]{3,2,1,0:T(8,128)(2,1)S(1)} %copy-done.10, bf16[1,32,2,128]{3,2,1,0:T(2,128)(2,1)S(1)} %copy-done.15, bf16[1,32,2,128]{3,2,1,0:T(2,128)(2,1)S(1)} %copy-done.16, bf16[128,2,128]{2,1,0:T(2,128)(2,1)S(1)} %copy-done.5, ...), custom_call_target="tpu_custom_call" | custom-call | tf_op jit(solution)/shard_map/attend/pallas_call | solution.py:565
  47.5 0.9 %prefix.2 = (f32[8,128]{1,0:T(8,128)S(1)}, bf16[128,2048]{1,0:T(8,128)(2,1)}) custom-call(bf16[208,512]{1,0:T(8,128)(2,1)S(1)} %collective-permute-done.11.refs_0_, bf16[320,512]{1,0:T(8,128)(2,1)S(1)} %collective-permute-done.10.refs_0_.refs_2_.refs_1_, bf16[192,512]{1,0:T(8,128)(2,1)S(1)} %collective-permute-done.14.refs_0_.refs_2_, ...), custom_call_target="tpu_custom_call" | custom-call | tf_op jit(solution)/shard_map/prefix/pallas_call | solution.py:565
  48.5 1.2 %collective-permute-done.13.refs_0_ = bf16[192,512]{1,0:T(8,128)(2,1)S(1)} collective-permute-done((bf16[192,512]{1,0:T(8,128)(2,1)S(1)}, bf16[192,512]{1,0:T(8,128)(2,1)S(1)}, u32[]{:S(2)}, u32[]{:S(2)}) %collective-permute-start.13) | collective-permute-done | bytes 196640 | tf_op jit(solution)/shard_map/ppermute | solution.py:615
  49.6 0.1 third.7
  49.7 0.1 collective-permute-start.16
  49.8 0.7 %prefix.3 = bf16[128,2048]{1,0:T(8,128)(2,1)} custom-call(bf16[192,512]{1,0:T(8,128)(2,1)S(1)} %collective-permute-done.13.refs_0_, f32[128,512]{1,0:T(8,128)S(1)} %get-tuple-element.81.refs_8_.refs_1_, f32[128,512]{1,0:T(8,128)S(1)} %get-tuple-element.82.refs_2_, f32[128,512]{1,0:T(8,128)S(1)} %get-tuple-element.83.refs_3_, ...), custom_call_target="tpu_custom_call", output_to_operand_aliasing={{}: (5, {})} | custom-call | tf_op jit(solution)/shard_map/prefix/pallas_call | solution.py:565
  50.5 0.6 %collective-permute-done.16.refs_4_ = bf16[32,2048]{1,0:T(8,128)(2,1)S(1)} collective-permute-done((bf16[32,2048]{1,0:T(8,128)(2,1)S(1)}, bf16[32,2048]{1,0:T(8,128)(2,1)S(1)}, u32[]{:S(2)}, u32[]{:S(2)}) %collective-permute-start.16) | collective-permute-done | bytes 131104 | tf_op jit(solution)/shard_map/ppermute | solution.py:612
  51.1 0.8 %close.1 = bf16[1,32,4096]{2,1,0:T(8,128)(2,1)} custom-call(s32[1]{0:T(128)S(6)} %copy.28.refs_0_, f32[32,4096]{1,0:T(8,128)S(1)} %get-tuple-element.77.refs_3_.refs_1_, f32[32,4096]{1,0:T(8,128)S(1)} %get-tuple-element.96.refs_2_, f32[32,2048]{1,0:T(8,128)S(1)} %get-tuple-element.94.refs_4_.refs_3_, bf16[32,2048]{1,0:T(8,128)(2,1)S(1)} %collective-permute-done.16.refs_4_), custom_call_target="tpu_custom_call" | custom-call | tf_op jit(solution)/shard_map/close/pallas_call | solution.py:565
  (34 shorter events, 0.2 us)
Async XLA Ops:
  0.6 6.2 %collective-permute-start = (bf16[1,32,4,256]{3,2,1,0:T(4,128)(2,1)}, bf16[1,32,4,256]{3,2,1,0:T(4,128)(2,1)S(1)}, u32[]{:S(2)}, u32[]{:S(2)}) collective-permute-start(bf16[1,32,4,256]{3,2,1,0:T(4,128)(2,1)} %refs_2_.2), channel_id=1, source_target_pairs={{0,1},{1,0},{2,3},{3,2},{4,5},{5,4},{6,7},{7,6},{8,9},{9,8},{10,11... | collective-permute-start | bytes 196616 | tf_op jit(solution)/shard_map/ppermute | solution.py:612
  1.1 5.7 %copy-start.8 = (bf16[1,32,4,256]{3,2,1,0:T(4,128)(2,1)S(1)}, bf16[1,32,4,256]{3,2,1,0:T(4,128)(2,1)}, u32[]{:S(2)}) copy-start(bf16[1,32,4,256]{3,2,1,0:T(4,128)(2,1)} %refs_2_.2) | copy-start | bytes 196612
  1.2 5.7 %copy-start.13 = (bf16[128,2,256]{2,1,0:T(2,128)(2,1)S(1)}, bf16[128,2,256]{2,1,0:T(2,128)(2,1)}, u32[]{:S(2)}) copy-start(bf16[128,2,256]{2,1,0:T(2,128)(2,1)} %refs_0_.7) | copy-start | bytes 393220
  1.2 7.1 %copy-start = (bf16[128,2048]{1,0:T(8,128)(2,1)S(1)}, bf16[128,2048]{1,0:T(8,128)(2,1)}, u32[]{:S(2)}) copy-start(bf16[128,2048]{1,0:T(8,128)(2,1)} %refs_0_.8) | copy-start | bytes 1572868
  4.1 9.2 %collective-permute-start.2 = (bf16[144,768]{1,0:T(8,128)(2,1)}, bf16[144,768]{1,0:T(8,128)(2,1)S(1)}, u32[]{:S(2)}, u32[]{:S(2)}) collective-permute-start(bf16[144,768]{1,0:T(8,128)(2,1)} %get-tuple-element.55.refs_2_.refs_3_.refs_4_), channel_id=1, source_target_pairs={{0,4},{4,0},{8,12},{12,8},{1,5},{5,1},{9,13},{13,9},{2,6},{6,2},{1... | collective-permute-start | bytes 663560 | tf_op jit(solution)/shard_map/ppermute | solution.py:615
  6.8 0.8 %copy-start.3 = (f32[128,32]{1,0:T(8,128)S(1)}, f32[128,32]{1,0:T(8,128)}, u32[]{:S(2)}) copy-start(f32[128,32]{1,0:T(8,128)} %get-tuple-element.52.refs_3_.refs_5_) | copy-start | bytes 49156
  7.7 0.9 %copy-start.9 = (bf16[128,768]{1,0:T(8,128)(2,1)S(1)}, bf16[128,768]{1,0:T(8,128)(2,1)}, u32[]{:S(2)}) copy-start(bf16[128,768]{1,0:T(8,128)(2,1)} %get-tuple-element.53.refs_6_) | copy-start | bytes 589828
  7.7 1.0 %copy-start.12 = (bf16[128,512]{1,0:T(8,128)(2,1)S(1)}, bf16[128,512]{1,0:T(8,128)(2,1)}, u32[]{:S(2)}) copy-start(bf16[128,512]{1,0:T(8,128)(2,1)} %get-tuple-element.51.refs_1_) | copy-start | bytes 393220
  8.2 0.7 %copy-start.19 = (f32[128]{0:T(128)S(1)}, f32[128]{0:T(128)}, u32[]{:S(2)}) copy-start(f32[128]{0:T(128)} %param.19) | copy-start | bytes 1540
  8.9 4.4 %copy-start.2 = (bf16[144,768]{1,0:T(8,128)(2,1)S(1)}, bf16[144,768]{1,0:T(8,128)(2,1)}, u32[]{:S(2)}) copy-start(bf16[144,768]{1,0:T(8,128)(2,1)} %get-tuple-element.55.refs_2_.refs_3_.refs_4_) | copy-start | bytes 663556
  9.9 3.4 %copy-start.18 = (f32[8,32]{1,0:T(8,128)S(1)}, f32[8,32]{1,0:T(8,128)}, u32[]{:S(2)}) copy-start(f32[8,32]{1,0:T(8,128)} %get-tuple-element.56.refs_4_.refs_8_) | copy-start | bytes 3076
  9.9 7.4 %collective-permute-start.1 = (bf16[128,768]{1,0:T(8,128)(2,1)S(1)}, bf16[128,768]{1,0:T(8,128)(2,1)S(1)}, u32[]{:S(2)}, u32[]{:S(2)}) collective-permute-start(bf16[128,768]{1,0:T(8,128)(2,1)S(1)} %get-tuple-element.54.refs_2_.refs_3_), channel_id=1, source_target_pairs={{0,4},{4,0},{8,12},{12,8},{1,5},{5,1},{9,13},{13,9},{2,6},{6,2},{1... | collective-permute-start | bytes 589832 | tf_op jit(solution)/shard_map/ppermute | solution.py:615
  13.3 4.1 %copy-start.1 = (bf16[128,768]{1,0:T(8,128)(2,1)S(1)}, bf16[128,768]{1,0:T(8,128)(2,1)}, u32[]{:S(2)}) copy-start(bf16[128,768]{1,0:T(8,128)(2,1)} %get-tuple-element.62.refs_8_) | copy-start | bytes 589828
  13.3 4.1 %copy-start.11 = (bf16[128,512]{1,0:T(8,128)(2,1)S(1)}, bf16[128,512]{1,0:T(8,128)(2,1)}, u32[]{:S(2)}) copy-start(bf16[128,512]{1,0:T(8,128)(2,1)} %get-tuple-element.63.refs_9_) | copy-start | bytes 393220
  13.3 4.1 %copy-start.20 = (bf16[128,256]{1,0:T(8,128)(2,1)S(1)}, bf16[128,256]{1,0:T(8,128)(2,1)}, u32[]{:S(2)}) copy-start(bf16[128,256]{1,0:T(8,128)(2,1)} %get-tuple-element.60.refs_6_) | copy-start | bytes 196612
  13.8 11.5 %collective-permute-start.8 = (bf16[272,512]{1,0:T(8,128)(2,1)S(1)}, bf16[272,512]{1,0:T(8,128)(2,1)S(1)}, u32[]{:S(2)}, u32[]{:S(2)}) collective-permute-start(bf16[272,512]{1,0:T(8,128)(2,1)S(1)} %get-tuple-element.61.refs_7_), channel_id=1, source_target_pairs={{0,1},{1,0},{4,8},{5,9},{8,4},{9,5},{12,13},{13,12},{2,3},{3,2},{6... | collective-permute-start | bytes 835592 | tf_op jit(solution)/shard_map/ppermute | solution.py:623
  13.9 7.8 %collective-permute-start.6 = (bf16[192,512]{1,0:T(8,128)(2,1)S(1)}, bf16[192,512]{1,0:T(8,128)(2,1)S(1)}, u32[]{:S(2)}, u32[]{:S(2)}) collective-permute-start(bf16[192,512]{1,0:T(8,128)(2,1)S(1)} %get-tuple-element.67.refs_6_), channel_id=1, source_target_pairs={{0,4},{4,0},{8,12},{12,8},{1,5},{5,1},{9,13},{13,9},{2,6},{6,2},{1... | collective-permute-start | bytes 589832 | tf_op jit(solution)/shard_map/ppermute | solution.py:615
  17.8 9.0 %collective-permute-start.5 = (bf16[256,512]{1,0:T(8,128)(2,1)S(1)}, bf16[256,512]{1,0:T(8,128)(2,1)S(1)}, u32[]{:S(2)}, u32[]{:S(2)}) collective-permute-start(bf16[256,512]{1,0:T(8,128)(2,1)S(1)} %get-tuple-element.66.refs_10_), channel_id=1, source_target_pairs={{0,1},{1,0},{4,8},{5,9},{8,4},{9,5},{12,13},{13,12},{2,3},{3,2},{6... | collective-permute-start | bytes 786440 | tf_op jit(solution)/shard_map/ppermute | solution.py:623
  17.8 8.4 %collective-permute-start.4 = (bf16[128,768]{1,0:T(8,128)(2,1)S(1)}, bf16[128,768]{1,0:T(8,128)(2,1)S(1)}, u32[]{:S(2)}, u32[]{:S(2)}) collective-permute-start(bf16[128,768]{1,0:T(8,128)(2,1)S(1)} %get-tuple-element.65.refs_2_.refs_3_.refs_4_), channel_id=1, source_target_pairs={{0,4},{4,0},{8,12},{12,8},{1,5},{5,1},{9,13},{13,9},{2,6},{6,2},{1... | collective-permute-start | bytes 589832 | tf_op jit(solution)/shard_map/ppermute | solution.py:615
  21.3 5.4 %collective-permute-start.7 = (bf16[256,256]{1,0:T(8,128)(2,1)S(1)}, bf16[256,256]{1,0:T(8,128)(2,1)S(1)}, u32[]{:S(2)}, u32[]{:S(2)}) collective-permute-start(bf16[256,256]{1,0:T(8,128)(2,1)S(1)} %get-tuple-element.68.refs_0_), channel_id=1, source_target_pairs={{0,1},{1,0},{4,8},{5,9},{8,4},{9,5},{12,13},{13,12},{2,3},{3,2},{6... | collective-permute-start | bytes 393224 | tf_op jit(solution)/shard_map/ppermute | solution.py:623
  21.7 12.9 %collective-permute-start.3 = (bf16[128,512]{1,0:T(8,128)(2,1)S(1)}, bf16[128,512]{1,0:T(8,128)(2,1)S(1)}, u32[]{:S(2)}, u32[]{:S(2)}) collective-permute-start(bf16[128,512]{1,0:T(8,128)(2,1)S(1)} %get-tuple-element.64.refs_2_.refs_3_), channel_id=1, source_target_pairs={{0,4},{12,8},{1,5},{13,9},{2,6},{14,10},{3,7},{15,11},{16,20},{28,... | collective-permute-start | bytes 393224 | tf_op jit(solution)/shard_map/ppermute | solution.py:626
  26.1 11.5 %collective-permute-start.11 = (bf16[208,512]{1,0:T(8,128)(2,1)S(1)}, bf16[208,512]{1,0:T(8,128)(2,1)S(1)}, u32[]{:S(2)}, u32[]{:S(2)}) collective-permute-start(bf16[208,512]{1,0:T(8,128)(2,1)S(1)} %get-tuple-element.75), channel_id=1, source_target_pairs={{0,4},{4,0},{8,12},{12,8},{1,5},{5,1},{9,13},{13,9},{2,6},{6,2},{1... | collective-permute-start | bytes 638984 | tf_op jit(solution)/shard_map/ppermute | solution.py:615
  26.6 11.2 %collective-permute-start.12 = (bf16[256,512]{1,0:T(8,128)(2,1)S(1)}, bf16[256,512]{1,0:T(8,128)(2,1)S(1)}, u32[]{:S(2)}, u32[]{:S(2)}) collective-permute-start(bf16[256,512]{1,0:T(8,128)(2,1)S(1)} %first.6.refs_10_), channel_id=1, source_target_pairs={{0,1},{1,0},{4,8},{5,9},{8,4},{9,5},{12,13},{13,12},{2,3},{3,2},{6... | collective-permute-start | bytes 786440 | tf_op jit(solution)/shard_map/ppermute | solution.py:623
  27.4 12.8 %collective-permute-start.10 = (bf16[320,512]{1,0:T(8,128)(2,1)S(1)}, bf16[320,512]{1,0:T(8,128)(2,1)S(1)}, u32[]{:S(2)}, u32[]{:S(2)}) collective-permute-start(bf16[320,512]{1,0:T(8,128)(2,1)S(1)} %get-tuple-element.73), channel_id=1, source_target_pairs={{0,4},{4,0},{8,12},{12,8},{1,5},{5,1},{9,13},{13,9},{2,6},{6,2},{1... | collective-permute-start | bytes 983048 | tf_op jit(solution)/shard_map/ppermute | solution.py:615
  34.6 0.8 %copy-start.4 = (f32[128,32]{1,0:T(8,128)S(1)}, f32[128,32]{1,0:T(8,128)}, u32[]{:S(2)}) copy-start(f32[128,32]{1,0:T(8,128)} %get-tuple-element.52.refs_3_.refs_5_) | copy-start | bytes 49156
  34.6 1.0 %copy-start.7 = (bf16[1,32,4096]{2,1,0:T(8,128)(2,1)S(1)}, bf16[1,32,4096]{2,1,0:T(8,128)(2,1)}, u32[]{:S(2)}) copy-start(bf16[1,32,4096]{2,1,0:T(8,128)(2,1)} %refs_0_.9) | copy-start | bytes 786436
  34.6 1.0 %copy-start.14 = (bf16[1,32,4,256]{3,2,1,0:T(4,128)(2,1)S(1)}, bf16[1,32,4,256]{3,2,1,0:T(4,128)(2,1)}, u32[]{:S(2)}) copy-start(bf16[1,32,4,256]{3,2,1,0:T(4,128)(2,1)} %refs_1_.6) | copy-start | bytes 196612
  34.6 1.0 %copy-start.17 = (f32[1,32,64]{2,1,0:T(8,128)S(1)}, f32[1,32,64]{2,1,0:T(8,128)}, u32[]{:S(2)}) copy-start(f32[1,32,64]{2,1,0:T(8,128)} %refs_3_.4) | copy-start | bytes 24580
  35.0 5.4 %collective-permute-start.9 = (bf16[256,512]{1,0:T(8,128)(2,1)S(1)}, bf16[256,512]{1,0:T(8,128)(2,1)S(1)}, u32[]{:S(2)}, u32[]{:S(2)}) collective-permute-start(bf16[256,512]{1,0:T(8,128)(2,1)S(1)} %first.7.refs_6_), channel_id=1, source_target_pairs={{0,1},{1,0},{4,8},{5,9},{8,4},{9,5},{12,13},{13,12},{2,3},{3,2},{6... | collective-permute-start | bytes 786440 | tf_op jit(solution)/shard_map/ppermute | solution.py:623
  38.6 8.9 %collective-permute-start.14 = (bf16[192,512]{1,0:T(8,128)(2,1)S(1)}, bf16[192,512]{1,0:T(8,128)(2,1)S(1)}, u32[]{:S(2)}, u32[]{:S(2)}) collective-permute-start(bf16[192,512]{1,0:T(8,128)(2,1)S(1)} %get-tuple-element.85), channel_id=1, source_target_pairs={{0,4},{4,0},{8,12},{12,8},{1,5},{5,1},{9,13},{13,9},{2,6},{6,2},{1... | collective-permute-start | bytes 589832 | tf_op jit(solution)/shard_map/ppermute | solution.py:615
  40.3 4.9 %collective-permute-start.15 = (bf16[384,256]{1,0:T(8,128)(2,1)S(1)}, bf16[384,256]{1,0:T(8,128)(2,1)S(1)}, u32[]{:S(2)}, u32[]{:S(2)}) collective-permute-start(bf16[384,256]{1,0:T(8,128)(2,1)S(1)} %collect.1.refs_9_.refs_6_), channel_id=1, source_target_pairs={{0,1},{1,0},{2,3},{3,2},{4,5},{5,4},{6,7},{7,6},{8,9},{9,8},{10,11... | collective-permute-start | bytes 589832 | tf_op jit(solution)/shard_map/ppermute | solution.py:612
  41.0 8.7 %collective-permute-start.13 = (bf16[192,512]{1,0:T(8,128)(2,1)S(1)}, bf16[192,512]{1,0:T(8,128)(2,1)S(1)}, u32[]{:S(2)}, u32[]{:S(2)}) collective-permute-start(bf16[192,512]{1,0:T(8,128)(2,1)S(1)} %second.8.refs_9_), channel_id=1, source_target_pairs={{0,4},{4,0},{8,12},{12,8},{1,5},{5,1},{9,13},{13,9},{2,6},{6,2},{1... | collective-permute-start | bytes 589832 | tf_op jit(solution)/shard_map/ppermute | solution.py:615
  44.6 0.8 %copy-start.5 = (bf16[128,2,128]{2,1,0:T(2,128)(2,1)S(1)}, bf16[128,2,128]{2,1,0:T(2,128)(2,1)}, u32[]{:S(2)}) copy-start(bf16[128,2,128]{2,1,0:T(2,128)(2,1)} %refs_4_.3) | copy-start | bytes 196612
  44.6 0.9 %copy-start.6 = (bf16[128,2,128]{2,1,0:T(2,128)(2,1)S(1)}, bf16[128,2,128]{2,1,0:T(2,128)(2,1)}, u32[]{:S(2)}) copy-start(bf16[128,2,128]{2,1,0:T(2,128)(2,1)} %refs_5_.1) | copy-start | bytes 196612
  44.6 1.0 %copy-start.10 = (bf16[1,32,16,128]{3,2,1,0:T(8,128)(2,1)S(1)}, bf16[1,32,16,128]{3,2,1,0:T(8,128)(2,1)}, u32[]{:S(2)}) copy-start(bf16[1,32,16,128]{3,2,1,0:T(8,128)(2,1)} %refs_1_.7) | copy-start | bytes 393220
  44.6 0.9 %copy-start.15 = (bf16[1,32,2,128]{3,2,1,0:T(2,128)(2,1)S(1)}, bf16[1,32,2,128]{3,2,1,0:T(2,128)(2,1)}, u32[]{:S(2)}) copy-start(bf16[1,32,2,128]{3,2,1,0:T(2,128)(2,1)} %refs_2_.3) | copy-start | bytes 49156
  44.6 0.9 %copy-start.16 = (bf16[1,32,2,128]{3,2,1,0:T(2,128)(2,1)S(1)}, bf16[1,32,2,128]{3,2,1,0:T(2,128)(2,1)}, u32[]{:S(2)}) copy-start(bf16[1,32,2,128]{3,2,1,0:T(2,128)(2,1)} %refs_3_.5) | copy-start | bytes 49156
  49.7 1.4 %collective-permute-start.16 = (bf16[32,2048]{1,0:T(8,128)(2,1)S(1)}, bf16[32,2048]{1,0:T(8,128)(2,1)S(1)}, u32[]{:S(2)}, u32[]{:S(2)}) collective-permute-start(bf16[32,2048]{1,0:T(8,128)(2,1)S(1)} %get-tuple-element.97), channel_id=1, source_target_pairs={{0,1},{1,0},{2,3},{3,2},{4,5},{5,4},{6,7},{7,6},{8,9},{9,8},{10,11... | collective-permute-start | bytes 393224 | tf_op jit(solution)/shard_map/ppermute | solution.py:612

commit v8 on v7

--- a/solution.py
+++ b/solution.py
@@ -289,8 +289,7 @@
         mine_ref, own_row_ref, near_row_ref, near_ref, send_ref = refs
         mine = mine_ref[:1, :]
         near = lines_to_totals(w_ref[tokens:, :heads])
-        own_row, near_row = as_row(mine, width), as_row(near, width)
-        own_row_ref[...] = own_row
+        own_row, near_row = own_row_ref[...], as_row(near, width)
         near_row_ref[...] = near_row
         near_ref[...] = jnp.broadcast_to(near, (8, heads))
         send_ref[state:, :] = jnp.zeros((16, cols), BF16)
@@ -414,7 +413,8 @@
     copy.wait()
 
 
-def intra_kernel(x_ref, b2_ref, c2_ref, cum_ref, skip_ref, *base_refs, groups):
+def intra_kernel(x_ref, b2_ref, c2_ref, cum_ref, skip_ref, *refs, groups):
+    *base_refs, row_ref = refs
     tokens, heads = cum_ref.shape
     width = x_ref.shape[1] // heads
     state = c2_ref.shape[1] // groups
@@ -422,6 +422,7 @@
     first = (lax.axis_index("head") * lax.axis_size("rep") + lax.axis_index("rep")) * heads
     skip = spread(jnp.broadcast_to(skip_ref[...], (8, skip_ref.shape[1])), width, first, heads)[:1]
     cum = cum_ref[...]
+    row_ref[...] = as_row(jnp.exp(-cum[tokens - 1 : tokens, :]), width)
     cum_t = cum.T
     shape = (tokens, tokens)
     hidden = jnp.where(iota(shape, 0) >= iota(shape, 1), 0.0, NEG)
@@ -671,7 +672,7 @@
         return call(
             functools.partial(intra_kernel, groups=groups),
             "intra",
-            [((tokens, count * width), F32) for count in counts],
+            [((tokens, count * width), F32) for count in counts] + [((8, wide), F32)],
             prefix_x,
             b2,
             cc,
@@ -739,7 +740,7 @@
             return got[q], got[p], loads[q], loads[p]
 
         def first(q, mark):
-            extra = [((8, wide), F32), ((8, wide), F32), ((8, heads), F32)] if q == 0 else []
+            extra = [((8, wide), F32), ((8, heads), F32)] if q == 0 else []
             results = call(
                 functools.partial(first_kernel, q=q, groups=groups, state=state, **shared),
                 "first",
@@ -747,7 +748,7 @@
                 + [((state + (16 if q == 0 else 0), counts[q] * width), BF16)]
                 + ([((2 * tokens, kv_shape[1]), BF16)] if q == 1 else []),
                 *inputs_of(q),
-                *([total] if q == 0 else [rows["own"], rows["near"]]),
+                *([total, rows["own"]] if q == 0 else [rows["own"], rows["near"]]),
                 *([kv] if q == 1 else []),
                 after=(mark,),
                 cost=FIRST_COST if q == 1 else 0.0,
@@ -760,7 +761,7 @@
                 *results, loads[2], loads[3] = results
                 got.extend((to_neighbour(loads[2]), inward(loads[3])))
             if q == 0:
-                rows["own"], rows["near"], rows["near_total"], *results = results
+                rows["near"], rows["near_total"], *results = results
             middle[q] = between_inner(results[0])
             if q == 1:
                 rows["kv"] = results[1]
@@ -829,7 +830,7 @@
                 ],
             )
 
-        *base, loads[1] = intra(cc, cc)
+        *base, rows["own"], loads[1] = intra(cc, cc)
         got = [to_neighbour(a) for a in loads[:2]]
         mark = first(0, base[0])
         mark = first(1, mark)
@@ -858,7 +859,7 @@
             halves = [halves[0], halves[1], mirrored, to_neighbour(mirrored)]
             if level < levels - 1:
                 halves = [jnp.concatenate([halves[0], halves[2]]), jnp.concatenate([halves[1], halves[3]])]
-        *base, loads[1] = intra(cc, cc)
+        *base, _, loads[1] = intra(cc, cc)
         mark = base[0]
         own = call(
             functools.partial(own_kernel, cols=cols, groups=groups, state=state, counts=counts),

time: 52.2 us -> 52.2 us (level)
  no operation moved by 1% of the time
where the time goes in v8:
time: 52.2 us; the launch traced here: 51.9 us
  starting transfers between devices  26.2 us (50%)
  Pallas kernels  16.1 us (31%)
  waiting for transfers between devices  5.44 us (10%)
  local copies, waits for them, and re-layouts  2.48 us (5%)
  between operations  1.65 us (3%)
    ppermute x8, starting transfers between devices, to_neighbour(): return lax.ppermute(array, 'seq', [(i, i ^ 1) for i in range(size)])  21.7 us
    pallas_call x22, Pallas kernels, call(): pl.pallas_call(body, out_shape=shapes, in_specs=[smem] * scalars + [anywh...  16.1 us
    ppermute x8, waiting for transfers between devices, to_neighbour(): return lax.ppermute(array, 'seq', [(i, i ^ 1) for i in range(size)])  4.83 us
    ppermute x1, starting transfers between devices, inward(): return lax.ppermute(array, 'seq', [(0, 1), (3, 2)])  3.63 us
    unnamed x42, local copies, waits for them, and re-layouts  2.48 us
  transfers between devices with their start and end apart: 17, of which 4 were waited for; matrix products, arithmetic and copies ran while one was open for 0% of the time, Pallas kernels for 29%

profile of v8, /device:TPU:0, one launch (start us, length us, event | category | flops | bytes accessed | tf_op | source)
XLA Modules:
  0.0 51.9 jit_solution(10063018620759264928)
XLA Ops:
  0.6 0.5 collective-permute-start
  1.2 3.0 %inputs.1 = (f32[128,32]{1,0:T(8,128)}, f32[8,32]{1,0:T(8,128)}, bf16[128,512]{1,0:T(8,128)(2,1)}, bf16[128,256]{1,0:T(8,128)(2,1)}, bf16[144,768]{1,0:T(8,128)(...) custom-call(bf16[128,2048]{1,0:T(8,128)(2,1)} %refs_0_.8, ...), custom_call_target="tpu_custom_call" | custom-call | tf_op jit(solution)/shard_map/inputs/pallas_call | solution.py:566
  4.1 2.7 %collective-permute-start.2 = (bf16[144,768]{1,0:T(8,128)(2,1)}, bf16[144,768]{1,0:T(8,128)(2,1)S(1)}, u32[]{:S(2)}, u32[]{:S(2)}) collective-permute-start(bf16[144,768]{1,0:T(8,128)(2,1)} %get-tuple-element.55.refs_2_.refs_3_.refs_4_), channel_id=1, source_target_pairs={{0,4},{4,0},{8,12},{12,8},{1,5},{5,1},{9,13},{13,9},{2,6},{6,2},{1... | collective-permute-start | bytes 663560 | tf_op jit(solution)/shard_map/ppermute | solution.py:616
  6.8 0.0 collective-permute-done.refs_2_
  6.8 0.8 %copy-done.3 = f32[128,32]{1,0:T(8,128)S(1)} copy-done((f32[128,32]{1,0:T(8,128)S(1)}, f32[128,32]{1,0:T(8,128)}, u32[]{:S(2)}) %copy-start.3) | copy-done | bytes 16408
  7.7 0.6 %projections.1.refs_2_.refs_5_.refs_7_ = bf16[192,512]{1,0:T(8,128)(2,1)S(1)} custom-call(bf16[128,2,256]{2,1,0:T(2,128)(2,1)S(1)} %copy-done.13, bf16[1,32,4,256]{3,2,1,0:T(4,128)(2,1)S(1)} %copy-done.8, bf16[1,32,4,256]{3,2,1,0:T(4,128)(2,1)S(1)} %collective-permute-done.refs_2_, f32[128,32]{1,0:T(8,128)S(1)} %copy-done.3), custom_call_target="tpu_custom_call" | custom-call | tf_op jit(solution)/shard_map/projections/pallas_call | solution.py:566
  8.2 0.0 copy-start.19
  8.3 0.3 copy-done.9
  8.6 0.1 copy-done.12
  8.7 0.3 copy-done.19
  8.9 1.0 %intra.1 = (f32[128,512]{1,0:T(8,128)S(1)}, f32[128,512]{1,0:T(8,128)S(1)}, f32[128,512]{1,0:T(8,128)S(1)}, f32[128,512]{1,0:T(8,128)S(1)}, f32[8,2048]{1,0:T(8,128)S(1)}, /*index=5*/bf16[128,768]{1,0:T(8,128)(2,1)S(1)}) custom-call(bf16[128,2048]{1,0:T(8,128)(2,1)S(1)} %copy-done, bf16[128,512]{1,0:T(8,128)(2,1)S(1)} %copy-done.12, ...), custom_call_target="tpu_custom_call", output_to_operand_aliasing={{5}: (6, {})} | custom-call | tf_op jit(solution)/shard_map/intra/pallas_call | solution.py:566
  10.0 0.1 collective-permute-start.1
  10.1 3.3 %collective-permute-done.2.refs_0_.refs_1_.refs_2_ = bf16[144,768]{1,0:T(8,128)(2,1)S(1)} collective-permute-done((bf16[144,768]{1,0:T(8,128)(2,1)}, bf16[144,768]{1,0:T(8,128)(2,1)S(1)}, u32[]{:S(2)}, u32[]{:S(2)}) %collective-permute-start.2) | collective-permute-done | bytes 221216 | tf_op jit(solution)/shard_map/ppermute | solution.py:616
  13.3 0.4 first.4
  13.7 0.1 collective-permute-start.8
  13.8 3.5 %collective-permute-start.6 = (bf16[192,512]{1,0:T(8,128)(2,1)S(1)}, bf16[192,512]{1,0:T(8,128)(2,1)S(1)}, u32[]{:S(2)}, u32[]{:S(2)}) collective-permute-start(bf16[192,512]{1,0:T(8,128)(2,1)S(1)} %get-tuple-element.67.refs_6_), channel_id=1, source_target_pairs={{0,4},{4,0},{8,12},{12,8},{1,5},{5,1},{9,13},{13,9},{2,6},{6,2},{1... | collective-permute-start | bytes 589832 | tf_op jit(solution)/shard_map/ppermute | solution.py:616
  17.3 0.0 collective-permute-done.1.refs_0_.refs_1_
  17.4 0.4 first.5
  17.7 0.1 collective-permute-start.5
  17.8 3.5 %collective-permute-start.4 = (bf16[128,768]{1,0:T(8,128)(2,1)S(1)}, bf16[128,768]{1,0:T(8,128)(2,1)S(1)}, u32[]{:S(2)}, u32[]{:S(2)}) collective-permute-start(bf16[128,768]{1,0:T(8,128)(2,1)S(1)} %get-tuple-element.65.refs_2_.refs_3_.refs_4_), channel_id=1, source_target_pairs={{0,4},{4,0},{8,12},{12,8},{1,5},{5,1},{9,13},{13,9},{2,6},{6,2},{1... | collective-permute-start | bytes 589832 | tf_op jit(solution)/shard_map/ppermute | solution.py:616
  21.3 0.0 collective-permute-start.7
  21.3 0.3 collective-permute-done.6.refs_7_
  21.7 3.6 %collective-permute-start.3 = (bf16[128,512]{1,0:T(8,128)(2,1)S(1)}, bf16[128,512]{1,0:T(8,128)(2,1)S(1)}, u32[]{:S(2)}, u32[]{:S(2)}) collective-permute-start(bf16[128,512]{1,0:T(8,128)(2,1)S(1)} %get-tuple-element.64.refs_2_.refs_3_), channel_id=1, source_target_pairs={{0,4},{12,8},{1,5},{13,9},{2,6},{14,10},{3,7},{15,11},{16,20},{28,... | collective-permute-start | bytes 393224 | tf_op jit(solution)/shard_map/ppermute | solution.py:627
  25.3 0.0 collective-permute-done.8.refs_0_
  25.3 0.8 %second.5 = (f32[8,2048]{1,0:T(8,128)S(1)}, f32[128,512]{1,0:T(8,128)S(1)}, f32[64,512]{1,0:T(8,128)S(1)}, bf16[208,512]{1,0:T(8,128)(2,1)S(1)}) custom-call(bf16[272,512]{1,0:T(8,128)(2,1)S(1)} %collective-permute-done.8.refs_0_, bf16[144,768]{1,0:T(8,128)(2,1)S(1)} %collective-permute-done.2.refs_0_.refs_1_.refs_2_, ...), custom_call_target="tpu_custom_call" | custom-call | flops 1000000000 | tf_op jit(solution)/shard_map/second/pallas_call | solution.py:566
  26.1 0.1 collective-permute-start.11
  26.2 0.0 collective-permute-done.4.refs_0_.refs_1_.refs_2_
  26.2 0.3 first.6.refs_10_
  26.6 0.1 collective-permute-start.12
  26.7 0.0 collective-permute-done.5.refs_0_
  26.7 0.7 %second.6 = (f32[128,512]{1,0:T(8,128)S(1)}, f32[64,512]{1,0:T(8,128)S(1)}, bf16[320,512]{1,0:T(8,128)(2,1)S(1)}) custom-call(bf16[256,512]{1,0:T(8,128)(2,1)S(1)} %collective-permute-done.5.refs_0_, bf16[128,768]{1,0:T(8,128)(2,1)S(1)} %collective-permute-done.1.refs_0_.refs_1_, bf16[144,768]{1,0:T(8,128)(2,1)S(1)} %collective-permute-done.2.refs_0_.refs_1_.refs_2_, ...), custom_call_target="tpu_custom_call" | custom-call | flops 1000000000 | tf_op jit(solution)/shard_map/second/pallas_call | solution.py:566
  27.4 7.2 %collective-permute-start.10 = (bf16[320,512]{1,0:T(8,128)(2,1)S(1)}, bf16[320,512]{1,0:T(8,128)(2,1)S(1)}, u32[]{:S(2)}, u32[]{:S(2)}) collective-permute-start(bf16[320,512]{1,0:T(8,128)(2,1)S(1)} %get-tuple-element.73), channel_id=1, source_target_pairs={{0,4},{4,0},{8,12},{12,8},{1,5},{5,1},{9,13},{13,9},{2,6},{6,2},{1... | collective-permute-start | bytes 983048 | tf_op jit(solution)/shard_map/ppermute | solution.py:616
  34.6 0.0 copy-start.17
  34.6 0.3 first.7.refs_6_
  34.9 0.1 collective-permute-start.9
  35.0 0.4 copy-done.4
  35.4 0.1 copy-done.7
  35.6 2.0 %candidates.1 = (f32[128,512]{1,0:T(8,128)S(1)}, f32[128,512]{1,0:T(8,128)S(1)}, f32[128,512]{1,0:T(8,128)S(1)}, f32[128,512]{1,0:T(8,128)S(1)}, f32[32,4096]{1,0:T(8,128)S(1)}, /*index=5*/f32[32,4096]{1,0:T(8,128)S(1)}) custom-call(bf16[1,32,4096]{2,1,0:T(8,128)(2,1)S(1)} %copy-done.7, bf16[1,32,4,256]{3,2,1,0:T(4,128)(2,1)S(1)} %copy-done.14, ...), custom_call_target="tpu_custom_call" | custom-call | tf_op jit(solution)/shard_map/candidates/pallas_call | solution.py:566
  37.6 0.0 collective-permute-done.11.refs_0_
  37.6 0.2 third.4
  37.8 0.0 collective-permute-done.12.refs_0_
  37.8 0.7 %second.7 = (f32[128,512]{1,0:T(8,128)S(1)}, f32[64,512]{1,0:T(8,128)S(1)}, bf16[192,512]{1,0:T(8,128)(2,1)S(1)}) custom-call(bf16[256,512]{1,0:T(8,128)(2,1)S(1)} %collective-permute-done.12.refs_0_, bf16[128,768]{1,0:T(8,128)(2,1)S(1)} %collective-permute-done.4.refs_0_.refs_1_.refs_2_, ...), custom_call_target="tpu_custom_call" | custom-call | flops 1000000000 | tf_op jit(solution)/shard_map/second/pallas_call | solution.py:566
  38.5 1.6 %collective-permute-start.14 = (bf16[192,512]{1,0:T(8,128)(2,1)S(1)}, bf16[192,512]{1,0:T(8,128)(2,1)S(1)}, u32[]{:S(2)}, u32[]{:S(2)}) collective-permute-start(bf16[192,512]{1,0:T(8,128)(2,1)S(1)} %get-tuple-element.85), channel_id=1, source_target_pairs={{0,4},{4,0},{8,12},{12,8},{1,5},{5,1},{9,13},{13,9},{2,6},{6,2},{1... | collective-permute-start | bytes 589832 | tf_op jit(solution)/shard_map/ppermute | solution.py:616
  40.3 0.1 collective-permute-start.15
  40.3 0.0 collective-permute-done.9.refs_0_
  40.3 0.6 %second.8.refs_9_ = bf16[192,512]{1,0:T(8,128)(2,1)S(1)} custom-call(bf16[256,512]{1,0:T(8,128)(2,1)S(1)} %collective-permute-done.9.refs_0_, bf16[128,512]{1,0:T(8,128)(2,1)S(1)} %collective-permute-done.3.refs_0_.refs_1_, bf16[128,768]{1,0:T(8,128)(2,1)S(1)} %collective-permute-done.4.refs_0_.refs_1_.refs_2_, ...), custom_call_target="tpu_custom_call" | custom-call | flops 1000000000 | tf_op jit(solution)/shard_map/second/pallas_call | solution.py:566
  40.9 2.9 %collective-permute-start.13 = (bf16[192,512]{1,0:T(8,128)(2,1)S(1)}, bf16[192,512]{1,0:T(8,128)(2,1)S(1)}, u32[]{:S(2)}, u32[]{:S(2)}) collective-permute-start(bf16[192,512]{1,0:T(8,128)(2,1)S(1)} %second.8.refs_9_), channel_id=1, source_target_pairs={{0,4},{4,0},{8,12},{12,8},{1,5},{5,1},{9,13},{13,9},{2,6},{6,2},{1... | collective-permute-start | bytes 589832 | tf_op jit(solution)/shard_map/ppermute | solution.py:616
  44.5 0.0 copy-start.5
  44.5 0.0 copy-start.6
  44.5 0.0 copy-start.10
  44.6 0.0 copy-start.15
  44.6 0.0 copy-start.16
  44.6 0.5 %second.9 = (f32[128,512]{1,0:T(8,128)S(1)}, f32[64,512]{1,0:T(8,128)S(1)}) custom-call(bf16[256,512]{1,0:T(8,128)(2,1)S(1)} %collective-permute-done.9.refs_0_, bf16[128,512]{1,0:T(8,128)(2,1)S(1)} %collective-permute-done.3.refs_0_.refs_1_, bf16[128,768]{1,0:T(8,128)(2,1)S(1)} %collective-permute-done.4.refs_0_.refs_1_.refs_2_, ...), custom_call_target="tpu_custom_call" | custom-call | flops 1000000000 | tf_op jit(solution)/shard_map/second/pallas_call | solution.py:566
  45.1 0.2 copy-done.5
  45.4 0.0 copy-done.6
  45.4 0.1 copy-done.10
  45.5 1.9 %attend.1 = (f32[8,128]{1,0:T(8,128)S(1)}, bf16[1,32,16,128]{3,2,1,0:T(8,128)(2,1)}) custom-call(s32[1]{0:T(128)S(6)} %copy.28.refs_0_, bf16[1,32,16,128]{3,2,1,0:T(8,128)(2,1)S(1)} %copy-done.10, bf16[1,32,2,128]{3,2,1,0:T(2,128)(2,1)S(1)} %copy-done.15, bf16[1,32,2,128]{3,2,1,0:T(2,128)(2,1)S(1)} %copy-done.16, bf16[128,2,128]{2,1,0:T(2,128)(2,1)S(1)} %copy-done.5, ...), custom_call_target="tpu_custom_call" | custom-call | tf_op jit(solution)/shard_map/attend/pallas_call | solution.py:566
  47.5 0.9 %prefix.2 = (f32[8,128]{1,0:T(8,128)S(1)}, bf16[128,2048]{1,0:T(8,128)(2,1)}) custom-call(bf16[208,512]{1,0:T(8,128)(2,1)S(1)} %collective-permute-done.11.refs_0_, bf16[320,512]{1,0:T(8,128)(2,1)S(1)} %collective-permute-done.10.refs_0_.refs_2_.refs_1_, bf16[192,512]{1,0:T(8,128)(2,1)S(1)} %collective-permute-done.14.refs_0_.refs_2_, ...), custom_call_target="tpu_custom_call" | custom-call | tf_op jit(solution)/shard_map/prefix/pallas_call | solution.py:566
  48.4 1.2 %collective-permute-done.13.refs_0_ = bf16[192,512]{1,0:T(8,128)(2,1)S(1)} collective-permute-done((bf16[192,512]{1,0:T(8,128)(2,1)S(1)}, bf16[192,512]{1,0:T(8,128)(2,1)S(1)}, u32[]{:S(2)}, u32[]{:S(2)}) %collective-permute-start.13) | collective-permute-done | bytes 196640 | tf_op jit(solution)/shard_map/ppermute | solution.py:616
  49.6 0.1 third.7
  49.7 0.1 collective-permute-start.16
  49.7 0.7 %prefix.3 = bf16[128,2048]{1,0:T(8,128)(2,1)} custom-call(bf16[192,512]{1,0:T(8,128)(2,1)S(1)} %collective-permute-done.13.refs_0_, f32[128,512]{1,0:T(8,128)S(1)} %get-tuple-element.81.refs_8_.refs_1_, f32[128,512]{1,0:T(8,128)S(1)} %get-tuple-element.82.refs_2_, f32[128,512]{1,0:T(8,128)S(1)} %get-tuple-element.83.refs_3_, ...), custom_call_target="tpu_custom_call", output_to_operand_aliasing={{}: (5, {})} | custom-call | tf_op jit(solution)/shard_map/prefix/pallas_call | solution.py:566
  50.5 0.6 %collective-permute-done.16.refs_4_ = bf16[32,2048]{1,0:T(8,128)(2,1)S(1)} collective-permute-done((bf16[32,2048]{1,0:T(8,128)(2,1)S(1)}, bf16[32,2048]{1,0:T(8,128)(2,1)S(1)}, u32[]{:S(2)}, u32[]{:S(2)}) %collective-permute-start.16) | collective-permute-done | bytes 131104 | tf_op jit(solution)/shard_map/ppermute | solution.py:613
  51.1 0.8 %close.1 = bf16[1,32,4096]{2,1,0:T(8,128)(2,1)} custom-call(s32[1]{0:T(128)S(6)} %copy.28.refs_0_, f32[32,4096]{1,0:T(8,128)S(1)} %get-tuple-element.77.refs_3_.refs_1_, f32[32,4096]{1,0:T(8,128)S(1)} %get-tuple-element.96.refs_2_, f32[32,2048]{1,0:T(8,128)S(1)} %get-tuple-element.94.refs_4_.refs_3_, bf16[32,2048]{1,0:T(8,128)(2,1)S(1)} %collective-permute-done.16.refs_4_), custom_call_target="tpu_custom_call" | custom-call | tf_op jit(solution)/shard_map/close/pallas_call | solution.py:566
  (34 shorter events, 0.2 us)
Async XLA Ops:
  0.6 6.2 %collective-permute-start = (bf16[1,32,4,256]{3,2,1,0:T(4,128)(2,1)}, bf16[1,32,4,256]{3,2,1,0:T(4,128)(2,1)S(1)}, u32[]{:S(2)}, u32[]{:S(2)}) collective-permute-start(bf16[1,32,4,256]{3,2,1,0:T(4,128)(2,1)} %refs_2_.2), channel_id=1, source_target_pairs={{0,1},{1,0},{2,3},{3,2},{4,5},{5,4},{6,7},{7,6},{8,9},{9,8},{10,11... | collective-permute-start | bytes 196616 | tf_op jit(solution)/shard_map/ppermute | solution.py:613
  1.1 5.7 %copy-start.8 = (bf16[1,32,4,256]{3,2,1,0:T(4,128)(2,1)S(1)}, bf16[1,32,4,256]{3,2,1,0:T(4,128)(2,1)}, u32[]{:S(2)}) copy-start(bf16[1,32,4,256]{3,2,1,0:T(4,128)(2,1)} %refs_2_.2) | copy-start | bytes 196612
  1.2 5.7 %copy-start.13 = (bf16[128,2,256]{2,1,0:T(2,128)(2,1)S(1)}, bf16[128,2,256]{2,1,0:T(2,128)(2,1)}, u32[]{:S(2)}) copy-start(bf16[128,2,256]{2,1,0:T(2,128)(2,1)} %refs_0_.7) | copy-start | bytes 393220
  1.2 7.1 %copy-start = (bf16[128,2048]{1,0:T(8,128)(2,1)S(1)}, bf16[128,2048]{1,0:T(8,128)(2,1)}, u32[]{:S(2)}) copy-start(bf16[128,2048]{1,0:T(8,128)(2,1)} %refs_0_.8) | copy-start | bytes 1572868
  4.1 9.2 %collective-permute-start.2 = (bf16[144,768]{1,0:T(8,128)(2,1)}, bf16[144,768]{1,0:T(8,128)(2,1)S(1)}, u32[]{:S(2)}, u32[]{:S(2)}) collective-permute-start(bf16[144,768]{1,0:T(8,128)(2,1)} %get-tuple-element.55.refs_2_.refs_3_.refs_4_), channel_id=1, source_target_pairs={{0,4},{4,0},{8,12},{12,8},{1,5},{5,1},{9,13},{13,9},{2,6},{6,2},{1... | collective-permute-start | bytes 663560 | tf_op jit(solution)/shard_map/ppermute | solution.py:616
  6.8 0.8 %copy-start.3 = (f32[128,32]{1,0:T(8,128)S(1)}, f32[128,32]{1,0:T(8,128)}, u32[]{:S(2)}) copy-start(f32[128,32]{1,0:T(8,128)} %get-tuple-element.52.refs_3_.refs_5_) | copy-start | bytes 49156
  7.7 0.9 %copy-start.9 = (bf16[128,768]{1,0:T(8,128)(2,1)S(1)}, bf16[128,768]{1,0:T(8,128)(2,1)}, u32[]{:S(2)}) copy-start(bf16[128,768]{1,0:T(8,128)(2,1)} %get-tuple-element.53.refs_6_) | copy-start | bytes 589828
  7.7 1.0 %copy-start.12 = (bf16[128,512]{1,0:T(8,128)(2,1)S(1)}, bf16[128,512]{1,0:T(8,128)(2,1)}, u32[]{:S(2)}) copy-start(bf16[128,512]{1,0:T(8,128)(2,1)} %get-tuple-element.51.refs_1_) | copy-start | bytes 393220
  8.2 0.7 %copy-start.19 = (f32[128]{0:T(128)S(1)}, f32[128]{0:T(128)}, u32[]{:S(2)}) copy-start(f32[128]{0:T(128)} %param.19) | copy-start | bytes 1540
  8.9 4.4 %copy-start.2 = (bf16[144,768]{1,0:T(8,128)(2,1)S(1)}, bf16[144,768]{1,0:T(8,128)(2,1)}, u32[]{:S(2)}) copy-start(bf16[144,768]{1,0:T(8,128)(2,1)} %get-tuple-element.55.refs_2_.refs_3_.refs_4_) | copy-start | bytes 663556
  9.9 3.4 %copy-start.18 = (f32[8,32]{1,0:T(8,128)S(1)}, f32[8,32]{1,0:T(8,128)}, u32[]{:S(2)}) copy-start(f32[8,32]{1,0:T(8,128)} %get-tuple-element.57.refs_4_.refs_8_) | copy-start | bytes 3076
  10.0 7.4 %collective-permute-start.1 = (bf16[128,768]{1,0:T(8,128)(2,1)S(1)}, bf16[128,768]{1,0:T(8,128)(2,1)S(1)}, u32[]{:S(2)}, u32[]{:S(2)}) collective-permute-start(bf16[128,768]{1,0:T(8,128)(2,1)S(1)} %get-tuple-element.54.refs_2_.refs_3_), channel_id=1, source_target_pairs={{0,4},{4,0},{8,12},{12,8},{1,5},{5,1},{9,13},{13,9},{2,6},{6,2},{1... | collective-permute-start | bytes 589832 | tf_op jit(solution)/shard_map/ppermute | solution.py:616
  13.3 4.1 %copy-start.1 = (bf16[128,768]{1,0:T(8,128)(2,1)S(1)}, bf16[128,768]{1,0:T(8,128)(2,1)}, u32[]{:S(2)}) copy-start(bf16[128,768]{1,0:T(8,128)(2,1)} %get-tuple-element.62.refs_8_) | copy-start | bytes 589828
  13.3 4.1 %copy-start.11 = (bf16[128,512]{1,0:T(8,128)(2,1)S(1)}, bf16[128,512]{1,0:T(8,128)(2,1)}, u32[]{:S(2)}) copy-start(bf16[128,512]{1,0:T(8,128)(2,1)} %get-tuple-element.63.refs_9_) | copy-start | bytes 393220
  13.3 4.1 %copy-start.20 = (bf16[128,256]{1,0:T(8,128)(2,1)S(1)}, bf16[128,256]{1,0:T(8,128)(2,1)}, u32[]{:S(2)}) copy-start(bf16[128,256]{1,0:T(8,128)(2,1)} %get-tuple-element.60.refs_6_) | copy-start | bytes 196612
  13.7 11.6 %collective-permute-start.8 = (bf16[272,512]{1,0:T(8,128)(2,1)S(1)}, bf16[272,512]{1,0:T(8,128)(2,1)S(1)}, u32[]{:S(2)}, u32[]{:S(2)}) collective-permute-start(bf16[272,512]{1,0:T(8,128)(2,1)S(1)} %get-tuple-element.61.refs_7_), channel_id=1, source_target_pairs={{0,1},{1,0},{4,8},{5,9},{8,4},{9,5},{12,13},{13,12},{2,3},{3,2},{6... | collective-permute-start | bytes 835592 | tf_op jit(solution)/shard_map/ppermute | solution.py:624
  13.8 7.8 %collective-permute-start.6 = (bf16[192,512]{1,0:T(8,128)(2,1)S(1)}, bf16[192,512]{1,0:T(8,128)(2,1)S(1)}, u32[]{:S(2)}, u32[]{:S(2)}) collective-permute-start(bf16[192,512]{1,0:T(8,128)(2,1)S(1)} %get-tuple-element.67.refs_6_), channel_id=1, source_target_pairs={{0,4},{4,0},{8,12},{12,8},{1,5},{5,1},{9,13},{13,9},{2,6},{6,2},{1... | collective-permute-start | bytes 589832 | tf_op jit(solution)/shard_map/ppermute | solution.py:616
  17.7 8.9 %collective-permute-start.5 = (bf16[256,512]{1,0:T(8,128)(2,1)S(1)}, bf16[256,512]{1,0:T(8,128)(2,1)S(1)}, u32[]{:S(2)}, u32[]{:S(2)}) collective-permute-start(bf16[256,512]{1,0:T(8,128)(2,1)S(1)} %get-tuple-element.66.refs_10_), channel_id=1, source_target_pairs={{0,1},{1,0},{4,8},{5,9},{8,4},{9,5},{12,13},{13,12},{2,3},{3,2},{6... | collective-permute-start | bytes 786440 | tf_op jit(solution)/shard_map/ppermute | solution.py:624
  17.8 8.4 %collective-permute-start.4 = (bf16[128,768]{1,0:T(8,128)(2,1)S(1)}, bf16[128,768]{1,0:T(8,128)(2,1)S(1)}, u32[]{:S(2)}, u32[]{:S(2)}) collective-permute-start(bf16[128,768]{1,0:T(8,128)(2,1)S(1)} %get-tuple-element.65.refs_2_.refs_3_.refs_4_), channel_id=1, source_target_pairs={{0,4},{4,0},{8,12},{12,8},{1,5},{5,1},{9,13},{13,9},{2,6},{6,2},{1... | collective-permute-start | bytes 589832 | tf_op jit(solution)/shard_map/ppermute | solution.py:616
  21.3 5.3 %collective-permute-start.7 = (bf16[256,256]{1,0:T(8,128)(2,1)S(1)}, bf16[256,256]{1,0:T(8,128)(2,1)S(1)}, u32[]{:S(2)}, u32[]{:S(2)}) collective-permute-start(bf16[256,256]{1,0:T(8,128)(2,1)S(1)} %get-tuple-element.68.refs_0_), channel_id=1, source_target_pairs={{0,1},{1,0},{4,8},{5,9},{8,4},{9,5},{12,13},{13,12},{2,3},{3,2},{6... | collective-permute-start | bytes 393224 | tf_op jit(solution)/shard_map/ppermute | solution.py:624
  21.7 12.9 %collective-permute-start.3 = (bf16[128,512]{1,0:T(8,128)(2,1)S(1)}, bf16[128,512]{1,0:T(8,128)(2,1)S(1)}, u32[]{:S(2)}, u32[]{:S(2)}) collective-permute-start(bf16[128,512]{1,0:T(8,128)(2,1)S(1)} %get-tuple-element.64.refs_2_.refs_3_), channel_id=1, source_target_pairs={{0,4},{12,8},{1,5},{13,9},{2,6},{14,10},{3,7},{15,11},{16,20},{28,... | collective-permute-start | bytes 393224 | tf_op jit(solution)/shard_map/ppermute | solution.py:627
  26.1 11.5 %collective-permute-start.11 = (bf16[208,512]{1,0:T(8,128)(2,1)S(1)}, bf16[208,512]{1,0:T(8,128)(2,1)S(1)}, u32[]{:S(2)}, u32[]{:S(2)}) collective-permute-start(bf16[208,512]{1,0:T(8,128)(2,1)S(1)} %get-tuple-element.75), channel_id=1, source_target_pairs={{0,4},{4,0},{8,12},{12,8},{1,5},{5,1},{9,13},{13,9},{2,6},{6,2},{1... | collective-permute-start | bytes 638984 | tf_op jit(solution)/shard_map/ppermute | solution.py:616
  26.6 11.2 %collective-permute-start.12 = (bf16[256,512]{1,0:T(8,128)(2,1)S(1)}, bf16[256,512]{1,0:T(8,128)(2,1)S(1)}, u32[]{:S(2)}, u32[]{:S(2)}) collective-permute-start(bf16[256,512]{1,0:T(8,128)(2,1)S(1)} %first.6.refs_10_), channel_id=1, source_target_pairs={{0,1},{1,0},{4,8},{5,9},{8,4},{9,5},{12,13},{13,12},{2,3},{3,2},{6... | collective-permute-start | bytes 786440 | tf_op jit(solution)/shard_map/ppermute | solution.py:624
  27.4 12.8 %collective-permute-start.10 = (bf16[320,512]{1,0:T(8,128)(2,1)S(1)}, bf16[320,512]{1,0:T(8,128)(2,1)S(1)}, u32[]{:S(2)}, u32[]{:S(2)}) collective-permute-start(bf16[320,512]{1,0:T(8,128)(2,1)S(1)} %get-tuple-element.73), channel_id=1, source_target_pairs={{0,4},{4,0},{8,12},{12,8},{1,5},{5,1},{9,13},{13,9},{2,6},{6,2},{1... | collective-permute-start | bytes 983048 | tf_op jit(solution)/shard_map/ppermute | solution.py:616
  34.6 0.8 %copy-start.4 = (f32[128,32]{1,0:T(8,128)S(1)}, f32[128,32]{1,0:T(8,128)}, u32[]{:S(2)}) copy-start(f32[128,32]{1,0:T(8,128)} %get-tuple-element.52.refs_3_.refs_5_) | copy-start | bytes 49156
  34.6 1.0 %copy-start.7 = (bf16[1,32,4096]{2,1,0:T(8,128)(2,1)S(1)}, bf16[1,32,4096]{2,1,0:T(8,128)(2,1)}, u32[]{:S(2)}) copy-start(bf16[1,32,4096]{2,1,0:T(8,128)(2,1)} %refs_0_.9) | copy-start | bytes 786436
  34.6 1.0 %copy-start.14 = (bf16[1,32,4,256]{3,2,1,0:T(4,128)(2,1)S(1)}, bf16[1,32,4,256]{3,2,1,0:T(4,128)(2,1)}, u32[]{:S(2)}) copy-start(bf16[1,32,4,256]{3,2,1,0:T(4,128)(2,1)} %refs_1_.6) | copy-start | bytes 196612
  34.6 1.0 %copy-start.17 = (f32[1,32,64]{2,1,0:T(8,128)S(1)}, f32[1,32,64]{2,1,0:T(8,128)}, u32[]{:S(2)}) copy-start(f32[1,32,64]{2,1,0:T(8,128)} %refs_3_.4) | copy-start | bytes 24580
  34.9 5.4 %collective-permute-start.9 = (bf16[256,512]{1,0:T(8,128)(2,1)S(1)}, bf16[256,512]{1,0:T(8,128)(2,1)S(1)}, u32[]{:S(2)}, u32[]{:S(2)}) collective-permute-start(bf16[256,512]{1,0:T(8,128)(2,1)S(1)} %first.7.refs_6_), channel_id=1, source_target_pairs={{0,1},{1,0},{4,8},{5,9},{8,4},{9,5},{12,13},{13,12},{2,3},{3,2},{6... | collective-permute-start | bytes 786440 | tf_op jit(solution)/shard_map/ppermute | solution.py:624
  38.5 8.9 %collective-permute-start.14 = (bf16[192,512]{1,0:T(8,128)(2,1)S(1)}, bf16[192,512]{1,0:T(8,128)(2,1)S(1)}, u32[]{:S(2)}, u32[]{:S(2)}) collective-permute-start(bf16[192,512]{1,0:T(8,128)(2,1)S(1)} %get-tuple-element.85), channel_id=1, source_target_pairs={{0,4},{4,0},{8,12},{12,8},{1,5},{5,1},{9,13},{13,9},{2,6},{6,2},{1... | collective-permute-start | bytes 589832 | tf_op jit(solution)/shard_map/ppermute | solution.py:616
  40.3 4.9 %collective-permute-start.15 = (bf16[384,256]{1,0:T(8,128)(2,1)S(1)}, bf16[384,256]{1,0:T(8,128)(2,1)S(1)}, u32[]{:S(2)}, u32[]{:S(2)}) collective-permute-start(bf16[384,256]{1,0:T(8,128)(2,1)S(1)} %collect.1.refs_9_.refs_6_), channel_id=1, source_target_pairs={{0,1},{1,0},{2,3},{3,2},{4,5},{5,4},{6,7},{7,6},{8,9},{9,8},{10,11... | collective-permute-start | bytes 589832 | tf_op jit(solution)/shard_map/ppermute | solution.py:613
  40.9 8.7 %collective-permute-start.13 = (bf16[192,512]{1,0:T(8,128)(2,1)S(1)}, bf16[192,512]{1,0:T(8,128)(2,1)S(1)}, u32[]{:S(2)}, u32[]{:S(2)}) collective-permute-start(bf16[192,512]{1,0:T(8,128)(2,1)S(1)} %second.8.refs_9_), channel_id=1, source_target_pairs={{0,4},{4,0},{8,12},{12,8},{1,5},{5,1},{9,13},{13,9},{2,6},{6,2},{1... | collective-permute-start | bytes 589832 | tf_op jit(solution)/shard_map/ppermute | solution.py:616
  44.5 0.8 %copy-start.5 = (bf16[128,2,128]{2,1,0:T(2,128)(2,1)S(1)}, bf16[128,2,128]{2,1,0:T(2,128)(2,1)}, u32[]{:S(2)}) copy-start(bf16[128,2,128]{2,1,0:T(2,128)(2,1)} %refs_4_.3) | copy-start | bytes 196612
  44.5 0.9 %copy-start.6 = (bf16[128,2,128]{2,1,0:T(2,128)(2,1)S(1)}, bf16[128,2,128]{2,1,0:T(2,128)(2,1)}, u32[]{:S(2)}) copy-start(bf16[128,2,128]{2,1,0:T(2,128)(2,1)} %refs_5_.1) | copy-start | bytes 196612
  44.5 1.0 %copy-start.10 = (bf16[1,32,16,128]{3,2,1,0:T(8,128)(2,1)S(1)}, bf16[1,32,16,128]{3,2,1,0:T(8,128)(2,1)}, u32[]{:S(2)}) copy-start(bf16[1,32,16,128]{3,2,1,0:T(8,128)(2,1)} %refs_1_.7) | copy-start | bytes 393220
  44.6 0.9 %copy-start.15 = (bf16[1,32,2,128]{3,2,1,0:T(2,128)(2,1)S(1)}, bf16[1,32,2,128]{3,2,1,0:T(2,128)(2,1)}, u32[]{:S(2)}) copy-start(bf16[1,32,2,128]{3,2,1,0:T(2,128)(2,1)} %refs_2_.3) | copy-start | bytes 49156
  44.6 0.9 %copy-start.16 = (bf16[1,32,2,128]{3,2,1,0:T(2,128)(2,1)S(1)}, bf16[1,32,2,128]{3,2,1,0:T(2,128)(2,1)}, u32[]{:S(2)}) copy-start(bf16[1,32,2,128]{3,2,1,0:T(2,128)(2,1)} %refs_3_.5) | copy-start | bytes 49156
  49.7 1.4 %collective-permute-start.16 = (bf16[32,2048]{1,0:T(8,128)(2,1)S(1)}, bf16[32,2048]{1,0:T(8,128)(2,1)S(1)}, u32[]{:S(2)}, u32[]{:S(2)}) collective-permute-start(bf16[32,2048]{1,0:T(8,128)(2,1)S(1)} %get-tuple-element.97), channel_id=1, source_target_pairs={{0,1},{1,0},{2,3},{3,2},{4,5},{5,4},{6,7},{7,6},{8,9},{9,8},{10,11... | collective-permute-start | bytes 393224 | tf_op jit(solution)/shard_map/ppermute | solution.py:613
